TPU v7x, 256 devices: a whole 4x4x8 slice. The times are simulated.
256 devices in a mesh: row: 16 (over z, core), col: 16 (over y, x).
Axes of the slice: x: 4, y: 4, z: 8, core: 2. Of those that a mesh axis runs over, the one named last changes fastest.
Arguments:
- a_blocks: bfloat16 [256, 32, 128, 128], P('row', 'col'), may hold values from -0.5 to 0.5
- a_cols: int32 [256, 32], P('row', 'col'), may hold values from 0 to 255, as said below
- p_blocks: bfloat16 [256, 2, 128, 128], P(('row', 'col')), may hold values from -0.5 to 0.5
- p_aggs: int32 [256, 2], replicated, may hold values from 0 to 31, as said below
- agglo: int32 [32], replicated, may hold values from 0 to 31, as said below
Outputs:
- coarse_operator: float32 [32, 128, 6, 128], P('row', 'col')
Inputs may be any that keep to these rules, and one draw needn't show every extreme that they name: `a_cols`: the entries of a block row are distinct, include the block row itself, and lie in block rows of the groups g - 1, g and g + 1 of the row's group g, groups of 16 block rows. `p_aggs`: each aggregate holds exactly 8 block rows, all of one group; the first entry of a block row is its own aggregate, the others are distinct further aggregates of the same group. `agglo`: within each group the 2 aggregates go to the group's 2 coarse block rows one to one.
All inputs are finite; a program needn't handle non-finite values.
Results may differ from a plain program's by a relative error of at most 0.0003.
Values may be sent and summed in bfloat16 or wider, within the bound.
No kernel may reach another device: no remote copies, remote signals or barrier semaphores. Data moves between devices by JAX's collectives and lax.ppermute only.
A program may use at most 64 MiB of HBM per device.

v0:
```python
import jax
import jax.numpy as jnp
from jax import lax
from jax.sharding import PartitionSpec as P

AGG = 8


def padded(shard, sides, width):
    for axis, dim in sides:
        count, length = (lax.axis_size(axis), shard.shape[dim])
        up = [(i, (i + 1) % count) for i in range(count - 1)]
        down = [(j, i) for i, j in up]
        last = lax.slice_in_dim(shard, length - width, length, axis=dim)
        leading = lax.slice_in_dim(shard, 0, width, axis=dim)
        before = lax.ppermute(last, axis, up)
        after = lax.ppermute(leading, axis, down)
        shard = jnp.concatenate([before, shard, after], axis=dim)
    return shard


def local(a_blocks, a_cols, p_blocks, p_aggs, agglo):
    highest = lax.Precision.HIGHEST
    stride_rows = 4
    row_count = a_cols.shape[0]
    block_width = a_blocks.shape[2]
    coarse_count = row_count // AGG
    band_width = 3 * coarse_count
    row_index = lax.axis_index("row")
    coarse_ids = agglo[p_aggs]
    gathered = lax.all_gather(p_blocks, "col", axis=0, tiled=True)
    nearby = padded(gathered, (("row", 0),), row_count)
    fetched = nearby[a_cols - (row_index - 1) * row_count]
    column_band = coarse_ids[a_cols] - (row_index - 1) * coarse_count
    row_coarse = (
        lax.dynamic_slice_in_dim(coarse_ids, row_index * row_count, row_count, 0)
        - row_index * coarse_count
    )
    targets = row_coarse[:, :, None, None] * band_width + column_band[:, None, :, :]
    products = jnp.einsum(
        "isab,isrbc->israc", a_blocks, fetched, preferred_element_type=jnp.float32
    )

    def accumulate(block_index, partial_value):
        first_row = block_index * stride_rows
        own_rows = lax.dynamic_slice_in_dim(gathered, first_row, stride_rows, 0)
        own_cut = own_rows.astype(jnp.float32)
        product_rows = lax.dynamic_slice_in_dim(products, first_row, stride_rows, 0)
        lifted = jnp.einsum("iqab,israc->iqsrbc", own_cut, product_rows, precision=highest)
        target_rows = lax.dynamic_slice_in_dim(targets, first_row, stride_rows, 0).reshape(-1)
        return partial_value.at[target_rows].add(lifted.reshape(-1, block_width, block_width))

    zero_term = jnp.zeros((coarse_count * band_width, block_width, block_width), jnp.float32)
    summed = lax.fori_loop(0, row_count // stride_rows, accumulate, zero_term)
    summed = summed.reshape(coarse_count, band_width, block_width, block_width).transpose(
        2, 0, 1, 3
    )
    coarse_share = lax.psum_scatter(
        summed.reshape(block_width, coarse_count, band_width * block_width),
        "col",
        scatter_dimension=0,
        tiled=True,
    )
    coarse_share = coarse_share.reshape(
        coarse_share.shape[0], coarse_count, band_width, block_width
    )
    return coarse_share.transpose(1, 0, 2, 3)


def solution(mesh):
    placed = (
        P("row", "col", None, None),
        P("row", "col"),
        P(("row", "col"), None, None, None),
        P(),
        P(),
    )
    return jax.shard_map(
        local, mesh=mesh, in_specs=placed, out_specs=P("row", "col", None, None), check_vma=False
    )
```

profile of v0, /device:TPU:96, one launch (start us, length us, event | category | flops | bytes accessed | tf_op | source)
XLA Modules:
  0.0 251.6 jit_solution(5809291009614186306)
XLA Ops:
  7.3 1.8 fusion.9
  9.1 2.1 fusion.8
  11.2 48.2 %all-gather.2.cloned.1.call-done = bf16[16,2,128,128]{3,2,1,0:T(8,128)(2,1)} async-done(((bf16[1,2,128,128]{3,2,1,0:T(8,128)(2,1)}), bf16[16,2,128,128]{3,2,1,0:T(8,128)(2,1)}) %all-gather.2.cloned.1.call-update) | async-done | bytes 1048592 | tf_op jit(solution)/shard_map/all_gather | solution.py:31
  59.4 1.9 collective-permute-start
  61.3 3.6 %collective-permute-start.1 = (bf16[16,2,128,128]{3,2,1,0:T(8,128)(2,1)}, bf16[16,2,128,128]{3,2,1,0:T(8,128)(2,1)S(1)}, u32[]{:S(2)}, u32[]{:S(2)}) collective-permute-start(bf16[16,2,128,128]{3,2,1,0:T(8,128)(2,1)} %all-gather.2.cloned.1.call-done), channel_id=1, source_target_pairs={{16,0},{32,16},{48,32},{64,48},{80,64},{96,80},{112,96},{128,112},... | collective-permute-start | bytes 3145736 | tf_op jit(solution)/shard_map/ppermute | solution.py:17
  65.0 20.8 %compare_select_fusion.2 = s32[256,2]{0,1:T(2,128)S(1)} fusion(s32[256,2]{0,1:T(2,128)} %param.10, s32[]{:T(128)} %bitcast.7, s32[]{:T(128)} %bitcast.8, s32[]{:T(128)} %bitcast.9, s32[]{:T(128)} %bitcast.10, s32[]{:T(128)} %bitcast.11, s32[]{:T(128)} %bitcast.12, s32[]{:T(128)} %bitcast.13, s32[]{:T(128)} %bitcast.14, s32[]{:T(128)} %bitcast.15, ...), kind=kLoop, calls=%fused_computation.20 | loop fusion | flops 33280 | bytes 4224 | tf_op jit(solution)/shard_map/gather | solution.py:30
  87.9 2.9 %pad_maximum_fusion = bf16[48,2,128,128]{3,2,1,0:T(8,128)(2,1)} fusion(bf16[16,2,128,128]{3,2,1,0:T(8,128)(2,1)S(1)} %collective-permute-done.1, bf16[16,2,128,128]{3,2,1,0:T(8,128)(2,1)} %all-gather.2.cloned.1.call-done, bf16[16,2,128,128]{3,2,1,0:T(8,128)(2,1)S(1)} %collective-permute-done), kind=kLoop, calls=%fused_computation.12 | loop fusion | flops 3145728 | bytes 6291456 | tf_op jit(solution)/shard_map/concatenate | solution.py:18
  90.8 2.8 %gather_fusion.1 = bf16[32,2,128,128]{3,2,1,0:T(8,128)(2,1)S(1)} fusion(bf16[48,2,128,128]{3,2,1,0:T(8,128)(2,1)} %pad_maximum_fusion, s32[1024]{0:T(1024)S(1)} %pad_clamp_fusion), kind=kCustom, calls=%fused_computation.1 | custom fusion | bytes 4194432 | tf_op jit(solution)/shard_map/gather | solution.py:33
  93.7 2.7 %convolution_bitcast_fusion.1 = f32[16,2,2,128,128]{3,4,2,1,0:T(8,128)} fusion(bf16[16,2,2,128,128]{4,3,2,1,0:T(8,128)(2,1)S(1)} %bitcast.77, bf16[16,2,128,128]{3,2,1,0:T(8,128)(2,1)S(1)} %copy-done), kind=kOutput, calls=%fused_computation.13 | convolution fusion | flops 268435456 | bytes 7340032 | tf_op jit(solution)/shard_map/isab,isrbc->israc/dot_general | solution.py:40
  97.3 46.6 %while.13 = (s32[]{:T(128)}, f32[12,128,128]{2,1,0:T(8,128)}, s32[16,2,2,2]{3,2,1,0:T(2,128)S(1)}, f32[16,2,2,128,128]{3,4,2,1,0:T(8,128)}, bf16[16,2,128,128]{3...) while((s32[]{:T(128)}, f32[12,128,128]{2,1,0:T(8,128)}, ...), condition=%wide.region_2.0_spmd, body=%wide.region_0.0_spmd.sunk | while | flops 805830784 | bytes 13895695 | solution.py:54
  97.3 3.6 %convolution_bitcast_fusion.3 = f32[4,2,2,2,128,128]{4,5,1,3,2,0:T(8,128)} fusion(f32[16,2,2,128,128]{3,4,2,1,0:T(8,128)} %get-tuple-element.196, s32[]{:T(128)S(6)} %select_n.50, bf16[16,2,128,128]{3,2,1,0:T(8,128)(2,1)} %get-tuple-element.197), kind=kOutput, calls=%fused_computation.3.clone.1 | convolution fusion | flops 805306368 | bytes 3408896 | tf_op jit(solution)/shard_map/while/body/eval_jaxpr/iqab,israc->iqsrbc/dot_general | solution.py:49
  100.9 1.9 copy.64
  102.9 6.1 %scatter_fusion = f32[12,128,128]{2,1,0:T(8,128)} fusion(f32[12,128,128]{2,1,0:T(8,128)} %get-tuple-element.185, s32[32]{0:T(128)S(1)} %fusion.16, f32[32,128,128]{2,1,0:T(8,128)S(1)} %bitcast.76), kind=kCustom, calls=%fused_computation.2.clone.1 | custom fusion | flops 524288 | bytes 6291584 | tf_op jit(solution)/shard_map/while/body/eval_jaxpr/scatter-add | solution.py:51
  109.0 3.6 %convolution_bitcast_fusion.3 = f32[4,2,2,2,128,128]{4,5,1,3,2,0:T(8,128)} fusion(f32[16,2,2,128,128]{3,4,2,1,0:T(8,128)} %get-tuple-element.196, s32[]{:T(128)S(6)} %select_n.50, bf16[16,2,128,128]{3,2,1,0:T(8,128)(2,1)} %get-tuple-element.197), kind=kOutput, calls=%fused_computation.3.clone.1 | convolution fusion | flops 805306368 | bytes 3408896 | tf_op jit(solution)/shard_map/while/body/eval_jaxpr/iqab,israc->iqsrbc/dot_general | solution.py:49
  112.5 1.9 copy.64
  114.6 6.0 %scatter_fusion = f32[12,128,128]{2,1,0:T(8,128)} fusion(f32[12,128,128]{2,1,0:T(8,128)} %get-tuple-element.185, s32[32]{0:T(128)S(1)} %fusion.16, f32[32,128,128]{2,1,0:T(8,128)S(1)} %bitcast.76), kind=kCustom, calls=%fused_computation.2.clone.1 | custom fusion | flops 524288 | bytes 6291584 | tf_op jit(solution)/shard_map/while/body/eval_jaxpr/scatter-add | solution.py:51
  120.6 3.6 %convolution_bitcast_fusion.3 = f32[4,2,2,2,128,128]{4,5,1,3,2,0:T(8,128)} fusion(f32[16,2,2,128,128]{3,4,2,1,0:T(8,128)} %get-tuple-element.196, s32[]{:T(128)S(6)} %select_n.50, bf16[16,2,128,128]{3,2,1,0:T(8,128)(2,1)} %get-tuple-element.197), kind=kOutput, calls=%fused_computation.3.clone.1 | convolution fusion | flops 805306368 | bytes 3408896 | tf_op jit(solution)/shard_map/while/body/eval_jaxpr/iqab,israc->iqsrbc/dot_general | solution.py:49
  124.2 1.9 copy.64
  126.2 6.0 %scatter_fusion = f32[12,128,128]{2,1,0:T(8,128)} fusion(f32[12,128,128]{2,1,0:T(8,128)} %get-tuple-element.185, s32[32]{0:T(128)S(1)} %fusion.16, f32[32,128,128]{2,1,0:T(8,128)S(1)} %bitcast.76), kind=kCustom, calls=%fused_computation.2.clone.1 | custom fusion | flops 524288 | bytes 6291584 | tf_op jit(solution)/shard_map/while/body/eval_jaxpr/scatter-add | solution.py:51
  132.2 3.6 %convolution_bitcast_fusion.3 = f32[4,2,2,2,128,128]{4,5,1,3,2,0:T(8,128)} fusion(f32[16,2,2,128,128]{3,4,2,1,0:T(8,128)} %get-tuple-element.196, s32[]{:T(128)S(6)} %select_n.50, bf16[16,2,128,128]{3,2,1,0:T(8,128)(2,1)} %get-tuple-element.197), kind=kOutput, calls=%fused_computation.3.clone.1 | convolution fusion | flops 805306368 | bytes 3408896 | tf_op jit(solution)/shard_map/while/body/eval_jaxpr/iqab,israc->iqsrbc/dot_general | solution.py:49
  135.8 1.9 copy.64
  137.8 6.1 %scatter_fusion = f32[12,128,128]{2,1,0:T(8,128)} fusion(f32[12,128,128]{2,1,0:T(8,128)} %get-tuple-element.185, s32[32]{0:T(128)S(1)} %fusion.16, f32[32,128,128]{2,1,0:T(8,128)S(1)} %bitcast.76), kind=kCustom, calls=%fused_computation.2.clone.1 | custom fusion | flops 524288 | bytes 6291584 | tf_op jit(solution)/shard_map/while/body/eval_jaxpr/scatter-add | solution.py:51
  143.9 1.4 copy.53
  147.8 95.5 %all-reduce.3.cloned.1.call-done = f32[128,2,768]{2,1,0:T(2,128)} async-done(((f32[128,2,768]{2,1,0:T(2,128)}), f32[128,2,768]{2,1,0:T(2,128)}) %all-reduce.3.cloned.1.call-update) | async-done | bytes 786448
  (42 shorter events, 7.4 us)
Async XLA Ops:
  6.5 87.1 %copy-start = (bf16[16,2,128,128]{3,2,1,0:T(8,128)(2,1)S(1)}, bf16[16,2,128,128]{3,2,1,0:T(8,128)(2,1)}, u32[]{:S(2)}) copy-start(bf16[16,2,128,128]{3,2,1,0:T(8,128)(2,1)} %param.7) | copy-start | bytes 3145732
  6.5 52.9 %all-gather.2.cloned.1.call-start = ((), (), s32[]{:S(2)}) async-start(), calls=%async_computation | async-start | bytes 1114112 | tf_op jit(solution)/shard_map/all_gather | solution.py:31
  7.3 236.0 %all-reduce.3.cloned.1.call-start = ((), (), s32[]{:S(2)}) async-start(), calls=%async_computation.1 | async-start | bytes 1572864
  59.4 28.4 %collective-permute-start = (bf16[16,2,128,128]{3,2,1,0:T(8,128)(2,1)}, bf16[16,2,128,128]{3,2,1,0:T(8,128)(2,1)S(1)}, u32[]{:S(2)}, u32[]{:S(2)}) collective-permute-start(bf16[16,2,128,128]{3,2,1,0:T(8,128)(2,1)} %all-gather.2.cloned.1.call-done), channel_id=1, source_target_pairs={{0,16},{16,32},{32,48},{48,64},{64,80},{80,96},{96,112},{112,128},... | collective-permute-start | bytes 3145736 | tf_op jit(solution)/shard_map/ppermute | solution.py:16
  61.3 26.5 %collective-permute-start.1 = (bf16[16,2,128,128]{3,2,1,0:T(8,128)(2,1)}, bf16[16,2,128,128]{3,2,1,0:T(8,128)(2,1)S(1)}, u32[]{:S(2)}, u32[]{:S(2)}) collective-permute-start(bf16[16,2,128,128]{3,2,1,0:T(8,128)(2,1)} %all-gather.2.cloned.1.call-done), channel_id=1, source_target_pairs={{16,0},{32,16},{48,32},{64,48},{80,64},{96,80},{112,96},{128,112},... | collective-permute-start | bytes 3145736 | tf_op jit(solution)/shard_map/ppermute | solution.py:17
  143.9 2.6 %copy-start.1 = (u32[256]{0:T(256)S(1)}, u32[256]{0:T(256)}, u32[]{:S(2)}) copy-start(u32[256]{0:T(256)} %constant.100) | copy-start | bytes 3076
Sparse Core Ops, SparseCore 0:
  9.8 49.5 all-gather.1
  146.7 96.5 all-reduce.2
where the time goes:
time: 254 us; the launch traced here: 252 us
  waiting for transfers between devices  144 us (57%)
  other arithmetic  48.8 us (19%)
  local copies, waits for them, and re-layouts  21.6 us (9%)
  matrix products  16.9 us (7%)
  between operations  14.2 us (6%)
  starting transfers between devices  5.59 us (2%)
    unnamed x3, waiting for transfers between devices  96.2 us
    all_gather x1, waiting for transfers between devices, local(): gathered = lax.all_gather(p_blocks, 'col', axis=0, tiled=True)  48.2 us
    scatter-add x4, other arithmetic, accumulate(): partial_value.at[target_rows]  24.2 us
    gather x1, other arithmetic, local(): coarse_ids = agglo[p_aggs]  20.8 us
    dot_general x4, matrix products, accumulate(): jnp.einsum('iqab,israc->iqsrbc', own_cut, product_rows, precision=highest)  14.2 us
    transpose x4, local copies, waits for them, and re-layouts, accumulate(): jnp.einsum('iqab,israc->iqsrbc', own_cut, product_rows, precision=highest)  7.67 us
  transfers between devices with their start and end apart: 4, of which 2 were waited for; matrix products, arithmetic and copies ran while one was open for 11% of the time, Pallas kernels for 0%

commit v1 on v0

v1 whole, which is shorter than its diff:
```python
import jax
import jax.numpy as jnp
from jax import lax
from jax.experimental import pallas as pl
from jax.experimental.pallas import tpu as pltpu
from jax.sharding import PartitionSpec as P

ROWS = 16
SIDE = 4
B = 128
BOTH = ("row", "col")


def moved(even, odd):
    pairs = []
    for r in range(ROWS):
        dy, dx = (even, odd)[r % 2]
        for y in range(SIDE):
            for x in range(SIDE):
                target = ((y + dy) % SIDE) * SIDE + (x + dx) % SIDE
                pairs.append((r * ROWS + y * SIDE + x, r * ROWS + target))
    return pairs


def first(step):
    return moved((0, step), (step, 0))


def second(step):
    return moved((step, 0), (0, step))


def row_pairs(start):
    pairs = []
    for r in range(start, ROWS - 1, 2):
        pairs += [(r, r + 1), (r + 1, r)]
    return pairs


def place():
    row = lax.axis_index("row")
    col = lax.axis_index("col")
    return row, row % 2, col // SIDE, col % SIDE


def slot_of(y, x, y2, x2, core):
    dy, dx = (y - y2) & 3, (x - x2) & 3
    return jnp.where(core == 0, dy * SIDE + dx, dx * SIDE + dy)


def coarse_kernel(cols, aggs, agglo, a, w, o0, o1, o2, o3, split, acc):
    row, core, y, x = place()

    def parity(j):
        return agglo[aggs[j, 0]] & 1

    acc[...] = jnp.zeros_like(acc)

    def lift(i, carry):
        swap = parity(row * ROWS + i)
        spot = slot_of(y, x, i // SIDE, i % SIDE, core) * 4
        left = jnp.concatenate([w[spot + swap], w[spot + 1 - swap]], axis=1)
        right = jnp.concatenate([a[i, 0], a[i, 1]], axis=1)
        lifted = lax.dot_general(
            left, right, (((0,), (0,)), ((), ())), preferred_element_type=jnp.float32
        )
        high = lifted.astype(jnp.bfloat16)
        low = (lifted - high.astype(jnp.float32)).astype(jnp.bfloat16)
        for s in range(2):
            split[i * 2 + s, :, :B] = high[:, s * B : (s + 1) * B]
            split[i * 2 + s, :, B:] = low[:, s * B : (s + 1) * B]
        return carry

    lax.fori_loop(0, ROWS, lift, 0, unroll=4)

    def add(i, carry):
        for s in range(2):
            j = cols[i, s]
            swap = parity(j)
            band = j // ROWS - row + 1
            y2, x2 = (j % ROWS) // SIDE, j % SIDE
            mine = slot_of(y, x, y2, x2, core) * 4 + jnp.where(band == 1, 0, 2)
            theirs = slot_of(y, x, y2, x2, 1 - core) * 2
            use_pair = band == jnp.where(core == 0, 2, 0)
            spot = jnp.where(use_pair, 64 + theirs, mine)
            right = jnp.concatenate([w[spot + swap], w[spot + 1 - swap]], axis=1)
            right = jnp.concatenate([right, right], axis=0)
            acc[band] += jnp.dot(split[i * 2 + s], right, preferred_element_type=jnp.float32)
        return carry

    lax.fori_loop(0, ROWS, add, 0, unroll=4)

    for rel, out in enumerate((o0, o1, o2, o3)):
        for m in range(SIDE):
            d = jnp.where(
                core == 0,
                ((y + m) & 3) * SIDE + ((x + rel) & 3),
                ((y + rel) & 3) * SIDE + ((x + m) & 3),
            )
            for k in range(2):
                start = pl.multiple_of(k * B + d * 8, 8)
                for t in range(3):
                    out[m, k, :, t * 256 : (t + 1) * 256] = acc[t, pl.ds(start, 8), :]


def finish_kernel(kept, f, d, b, out):
    for k in range(2):
        total = kept[k] + f[k] + d[k] + b[k]
        for j in range(6):
            out[k, j] = total[:, j * B : (j + 1) * B]


def vmem():
    return pl.BlockSpec(memory_space=pltpu.VMEM)


def smem():
    return pl.BlockSpec(memory_space=pltpu.SMEM)


def local(a_blocks, a_cols, p_blocks, p_aggs, agglo):
    shard = p_blocks[0]
    beside = lax.ppermute(shard, "row", row_pairs(1))
    line = jnp.stack([shard, beside])
    line_f = lax.ppermute(line, BOTH, first(1))
    line_b = lax.ppermute(line, BOTH, first(-1))
    line_d = lax.ppermute(line, BOTH, first(2))
    line = jnp.stack([line, line_f, line_d, line_b])
    plane_f = lax.ppermute(line, BOTH, second(1))
    plane_b = lax.ppermute(line, BOTH, second(-1))
    plane_d = lax.ppermute(line, BOTH, second(2))
    plane = jnp.stack([line, plane_f, plane_d, plane_b])
    own = plane[:, :, 0].reshape(32, B, B)
    pair = lax.ppermute(own, "row", row_pairs(0))
    blocks = jnp.concatenate([plane.reshape(64, B, B), pair])

    piece = jax.ShapeDtypeStruct((SIDE, 2, 8, 768), jnp.float32)
    o0, o1, o2, o3 = pl.pallas_call(
        coarse_kernel,
        out_shape=[piece] * 4,
        in_specs=[smem(), smem(), smem(), vmem(), vmem()],
        out_specs=[vmem()] * 4,
        scratch_shapes=[
            pltpu.VMEM((32, 256, 256), jnp.bfloat16),
            pltpu.VMEM((3, 256, 256), jnp.float32),
        ],
        compiler_params=pltpu.CompilerParams(vmem_limit_bytes=24 * 2**20),
        name="coarse",
    )(a_cols, p_aggs, agglo, a_blocks, blocks)

    f = lax.ppermute(o1, BOTH, first(1))
    b = lax.ppermute(o3, BOTH, first(-1))
    d = lax.ppermute(o2, BOTH, first(2))
    line_sum = o0 + f + d + b
    f = lax.ppermute(line_sum[1], BOTH, second(1))
    b = lax.ppermute(line_sum[3], BOTH, second(-1))
    d = lax.ppermute(line_sum[2], BOTH, second(2))
    out = pl.pallas_call(
        finish_kernel,
        out_shape=jax.ShapeDtypeStruct((2, 6, 8, B), jnp.float32),
        in_specs=[vmem()] * 4,
        out_specs=vmem(),
        name="finish",
    )(line_sum[0], f, d, b)
    return out.transpose(0, 2, 1, 3)


def solution(mesh):
    placed = (
        P("row", "col", None, None),
        P("row", "col"),
        P(("row", "col"), None, None, None),
        P(),
        P(),
    )
    return jax.shard_map(
        local, mesh=mesh, in_specs=placed, out_specs=P("row", "col", None, None), check_vma=False
    )
```

time: 254 us -> 73.2 us (0.29)
  the two profiles are of different devices: /device:TPU:96 before, /device:TPU:248 now
where the time goes in v1:
time: 73.2 us; the launch traced here: 73 us
  waiting for transfers between devices  40.1 us (55%)
  starting transfers between devices  20.1 us (27%)
  Pallas kernels  7.83 us (11%)
  other arithmetic  2.84 us (4%)
  local copies, waits for them, and re-layouts  2.04 us (3%)
    pallas_call x1, Pallas kernels, local(): pl.pallas_call(coarse_kernel, out_shape=[piece] * 4, in_specs=[smem(), sm...  6.33 us
    ppermute x1, waiting for transfers between devices, local(): plane_f = lax.ppermute(line, BOTH, second(1))  6.23 us
    ppermute x1, waiting for transfers between devices, local(): f = lax.ppermute(o1, BOTH, first(1))  5.8 us
    ppermute x1, waiting for transfers between devices, local(): plane_b = lax.ppermute(line, BOTH, second(-1))  5.51 us
    ppermute x1, starting transfers between devices, local(): b = lax.ppermute(o3, BOTH, first(-1))  3.92 us
    ppermute x1, waiting for transfers between devices, local(): line_b = lax.ppermute(line, BOTH, first(-1))  3.86 us
    ppermute x1, waiting for transfers between devices, local(): line_d = lax.ppermute(line, BOTH, first(2))  3.8 us
    ppermute x1, waiting for transfers between devices, local(): beside = lax.ppermute(shard, 'row', row_pairs(1))  3.43 us
  transfers between devices with their start and end apart: 14, of which 13 were waited for; matrix products, arithmetic and copies ran while one was open for 0% of the time, Pallas kernels for 0%

profile of v1, /device:TPU:248, one launch (start us, length us, event | category | flops | bytes accessed | tf_op | source)
XLA Modules:
  0.0 73.0 jit_solution(1699513144349752639)
XLA Ops:
  0.0 2.3 %collective-permute-start = (bf16[2,128,128]{2,1,0:T(8,128)(2,1)}, bf16[2,128,128]{2,1,0:T(8,128)(2,1)S(1)}, u32[]{:S(2)}, u32[]{:S(2)}) collective-permute-start(bf16[2,128,128]{2,1,0:T(8,128)(2,1)} %bitcast.31), channel_id=1, source_target_pairs={{16,32},{32,16},{48,64},{64,48},{80,96},{96,80},{112,128},{128,112... | collective-permute-start | bytes 196616 | tf_op jit(solution)/shard_map/ppermute | solution.py:123
  2.4 3.4 %collective-permute-done = bf16[2,128,128]{2,1,0:T(8,128)(2,1)S(1)} collective-permute-done((bf16[2,128,128]{2,1,0:T(8,128)(2,1)}, bf16[2,128,128]{2,1,0:T(8,128)(2,1)S(1)}, u32[]{:S(2)}, u32[]{:S(2)}) %collective-permute-start) | collective-permute-done | bytes 65568 | tf_op jit(solution)/shard_map/ppermute | solution.py:123
  5.8 0.9 %fusion = (bf16[1,2,2,128,128]{4,3,2,1,0:T(8,128)(2,1)S(1)}, bf16[2,2,128,128]{3,2,1,0:T(8,128)(2,1)S(1)}) fusion(bf16[1,2,128,128]{3,2,1,0:T(8,128)(2,1)S(1)} %bitcast.32, bf16[1,2,128,128]{3,2,1,0:T(8,128)(2,1)} %param.7), kind=kLoop, calls=%fused_computation.9 | loop fusion | flops 65536 | bytes 393216 | tf_op jit(solution)/shard_map/stack | solution.py:128
  6.6 1.6 %collective-permute-start.1 = (bf16[2,2,128,128]{3,2,1,0:T(8,128)(2,1)S(1)}, bf16[2,2,128,128]{3,2,1,0:T(8,128)(2,1)S(1)}, u32[]{:S(2)}, u32[]{:S(2)}) collective-permute-start(bf16[2,2,128,128]{3,2,1,0:T(8,128)(2,1)S(1)} %get-tuple-element.20), channel_id=1, source_target_pairs={{0,1},{1,2},{2,3},{3,0},{4,5},{5,6},{6,7},{7,4},{8,9},{9,10},{10,1... | collective-permute-start | bytes 393224 | tf_op jit(solution)/shard_map/ppermute | solution.py:125
  8.2 2.7 %collective-permute-start.2 = (bf16[2,2,128,128]{3,2,1,0:T(8,128)(2,1)S(1)}, bf16[2,2,128,128]{3,2,1,0:T(8,128)(2,1)S(1)}, u32[]{:S(2)}, u32[]{:S(2)}) collective-permute-start(bf16[2,2,128,128]{3,2,1,0:T(8,128)(2,1)S(1)} %get-tuple-element.20), channel_id=1, source_target_pairs={{0,2},{1,3},{2,0},{3,1},{4,6},{5,7},{6,4},{7,5},{8,10},{9,11},{10,... | collective-permute-start | bytes 393224 | tf_op jit(solution)/shard_map/ppermute | solution.py:127
  10.9 1.4 %collective-permute-start.3 = (bf16[2,2,128,128]{3,2,1,0:T(8,128)(2,1)S(1)}, bf16[2,2,128,128]{3,2,1,0:T(8,128)(2,1)S(1)}, u32[]{:S(2)}, u32[]{:S(2)}) collective-permute-start(bf16[2,2,128,128]{3,2,1,0:T(8,128)(2,1)S(1)} %get-tuple-element.20), channel_id=1, source_target_pairs={{0,3},{1,0},{2,1},{3,2},{4,7},{5,4},{6,5},{7,6},{8,11},{9,8},{10,9... | collective-permute-start | bytes 393224 | tf_op jit(solution)/shard_map/ppermute | solution.py:126
  13.1 3.8 %collective-permute-done.2 = bf16[2,2,128,128]{3,2,1,0:T(8,128)(2,1)S(1)} collective-permute-done((bf16[2,2,128,128]{3,2,1,0:T(8,128)(2,1)S(1)}, bf16[2,2,128,128]{3,2,1,0:T(8,128)(2,1)S(1)}, u32[]{:S(2)}, u32[]{:S(2)}) %collective-permute-start.2) | collective-permute-done | bytes 131104 | tf_op jit(solution)/shard_map/ppermute | solution.py:127
  16.9 3.9 %collective-permute-done.3 = bf16[2,2,128,128]{3,2,1,0:T(8,128)(2,1)S(1)} collective-permute-done((bf16[2,2,128,128]{3,2,1,0:T(8,128)(2,1)S(1)}, bf16[2,2,128,128]{3,2,1,0:T(8,128)(2,1)S(1)}, u32[]{:S(2)}, u32[]{:S(2)}) %collective-permute-start.3) | collective-permute-done | bytes 131104 | tf_op jit(solution)/shard_map/ppermute | solution.py:126
  20.9 2.9 %collective-permute-start.5 = (bf16[4,2,2,128,128]{4,3,2,1,0:T(8,128)(2,1)S(1)}, bf16[4,2,2,128,128]{4,3,2,1,0:T(8,128)(2,1)S(1)}, u32[]{:S(2)}, u32[]{:S(2)}) collective-permute-start(bf16[4,2,2,128,128]{4,3,2,1,0:T(8,128)(2,1)S(1)} %get-tuple-element.14), channel_id=1, source_target_pairs={{0,8},{1,9},{2,10},{3,11},{4,12},{5,13},{6,14},{7,15},{8,0},{9,1},... | collective-permute-start | bytes 1572872 | tf_op jit(solution)/shard_map/ppermute | solution.py:131
  23.8 6.2 %collective-permute-done.4 = bf16[4,2,2,128,128]{4,3,2,1,0:T(8,128)(2,1)S(1)} collective-permute-done((bf16[4,2,2,128,128]{4,3,2,1,0:T(8,128)(2,1)S(1)}, bf16[4,2,2,128,128]{4,3,2,1,0:T(8,128)(2,1)S(1)}, u32[]{:S(2)}, u32[]{:S(2)}) %collective-permute-start.4) | collective-permute-done | bytes 524320 | tf_op jit(solution)/shard_map/ppermute | solution.py:129
  30.1 1.7 %collective-permute-done.5 = bf16[4,2,2,128,128]{4,3,2,1,0:T(8,128)(2,1)S(1)} collective-permute-done((bf16[4,2,2,128,128]{4,3,2,1,0:T(8,128)(2,1)S(1)}, bf16[4,2,2,128,128]{4,3,2,1,0:T(8,128)(2,1)S(1)}, u32[]{:S(2)}, u32[]{:S(2)}) %collective-permute-start.5) | collective-permute-done | bytes 524320 | tf_op jit(solution)/shard_map/ppermute | solution.py:131
  31.8 5.5 %collective-permute-done.6 = bf16[4,2,2,128,128]{4,3,2,1,0:T(8,128)(2,1)S(1)} collective-permute-done((bf16[4,2,2,128,128]{4,3,2,1,0:T(8,128)(2,1)S(1)}, bf16[4,2,2,128,128]{4,3,2,1,0:T(8,128)(2,1)S(1)}, u32[]{:S(2)}, u32[]{:S(2)}) %collective-permute-start.6) | collective-permute-done | bytes 524320 | tf_op jit(solution)/shard_map/ppermute | solution.py:130
  38.5 2.1 %collective-permute-done.7 = bf16[32,128,128]{2,1,0:T(8,128)(2,1)} collective-permute-done((bf16[32,128,128]{2,1,0:T(8,128)(2,1)S(1)}, bf16[32,128,128]{2,1,0:T(8,128)(2,1)}, u32[]{:S(2)}, u32[]{:S(2)}) %collective-permute-start.7) | collective-permute-done | bytes 1048608 | tf_op jit(solution)/shard_map/ppermute | solution.py:134
  40.6 1.6 %pad_maximum_fusion.w = bf16[96,128,128]{2,1,0:T(8,128)(2,1)S(1)} fusion(bf16[32,128,128]{2,1,0:T(8,128)(2,1)} %collective-permute-done.7, bf16[64,128,128]{2,1,0:T(8,128)(2,1)S(1)} %bitcast.23), kind=kLoop, calls=%fused_computation | loop fusion | flops 1572864 | bytes 6291456 | tf_op jit(solution)/shard_map/concatenate | solution.py:135
  42.2 6.3 %coarse.1 = (f32[4,2,8,768]{3,2,1,0:T(8,128)S(1)}, f32[4,2,8,768]{3,2,1,0:T(8,128)S(1)}, f32[4,2,8,768]{3,2,1,0:T(8,128)S(1)}, f32[4,2,8,768]{3,2,1,0:T(8,128)S(1)}) custom-call(s32[16,2]{1,0:T(8,128)S(1)} %copy.6.cols, s32[256,2]{1,0:T(8,128)S(1)} %copy.7.aggs, s32[32]{0:T(128)S(1)} %copy-done.1, bf16[16,2,128,128]{3,2,1,0:T(8,128)(2,1)S(1)} %copy-done, ...), custom_call_target="tpu_custom_call" | custom-call | tf_op jit(solution)/shard_map/coarse/pallas_call | solution.py:138
  48.5 3.9 %collective-permute-start.10 = (f32[4,2,8,768]{3,2,1,0:T(8,128)S(1)}, f32[4,2,8,768]{3,2,1,0:T(8,128)S(1)}, u32[]{:S(2)}, u32[]{:S(2)}) collective-permute-start(f32[4,2,8,768]{3,2,1,0:T(8,128)S(1)} %get-tuple-element.12), channel_id=1, source_target_pairs={{0,3},{1,0},{2,1},{3,2},{4,7},{5,4},{6,5},{7,6},{8,11},{9,8},{10,9... | collective-permute-start | bytes 589832 | tf_op jit(solution)/shard_map/ppermute | solution.py:152
  52.4 1.5 %collective-permute-start.9 = (f32[4,2,8,768]{3,2,1,0:T(8,128)S(1)}, f32[4,2,8,768]{3,2,1,0:T(8,128)S(1)}, u32[]{:S(2)}, u32[]{:S(2)}) collective-permute-start(f32[4,2,8,768]{3,2,1,0:T(8,128)S(1)} %get-tuple-element.11), channel_id=1, source_target_pairs={{0,2},{1,3},{2,0},{3,1},{4,6},{5,7},{6,4},{7,5},{8,10},{9,11},{10,... | collective-permute-start | bytes 589832 | tf_op jit(solution)/shard_map/ppermute | solution.py:153
  54.0 1.6 %collective-permute-done.10 = f32[4,2,8,768]{3,2,1,0:T(8,128)S(1)} collective-permute-done((f32[4,2,8,768]{3,2,1,0:T(8,128)S(1)}, f32[4,2,8,768]{3,2,1,0:T(8,128)S(1)}, u32[]{:S(2)}, u32[]{:S(2)}) %collective-permute-start.10) | collective-permute-done | bytes 196640 | tf_op jit(solution)/shard_map/ppermute | solution.py:152
  55.6 5.8 %collective-permute-done.8 = f32[4,2,8,768]{3,2,1,0:T(8,128)S(1)} collective-permute-done((f32[4,2,8,768]{3,2,1,0:T(8,128)S(1)}, f32[4,2,8,768]{3,2,1,0:T(8,128)S(1)}, u32[]{:S(2)}, u32[]{:S(2)}) %collective-permute-start.8) | collective-permute-done | bytes 196640 | tf_op jit(solution)/shard_map/ppermute | solution.py:151
  62.1 1.1 %collective-permute-start.11 = (f32[2,8,768]{2,1,0:T(8,128)S(1)}, f32[2,8,768]{2,1,0:T(8,128)S(1)}, u32[]{:S(2)}, u32[]{:S(2)}) collective-permute-start(f32[2,8,768]{2,1,0:T(8,128)S(1)} %get-tuple-element.17), channel_id=1, source_target_pairs={{0,4},{1,5},{2,6},{3,7},{4,8},{5,9},{6,10},{7,11},{8,12},{9,13},{1... | collective-permute-start | bytes 147464 | tf_op jit(solution)/shard_map/ppermute | solution.py:155
  63.2 2.4 %collective-permute-start.12 = (f32[2,8,768]{2,1,0:T(8,128)S(1)}, f32[2,8,768]{2,1,0:T(8,128)S(1)}, u32[]{:S(2)}, u32[]{:S(2)}) collective-permute-start(f32[2,8,768]{2,1,0:T(8,128)S(1)} %get-tuple-element.16), channel_id=1, source_target_pairs={{0,8},{1,9},{2,10},{3,11},{4,12},{5,13},{6,14},{7,15},{8,0},{9,1},... | collective-permute-start | bytes 147464 | tf_op jit(solution)/shard_map/ppermute | solution.py:157
  66.2 2.6 %collective-permute-done.12.d = f32[2,8,768]{2,1,0:T(8,128)S(1)} collective-permute-done((f32[2,8,768]{2,1,0:T(8,128)S(1)}, f32[2,8,768]{2,1,0:T(8,128)S(1)}, u32[]{:S(2)}, u32[]{:S(2)}) %collective-permute-start.12) | collective-permute-done | bytes 49184 | tf_op jit(solution)/shard_map/ppermute | solution.py:157
  68.8 2.1 %collective-permute-done.13.b = f32[2,8,768]{2,1,0:T(8,128)S(1)} collective-permute-done((f32[2,8,768]{2,1,0:T(8,128)S(1)}, f32[2,8,768]{2,1,0:T(8,128)S(1)}, u32[]{:S(2)}, u32[]{:S(2)}) %collective-permute-start.13) | collective-permute-done | bytes 49184 | tf_op jit(solution)/shard_map/ppermute | solution.py:156
  71.5 1.5 %finish.1 = f32[2,6,8,128]{3,2,1,0:T(8,128)} custom-call(f32[2,8,768]{2,1,0:T(8,128)} %get-tuple-element.18.kept, f32[2,8,768]{2,1,0:T(8,128)} %copy-done.2, f32[2,8,768]{2,1,0:T(8,128)} %copy-done.3, f32[2,8,768]{2,1,0:T(8,128)} %copy-done.4), custom_call_target="tpu_custom_call" | custom-call | tf_op jit(solution)/shard_map/finish/pallas_call | solution.py:158
  (29 shorter events, 4.0 us)
Async XLA Ops:
  0.0 5.8 %collective-permute-start = (bf16[2,128,128]{2,1,0:T(8,128)(2,1)}, bf16[2,128,128]{2,1,0:T(8,128)(2,1)S(1)}, u32[]{:S(2)}, u32[]{:S(2)}) collective-permute-start(bf16[2,128,128]{2,1,0:T(8,128)(2,1)} %bitcast.31), channel_id=1, source_target_pairs={{16,32},{32,16},{48,64},{64,48},{80,96},{96,80},{112,128},{128,112... | collective-permute-start | bytes 196616 | tf_op jit(solution)/shard_map/ppermute | solution.py:123
  6.6 6.4 %collective-permute-start.1 = (bf16[2,2,128,128]{3,2,1,0:T(8,128)(2,1)S(1)}, bf16[2,2,128,128]{3,2,1,0:T(8,128)(2,1)S(1)}, u32[]{:S(2)}, u32[]{:S(2)}) collective-permute-start(bf16[2,2,128,128]{3,2,1,0:T(8,128)(2,1)S(1)} %get-tuple-element.20), channel_id=1, source_target_pairs={{0,1},{1,2},{2,3},{3,0},{4,5},{5,6},{6,7},{7,4},{8,9},{9,10},{10,1... | collective-permute-start | bytes 393224 | tf_op jit(solution)/shard_map/ppermute | solution.py:125
  8.2 8.7 %collective-permute-start.2 = (bf16[2,2,128,128]{3,2,1,0:T(8,128)(2,1)S(1)}, bf16[2,2,128,128]{3,2,1,0:T(8,128)(2,1)S(1)}, u32[]{:S(2)}, u32[]{:S(2)}) collective-permute-start(bf16[2,2,128,128]{3,2,1,0:T(8,128)(2,1)S(1)} %get-tuple-element.20), channel_id=1, source_target_pairs={{0,2},{1,3},{2,0},{3,1},{4,6},{5,7},{6,4},{7,5},{8,10},{9,11},{10,... | collective-permute-start | bytes 393224 | tf_op jit(solution)/shard_map/ppermute | solution.py:127
  10.9 9.8 %collective-permute-start.3 = (bf16[2,2,128,128]{3,2,1,0:T(8,128)(2,1)S(1)}, bf16[2,2,128,128]{3,2,1,0:T(8,128)(2,1)S(1)}, u32[]{:S(2)}, u32[]{:S(2)}) collective-permute-start(bf16[2,2,128,128]{3,2,1,0:T(8,128)(2,1)S(1)} %get-tuple-element.20), channel_id=1, source_target_pairs={{0,3},{1,0},{2,1},{3,2},{4,7},{5,4},{6,5},{7,6},{8,11},{9,8},{10,9... | collective-permute-start | bytes 393224 | tf_op jit(solution)/shard_map/ppermute | solution.py:126
  20.8 9.3 %collective-permute-start.4 = (bf16[4,2,2,128,128]{4,3,2,1,0:T(8,128)(2,1)S(1)}, bf16[4,2,2,128,128]{4,3,2,1,0:T(8,128)(2,1)S(1)}, u32[]{:S(2)}, u32[]{:S(2)}) collective-permute-start(bf16[4,2,2,128,128]{4,3,2,1,0:T(8,128)(2,1)S(1)} %get-tuple-element.14), channel_id=1, source_target_pairs={{0,4},{1,5},{2,6},{3,7},{4,8},{5,9},{6,10},{7,11},{8,12},{9,13},{1... | collective-permute-start | bytes 1572872 | tf_op jit(solution)/shard_map/ppermute | solution.py:129
  20.9 10.9 %collective-permute-start.5 = (bf16[4,2,2,128,128]{4,3,2,1,0:T(8,128)(2,1)S(1)}, bf16[4,2,2,128,128]{4,3,2,1,0:T(8,128)(2,1)S(1)}, u32[]{:S(2)}, u32[]{:S(2)}) collective-permute-start(bf16[4,2,2,128,128]{4,3,2,1,0:T(8,128)(2,1)S(1)} %get-tuple-element.14), channel_id=1, source_target_pairs={{0,8},{1,9},{2,10},{3,11},{4,12},{5,13},{6,14},{7,15},{8,0},{9,1},... | collective-permute-start | bytes 1572872 | tf_op jit(solution)/shard_map/ppermute | solution.py:131
  23.8 13.5 %collective-permute-start.6 = (bf16[4,2,2,128,128]{4,3,2,1,0:T(8,128)(2,1)S(1)}, bf16[4,2,2,128,128]{4,3,2,1,0:T(8,128)(2,1)S(1)}, u32[]{:S(2)}, u32[]{:S(2)}) collective-permute-start(bf16[4,2,2,128,128]{4,3,2,1,0:T(8,128)(2,1)S(1)} %get-tuple-element.14), channel_id=1, source_target_pairs={{0,12},{1,13},{2,14},{3,15},{4,0},{5,1},{6,2},{7,3},{8,4},{9,5},{1... | collective-permute-start | bytes 1572872 | tf_op jit(solution)/shard_map/ppermute | solution.py:130
  37.6 0.7 copy-start.5
  37.6 0.8 %copy-start.6 = (s32[16,2]{0,1:T(2,128)S(1)}, s32[16,2]{0,1:T(2,128)}, u32[]{:S(2)}) copy-start(s32[16,2]{0,1:T(2,128)} %param.6) | copy-start | bytes 388
  37.7 2.9 %collective-permute-start.7 = (bf16[32,128,128]{2,1,0:T(8,128)(2,1)S(1)}, bf16[32,128,128]{2,1,0:T(8,128)(2,1)}, u32[]{:S(2)}, u32[]{:S(2)}) collective-permute-start(bf16[32,128,128]{2,1,0:T(8,128)(2,1)S(1)} %bitcast.24), channel_id=1, source_target_pairs={{0,16},{16,0},{32,48},{48,32},{64,80},{80,64},{96,112},{112,96},{1... | collective-permute-start | bytes 3145736 | tf_op jit(solution)/shard_map/ppermute | solution.py:134
  40.6 1.6 %copy-start = (bf16[16,2,128,128]{3,2,1,0:T(8,128)(2,1)S(1)}, bf16[16,2,128,128]{3,2,1,0:T(8,128)(2,1)}, u32[]{:S(2)}) copy-start(bf16[16,2,128,128]{3,2,1,0:T(8,128)(2,1)} %a.1) | copy-start | bytes 3145732
  40.6 1.6 %copy-start.1 = (s32[32]{0:T(128)S(1)}, s32[32]{0:T(128)}, u32[]{:S(2)}) copy-start(s32[32]{0:T(128)} %agglo.1) | copy-start | bytes 388
  48.5 7.1 %collective-permute-start.10 = (f32[4,2,8,768]{3,2,1,0:T(8,128)S(1)}, f32[4,2,8,768]{3,2,1,0:T(8,128)S(1)}, u32[]{:S(2)}, u32[]{:S(2)}) collective-permute-start(f32[4,2,8,768]{3,2,1,0:T(8,128)S(1)} %get-tuple-element.12), channel_id=1, source_target_pairs={{0,3},{1,0},{2,1},{3,2},{4,7},{5,4},{6,5},{7,6},{8,11},{9,8},{10,9... | collective-permute-start | bytes 589832 | tf_op jit(solution)/shard_map/ppermute | solution.py:152
  52.4 9.0 %collective-permute-start.8 = (f32[4,2,8,768]{3,2,1,0:T(8,128)S(1)}, f32[4,2,8,768]{3,2,1,0:T(8,128)S(1)}, u32[]{:S(2)}, u32[]{:S(2)}) collective-permute-start(f32[4,2,8,768]{3,2,1,0:T(8,128)S(1)} %get-tuple-element.10), channel_id=1, source_target_pairs={{0,1},{1,2},{2,3},{3,0},{4,5},{5,6},{6,7},{7,4},{8,9},{9,10},{10,1... | collective-permute-start | bytes 589832 | tf_op jit(solution)/shard_map/ppermute | solution.py:151
  52.4 9.0 %collective-permute-start.9 = (f32[4,2,8,768]{3,2,1,0:T(8,128)S(1)}, f32[4,2,8,768]{3,2,1,0:T(8,128)S(1)}, u32[]{:S(2)}, u32[]{:S(2)}) collective-permute-start(f32[4,2,8,768]{3,2,1,0:T(8,128)S(1)} %get-tuple-element.11), channel_id=1, source_target_pairs={{0,2},{1,3},{2,0},{3,1},{4,6},{5,7},{6,4},{7,5},{8,10},{9,11},{10,... | collective-permute-start | bytes 589832 | tf_op jit(solution)/shard_map/ppermute | solution.py:153
  62.1 4.1 %collective-permute-start.11 = (f32[2,8,768]{2,1,0:T(8,128)S(1)}, f32[2,8,768]{2,1,0:T(8,128)S(1)}, u32[]{:S(2)}, u32[]{:S(2)}) collective-permute-start(f32[2,8,768]{2,1,0:T(8,128)S(1)} %get-tuple-element.17), channel_id=1, source_target_pairs={{0,4},{1,5},{2,6},{3,7},{4,8},{5,9},{6,10},{7,11},{8,12},{9,13},{1... | collective-permute-start | bytes 147464 | tf_op jit(solution)/shard_map/ppermute | solution.py:155
  63.2 5.6 %collective-permute-start.12 = (f32[2,8,768]{2,1,0:T(8,128)S(1)}, f32[2,8,768]{2,1,0:T(8,128)S(1)}, u32[]{:S(2)}, u32[]{:S(2)}) collective-permute-start(f32[2,8,768]{2,1,0:T(8,128)S(1)} %get-tuple-element.16), channel_id=1, source_target_pairs={{0,8},{1,9},{2,10},{3,11},{4,12},{5,13},{6,14},{7,15},{8,0},{9,1},... | collective-permute-start | bytes 147464 | tf_op jit(solution)/shard_map/ppermute | solution.py:157
  65.6 5.3 %collective-permute-start.13 = (f32[2,8,768]{2,1,0:T(8,128)S(1)}, f32[2,8,768]{2,1,0:T(8,128)S(1)}, u32[]{:S(2)}, u32[]{:S(2)}) collective-permute-start(f32[2,8,768]{2,1,0:T(8,128)S(1)} %get-tuple-element.15), channel_id=1, source_target_pairs={{0,12},{1,13},{2,14},{3,15},{4,0},{5,1},{6,2},{7,3},{8,4},{9,5},{1... | collective-permute-start | bytes 147464 | tf_op jit(solution)/shard_map/ppermute | solution.py:156
  66.2 4.7 %copy-start.2 = (f32[2,8,768]{2,1,0:T(8,128)}, f32[2,8,768]{2,1,0:T(8,128)S(1)}, u32[]{:S(2)}) copy-start(f32[2,8,768]{2,1,0:T(8,128)S(1)} %collective-permute-done.11.f) | copy-start | bytes 147460
  68.8 2.1 %copy-start.3 = (f32[2,8,768]{2,1,0:T(8,128)}, f32[2,8,768]{2,1,0:T(8,128)S(1)}, u32[]{:S(2)}) copy-start(f32[2,8,768]{2,1,0:T(8,128)S(1)} %collective-permute-done.12.d) | copy-start | bytes 147460
  70.9 0.6 copy-start.4

commit v2 on v1

v2 whole, which is shorter than its diff:
```python
import jax
import jax.numpy as jnp
from jax import lax
from jax.experimental import pallas as pl
from jax.experimental.pallas import tpu as pltpu
from jax.sharding import PartitionSpec as P

ROWS = 16
SIDE = 4
B = 128
CHUNK = 4
BOTH = ("row", "col")


def moved(even, odd, rows=range(ROWS)):
    pairs = []
    for r in rows:
        dy, dx = (even, odd)[r % 2]
        for y in range(SIDE):
            for x in range(SIDE):
                target = ((y + dy) % SIDE) * SIDE + (x + dx) % SIDE
                pairs.append((r * ROWS + y * SIDE + x, r * ROWS + target))
    return pairs


def first(step, rows=range(ROWS)):
    return moved((0, step), (step, 0), rows)


def second(step):
    return moved((step, 0), (0, step))


def row_pairs(start):
    pairs = []
    for r in range(start, ROWS - 1, 2):
        pairs += [(r, r + 1), (r + 1, r)]
    return pairs


def place():
    row = lax.axis_index("row")
    col = lax.axis_index("col")
    return row, row % 2, col // SIDE, col % SIDE


def slot_of(y, x, j, core):
    dy, dx = (y - (j % ROWS) // SIDE) & 3, (x - j % SIDE) & 3
    return jnp.where(core == 0, dy * SIDE + dx, dx * SIDE + dy)


def parity(aggs, agglo, j):
    return agglo[aggs[j, 0]] & 1


def gather_products(band, core, y, x, row, cols, aggs, agglo, order, blocks, split):
    def scan(e, count):
        j = cols[e // 2, e % 2]

        @pl.when(j // ROWS - row + 1 == band)
        def _():
            order[0, count] = e
            spot = slot_of(y, x, j, core) * 2
            swap = parity(aggs, agglo, j)
            order[1, count] = spot + swap
            order[2, count] = spot + 1 - swap

        return count + (j // ROWS - row + 1 == band).astype(jnp.int32)

    count = lax.fori_loop(0, 2 * ROWS, scan, 0)
    for c in range(CHUNK - 1):
        order[0, count + c] = 2 * ROWS
        order[1, count + c] = 0
        order[2, count + c] = 0

    def chunk(c, total):
        left, right = [], []
        for u in range(CHUNK):
            p = c * CHUNK + u
            left.append(split[order[0, p]])
            one = jnp.concatenate([blocks[order[1, p]], blocks[order[2, p]]], axis=1)
            right += [one, one]
        return total + jnp.dot(
            jnp.concatenate(left, axis=1),
            jnp.concatenate(right, axis=0),
            preferred_element_type=jnp.float32,
        )

    return lax.fori_loop(
        0, (count + CHUNK - 1) // CHUNK, chunk, jnp.zeros((256, 256), jnp.float32)
    )


def own_kernel(cols, aggs, agglo, a, plane, split, acc, order):
    row, core, y, x = place()
    split[2 * ROWS] = jnp.zeros((256, 256), jnp.bfloat16)

    def lift(i, carry):
        swap = parity(aggs, agglo, row * ROWS + i)
        spot = slot_of(y, x, i, core) * 2
        left = jnp.concatenate([plane[spot + swap], plane[spot + 1 - swap]], axis=1)
        right = jnp.concatenate([a[i, 0], a[i, 1]], axis=1)
        lifted = lax.dot_general(
            left, right, (((0,), (0,)), ((), ())), preferred_element_type=jnp.float32
        )
        high = lifted.astype(jnp.bfloat16)
        low = (lifted - high.astype(jnp.float32)).astype(jnp.bfloat16)
        for s in range(2):
            split[i * 2 + s, :, :B] = high[:, s * B : (s + 1) * B]
            split[i * 2 + s, :, B:] = low[:, s * B : (s + 1) * B]
        return carry

    lax.fori_loop(0, ROWS, lift, 0, unroll=4)
    acc[...] = gather_products(1, core, y, x, row, cols, aggs, agglo, order, plane, split)


def pair_kernel(cols, aggs, agglo, split, pair, acc, order):
    row, core, y, x = place()
    band = 2 - 2 * core
    acc[...] = gather_products(band, 1 - core, y, x, row, cols, aggs, agglo, order, pair, split)


def beside_kernel(
    cols, aggs, agglo, split, n0, n1, n2, n3, acc_own, acc_pair, o0, o1, o2, o3, blocks, acc, order
):
    row, core, y, x = place()
    band = 2 * core
    for m, n in enumerate((n0, n1, n2, n3)):
        blocks[m * 8 : (m + 1) * 8] = n[...]
    acc[...] = gather_products(
        band, 1 - core, y, x, row, cols, aggs, agglo, order, blocks, split
    )
    for rel, out in enumerate((o0, o1, o2, o3)):
        for m in range(SIDE):
            d = jnp.where(
                core == 0,
                ((y + m) & 3) * SIDE + ((x + rel) & 3),
                ((y + rel) & 3) * SIDE + ((x + m) & 3),
            )
            for k in range(2):
                rows = pl.ds(pl.multiple_of(k * B + d * 8, 8), 8)
                out[m, k, :, 256:512] = acc_own[rows, :]
                beside, partner = acc[rows, :], acc_pair[rows, :]
                out[m, k, :, 0:256] = jnp.where(core == 0, beside, partner)
                out[m, k, :, 512:768] = jnp.where(core == 0, partner, beside)


def vmem():
    return pl.BlockSpec(memory_space=pltpu.VMEM)


def smem():
    return pl.BlockSpec(memory_space=pltpu.SMEM)


def local(a_blocks, a_cols, p_blocks, p_aggs, agglo):
    inner = range(1, ROWS - 1)
    shard = p_blocks[0]
    f = lax.ppermute(shard, BOTH, first(1))
    b = lax.ppermute(shard, BOTH, first(-1))
    d = lax.ppermute(shard, BOTH, first(2))
    line = jnp.concatenate([shard, f, d, b])
    plane_d = lax.ppermute(line, BOTH, second(2))
    beside_0 = lax.ppermute(line, "row", row_pairs(1))
    plane_f = lax.ppermute(line, BOTH, second(1))
    plane_b = lax.ppermute(line, BOTH, second(-1))
    plane_d, beside_0 = lax.optimization_barrier((plane_d, beside_0))
    beside_f = lax.ppermute(beside_0, BOTH, first(1, inner))
    beside_b = lax.ppermute(beside_0, BOTH, first(-1, inner))
    beside_d = lax.ppermute(plane_d, "row", row_pairs(1))
    plane_f, plane_b, beside_0 = lax.optimization_barrier((plane_f, plane_b, beside_0))
    plane = jnp.concatenate([line, plane_f, plane_d, plane_b])
    pair = lax.ppermute(plane, "row", row_pairs(0))

    scalars = (a_cols, p_aggs, agglo)
    order = pltpu.SMEM((3, 40), jnp.int32)
    square = jax.ShapeDtypeStruct((256, 256), jnp.float32)
    split, acc_own = pl.pallas_call(
        own_kernel,
        out_shape=[jax.ShapeDtypeStruct((33, 256, 256), jnp.bfloat16), square],
        in_specs=[smem(), smem(), smem(), vmem(), vmem()],
        out_specs=[vmem()] * 2,
        scratch_shapes=[order],
        compiler_params=pltpu.CompilerParams(vmem_limit_bytes=24 * 2**20),
        cost_estimate=pl.CostEstimate(flops=10**6, bytes_accessed=2**12, transcendentals=0),
        name="own",
    )(*scalars, a_blocks, plane)
    acc_pair = pl.pallas_call(
        pair_kernel,
        out_shape=square,
        in_specs=[smem(), smem(), smem(), vmem(), vmem()],
        out_specs=vmem(),
        scratch_shapes=[order],
        compiler_params=pltpu.CompilerParams(vmem_limit_bytes=24 * 2**20),
        cost_estimate=pl.CostEstimate(flops=10**6, bytes_accessed=2**12, transcendentals=0),
        name="pair",
    )(*scalars, split, pair)
    piece = jax.ShapeDtypeStruct((SIDE, 2, 8, 768), jnp.float32)
    o0, o1, o2, o3 = pl.pallas_call(
        beside_kernel,
        out_shape=[piece] * 4,
        in_specs=[smem(), smem(), smem()] + [vmem()] * 7,
        out_specs=[vmem()] * 4,
        scratch_shapes=[
            pltpu.VMEM((32, B, B), jnp.bfloat16),
            pltpu.VMEM((256, 256), jnp.float32),
            order,
        ],
        compiler_params=pltpu.CompilerParams(vmem_limit_bytes=24 * 2**20),
        cost_estimate=pl.CostEstimate(flops=10**6, bytes_accessed=2**12, transcendentals=0),
        name="beside",
    )(*scalars, split, beside_0, beside_f, beside_d, beside_b, acc_own, acc_pair)

    f = lax.ppermute(o1, BOTH, first(1))
    b = lax.ppermute(o3, BOTH, first(-1))
    d = lax.ppermute(o2, BOTH, first(2))
    kept, to_f, to_d, to_b = (o0[m] + f[m] + d[m] + b[m] for m in range(SIDE))
    f = lax.ppermute(to_f, BOTH, second(1))
    b = lax.ppermute(to_b, BOTH, second(-1))
    d = lax.ppermute(to_d, BOTH, second(2))
    return (kept + f + d + b).reshape(2, 8, 6, B)


def solution(mesh):
    placed = (
        P("row", "col", None, None),
        P("row", "col"),
        P(("row", "col"), None, None, None),
        P(),
        P(),
    )
    return jax.shard_map(
        local, mesh=mesh, in_specs=placed, out_specs=P("row", "col", None, None), check_vma=False
    )
```

time: 73.2 us -> 72.8 us (level)
  the two profiles are of different devices: /device:TPU:248 before, /device:TPU:96 now
where the time goes in v2:
time: 72.8 us; the launch traced here: 71.5 us
  starting transfers between devices  32.9 us (45%)
  Pallas kernels  16.7 us (23%)
  waiting for transfers between devices  15.7 us (22%)
  local copies, waits for them, and re-layouts  4.48 us (6%)
  other arithmetic  1.54 us (2%)
    pallas_call x1, Pallas kernels, local(): pl.pallas_call(own_kernel, out_shape=[jax.ShapeDtypeStruct((33, 256, 256)...  6.51 us
    pallas_call x1, Pallas kernels, local(): pl.pallas_call(beside_kernel, out_shape=[piece] * 4, in_specs=[smem(), sm...  5.18 us
    pallas_call x1, Pallas kernels, local(): pl.pallas_call(pair_kernel, out_shape=square, in_specs=[smem(), smem(), s...  5.03 us
    unnamed x12, local copies, waits for them, and re-layouts  4.44 us
    ppermute x1, starting transfers between devices, local(): beside_b = lax.ppermute(beside_0, BOTH, first(-1, inner))  4.32 us
    ppermute x1, starting transfers between devices, local(): plane_d = lax.ppermute(line, BOTH, second(2))  3.28 us
    ppermute x1, starting transfers between devices, local(): d = lax.ppermute(o2, BOTH, first(2))  3.2 us
    ppermute x1, waiting for transfers between devices, local(): f = lax.ppermute(o1, BOTH, first(1))  2.85 us
  transfers between devices with their start and end apart: 17, of which 10 were waited for; matrix products, arithmetic and copies ran while one was open for 3% of the time, Pallas kernels for 16%

profile of v2, /device:TPU:96, one launch (start us, length us, event | category | flops | bytes accessed | tf_op | source)
XLA Modules:
  0.0 71.5 jit_solution(10586245891103493759)
XLA Ops:
  0.0 1.5 %collective-permute-start = (bf16[2,128,128]{2,1,0:T(8,128)(2,1)}, bf16[2,128,128]{2,1,0:T(8,128)(2,1)S(1)}, u32[]{:S(2)}, u32[]{:S(2)}) collective-permute-start(bf16[2,128,128]{2,1,0:T(8,128)(2,1)} %bitcast.20), channel_id=1, source_target_pairs={{0,1},{1,2},{2,3},{3,0},{4,5},{5,6},{6,7},{7,4},{8,9},{9,10},{10,1... | collective-permute-start | bytes 196616 | tf_op jit(solution)/shard_map/ppermute | solution.py:159
  1.5 2.7 %collective-permute-start.1 = (bf16[2,128,128]{2,1,0:T(8,128)(2,1)}, bf16[2,128,128]{2,1,0:T(8,128)(2,1)S(1)}, u32[]{:S(2)}, u32[]{:S(2)}) collective-permute-start(bf16[2,128,128]{2,1,0:T(8,128)(2,1)} %bitcast.21), channel_id=1, source_target_pairs={{0,2},{1,3},{2,0},{3,1},{4,6},{5,7},{6,4},{7,5},{8,10},{9,11},{10,... | collective-permute-start | bytes 196616 | tf_op jit(solution)/shard_map/ppermute | solution.py:161
  4.2 1.4 %collective-permute-start.2 = (bf16[2,128,128]{2,1,0:T(8,128)(2,1)}, bf16[2,128,128]{2,1,0:T(8,128)(2,1)S(1)}, u32[]{:S(2)}, u32[]{:S(2)}) collective-permute-start(bf16[2,128,128]{2,1,0:T(8,128)(2,1)} %bitcast.22), channel_id=1, source_target_pairs={{0,3},{1,0},{2,1},{3,2},{4,7},{5,4},{6,5},{7,6},{8,11},{9,8},{10,9... | collective-permute-start | bytes 196616 | tf_op jit(solution)/shard_map/ppermute | solution.py:160
  6.5 0.9 %collective-permute-done.1 = bf16[2,128,128]{2,1,0:T(8,128)(2,1)S(1)} collective-permute-done((bf16[2,128,128]{2,1,0:T(8,128)(2,1)}, bf16[2,128,128]{2,1,0:T(8,128)(2,1)S(1)}, u32[]{:S(2)}, u32[]{:S(2)}) %collective-permute-start.1) | collective-permute-done | bytes 65568 | tf_op jit(solution)/shard_map/ppermute | solution.py:161
  7.5 1.2 %collective-permute-done.2 = bf16[2,128,128]{2,1,0:T(8,128)(2,1)S(1)} collective-permute-done((bf16[2,128,128]{2,1,0:T(8,128)(2,1)}, bf16[2,128,128]{2,1,0:T(8,128)(2,1)S(1)}, u32[]{:S(2)}, u32[]{:S(2)}) %collective-permute-start.2) | collective-permute-done | bytes 65568 | tf_op jit(solution)/shard_map/ppermute | solution.py:160
  9.6 3.3 %collective-permute-start.5 = (bf16[8,128,128]{2,1,0:T(8,128)(2,1)S(1)}, bf16[8,128,128]{2,1,0:T(8,128)(2,1)S(1)}, u32[]{:S(2)}, u32[]{:S(2)}) collective-permute-start(bf16[8,128,128]{2,1,0:T(8,128)(2,1)S(1)} %pad_maximum_fusion), channel_id=1, source_target_pairs={{0,8},{1,9},{2,10},{3,11},{4,12},{5,13},{6,14},{7,15},{8,0},{9,1},... | collective-permute-start | bytes 786440 | tf_op jit(solution)/shard_map/ppermute | solution.py:163
  12.9 1.9 %collective-permute-start.6 = (bf16[8,128,128]{2,1,0:T(8,128)(2,1)S(1)}, bf16[8,128,128]{2,1,0:T(8,128)(2,1)S(1)}, u32[]{:S(2)}, u32[]{:S(2)}) collective-permute-start(bf16[8,128,128]{2,1,0:T(8,128)(2,1)S(1)} %pad_maximum_fusion), channel_id=1, source_target_pairs={{16,32},{32,16},{48,64},{64,48},{80,96},{96,80},{112,128},{128,112... | collective-permute-start | bytes 786440 | tf_op jit(solution)/shard_map/ppermute | solution.py:164
  15.5 2.6 %collective-permute-start.4 = (bf16[8,128,128]{2,1,0:T(8,128)(2,1)S(1)}, bf16[8,128,128]{2,1,0:T(8,128)(2,1)S(1)}, u32[]{:S(2)}, u32[]{:S(2)}) collective-permute-start(bf16[8,128,128]{2,1,0:T(8,128)(2,1)S(1)} %pad_maximum_fusion), channel_id=1, source_target_pairs={{0,12},{1,13},{2,14},{3,15},{4,0},{5,1},{6,2},{7,3},{8,4},{9,5},{1... | collective-permute-start | bytes 786440 | tf_op jit(solution)/shard_map/ppermute | solution.py:166
  18.2 2.4 %collective-permute-done.6.n0 = bf16[8,128,128]{2,1,0:T(8,128)(2,1)S(1)} collective-permute-done((bf16[8,128,128]{2,1,0:T(8,128)(2,1)S(1)}, bf16[8,128,128]{2,1,0:T(8,128)(2,1)S(1)}, u32[]{:S(2)}, u32[]{:S(2)}) %collective-permute-start.6) | collective-permute-done | bytes 262176 | tf_op jit(solution)/shard_map/ppermute | solution.py:164
  20.5 1.9 %collective-permute-done.3 = bf16[8,128,128]{2,1,0:T(8,128)(2,1)S(1)} collective-permute-done((bf16[8,128,128]{2,1,0:T(8,128)(2,1)S(1)}, bf16[8,128,128]{2,1,0:T(8,128)(2,1)S(1)}, u32[]{:S(2)}, u32[]{:S(2)}) %collective-permute-start.3) | collective-permute-done | bytes 262176 | tf_op jit(solution)/shard_map/ppermute | solution.py:165
  22.6 2.2 %collective-permute-start.10 = (bf16[32,128,128]{2,1,0:T(8,128)(2,1)S(1)}, bf16[32,128,128]{2,1,0:T(8,128)(2,1)S(1)}, u32[]{:S(2)}, u32[]{:S(2)}) collective-permute-start(bf16[32,128,128]{2,1,0:T(8,128)(2,1)S(1)} %constant_dynamic-update-slice_fusion.plane), channel_id=1, source_target_pairs={{0,16},{16,0},{32,48},{48,32},{64,80},{80,64},{96,112},{112,96},{1... | collective-permute-start | bytes 3145736 | tf_op jit(solution)/shard_map/ppermute | solution.py:173
  24.7 2.7 %collective-permute-start.7 = (bf16[8,128,128]{2,1,0:T(8,128)(2,1)S(1)}, bf16[8,128,128]{2,1,0:T(8,128)(2,1)S(1)}, u32[]{:S(2)}, u32[]{:S(2)}) collective-permute-start(bf16[8,128,128]{2,1,0:T(8,128)(2,1)S(1)} %collective-permute-done.6.n0), channel_id=1, source_target_pairs={{16,20},{17,21},{18,22},{19,23},{20,24},{21,25},{22,26},{23,27},{2... | collective-permute-start | bytes 786440 | tf_op jit(solution)/shard_map/ppermute | solution.py:168
  27.5 4.3 %collective-permute-start.9 = (bf16[8,128,128]{2,1,0:T(8,128)(2,1)S(1)}, bf16[8,128,128]{2,1,0:T(8,128)(2,1)S(1)}, u32[]{:S(2)}, u32[]{:S(2)}) collective-permute-start(bf16[8,128,128]{2,1,0:T(8,128)(2,1)S(1)} %collective-permute-done.6.n0), channel_id=1, source_target_pairs={{16,28},{17,29},{18,30},{19,31},{20,16},{21,17},{22,18},{23,19},{2... | collective-permute-start | bytes 786440 | tf_op jit(solution)/shard_map/ppermute | solution.py:169
  31.8 1.9 %collective-permute-start.8 = (bf16[8,128,128]{2,1,0:T(8,128)(2,1)S(1)}, bf16[8,128,128]{2,1,0:T(8,128)(2,1)S(1)}, u32[]{:S(2)}, u32[]{:S(2)}) collective-permute-start(bf16[8,128,128]{2,1,0:T(8,128)(2,1)S(1)} %collective-permute-done.5), channel_id=1, source_target_pairs={{16,32},{32,16},{48,64},{64,48},{80,96},{96,80},{112,128},{128,112... | collective-permute-start | bytes 786440 | tf_op jit(solution)/shard_map/ppermute | solution.py:170
  35.3 1.2 %copy-done = bf16[16,2,128,128]{3,2,1,0:T(8,128)(2,1)S(1)} copy-done((bf16[16,2,128,128]{3,2,1,0:T(8,128)(2,1)S(1)}, bf16[16,2,128,128]{3,2,1,0:T(8,128)(2,1)}, u32[]{:S(2)}) %copy-start) | copy-done | bytes 1048600
  37.2 6.5 %own.1 = (bf16[33,256,256]{2,1,0:T(8,128)(2,1)S(1)}, f32[256,256]{1,0:T(8,128)S(1)}) custom-call(s32[16,2]{1,0:T(8,128)S(1)} %copy.10.cols, s32[256,2]{1,0:T(8,128)S(1)} %copy.11.aggs, s32[32]{0:T(128)S(1)} %copy-done.1, bf16[16,2,128,128]{3,2,1,0:T(8,128)(2,1)S(1)} %copy-done, bf16[32,128,128]{2,1,0:T(8,128)(2,1)S(1)} %constant_dynamic-update-slice_fusion.plane), custom_call_target="tpu_custom_call" | custom-call | flops 1000000 | bytes 4096 | tf_op jit(solution)/shard_map/own/pallas_call | solution.py:178
  43.7 5.0 %pair.1.acc_pair = f32[256,256]{1,0:T(8,128)S(1)} custom-call(s32[16,2]{1,0:T(8,128)S(1)} %copy.10.cols, s32[256,2]{1,0:T(8,128)S(1)} %copy.11.aggs, s32[32]{0:T(128)S(1)} %copy-done.1, bf16[33,256,256]{2,1,0:T(8,128)(2,1)S(1)} %get-tuple-element.20.split, bf16[32,128,128]{2,1,0:T(8,128)(2,1)S(1)} %collective-permute-done.10.pair), custom_call_target="tpu_custom_call" | custom-call | flops 1000000 | bytes 4096 | tf_op jit(solution)/shard_map/pair/pallas_call | solution.py:188
  48.8 5.2 %beside.1 = (f32[4,2,8,768]{3,2,1,0:T(8,128)S(1)}, f32[4,2,8,768]{3,2,1,0:T(8,128)S(1)}, f32[4,2,8,768]{3,2,1,0:T(8,128)S(1)}, f32[4,2,8,768]{3,2,1,0:T(8,128)S(1)}) custom-call(s32[16,2]{1,0:T(8,128)S(1)} %copy.10.cols, s32[256,2]{1,0:T(8,128)S(1)} %copy.11.aggs, s32[32]{0:T(128)S(1)} %copy-done.1, bf16[33,256,256]{2,1,0:T(8,128)(2,1)S(1)} %get-tuple-element.20.split, ...), custom_call_target="tpu_custom_call" | custom-call | flops 1000000 | bytes 4096 | tf_op jit(solution)/shard_map/beside/pallas_call | solution.py:199
  54.1 3.2 %collective-permute-start.12 = (f32[4,2,8,768]{3,2,1,0:T(8,128)S(1)}, f32[4,2,8,768]{3,2,1,0:T(8,128)S(1)}, u32[]{:S(2)}, u32[]{:S(2)}) collective-permute-start(f32[4,2,8,768]{3,2,1,0:T(8,128)S(1)} %get-tuple-element.25), channel_id=1, source_target_pairs={{0,2},{1,3},{2,0},{3,1},{4,6},{5,7},{6,4},{7,5},{8,10},{9,11},{10,... | collective-permute-start | bytes 589832 | tf_op jit(solution)/shard_map/ppermute | solution.py:216
  58.1 2.9 %collective-permute-done.11 = f32[4,2,8,768]{3,2,1,0:T(8,128)S(1)} collective-permute-done((f32[4,2,8,768]{3,2,1,0:T(8,128)S(1)}, f32[4,2,8,768]{3,2,1,0:T(8,128)S(1)}, u32[]{:S(2)}, u32[]{:S(2)}) %collective-permute-start.11) | collective-permute-done | bytes 196640 | tf_op jit(solution)/shard_map/ppermute | solution.py:214
  60.9 2.1 %collective-permute-done.12 = f32[4,2,8,768]{3,2,1,0:T(8,128)S(1)} collective-permute-done((f32[4,2,8,768]{3,2,1,0:T(8,128)S(1)}, f32[4,2,8,768]{3,2,1,0:T(8,128)S(1)}, u32[]{:S(2)}, u32[]{:S(2)}) %collective-permute-start.12) | collective-permute-done | bytes 196640 | tf_op jit(solution)/shard_map/ppermute | solution.py:216
  64.7 2.1 %collective-permute-start.15 = (f32[2,8,768]{2,1,0:T(8,128)S(1)}, f32[2,8,768]{2,1,0:T(8,128)S(1)}, u32[]{:S(2)}, u32[]{:S(2)}) collective-permute-start(f32[2,8,768]{2,1,0:T(8,128)S(1)} %get-tuple-element.29), channel_id=1, source_target_pairs={{0,8},{1,9},{2,10},{3,11},{4,12},{5,13},{6,14},{7,15},{8,0},{9,1},... | collective-permute-start | bytes 147464 | tf_op jit(solution)/shard_map/ppermute | solution.py:220
  67.5 1.9 %collective-permute-done.14 = f32[2,8,768]{2,1,0:T(8,128)S(1)} collective-permute-done((f32[2,8,768]{2,1,0:T(8,128)S(1)}, f32[2,8,768]{2,1,0:T(8,128)S(1)}, u32[]{:S(2)}, u32[]{:S(2)}) %collective-permute-start.14) | collective-permute-done | bytes 49184 | tf_op jit(solution)/shard_map/ppermute | solution.py:218
  69.3 1.0 %collective-permute-done.15 = f32[2,8,768]{2,1,0:T(8,128)S(1)} collective-permute-done((f32[2,8,768]{2,1,0:T(8,128)S(1)}, f32[2,8,768]{2,1,0:T(8,128)S(1)}, u32[]{:S(2)}, u32[]{:S(2)}) %collective-permute-start.15) | collective-permute-done | bytes 49184 | tf_op jit(solution)/shard_map/ppermute | solution.py:220
  (29 shorter events, 9.4 us)
Async XLA Ops:
  0.0 6.5 %collective-permute-start = (bf16[2,128,128]{2,1,0:T(8,128)(2,1)}, bf16[2,128,128]{2,1,0:T(8,128)(2,1)S(1)}, u32[]{:S(2)}, u32[]{:S(2)}) collective-permute-start(bf16[2,128,128]{2,1,0:T(8,128)(2,1)} %bitcast.20), channel_id=1, source_target_pairs={{0,1},{1,2},{2,3},{3,0},{4,5},{5,6},{6,7},{7,4},{8,9},{9,10},{10,1... | collective-permute-start | bytes 196616 | tf_op jit(solution)/shard_map/ppermute | solution.py:159
  1.5 6.0 %collective-permute-start.1 = (bf16[2,128,128]{2,1,0:T(8,128)(2,1)}, bf16[2,128,128]{2,1,0:T(8,128)(2,1)S(1)}, u32[]{:S(2)}, u32[]{:S(2)}) collective-permute-start(bf16[2,128,128]{2,1,0:T(8,128)(2,1)} %bitcast.21), channel_id=1, source_target_pairs={{0,2},{1,3},{2,0},{3,1},{4,6},{5,7},{6,4},{7,5},{8,10},{9,11},{10,... | collective-permute-start | bytes 196616 | tf_op jit(solution)/shard_map/ppermute | solution.py:161
  4.2 4.5 %collective-permute-start.2 = (bf16[2,128,128]{2,1,0:T(8,128)(2,1)}, bf16[2,128,128]{2,1,0:T(8,128)(2,1)S(1)}, u32[]{:S(2)}, u32[]{:S(2)}) collective-permute-start(bf16[2,128,128]{2,1,0:T(8,128)(2,1)} %bitcast.22), channel_id=1, source_target_pairs={{0,3},{1,0},{2,1},{3,2},{4,7},{5,4},{6,5},{7,6},{8,11},{9,8},{10,9... | collective-permute-start | bytes 196616 | tf_op jit(solution)/shard_map/ppermute | solution.py:160
  9.6 8.6 %collective-permute-start.5 = (bf16[8,128,128]{2,1,0:T(8,128)(2,1)S(1)}, bf16[8,128,128]{2,1,0:T(8,128)(2,1)S(1)}, u32[]{:S(2)}, u32[]{:S(2)}) collective-permute-start(bf16[8,128,128]{2,1,0:T(8,128)(2,1)S(1)} %pad_maximum_fusion), channel_id=1, source_target_pairs={{0,8},{1,9},{2,10},{3,11},{4,12},{5,13},{6,14},{7,15},{8,0},{9,1},... | collective-permute-start | bytes 786440 | tf_op jit(solution)/shard_map/ppermute | solution.py:163
  12.9 7.7 %collective-permute-start.6 = (bf16[8,128,128]{2,1,0:T(8,128)(2,1)S(1)}, bf16[8,128,128]{2,1,0:T(8,128)(2,1)S(1)}, u32[]{:S(2)}, u32[]{:S(2)}) collective-permute-start(bf16[8,128,128]{2,1,0:T(8,128)(2,1)S(1)} %pad_maximum_fusion), channel_id=1, source_target_pairs={{16,32},{32,16},{48,64},{64,48},{80,96},{96,80},{112,128},{128,112... | collective-permute-start | bytes 786440 | tf_op jit(solution)/shard_map/ppermute | solution.py:164
  14.8 7.7 %collective-permute-start.3 = (bf16[8,128,128]{2,1,0:T(8,128)(2,1)S(1)}, bf16[8,128,128]{2,1,0:T(8,128)(2,1)S(1)}, u32[]{:S(2)}, u32[]{:S(2)}) collective-permute-start(bf16[8,128,128]{2,1,0:T(8,128)(2,1)S(1)} %pad_maximum_fusion), channel_id=1, source_target_pairs={{0,4},{1,5},{2,6},{3,7},{4,8},{5,9},{6,10},{7,11},{8,12},{9,13},{1... | collective-permute-start | bytes 786440 | tf_op jit(solution)/shard_map/ppermute | solution.py:165
  15.5 6.9 %collective-permute-start.4 = (bf16[8,128,128]{2,1,0:T(8,128)(2,1)S(1)}, bf16[8,128,128]{2,1,0:T(8,128)(2,1)S(1)}, u32[]{:S(2)}, u32[]{:S(2)}) collective-permute-start(bf16[8,128,128]{2,1,0:T(8,128)(2,1)S(1)} %pad_maximum_fusion), channel_id=1, source_target_pairs={{0,12},{1,13},{2,14},{3,15},{4,0},{5,1},{6,2},{7,3},{8,4},{9,5},{1... | collective-permute-start | bytes 786440 | tf_op jit(solution)/shard_map/ppermute | solution.py:166
  22.6 21.1 %collective-permute-start.10 = (bf16[32,128,128]{2,1,0:T(8,128)(2,1)S(1)}, bf16[32,128,128]{2,1,0:T(8,128)(2,1)S(1)}, u32[]{:S(2)}, u32[]{:S(2)}) collective-permute-start(bf16[32,128,128]{2,1,0:T(8,128)(2,1)S(1)} %constant_dynamic-update-slice_fusion.plane), channel_id=1, source_target_pairs={{0,16},{16,0},{32,48},{48,32},{64,80},{80,64},{96,112},{112,96},{1... | collective-permute-start | bytes 3145736 | tf_op jit(solution)/shard_map/ppermute | solution.py:173
  24.7 24.0 %collective-permute-start.7 = (bf16[8,128,128]{2,1,0:T(8,128)(2,1)S(1)}, bf16[8,128,128]{2,1,0:T(8,128)(2,1)S(1)}, u32[]{:S(2)}, u32[]{:S(2)}) collective-permute-start(bf16[8,128,128]{2,1,0:T(8,128)(2,1)S(1)} %collective-permute-done.6.n0), channel_id=1, source_target_pairs={{16,20},{17,21},{18,22},{19,23},{20,24},{21,25},{22,26},{23,27},{2... | collective-permute-start | bytes 786440 | tf_op jit(solution)/shard_map/ppermute | solution.py:168
  27.5 21.3 %collective-permute-start.9 = (bf16[8,128,128]{2,1,0:T(8,128)(2,1)S(1)}, bf16[8,128,128]{2,1,0:T(8,128)(2,1)S(1)}, u32[]{:S(2)}, u32[]{:S(2)}) collective-permute-start(bf16[8,128,128]{2,1,0:T(8,128)(2,1)S(1)} %collective-permute-done.6.n0), channel_id=1, source_target_pairs={{16,28},{17,29},{18,30},{19,31},{20,16},{21,17},{22,18},{23,19},{2... | collective-permute-start | bytes 786440 | tf_op jit(solution)/shard_map/ppermute | solution.py:169
  31.8 17.0 %collective-permute-start.8 = (bf16[8,128,128]{2,1,0:T(8,128)(2,1)S(1)}, bf16[8,128,128]{2,1,0:T(8,128)(2,1)S(1)}, u32[]{:S(2)}, u32[]{:S(2)}) collective-permute-start(bf16[8,128,128]{2,1,0:T(8,128)(2,1)S(1)} %collective-permute-done.5), channel_id=1, source_target_pairs={{16,32},{32,16},{48,64},{64,48},{80,96},{96,80},{112,128},{128,112... | collective-permute-start | bytes 786440 | tf_op jit(solution)/shard_map/ppermute | solution.py:170
  35.3 1.2 %copy-start = (bf16[16,2,128,128]{3,2,1,0:T(8,128)(2,1)S(1)}, bf16[16,2,128,128]{3,2,1,0:T(8,128)(2,1)}, u32[]{:S(2)}) copy-start(bf16[16,2,128,128]{3,2,1,0:T(8,128)(2,1)} %a.1) | copy-start | bytes 3145732
  36.5 0.7 copy-start.1
  54.0 7.0 %collective-permute-start.11 = (f32[4,2,8,768]{3,2,1,0:T(8,128)S(1)}, f32[4,2,8,768]{3,2,1,0:T(8,128)S(1)}, u32[]{:S(2)}, u32[]{:S(2)}) collective-permute-start(f32[4,2,8,768]{3,2,1,0:T(8,128)S(1)} %get-tuple-element.24), channel_id=1, source_target_pairs={{0,1},{1,2},{2,3},{3,0},{4,5},{5,6},{6,7},{7,4},{8,9},{9,10},{10,1... | collective-permute-start | bytes 589832 | tf_op jit(solution)/shard_map/ppermute | solution.py:214
  54.1 9.0 %collective-permute-start.12 = (f32[4,2,8,768]{3,2,1,0:T(8,128)S(1)}, f32[4,2,8,768]{3,2,1,0:T(8,128)S(1)}, u32[]{:S(2)}, u32[]{:S(2)}) collective-permute-start(f32[4,2,8,768]{3,2,1,0:T(8,128)S(1)} %get-tuple-element.25), channel_id=1, source_target_pairs={{0,2},{1,3},{2,0},{3,1},{4,6},{5,7},{6,4},{7,5},{8,10},{9,11},{10,... | collective-permute-start | bytes 589832 | tf_op jit(solution)/shard_map/ppermute | solution.py:216
  57.2 6.6 %collective-permute-start.13 = (f32[4,2,8,768]{3,2,1,0:T(8,128)S(1)}, f32[4,2,8,768]{3,2,1,0:T(8,128)S(1)}, u32[]{:S(2)}, u32[]{:S(2)}) collective-permute-start(f32[4,2,8,768]{3,2,1,0:T(8,128)S(1)} %get-tuple-element.26), channel_id=1, source_target_pairs={{0,3},{1,0},{2,1},{3,2},{4,7},{5,4},{6,5},{7,6},{8,11},{9,8},{10,9... | collective-permute-start | bytes 589832 | tf_op jit(solution)/shard_map/ppermute | solution.py:215
  63.9 5.4 %collective-permute-start.14 = (f32[2,8,768]{2,1,0:T(8,128)S(1)}, f32[2,8,768]{2,1,0:T(8,128)S(1)}, u32[]{:S(2)}, u32[]{:S(2)}) collective-permute-start(f32[2,8,768]{2,1,0:T(8,128)S(1)} %get-tuple-element.27), channel_id=1, source_target_pairs={{0,4},{1,5},{2,6},{3,7},{4,8},{5,9},{6,10},{7,11},{8,12},{9,13},{1... | collective-permute-start | bytes 147464 | tf_op jit(solution)/shard_map/ppermute | solution.py:218
  64.7 5.6 %collective-permute-start.15 = (f32[2,8,768]{2,1,0:T(8,128)S(1)}, f32[2,8,768]{2,1,0:T(8,128)S(1)}, u32[]{:S(2)}, u32[]{:S(2)}) collective-permute-start(f32[2,8,768]{2,1,0:T(8,128)S(1)} %get-tuple-element.29), channel_id=1, source_target_pairs={{0,8},{1,9},{2,10},{3,11},{4,12},{5,13},{6,14},{7,15},{8,0},{9,1},... | collective-permute-start | bytes 147464 | tf_op jit(solution)/shard_map/ppermute | solution.py:220
  66.8 4.1 %collective-permute-start.16 = (f32[2,8,768]{2,1,0:T(8,128)S(1)}, f32[2,8,768]{2,1,0:T(8,128)S(1)}, u32[]{:S(2)}, u32[]{:S(2)}) collective-permute-start(f32[2,8,768]{2,1,0:T(8,128)S(1)} %get-tuple-element.28), channel_id=1, source_target_pairs={{0,12},{1,13},{2,14},{3,15},{4,0},{5,1},{6,2},{7,3},{8,4},{9,5},{1... | collective-permute-start | bytes 147464 | tf_op jit(solution)/shard_map/ppermute | solution.py:219

commit v3 on v1

v3 whole, which is shorter than its diff:
```python
import jax
import jax.numpy as jnp
from jax import lax
from jax.experimental import pallas as pl
from jax.experimental.pallas import tpu as pltpu
from jax.sharding import PartitionSpec as P

ROWS = 16
SIDE = 4
B = 128
BOTH = ("row", "col")


def crossed(row):
    return (row + 1) // 2 % 2


def moved(along, step):
    pairs = []
    for r in range(ROWS):
        dy, dx = ((0, step), (step, 0))[crossed(r) ^ along]
        for y in range(SIDE):
            for x in range(SIDE):
                target = ((y + dy) % SIDE) * SIDE + (x + dx) % SIDE
                pairs.append((r * ROWS + y * SIDE + x, r * ROWS + target))
    return pairs


def first(step):
    return moved(0, step)


def second(step):
    return moved(1, step)


def row_pairs(start):
    pairs = []
    for r in range(start, ROWS - 1, 2):
        pairs += [(r, r + 1), (r + 1, r)]
    return pairs


def place():
    row = lax.axis_index("row")
    col = lax.axis_index("col")
    return row, crossed(row), col // SIDE, col % SIDE


def slot_of(y, x, j, cross):
    dy, dx = (y - (j % ROWS) // SIDE) & 3, (x - j % SIDE) & 3
    return jnp.where(cross == 0, dy * SIDE + dx, dx * SIDE + dy)


def fetch_kernel(a, shard, a_near, shard_near, sems):
    copies = [
        pltpu.make_async_copy(shard, shard_near, sems.at[0]),
        pltpu.make_async_copy(a, a_near, sems.at[1]),
    ]
    for copy in copies:
        copy.start()
    for copy in copies:
        copy.wait()


def lift_kernel(aggs, agglo, a, plane, split):
    row, cross, y, x = place()
    for i in range(ROWS):
        swap = agglo[aggs[0, row * ROWS + i]] & 1
        spot = slot_of(y, x, i, cross) * 2
        left = jnp.concatenate([plane[spot + swap], plane[spot + 1 - swap]], axis=1)
        right = jnp.concatenate([a[i, 0], a[i, 1]], axis=1)
        lifted = lax.dot_general(
            left, right, (((0,), (0,)), ((), ())), preferred_element_type=jnp.float32
        )
        high = lifted.astype(jnp.bfloat16)
        low = (lifted - high.astype(jnp.float32)).astype(jnp.bfloat16)
        for s in range(2):
            split[i * 2 + s, :, :B] = high[:, s * B : (s + 1) * B]
            split[i * 2 + s, :, B:] = low[:, s * B : (s + 1) * B]


def band_kernel(
    cols, aggs, agglo, split, plane, near, f, b, far, pair, o0, o1, o2, o3, blocks, acc
):
    row, cross, y, x = place()
    blocks[0:32] = plane[...]
    blocks[32:40] = near[...]
    blocks[40:48] = f[8:16]
    blocks[48:56] = far[...]
    blocks[56:64] = b[8:16]
    blocks[64:96] = pair[...]
    acc[...] = jnp.zeros_like(acc)
    pair_band = 2 - 2 * (row % 2)
    for i in range(ROWS):
        for s in range(2):
            j = cols[s, i]
            swap = agglo[aggs[0, j]] & 1
            band = j // ROWS - row + 1
            base = jnp.where(band == 1, 0, jnp.where(band == pair_band, 64, 32))
            spot = base + slot_of(y, x, j, jnp.where(band == pair_band, 1 - cross, cross)) * 2
            right = jnp.concatenate([blocks[spot + swap], blocks[spot + 1 - swap]], axis=1)
            right = jnp.concatenate([right, right], axis=0)
            acc[band] += jnp.dot(split[i * 2 + s], right, preferred_element_type=jnp.float32)
    for rel, out in enumerate((o0, o1, o2, o3)):
        for m in range(SIDE):
            d = jnp.where(
                cross == 0,
                ((y + m) & 3) * SIDE + ((x + rel) & 3),
                ((y + rel) & 3) * SIDE + ((x + m) & 3),
            )
            for k in range(2):
                start = pl.multiple_of(k * B + d * 8, 8)
                for t in range(3):
                    out[m, k, :, t * 256 : (t + 1) * 256] = acc[t, pl.ds(start, 8), :]


def vmem():
    return pl.BlockSpec(memory_space=pltpu.VMEM)


def smem():
    return pl.BlockSpec(memory_space=pltpu.SMEM)


def params(mib):
    return pltpu.CompilerParams(vmem_limit_bytes=mib * 2**20)


def local(a_blocks, a_cols, p_blocks, p_aggs, agglo):
    shard = p_blocks[0]
    line_f = lax.ppermute(shard, BOTH, first(1))
    line_b = lax.ppermute(shard, BOTH, first(-1))
    line_d = lax.ppermute(shard, BOTH, first(2))
    a_near, shard_near = pl.pallas_call(
        fetch_kernel,
        out_shape=[
            jax.ShapeDtypeStruct(a_blocks.shape, a_blocks.dtype),
            jax.ShapeDtypeStruct(shard.shape, shard.dtype),
        ],
        in_specs=[pl.BlockSpec(memory_space=pl.ANY)] * 2,
        out_specs=[vmem()] * 2,
        scratch_shapes=[pltpu.SemaphoreType.DMA((2,))],
        compiler_params=params(8),
        name="fetch",
    )(a_blocks, shard)
    line = jnp.concatenate([shard_near, line_f, line_d, line_b])
    plane_d = lax.ppermute(line, BOTH, second(2))
    near = lax.ppermute(line, "row", row_pairs(1))
    plane_d, near = lax.optimization_barrier((plane_d, near))
    lines = jnp.concatenate([line, near])
    plane_f = lax.ppermute(lines, BOTH, second(1))
    plane_b = lax.ppermute(lines, BOTH, second(-1))
    far = lax.ppermute(plane_d, "row", row_pairs(1))
    plane_f, plane_b, far = lax.optimization_barrier((plane_f, plane_b, far))
    plane = jnp.concatenate([line, plane_f[:8], plane_d, plane_b[:8]])
    pair = lax.ppermute(plane, "row", row_pairs(0))

    cols, aggs = a_cols.T, p_aggs.T
    split = pl.pallas_call(
        lift_kernel,
        out_shape=jax.ShapeDtypeStruct((2 * ROWS, 256, 256), jnp.bfloat16),
        in_specs=[smem(), smem(), vmem(), vmem()],
        out_specs=vmem(),
        compiler_params=params(16),
        name="lift",
    )(aggs, agglo, a_near, plane)
    piece = jax.ShapeDtypeStruct((SIDE, 2, 8, 768), jnp.float32)
    o0, o1, o2, o3 = pl.pallas_call(
        band_kernel,
        out_shape=[piece] * 4,
        in_specs=[smem()] * 3 + [vmem()] * 7,
        out_specs=[vmem()] * 4,
        scratch_shapes=[
            pltpu.VMEM((96, B, B), jnp.bfloat16),
            pltpu.VMEM((3, 256, 256), jnp.float32),
        ],
        compiler_params=params(24),
        name="bands",
    )(cols, aggs, agglo, split, plane, near, plane_f, plane_b, far, pair)

    d = lax.ppermute(o2, BOTH, first(2))
    f = lax.ppermute(o1, BOTH, first(1))
    b = lax.ppermute(o3, BOTH, first(-1))
    kept, to_f, to_d, to_b = (o0[m] + f[m] + d[m] + b[m] for m in range(SIDE))
    d = lax.ppermute(to_d, BOTH, second(2))
    f = lax.ppermute(to_f, BOTH, second(1))
    b = lax.ppermute(to_b, BOTH, second(-1))
    return (kept + f + d + b).reshape(2, 8, 6, B)


def solution(mesh):
    placed = (
        P("row", "col", None, None),
        P("row", "col"),
        P(("row", "col"), None, None, None),
        P(),
        P(),
    )
    return jax.shard_map(
        local, mesh=mesh, in_specs=placed, out_specs=P("row", "col", None, None), check_vma=False
    )
```

time: 73.2 us -> 56.9 us (0.78)
  the two profiles are of different devices: /device:TPU:248 before, /device:TPU:96 now
where the time goes in v3:
time: 56.9 us; the launch traced here: 56.7 us
  starting transfers between devices  25.3 us (44%)
  waiting for transfers between devices  24.2 us (43%)
  Pallas kernels  4.09 us (7%)
  local copies, waits for them, and re-layouts  2.38 us (4%)
  other arithmetic  0.67 us (1%)
    ppermute x1, waiting for transfers between devices, local(): far = lax.ppermute(plane_d, 'row', row_pairs(1))  5.76 us
    ppermute x1, waiting for transfers between devices, local(): d = lax.ppermute(o2, BOTH, first(2))  5.06 us
    ppermute x1, starting transfers between devices, local(): d = lax.ppermute(to_d, BOTH, second(2))  3.53 us
    ppermute x1, starting transfers between devices, local(): plane_d = lax.ppermute(line, BOTH, second(2))  3.11 us
    ppermute x1, waiting for transfers between devices, local(): plane_d = lax.ppermute(line, BOTH, second(2))  2.94 us
    ppermute x1, starting transfers between devices, local(): line_d = lax.ppermute(shard, BOTH, first(2))  2.9 us
    ppermute x1, waiting for transfers between devices, local(): near = lax.ppermute(line, 'row', row_pairs(1))  2.83 us
    ppermute x1, starting transfers between devices, local(): pair = lax.ppermute(plane, 'row', row_pairs(0))  2.72 us
  transfers between devices with their start and end apart: 15, of which 10 were waited for; matrix products, arithmetic and copies ran while one was open for 0% of the time, Pallas kernels for 3%

profile of v3, /device:TPU:96, one launch (start us, length us, event | category | flops | bytes accessed | tf_op | source)
XLA Modules:
  0.0 56.7 jit_solution(10396814523415524725)
XLA Ops:
  0.0 1.6 %collective-permute-start = (bf16[2,128,128]{2,1,0:T(8,128)(2,1)}, bf16[2,128,128]{2,1,0:T(8,128)(2,1)S(1)}, u32[]{:S(2)}, u32[]{:S(2)}) collective-permute-start(bf16[2,128,128]{2,1,0:T(8,128)(2,1)} %bitcast.21), channel_id=1, source_target_pairs={{0,1},{1,2},{2,3},{3,0},{4,5},{5,6},{6,7},{7,4},{8,9},{9,10},{10,1... | collective-permute-start | bytes 196616 | tf_op jit(solution)/shard_map/ppermute | solution.py:132
  1.6 2.9 %collective-permute-start.1 = (bf16[2,128,128]{2,1,0:T(8,128)(2,1)}, bf16[2,128,128]{2,1,0:T(8,128)(2,1)S(1)}, u32[]{:S(2)}, u32[]{:S(2)}) collective-permute-start(bf16[2,128,128]{2,1,0:T(8,128)(2,1)} %bitcast.22), channel_id=1, source_target_pairs={{0,2},{1,3},{2,0},{3,1},{4,6},{5,7},{6,4},{7,5},{8,10},{9,11},{10,... | collective-permute-start | bytes 196616 | tf_op jit(solution)/shard_map/ppermute | solution.py:134
  4.5 1.3 %collective-permute-start.2 = (bf16[2,128,128]{2,1,0:T(8,128)(2,1)}, bf16[2,128,128]{2,1,0:T(8,128)(2,1)S(1)}, u32[]{:S(2)}, u32[]{:S(2)}) collective-permute-start(bf16[2,128,128]{2,1,0:T(8,128)(2,1)} %bitcast.23), channel_id=1, source_target_pairs={{0,3},{1,0},{2,1},{3,2},{4,7},{5,4},{6,5},{7,6},{8,11},{9,8},{10,9... | collective-permute-start | bytes 196616 | tf_op jit(solution)/shard_map/ppermute | solution.py:133
  5.8 1.2 %copy-done = bf16[16,2,128,128]{3,2,1,0:T(8,128)(2,1)S(1)} copy-done((bf16[16,2,128,128]{3,2,1,0:T(8,128)(2,1)S(1)}, bf16[16,2,128,128]{3,2,1,0:T(8,128)(2,1)}, u32[]{:S(2)}) %copy-start) | copy-done | bytes 1048600
  7.1 0.8 %copy-done.1 = bf16[1,2,128,128]{3,2,1,0:T(8,128)(2,1)S(1)} copy-done((bf16[1,2,128,128]{3,2,1,0:T(8,128)(2,1)S(1)}, bf16[1,2,128,128]{3,2,1,0:T(8,128)(2,1)}, u32[]{:S(2)}) %copy-start.1) | copy-done | bytes 65560
  8.2 0.7 %collective-permute-done.2 = bf16[2,128,128]{2,1,0:T(8,128)(2,1)S(1)} collective-permute-done((bf16[2,128,128]{2,1,0:T(8,128)(2,1)}, bf16[2,128,128]{2,1,0:T(8,128)(2,1)S(1)}, u32[]{:S(2)}, u32[]{:S(2)}) %collective-permute-start.2) | collective-permute-done | bytes 65568 | tf_op jit(solution)/shard_map/ppermute | solution.py:133
  9.0 3.1 %collective-permute-start.3 = (bf16[8,128,128]{2,1,0:T(8,128)(2,1)S(1)}, bf16[8,128,128]{2,1,0:T(8,128)(2,1)S(1)}, u32[]{:S(2)}, u32[]{:S(2)}) collective-permute-start(bf16[8,128,128]{2,1,0:T(8,128)(2,1)S(1)} %get-tuple-element.30), channel_id=1, source_target_pairs={{0,8},{1,9},{2,10},{3,11},{4,12},{5,13},{6,14},{7,15},{8,0},{9,1},... | collective-permute-start | bytes 786440 | tf_op jit(solution)/shard_map/ppermute | solution.py:148
  12.1 1.9 %collective-permute-start.4 = (bf16[8,128,128]{2,1,0:T(8,128)(2,1)S(1)}, bf16[8,128,128]{2,1,0:T(8,128)(2,1)S(1)}, u32[]{:S(2)}, u32[]{:S(2)}) collective-permute-start(bf16[8,128,128]{2,1,0:T(8,128)(2,1)S(1)} %get-tuple-element.30), channel_id=1, source_target_pairs={{16,32},{32,16},{48,64},{64,48},{80,96},{96,80},{112,128},{128,112... | collective-permute-start | bytes 786440 | tf_op jit(solution)/shard_map/ppermute | solution.py:149
  14.0 2.9 %collective-permute-done.3 = bf16[8,128,128]{2,1,0:T(8,128)(2,1)S(1)} collective-permute-done((bf16[8,128,128]{2,1,0:T(8,128)(2,1)S(1)}, bf16[8,128,128]{2,1,0:T(8,128)(2,1)S(1)}, u32[]{:S(2)}, u32[]{:S(2)}) %collective-permute-start.3) | collective-permute-done | bytes 262176 | tf_op jit(solution)/shard_map/ppermute | solution.py:148
  17.0 2.8 %collective-permute-done.4.near = bf16[8,128,128]{2,1,0:T(8,128)(2,1)S(1)} collective-permute-done((bf16[8,128,128]{2,1,0:T(8,128)(2,1)S(1)}, bf16[8,128,128]{2,1,0:T(8,128)(2,1)S(1)}, u32[]{:S(2)}, u32[]{:S(2)}) %collective-permute-start.4) | collective-permute-done | bytes 262176 | tf_op jit(solution)/shard_map/ppermute | solution.py:149
  20.5 2.6 %collective-permute-start.6 = (bf16[16,128,128]{2,1,0:T(8,128)(2,1)S(1)}, bf16[16,128,128]{2,1,0:T(8,128)(2,1)S(1)}, u32[]{:S(2)}, u32[]{:S(2)}) collective-permute-start(bf16[16,128,128]{2,1,0:T(8,128)(2,1)S(1)} %constant_dynamic-update-slice_fusion.4), channel_id=1, source_target_pairs={{0,12},{1,13},{2,14},{3,15},{4,0},{5,1},{6,2},{7,3},{8,4},{9,5},{1... | collective-permute-start | bytes 1572872 | tf_op jit(solution)/shard_map/ppermute | solution.py:153
  23.2 1.9 %collective-permute-start.7 = (bf16[8,128,128]{2,1,0:T(8,128)(2,1)S(1)}, bf16[8,128,128]{2,1,0:T(8,128)(2,1)S(1)}, u32[]{:S(2)}, u32[]{:S(2)}) collective-permute-start(bf16[8,128,128]{2,1,0:T(8,128)(2,1)S(1)} %collective-permute-done.3), channel_id=1, source_target_pairs={{16,32},{32,16},{48,64},{64,48},{80,96},{96,80},{112,128},{128,112... | collective-permute-start | bytes 786440 | tf_op jit(solution)/shard_map/ppermute | solution.py:154
  25.1 5.8 %collective-permute-done.7.far = bf16[8,128,128]{2,1,0:T(8,128)(2,1)S(1)} collective-permute-done((bf16[8,128,128]{2,1,0:T(8,128)(2,1)S(1)}, bf16[8,128,128]{2,1,0:T(8,128)(2,1)S(1)}, u32[]{:S(2)}, u32[]{:S(2)}) %collective-permute-start.7) | collective-permute-done | bytes 262176 | tf_op jit(solution)/shard_map/ppermute | solution.py:154
  31.0 2.7 %collective-permute-start.8 = (bf16[32,128,128]{2,1,0:T(8,128)(2,1)S(1)}, bf16[32,128,128]{2,1,0:T(8,128)(2,1)S(1)}, u32[]{:S(2)}, u32[]{:S(2)}) collective-permute-start(bf16[32,128,128]{2,1,0:T(8,128)(2,1)S(1)} %slice_dynamic-update-slice_fusion.plane), channel_id=1, source_target_pairs={{0,16},{16,0},{32,48},{48,32},{64,80},{80,64},{96,112},{112,96},{1... | collective-permute-start | bytes 3145736 | tf_op jit(solution)/shard_map/ppermute | solution.py:157
  33.7 1.5 %lift.1.split = bf16[32,256,256]{2,1,0:T(8,128)(2,1)S(1)} custom-call(s32[2,256]{1,0:T(2,128)S(1)} %bitcast.25, s32[32]{0:T(128)S(1)} %copy-done.3, bf16[16,2,128,128]{3,2,1,0:T(8,128)(2,1)S(1)} %get-tuple-element.16.a, bf16[32,128,128]{2,1,0:T(8,128)(2,1)S(1)} %slice_dynamic-update-slice_fusion.plane), custom_call_target="tpu_custom_call" | custom-call | tf_op jit(solution)/shard_map/lift/pallas_call | solution.py:160
  35.2 0.8 %collective-permute-done.8.pair = bf16[32,128,128]{2,1,0:T(8,128)(2,1)S(1)} collective-permute-done((bf16[32,128,128]{2,1,0:T(8,128)(2,1)S(1)}, bf16[32,128,128]{2,1,0:T(8,128)(2,1)S(1)}, u32[]{:S(2)}, u32[]{:S(2)}) %collective-permute-start.8) | collective-permute-done | bytes 1048608 | tf_op jit(solution)/shard_map/ppermute | solution.py:157
  36.0 2.4 %bands.1 = (f32[4,2,8,768]{3,2,1,0:T(8,128)S(1)}, f32[4,2,8,768]{3,2,1,0:T(8,128)S(1)}, f32[4,2,8,768]{3,2,1,0:T(8,128)S(1)}, f32[4,2,8,768]{3,2,1,0:T(8,128)S(1)}) custom-call(s32[2,16]{1,0:T(2,128)S(1)} %bitcast.27, s32[2,256]{1,0:T(2,128)S(1)} %bitcast.26, s32[32]{0:T(128)S(1)} %copy-done.3, bf16[32,256,256]{2,1,0:T(8,128)(2,1)S(1)} %lift.1.split, ...), custom_call_target="tpu_custom_call" | custom-call | tf_op jit(solution)/shard_map/bands/pallas_call | solution.py:169
  38.5 2.1 %collective-permute-start.11 = (f32[4,2,8,768]{3,2,1,0:T(8,128)S(1)}, f32[4,2,8,768]{3,2,1,0:T(8,128)S(1)}, u32[]{:S(2)}, u32[]{:S(2)}) collective-permute-start(f32[4,2,8,768]{3,2,1,0:T(8,128)S(1)} %get-tuple-element.26), channel_id=1, source_target_pairs={{0,3},{1,0},{2,1},{3,2},{4,7},{5,4},{6,5},{7,6},{8,11},{9,8},{10,9... | collective-permute-start | bytes 589832 | tf_op jit(solution)/shard_map/ppermute | solution.py:184
  40.7 5.1 %collective-permute-done.10 = f32[4,2,8,768]{3,2,1,0:T(8,128)S(1)} collective-permute-done((f32[4,2,8,768]{3,2,1,0:T(8,128)S(1)}, f32[4,2,8,768]{3,2,1,0:T(8,128)S(1)}, u32[]{:S(2)}, u32[]{:S(2)}) %collective-permute-start.10) | collective-permute-done | bytes 196640 | tf_op jit(solution)/shard_map/ppermute | solution.py:182
  45.7 2.1 %collective-permute-done.9 = f32[4,2,8,768]{3,2,1,0:T(8,128)S(1)} collective-permute-done((f32[4,2,8,768]{3,2,1,0:T(8,128)S(1)}, f32[4,2,8,768]{3,2,1,0:T(8,128)S(1)}, u32[]{:S(2)}, u32[]{:S(2)}) %collective-permute-start.9) | collective-permute-done | bytes 196640 | tf_op jit(solution)/shard_map/ppermute | solution.py:183
  48.5 3.5 %collective-permute-start.13 = (f32[2,8,768]{2,1,0:T(8,128)S(1)}, f32[2,8,768]{2,1,0:T(8,128)S(1)}, u32[]{:S(2)}, u32[]{:S(2)}) collective-permute-start(f32[2,8,768]{2,1,0:T(8,128)S(1)} %get-tuple-element.29), channel_id=1, source_target_pairs={{0,8},{1,9},{2,10},{3,11},{4,12},{5,13},{6,14},{7,15},{8,0},{9,1},... | collective-permute-start | bytes 147464 | tf_op jit(solution)/shard_map/ppermute | solution.py:186
  52.1 1.1 %collective-permute-done.12 = f32[2,8,768]{2,1,0:T(8,128)S(1)} collective-permute-done((f32[2,8,768]{2,1,0:T(8,128)S(1)}, f32[2,8,768]{2,1,0:T(8,128)S(1)}, u32[]{:S(2)}, u32[]{:S(2)}) %collective-permute-start.12) | collective-permute-done | bytes 49184 | tf_op jit(solution)/shard_map/ppermute | solution.py:187
  53.2 1.4 %collective-permute-done.13 = f32[2,8,768]{2,1,0:T(8,128)S(1)} collective-permute-done((f32[2,8,768]{2,1,0:T(8,128)S(1)}, f32[2,8,768]{2,1,0:T(8,128)S(1)}, u32[]{:S(2)}, u32[]{:S(2)}) %collective-permute-start.13) | collective-permute-done | bytes 49184 | tf_op jit(solution)/shard_map/ppermute | solution.py:186
  54.6 1.5 %collective-permute-done.14 = f32[2,8,768]{2,1,0:T(8,128)S(1)} collective-permute-done((f32[2,8,768]{2,1,0:T(8,128)S(1)}, f32[2,8,768]{2,1,0:T(8,128)S(1)}, u32[]{:S(2)}, u32[]{:S(2)}) %collective-permute-start.14) | collective-permute-done | bytes 49184 | tf_op jit(solution)/shard_map/ppermute | solution.py:188
  (29 shorter events, 2.7 us)
Async XLA Ops:
  0.0 33.7 %copy-start.3 = (s32[32]{0:T(128)S(1)}, s32[32]{0:T(128)}, u32[]{:S(2)}) copy-start(s32[32]{0:T(128)} %agglo.3) | copy-start | bytes 388
  0.0 8.1 %collective-permute-start = (bf16[2,128,128]{2,1,0:T(8,128)(2,1)}, bf16[2,128,128]{2,1,0:T(8,128)(2,1)S(1)}, u32[]{:S(2)}, u32[]{:S(2)}) collective-permute-start(bf16[2,128,128]{2,1,0:T(8,128)(2,1)} %bitcast.21), channel_id=1, source_target_pairs={{0,1},{1,2},{2,3},{3,0},{4,5},{5,6},{6,7},{7,4},{8,9},{9,10},{10,1... | collective-permute-start | bytes 196616 | tf_op jit(solution)/shard_map/ppermute | solution.py:132
  1.6 6.6 %collective-permute-start.1 = (bf16[2,128,128]{2,1,0:T(8,128)(2,1)}, bf16[2,128,128]{2,1,0:T(8,128)(2,1)S(1)}, u32[]{:S(2)}, u32[]{:S(2)}) collective-permute-start(bf16[2,128,128]{2,1,0:T(8,128)(2,1)} %bitcast.22), channel_id=1, source_target_pairs={{0,2},{1,3},{2,0},{3,1},{4,6},{5,7},{6,4},{7,5},{8,10},{9,11},{10,... | collective-permute-start | bytes 196616 | tf_op jit(solution)/shard_map/ppermute | solution.py:134
  4.5 4.5 %collective-permute-start.2 = (bf16[2,128,128]{2,1,0:T(8,128)(2,1)}, bf16[2,128,128]{2,1,0:T(8,128)(2,1)S(1)}, u32[]{:S(2)}, u32[]{:S(2)}) collective-permute-start(bf16[2,128,128]{2,1,0:T(8,128)(2,1)} %bitcast.23), channel_id=1, source_target_pairs={{0,3},{1,0},{2,1},{3,2},{4,7},{5,4},{6,5},{7,6},{8,11},{9,8},{10,9... | collective-permute-start | bytes 196616 | tf_op jit(solution)/shard_map/ppermute | solution.py:133
  5.8 1.2 %copy-start = (bf16[16,2,128,128]{3,2,1,0:T(8,128)(2,1)S(1)}, bf16[16,2,128,128]{3,2,1,0:T(8,128)(2,1)}, u32[]{:S(2)}) copy-start(bf16[16,2,128,128]{3,2,1,0:T(8,128)(2,1)} %a.1) | copy-start | bytes 3145732
  7.1 0.8 %copy-start.1 = (bf16[1,2,128,128]{3,2,1,0:T(8,128)(2,1)S(1)}, bf16[1,2,128,128]{3,2,1,0:T(8,128)(2,1)}, u32[]{:S(2)}) copy-start(bf16[1,2,128,128]{3,2,1,0:T(8,128)(2,1)} %param.7) | copy-start | bytes 196612
  7.9 25.8 %copy-start.2 = (s32[256,2]{0,1:T(2,128)S(1)}, s32[256,2]{0,1:T(2,128)}, u32[]{:S(2)}) copy-start(s32[256,2]{0,1:T(2,128)} %param.8) | copy-start | bytes 6148
  9.0 8.0 %collective-permute-start.3 = (bf16[8,128,128]{2,1,0:T(8,128)(2,1)S(1)}, bf16[8,128,128]{2,1,0:T(8,128)(2,1)S(1)}, u32[]{:S(2)}, u32[]{:S(2)}) collective-permute-start(bf16[8,128,128]{2,1,0:T(8,128)(2,1)S(1)} %get-tuple-element.30), channel_id=1, source_target_pairs={{0,8},{1,9},{2,10},{3,11},{4,12},{5,13},{6,14},{7,15},{8,0},{9,1},... | collective-permute-start | bytes 786440 | tf_op jit(solution)/shard_map/ppermute | solution.py:148
  12.1 7.7 %collective-permute-start.4 = (bf16[8,128,128]{2,1,0:T(8,128)(2,1)S(1)}, bf16[8,128,128]{2,1,0:T(8,128)(2,1)S(1)}, u32[]{:S(2)}, u32[]{:S(2)}) collective-permute-start(bf16[8,128,128]{2,1,0:T(8,128)(2,1)S(1)} %get-tuple-element.30), channel_id=1, source_target_pairs={{16,32},{32,16},{48,64},{64,48},{80,96},{96,80},{112,128},{128,112... | collective-permute-start | bytes 786440 | tf_op jit(solution)/shard_map/ppermute | solution.py:149
  19.8 16.2 %copy-start.4 = (s32[16,2]{0,1:T(2,128)S(1)}, s32[16,2]{0,1:T(2,128)}, u32[]{:S(2)}) copy-start(s32[16,2]{0,1:T(2,128)} %param.6) | copy-start | bytes 388
  19.8 11.0 %collective-permute-start.5 = (bf16[16,128,128]{2,1,0:T(8,128)(2,1)S(1)}, bf16[16,128,128]{2,1,0:T(8,128)(2,1)S(1)}, u32[]{:S(2)}, u32[]{:S(2)}) collective-permute-start(bf16[16,128,128]{2,1,0:T(8,128)(2,1)S(1)} %constant_dynamic-update-slice_fusion.4), channel_id=1, source_target_pairs={{0,4},{1,5},{2,6},{3,7},{4,8},{5,9},{6,10},{7,11},{8,12},{9,13},{1... | collective-permute-start | bytes 1572872 | tf_op jit(solution)/shard_map/ppermute | solution.py:152
  20.5 10.3 %collective-permute-start.6 = (bf16[16,128,128]{2,1,0:T(8,128)(2,1)S(1)}, bf16[16,128,128]{2,1,0:T(8,128)(2,1)S(1)}, u32[]{:S(2)}, u32[]{:S(2)}) collective-permute-start(bf16[16,128,128]{2,1,0:T(8,128)(2,1)S(1)} %constant_dynamic-update-slice_fusion.4), channel_id=1, source_target_pairs={{0,12},{1,13},{2,14},{3,15},{4,0},{5,1},{6,2},{7,3},{8,4},{9,5},{1... | collective-permute-start | bytes 1572872 | tf_op jit(solution)/shard_map/ppermute | solution.py:153
  23.2 7.7 %collective-permute-start.7 = (bf16[8,128,128]{2,1,0:T(8,128)(2,1)S(1)}, bf16[8,128,128]{2,1,0:T(8,128)(2,1)S(1)}, u32[]{:S(2)}, u32[]{:S(2)}) collective-permute-start(bf16[8,128,128]{2,1,0:T(8,128)(2,1)S(1)} %collective-permute-done.3), channel_id=1, source_target_pairs={{16,32},{32,16},{48,64},{64,48},{80,96},{96,80},{112,128},{128,112... | collective-permute-start | bytes 786440 | tf_op jit(solution)/shard_map/ppermute | solution.py:154
  31.0 5.0 %collective-permute-start.8 = (bf16[32,128,128]{2,1,0:T(8,128)(2,1)S(1)}, bf16[32,128,128]{2,1,0:T(8,128)(2,1)S(1)}, u32[]{:S(2)}, u32[]{:S(2)}) collective-permute-start(bf16[32,128,128]{2,1,0:T(8,128)(2,1)S(1)} %slice_dynamic-update-slice_fusion.plane), channel_id=1, source_target_pairs={{0,16},{16,0},{32,48},{48,32},{64,80},{80,64},{96,112},{112,96},{1... | collective-permute-start | bytes 3145736 | tf_op jit(solution)/shard_map/ppermute | solution.py:157
  38.4 7.3 %collective-permute-start.10 = (f32[4,2,8,768]{3,2,1,0:T(8,128)S(1)}, f32[4,2,8,768]{3,2,1,0:T(8,128)S(1)}, u32[]{:S(2)}, u32[]{:S(2)}) collective-permute-start(f32[4,2,8,768]{3,2,1,0:T(8,128)S(1)} %get-tuple-element.25), channel_id=1, source_target_pairs={{0,2},{1,3},{2,0},{3,1},{4,6},{5,7},{6,4},{7,5},{8,10},{9,11},{10,... | collective-permute-start | bytes 589832 | tf_op jit(solution)/shard_map/ppermute | solution.py:182
  38.5 7.2 %collective-permute-start.11 = (f32[4,2,8,768]{3,2,1,0:T(8,128)S(1)}, f32[4,2,8,768]{3,2,1,0:T(8,128)S(1)}, u32[]{:S(2)}, u32[]{:S(2)}) collective-permute-start(f32[4,2,8,768]{3,2,1,0:T(8,128)S(1)} %get-tuple-element.26), channel_id=1, source_target_pairs={{0,3},{1,0},{2,1},{3,2},{4,7},{5,4},{6,5},{7,6},{8,11},{9,8},{10,9... | collective-permute-start | bytes 589832 | tf_op jit(solution)/shard_map/ppermute | solution.py:184
  40.7 7.1 %collective-permute-start.9 = (f32[4,2,8,768]{3,2,1,0:T(8,128)S(1)}, f32[4,2,8,768]{3,2,1,0:T(8,128)S(1)}, u32[]{:S(2)}, u32[]{:S(2)}) collective-permute-start(f32[4,2,8,768]{3,2,1,0:T(8,128)S(1)} %get-tuple-element.24), channel_id=1, source_target_pairs={{0,1},{1,2},{2,3},{3,0},{4,5},{5,6},{6,7},{7,4},{8,9},{9,10},{10,1... | collective-permute-start | bytes 589832 | tf_op jit(solution)/shard_map/ppermute | solution.py:183
  47.8 5.4 %collective-permute-start.12 = (f32[2,8,768]{2,1,0:T(8,128)S(1)}, f32[2,8,768]{2,1,0:T(8,128)S(1)}, u32[]{:S(2)}, u32[]{:S(2)}) collective-permute-start(f32[2,8,768]{2,1,0:T(8,128)S(1)} %get-tuple-element.27), channel_id=1, source_target_pairs={{0,4},{1,5},{2,6},{3,7},{4,8},{5,9},{6,10},{7,11},{8,12},{9,13},{1... | collective-permute-start | bytes 147464 | tf_op jit(solution)/shard_map/ppermute | solution.py:187
  48.5 6.1 %collective-permute-start.13 = (f32[2,8,768]{2,1,0:T(8,128)S(1)}, f32[2,8,768]{2,1,0:T(8,128)S(1)}, u32[]{:S(2)}, u32[]{:S(2)}) collective-permute-start(f32[2,8,768]{2,1,0:T(8,128)S(1)} %get-tuple-element.29), channel_id=1, source_target_pairs={{0,8},{1,9},{2,10},{3,11},{4,12},{5,13},{6,14},{7,15},{8,0},{9,1},... | collective-permute-start | bytes 147464 | tf_op jit(solution)/shard_map/ppermute | solution.py:186
  52.0 4.1 %collective-permute-start.14 = (f32[2,8,768]{2,1,0:T(8,128)S(1)}, f32[2,8,768]{2,1,0:T(8,128)S(1)}, u32[]{:S(2)}, u32[]{:S(2)}) collective-permute-start(f32[2,8,768]{2,1,0:T(8,128)S(1)} %get-tuple-element.28), channel_id=1, source_target_pairs={{0,12},{1,13},{2,14},{3,15},{4,0},{5,1},{6,2},{7,3},{8,4},{9,5},{1... | collective-permute-start | bytes 147464 | tf_op jit(solution)/shard_map/ppermute | solution.py:188

commit v4 on v3

v4 whole, which is shorter than its diff:
```python
import jax
import jax.numpy as jnp
from jax import lax
from jax.experimental import pallas as pl
from jax.experimental.pallas import tpu as pltpu
from jax.sharding import PartitionSpec as P

ROWS = 16
SIDE = 4
B = 128
BOTH = ("row", "col")


def crossed(row):
    return (row + 1) // 2 % 2


def moved(along, step):
    pairs = []
    for r in range(ROWS):
        dy, dx = ((0, step), (step, 0))[crossed(r) ^ along]
        for y in range(SIDE):
            for x in range(SIDE):
                target = ((y + dy) % SIDE) * SIDE + (x + dx) % SIDE
                pairs.append((r * ROWS + y * SIDE + x, r * ROWS + target))
    return pairs


def first(step):
    return moved(0, step)


def second(step):
    return moved(1, step)


def row_pairs(start):
    pairs = []
    for r in range(start, ROWS - 1, 2):
        pairs += [(r, r + 1), (r + 1, r)]
    return pairs


def place():
    row = lax.axis_index("row")
    col = lax.axis_index("col")
    return row, crossed(row), col // SIDE, col % SIDE


def groups_of_eight():
    groups = []
    for r in range(1, ROWS, 2):
        for q in range(SIDE):
            group = []
            for row in (r, (r + 1) % ROWS):
                for c in range(SIDE):
                    y, x = (c, q) if crossed(row) else (q, c)
                    group.append(row * ROWS + y * SIDE + x)
            groups.append(group)
    return groups


def spot_of(y, x, j, cross):
    y2, x2 = (j % ROWS) // SIDE, j % SIDE
    back = jnp.where(cross == 0, y - y2, x - x2) & 3
    return back, jnp.where(cross == 0, x2, y2)


def lift_kernel(aggs, agglo, a, plane, split):
    row, cross, y, x = place()
    for i in range(ROWS):
        swap = agglo[aggs[0, row * ROWS + i]] & 1
        back, along = spot_of(y, x, i, cross)
        spot = (back * SIDE + along) * 2
        left = jnp.concatenate([plane[spot + swap], plane[spot + 1 - swap]], axis=1)
        right = jnp.concatenate([a[i, 0], a[i, 1]], axis=1)
        lifted = lax.dot_general(
            left, right, (((0,), (0,)), ((), ())), preferred_element_type=jnp.float32
        )
        high = lifted.astype(jnp.bfloat16)
        low = (lifted - high.astype(jnp.float32)).astype(jnp.bfloat16)
        for s in range(2):
            split[i * 2 + s, :, :B] = high[:, s * B : (s + 1) * B]
            split[i * 2 + s, :, B:] = low[:, s * B : (s + 1) * B]


def band_kernel(cols, aggs, agglo, split, lines, f, b, d, far, pair, out, blocks, acc):
    row, cross, y, x = place()
    own_half = 1 - row % 2
    blocks[0:16] = lines[...]
    blocks[16:32] = f[...]
    blocks[pl.ds(32 + own_half * 8, 8)] = d[...]
    blocks[pl.ds(40 - own_half * 8, 8)] = far[...]
    blocks[48:64] = b[...]
    blocks[64:96] = pair[...]
    acc[...] = jnp.zeros_like(acc)
    pair_band = 2 - 2 * (row % 2)
    for i in range(ROWS):
        for s in range(2):
            j = cols[s, i]
            swap = agglo[aggs[0, j]] & 1
            band = j // ROWS - row + 1
            of_pair = band == pair_band
            half = jnp.where(band == 1, own_half, 1 - own_half)
            back, along = spot_of(y, x, j, jnp.where(of_pair, 1 - cross, cross))
            spot = jnp.where(
                of_pair,
                64 + (back * SIDE + along) * 2,
                back * 16 + half * 8 + along * 2,
            )
            right = jnp.concatenate([blocks[spot + swap], blocks[spot + 1 - swap]], axis=1)
            right = jnp.concatenate([right, right], axis=0)
            acc[band] += jnp.dot(split[i * 2 + s], right, preferred_element_type=jnp.float32)
    for d in range(ROWS):
        for k in range(2):
            for t in range(3):
                out[d, k, :, t * 256 : (t + 1) * 256] = acc[t, k * B + d * 8 : k * B + d * 8 + 8, :]


def vmem():
    return pl.BlockSpec(memory_space=pltpu.VMEM)


def smem():
    return pl.BlockSpec(memory_space=pltpu.SMEM)


def params(mib):
    return pltpu.CompilerParams(vmem_limit_bytes=mib * 2**20)


def local(a_blocks, a_cols, p_blocks, p_aggs, agglo):
    own = (1 - (lax.axis_index("row") & 1)) * 8

    def own_half(lines):
        return lax.dynamic_slice_in_dim(lines, own, 8, 0)

    copies = jnp.broadcast_to(p_blocks, (8, 2, B, B))
    lines = lax.all_to_all(
        copies, BOTH, 0, 0, axis_index_groups=groups_of_eight(), tiled=True
    ).reshape(16, B, B)
    line = own_half(lines)
    plane_d = lax.ppermute(line, BOTH, second(2))
    plane_f = lax.ppermute(lines, BOTH, second(1))
    plane_b = lax.ppermute(lines, BOTH, second(-1))
    far = lax.ppermute(plane_d, "row", row_pairs(1))
    plane_f, plane_b, far = lax.optimization_barrier((plane_f, plane_b, far))
    plane = jnp.concatenate([line, own_half(plane_f), plane_d, own_half(plane_b)])
    pair = lax.ppermute(plane, "row", row_pairs(0))

    cols, aggs = a_cols.T, p_aggs.T
    split = pl.pallas_call(
        lift_kernel,
        out_shape=jax.ShapeDtypeStruct((2 * ROWS, 256, 256), jnp.bfloat16),
        in_specs=[smem(), smem(), vmem(), vmem()],
        out_specs=vmem(),
        compiler_params=params(16),
        name="lift",
    )(aggs, agglo, a_blocks, plane)
    partial = pl.pallas_call(
        band_kernel,
        out_shape=jax.ShapeDtypeStruct((ROWS, 2, 8, 768), jnp.float32),
        in_specs=[smem()] * 3 + [vmem()] * 7,
        out_specs=vmem(),
        scratch_shapes=[
            pltpu.VMEM((96, B, B), jnp.bfloat16),
            pltpu.VMEM((3, 256, 256), jnp.float32),
        ],
        compiler_params=params(24),
        name="bands",
    )(cols, aggs, agglo, split, lines, plane_f, plane_b, plane_d, far, pair)
    parts = lax.all_to_all(partial, "col", 0, 0, tiled=True)
    return parts.sum(0).reshape(2, 8, 6, B)


def solution(mesh):
    placed = (
        P("row", "col", None, None),
        P("row", "col"),
        P(("row", "col"), None, None, None),
        P(),
        P(),
    )
    return jax.shard_map(
        local, mesh=mesh, in_specs=placed, out_specs=P("row", "col", None, None), check_vma=False
    )
```

time: 56.9 us -> 59.5 us (1.046)
  blocking collectives: 0 us -> 20.1 us
  starting transfers between devices: 25.3 us -> 15.9 us
  waiting for transfers between devices: 24.2 us -> 16.6 us
    all_to_all x0 -> x1, blocking collectives: none -> 20.1 us  [local(): parts = lax.all_to_all(partial, 'col', 0, 0, tiled=True)]
    ppermute x10 -> x0, waiting for transfers between devices: 14.7 us -> none  [the longest x1 5.06 us: local(): d = lax.ppermute(o2, BOTH, first(2))]
    ppermute x10 -> x0, starting transfers between devices: 14.2 us -> none  [the longest x1 3.53 us: local(): d = lax.ppermute(to_d, BOTH, second(2))]
    all_to_all x0 -> x1, waiting for transfers between devices: none -> 7.23 us  [local(): lax.all_to_all(copies, BOTH, 0, 0, axis_index_groups=groups_of_eight(), t...]
    all_to_all x0 -> x1, starting transfers between devices: none -> 5.65 us  [local(): lax.all_to_all(copies, BOTH, 0, 0, axis_index_groups=groups_of_eight(), t...]
    unnamed x15 -> x8, local copies, waits for them, and re-layouts: 2.27 us -> 0.02 us
    broadcast_in_dim x0 -> x1, local copies, waits for them, and re-layouts: none -> 1.83 us  [local(): copies = jnp.broadcast_to(p_blocks, (8, 2, B, B))]
    ppermute x1, starting transfers between devices: 2.64 us -> 1.14 us  [local(): plane_b = lax.ppermute(lines, BOTH, second(-1))]
  transfers between devices with their start and end apart: 15 -> 6, of which waited for: 10 -> 4; matrix products, arithmetic and copies ran while one was open for 0% -> 0% of each run, Pallas kernels for 3% -> 3%
where the time goes in v4:
time: 59.5 us; the launch traced here: 59.2 us
  blocking collectives  20.1 us (34%)
  waiting for transfers between devices  16.6 us (28%)
  starting transfers between devices  15.9 us (27%)
  Pallas kernels  3.93 us (7%)
  local copies, waits for them, and re-layouts  1.91 us (3%)
  other arithmetic  0.8 us (1%)
    all_to_all x1, blocking collectives, local(): parts = lax.all_to_all(partial, 'col', 0, 0, tiled=True)  20.1 us
    all_to_all x1, waiting for transfers between devices, local(): lax.all_to_all(copies, BOTH, 0, 0, axis_index_groups=groups_of_eight(), t...  7.23 us
    ppermute x1, waiting for transfers between devices, local(): far = lax.ppermute(plane_d, 'row', row_pairs(1))  5.76 us
    all_to_all x1, starting transfers between devices, local(): lax.all_to_all(copies, BOTH, 0, 0, axis_index_groups=groups_of_eight(), t...  5.65 us
    ppermute x1, starting transfers between devices, local(): pair = lax.ppermute(plane, 'row', row_pairs(0))  3.16 us
    ppermute x1, starting transfers between devices, local(): plane_d = lax.ppermute(line, BOTH, second(2))  3.11 us
    ppermute x1, waiting for transfers between devices, local(): plane_d = lax.ppermute(line, BOTH, second(2))  2.83 us
    pallas_call x1, Pallas kernels, local(): pl.pallas_call(band_kernel, out_shape=jax.ShapeDtypeStruct((ROWS, 2, 8, 7...  2.43 us
  transfers between devices with their start and end apart: 6, of which 4 were waited for; matrix products, arithmetic and copies ran while one was open for 0% of the time, Pallas kernels for 3%

profile of v4, /device:TPU:96, one launch (start us, length us, event | category | flops | bytes accessed | tf_op | source)
XLA Modules:
  0.0 59.2 jit_solution(4653768287502919697)
XLA Ops:
  0.0 0.0 copy-start.2
  0.0 1.8 %broadcast_in_dim.8 = bf16[8,2,128,128]{3,2,1,0:T(8,128)(2,1)} broadcast(bf16[2,128,128]{2,1,0:T(8,128)(2,1)} %bitcast.12), dimensions={1,2,3} | broadcast | bytes 589824 | tf_op jit(solution)/shard_map/broadcast_in_dim | solution.py:138
  1.8 5.6 %all-to-all-start = ((bf16[8,2,128,128]{3,2,1,0:T(8,128)(2,1)}), bf16[8,2,128,128]{3,2,1,0:T(8,128)(2,1)S(1)}, u32[]{:S(2)}, u32[]{:S(2)}) async-start(bf16[8,2,128,128]{3,2,1,0:T(8,128)(2,1)} %broadcast_in_dim.8), calls=%async_computation | async-start | bytes 1048576 | tf_op jit(solution)/shard_map/all_to_all | solution.py:139
  7.5 7.2 %all-to-all-done = bf16[8,2,128,128]{3,2,1,0:T(8,128)(2,1)S(1)} async-done(((bf16[8,2,128,128]{3,2,1,0:T(8,128)(2,1)}), bf16[8,2,128,128]{3,2,1,0:T(8,128)(2,1)S(1)}, u32[]{:S(2)}, u32[]{:S(2)}) %all-to-all-start) | async-done | bytes 524320 | tf_op jit(solution)/shard_map/all_to_all | solution.py:139
  14.7 3.1 %collective-permute-start.2 = (bf16[8,128,128]{2,1,0:T(8,128)(2,1)S(1)}, bf16[8,128,128]{2,1,0:T(8,128)(2,1)S(1)}, u32[]{:S(2)}, u32[]{:S(2)}) collective-permute-start(bf16[8,128,128]{2,1,0:T(8,128)(2,1)S(1)} %constant_dynamic-slice_fusion.2), channel_id=1, source_target_pairs={{0,8},{1,9},{2,10},{3,11},{4,12},{5,13},{6,14},{7,15},{8,0},{9,1},... | collective-permute-start | bytes 786440 | tf_op jit(solution)/shard_map/ppermute | solution.py:143
  17.9 1.1 %collective-permute-start.1 = (bf16[16,128,128]{2,1,0:T(8,128)(2,1)S(1)}, bf16[16,128,128]{2,1,0:T(8,128)(2,1)S(1)}, u32[]{:S(2)}, u32[]{:S(2)}) collective-permute-start(bf16[16,128,128]{2,1,0:T(8,128)(2,1)S(1)} %bitcast.6), channel_id=1, source_target_pairs={{0,12},{1,13},{2,14},{3,15},{4,0},{5,1},{6,2},{7,3},{8,4},{9,5},{1... | collective-permute-start | bytes 1572872 | tf_op jit(solution)/shard_map/ppermute | solution.py:145
  19.0 0.9 %collective-permute-start = (bf16[16,128,128]{2,1,0:T(8,128)(2,1)S(1)}, bf16[16,128,128]{2,1,0:T(8,128)(2,1)S(1)}, u32[]{:S(2)}, u32[]{:S(2)}) collective-permute-start(bf16[16,128,128]{2,1,0:T(8,128)(2,1)S(1)} %bitcast.7), channel_id=1, source_target_pairs={{0,4},{1,5},{2,6},{3,7},{4,8},{5,9},{6,10},{7,11},{8,12},{9,13},{1... | collective-permute-start | bytes 1572872 | tf_op jit(solution)/shard_map/ppermute | solution.py:144
  19.9 2.8 %collective-permute-done.2.d = bf16[8,128,128]{2,1,0:T(8,128)(2,1)S(1)} collective-permute-done((bf16[8,128,128]{2,1,0:T(8,128)(2,1)S(1)}, bf16[8,128,128]{2,1,0:T(8,128)(2,1)S(1)}, u32[]{:S(2)}, u32[]{:S(2)}) %collective-permute-start.2) | collective-permute-done | bytes 262176 | tf_op jit(solution)/shard_map/ppermute | solution.py:143
  22.7 1.9 %collective-permute-start.3 = (bf16[8,128,128]{2,1,0:T(8,128)(2,1)S(1)}, bf16[8,128,128]{2,1,0:T(8,128)(2,1)S(1)}, u32[]{:S(2)}, u32[]{:S(2)}) collective-permute-start(bf16[8,128,128]{2,1,0:T(8,128)(2,1)S(1)} %collective-permute-done.2.d), channel_id=1, source_target_pairs={{16,32},{32,16},{48,64},{64,48},{80,96},{96,80},{112,128},{128,112... | collective-permute-start | bytes 786440 | tf_op jit(solution)/shard_map/ppermute | solution.py:146
  24.6 5.8 %collective-permute-done.3.far = bf16[8,128,128]{2,1,0:T(8,128)(2,1)S(1)} collective-permute-done((bf16[8,128,128]{2,1,0:T(8,128)(2,1)S(1)}, bf16[8,128,128]{2,1,0:T(8,128)(2,1)S(1)}, u32[]{:S(2)}, u32[]{:S(2)}) %collective-permute-start.3) | collective-permute-done | bytes 262176 | tf_op jit(solution)/shard_map/ppermute | solution.py:146
  30.4 0.0 collective-permute-done.1.b
  30.4 0.0 collective-permute-done.f
  30.4 0.0 copy-start.3
  30.5 0.1 pad_maximum_fusion.plane
  30.6 3.2 %collective-permute-start.4 = (bf16[32,128,128]{2,1,0:T(8,128)(2,1)S(1)}, bf16[32,128,128]{2,1,0:T(8,128)(2,1)S(1)}, u32[]{:S(2)}, u32[]{:S(2)}) collective-permute-start(bf16[32,128,128]{2,1,0:T(8,128)(2,1)S(1)} %pad_maximum_fusion.plane), channel_id=1, source_target_pairs={{0,16},{16,0},{32,48},{48,32},{64,80},{80,64},{96,112},{112,96},{1... | collective-permute-start | bytes 3145736 | tf_op jit(solution)/shard_map/ppermute | solution.py:149
  33.8 0.0 copy-done.2
  33.8 0.0 copy-done.1
  33.8 0.0 copy-done
  33.8 1.5 %lift.1.split = bf16[32,256,256]{2,1,0:T(8,128)(2,1)S(1)} custom-call(s32[2,256]{1,0:T(2,128)S(1)} %bitcast.9, s32[32]{0:T(128)S(1)} %copy-done.2, bf16[16,2,128,128]{3,2,1,0:T(8,128)(2,1)S(1)} %copy-done, bf16[32,128,128]{2,1,0:T(8,128)(2,1)S(1)} %pad_maximum_fusion.plane), custom_call_target="tpu_custom_call" | custom-call | tf_op jit(solution)/shard_map/lift/pallas_call | solution.py:152
  35.3 0.8 %collective-permute-done.4.pair = bf16[32,128,128]{2,1,0:T(8,128)(2,1)S(1)} collective-permute-done((bf16[32,128,128]{2,1,0:T(8,128)(2,1)S(1)}, bf16[32,128,128]{2,1,0:T(8,128)(2,1)S(1)}, u32[]{:S(2)}, u32[]{:S(2)}) %collective-permute-start.4) | collective-permute-done | bytes 1048608 | tf_op jit(solution)/shard_map/ppermute | solution.py:149
  36.0 0.0 copy-done.3
  36.0 2.4 %bands.1 = f32[16,2,8,768]{3,2,1,0:T(8,128)S(1)} custom-call(s32[2,16]{1,0:T(2,128)S(1)} %bitcast.11, s32[2,256]{1,0:T(2,128)S(1)} %bitcast.10, s32[32]{0:T(128)S(1)} %copy-done.2, bf16[32,256,256]{2,1,0:T(8,128)(2,1)S(1)} %lift.1.split, bf16[16,128,128]{2,1,0:T(8,128)(2,1)S(1)} %bitcast.8, bf16[16,128,128]{2,1,0:T(8,128)(2,1)S(1)} %collective-permute-done.f, ...), custom_call_target="tpu_custom_call" | custom-call | tf_op jit(solution)/shard_map/bands/pallas_call | solution.py:160
  38.5 20.1 %all_to_all.10 = f32[16,2,8,768]{3,2,1,0:T(8,128)S(1)} all-to-all(f32[16,2,8,768]{3,2,1,0:T(8,128)S(1)} %bands.1), channel_id=1, replica_groups=mesh['row'=16,'col'=16] {'col'}, dimensions={0} | all-to-all | bytes 1572864 | tf_op jit(solution)/shard_map/all_to_all | solution.py:172
  58.6 0.7 %reduce_sum.9 = f32[2,8,768]{2,1,0:T(8,128)} reduce(f32[16,2,8,768]{3,2,1,0:T(8,128)S(1)} %all_to_all.10, f32[]{:T(128)} %constant.14.clone.1), dimensions={0}, to_apply=%region_0.0 | reduce | flops 184320 | bytes 835588 | tf_op jit(solution)/shard_map/reduce_sum | solution.py:173
  (4 shorter events, 0.1 us)
Async XLA Ops:
  0.0 33.8 %copy-start.2 = (s32[32]{0:T(128)S(1)}, s32[32]{0:T(128)}, u32[]{:S(2)}) copy-start(s32[32]{0:T(128)} %agglo.3) | copy-start | bytes 388
  0.0 33.8 %copy-start.1 = (s32[256,2]{0,1:T(2,128)S(1)}, s32[256,2]{0,1:T(2,128)}, u32[]{:S(2)}) copy-start(s32[256,2]{0,1:T(2,128)} %param.8) | copy-start | bytes 6148
  0.0 33.8 %copy-start = (bf16[16,2,128,128]{3,2,1,0:T(8,128)(2,1)S(1)}, bf16[16,2,128,128]{3,2,1,0:T(8,128)(2,1)}, u32[]{:S(2)}) copy-start(bf16[16,2,128,128]{3,2,1,0:T(8,128)(2,1)} %a.1) | copy-start | bytes 3145732
  1.8 12.9 %all-to-all-start = ((bf16[8,2,128,128]{3,2,1,0:T(8,128)(2,1)}), bf16[8,2,128,128]{3,2,1,0:T(8,128)(2,1)S(1)}, u32[]{:S(2)}, u32[]{:S(2)}) async-start(bf16[8,2,128,128]{3,2,1,0:T(8,128)(2,1)} %broadcast_in_dim.8), calls=%async_computation | async-start | bytes 1048576 | tf_op jit(solution)/shard_map/all_to_all | solution.py:139
  14.7 8.0 %collective-permute-start.2 = (bf16[8,128,128]{2,1,0:T(8,128)(2,1)S(1)}, bf16[8,128,128]{2,1,0:T(8,128)(2,1)S(1)}, u32[]{:S(2)}, u32[]{:S(2)}) collective-permute-start(bf16[8,128,128]{2,1,0:T(8,128)(2,1)S(1)} %constant_dynamic-slice_fusion.2), channel_id=1, source_target_pairs={{0,8},{1,9},{2,10},{3,11},{4,12},{5,13},{6,14},{7,15},{8,0},{9,1},... | collective-permute-start | bytes 786440 | tf_op jit(solution)/shard_map/ppermute | solution.py:143
  17.9 12.5 %collective-permute-start.1 = (bf16[16,128,128]{2,1,0:T(8,128)(2,1)S(1)}, bf16[16,128,128]{2,1,0:T(8,128)(2,1)S(1)}, u32[]{:S(2)}, u32[]{:S(2)}) collective-permute-start(bf16[16,128,128]{2,1,0:T(8,128)(2,1)S(1)} %bitcast.6), channel_id=1, source_target_pairs={{0,12},{1,13},{2,14},{3,15},{4,0},{5,1},{6,2},{7,3},{8,4},{9,5},{1... | collective-permute-start | bytes 1572872 | tf_op jit(solution)/shard_map/ppermute | solution.py:145
  19.0 11.4 %collective-permute-start = (bf16[16,128,128]{2,1,0:T(8,128)(2,1)S(1)}, bf16[16,128,128]{2,1,0:T(8,128)(2,1)S(1)}, u32[]{:S(2)}, u32[]{:S(2)}) collective-permute-start(bf16[16,128,128]{2,1,0:T(8,128)(2,1)S(1)} %bitcast.7), channel_id=1, source_target_pairs={{0,4},{1,5},{2,6},{3,7},{4,8},{5,9},{6,10},{7,11},{8,12},{9,13},{1... | collective-permute-start | bytes 1572872 | tf_op jit(solution)/shard_map/ppermute | solution.py:144
  22.7 7.7 %collective-permute-start.3 = (bf16[8,128,128]{2,1,0:T(8,128)(2,1)S(1)}, bf16[8,128,128]{2,1,0:T(8,128)(2,1)S(1)}, u32[]{:S(2)}, u32[]{:S(2)}) collective-permute-start(bf16[8,128,128]{2,1,0:T(8,128)(2,1)S(1)} %collective-permute-done.2.d), channel_id=1, source_target_pairs={{16,32},{32,16},{48,64},{64,48},{80,96},{96,80},{112,128},{128,112... | collective-permute-start | bytes 786440 | tf_op jit(solution)/shard_map/ppermute | solution.py:146
  30.4 5.6 %copy-start.3 = (s32[16,2]{0,1:T(2,128)S(1)}, s32[16,2]{0,1:T(2,128)}, u32[]{:S(2)}) copy-start(s32[16,2]{0,1:T(2,128)} %param.6) | copy-start | bytes 388
  30.6 5.4 %collective-permute-start.4 = (bf16[32,128,128]{2,1,0:T(8,128)(2,1)S(1)}, bf16[32,128,128]{2,1,0:T(8,128)(2,1)S(1)}, u32[]{:S(2)}, u32[]{:S(2)}) collective-permute-start(bf16[32,128,128]{2,1,0:T(8,128)(2,1)S(1)} %pad_maximum_fusion.plane), channel_id=1, source_target_pairs={{0,16},{16,0},{32,48},{48,32},{64,80},{80,64},{96,112},{112,96},{1... | collective-permute-start | bytes 3145736 | tf_op jit(solution)/shard_map/ppermute | solution.py:149

commit v5 on v3

--- a/solution.py
+++ b/solution.py
@@ -15,23 +15,22 @@
     return (row + 1) // 2 % 2
 
 
-def moved(along, step):
+def swapped(along, k):
     pairs = []
     for r in range(ROWS):
-        dy, dx = ((0, step), (step, 0))[crossed(r) ^ along]
+        dy, dx = ((0, k), (k, 0))[crossed(r) ^ along]
         for y in range(SIDE):
             for x in range(SIDE):
-                target = ((y + dy) % SIDE) * SIDE + (x + dx) % SIDE
-                pairs.append((r * ROWS + y * SIDE + x, r * ROWS + target))
+                pairs.append((r * ROWS + y * SIDE + x, r * ROWS + (y ^ dy) * SIDE + (x ^ dx)))
     return pairs
 
 
-def first(step):
-    return moved(0, step)
+def first(k):
+    return swapped(0, k)
 
 
-def second(step):
-    return moved(1, step)
+def second(k):
+    return swapped(1, k)
 
 
 def row_pairs(start):
@@ -48,19 +47,12 @@
 
 
 def slot_of(y, x, j, cross):
-    dy, dx = (y - (j % ROWS) // SIDE) & 3, (x - j % SIDE) & 3
+    dy, dx = y ^ ((j % ROWS) // SIDE), x ^ (j % SIDE)
     return jnp.where(cross == 0, dy * SIDE + dx, dx * SIDE + dy)
 
 
-def fetch_kernel(a, shard, a_near, shard_near, sems):
-    copies = [
-        pltpu.make_async_copy(shard, shard_near, sems.at[0]),
-        pltpu.make_async_copy(a, a_near, sems.at[1]),
-    ]
-    for copy in copies:
-        copy.start()
-    for copy in copies:
-        copy.wait()
+def fetch_kernel(shard, near):
+    near[...] = shard[...]
 
 
 def lift_kernel(aggs, agglo, a, plane, split):
@@ -106,8 +98,8 @@
         for m in range(SIDE):
             d = jnp.where(
                 cross == 0,
-                ((y + m) & 3) * SIDE + ((x + rel) & 3),
-                ((y + rel) & 3) * SIDE + ((x + m) & 3),
+                (y ^ m) * SIDE + (x ^ rel),
+                (y ^ rel) * SIDE + (x ^ m),
             )
             for k in range(2):
                 start = pl.multiple_of(k * B + d * 8, 8)
@@ -129,31 +121,25 @@
 
 def local(a_blocks, a_cols, p_blocks, p_aggs, agglo):
     shard = p_blocks[0]
-    line_f = lax.ppermute(shard, BOTH, first(1))
-    line_b = lax.ppermute(shard, BOTH, first(-1))
-    line_d = lax.ppermute(shard, BOTH, first(2))
-    a_near, shard_near = pl.pallas_call(
+    line_1, line_3, line_2 = (lax.ppermute(shard, BOTH, first(k)) for k in (1, 3, 2))
+    shard_near = pl.pallas_call(
         fetch_kernel,
-        out_shape=[
-            jax.ShapeDtypeStruct(a_blocks.shape, a_blocks.dtype),
-            jax.ShapeDtypeStruct(shard.shape, shard.dtype),
-        ],
-        in_specs=[pl.BlockSpec(memory_space=pl.ANY)] * 2,
-        out_specs=[vmem()] * 2,
-        scratch_shapes=[pltpu.SemaphoreType.DMA((2,))],
+        out_shape=jax.ShapeDtypeStruct(shard.shape, shard.dtype),
+        in_specs=[vmem()],
+        out_specs=vmem(),
         compiler_params=params(8),
         name="fetch",
-    )(a_blocks, shard)
-    line = jnp.concatenate([shard_near, line_f, line_d, line_b])
-    plane_d = lax.ppermute(line, BOTH, second(2))
+    )(shard)
+    line = jnp.concatenate([shard_near, line_1, line_2, line_3])
+    plane_2 = lax.ppermute(line, BOTH, second(2))
     near = lax.ppermute(line, "row", row_pairs(1))
-    plane_d, near = lax.optimization_barrier((plane_d, near))
+    plane_2, near = lax.optimization_barrier((plane_2, near))
     lines = jnp.concatenate([line, near])
-    plane_f = lax.ppermute(lines, BOTH, second(1))
-    plane_b = lax.ppermute(lines, BOTH, second(-1))
-    far = lax.ppermute(plane_d, "row", row_pairs(1))
-    plane_f, plane_b, far = lax.optimization_barrier((plane_f, plane_b, far))
-    plane = jnp.concatenate([line, plane_f[:8], plane_d, plane_b[:8]])
+    plane_1 = lax.ppermute(lines, BOTH, second(1))
+    plane_3 = lax.ppermute(lines, BOTH, second(3))
+    far = lax.ppermute(plane_2, "row", row_pairs(1))
+    plane_1, plane_3, far = lax.optimization_barrier((plane_1, plane_3, far))
+    plane = jnp.concatenate([line, plane_1[:8], plane_2, plane_3[:8]])
     pair = lax.ppermute(plane, "row", row_pairs(0))
 
     cols, aggs = a_cols.T, p_aggs.T
@@ -164,7 +150,7 @@
         out_specs=vmem(),
         compiler_params=params(16),
         name="lift",
-    )(aggs, agglo, a_near, plane)
+    )(aggs, agglo, a_blocks, plane)
     piece = jax.ShapeDtypeStruct((SIDE, 2, 8, 768), jnp.float32)
     o0, o1, o2, o3 = pl.pallas_call(
         band_kernel,
@@ -177,16 +163,12 @@
         ],
         compiler_params=params(24),
         name="bands",
-    )(cols, aggs, agglo, split, plane, near, plane_f, plane_b, far, pair)
+    )(cols, aggs, agglo, split, plane, near, plane_1, plane_3, far, pair)
 
-    d = lax.ppermute(o2, BOTH, first(2))
-    f = lax.ppermute(o1, BOTH, first(1))
-    b = lax.ppermute(o3, BOTH, first(-1))
-    kept, to_f, to_d, to_b = (o0[m] + f[m] + d[m] + b[m] for m in range(SIDE))
-    d = lax.ppermute(to_d, BOTH, second(2))
-    f = lax.ppermute(to_f, BOTH, second(1))
-    b = lax.ppermute(to_b, BOTH, second(-1))
-    return (kept + f + d + b).reshape(2, 8, 6, B)
+    p1, p3, p2 = (lax.ppermute(o, BOTH, first(k)) for o, k in ((o1, 1), (o3, 3), (o2, 2)))
+    sums = [o0[m] + p1[m] + p2[m] + p3[m] for m in range(SIDE)]
+    q1, q3, q2 = (lax.ppermute(sums[k], BOTH, second(k)) for k in (1, 3, 2))
+    return (sums[0] + q1 + q2 + q3).reshape(2, 8, 6, B)
 
 
 def solution(mesh):

time: 56.9 us -> 58.3 us (1.025)
  waiting for transfers between devices: 24.2 us -> 26.1 us
  starting transfers between devices: 25.3 us -> 24.7 us
    ppermute x13, waiting for transfers between devices: 20.6 us -> 23.6 us  [the longest x3 6.33 us: local(): lax.ppermute(o, BOTH, first(k))]
    ppermute x1, starting transfers between devices: 2.72 us -> 1.61 us  [local(): pair = lax.ppermute(plane, 'row', row_pairs(0))]
    ppermute x1, waiting for transfers between devices: 0.77 us -> 0.01 us  [local(): pair = lax.ppermute(plane, 'row', row_pairs(0))]
    unnamed x15 -> x18, local copies, waits for them, and re-layouts: 2.27 us -> 2.39 us
  transfers between devices with their start and end apart: 15 -> 15, of which waited for: 10 -> 11; matrix products, arithmetic and copies ran while one was open for 0% -> 0% of each run, Pallas kernels for 3% -> 3%
where the time goes in v5:
time: 58.3 us; the launch traced here: 58.1 us
  waiting for transfers between devices  26.1 us (45%)
  starting transfers between devices  24.7 us (42%)
  Pallas kernels  3.95 us (7%)
  local copies, waits for them, and re-layouts  2.46 us (4%)
  other arithmetic  0.7 us (1%)
    ppermute x3, waiting for transfers between devices, local(): lax.ppermute(o, BOTH, first(k))  6.33 us
    ppermute x1, waiting for transfers between devices, local(): far = lax.ppermute(plane_2, 'row', row_pairs(1))  5.69 us
    ppermute x3, starting transfers between devices, local(): lax.ppermute(o, BOTH, first(k))  4.78 us
    ppermute x3, starting transfers between devices, local(): q1, q3, q2 = (lax.ppermute(sums[k], BOTH, second(k)) for k in (1, 3, 2))  4.18 us
    ppermute x3, starting transfers between devices, local(): lax.ppermute(shard, BOTH, first(k))  4.09 us
    ppermute x3, waiting for transfers between devices, local(): q1, q3, q2 = (lax.ppermute(sums[k], BOTH, second(k)) for k in (1, 3, 2))  4.09 us
    ppermute x3, waiting for transfers between devices, local(): lax.ppermute(shard, BOTH, first(k))  4 us
    ppermute x1, starting transfers between devices, local(): plane_2 = lax.ppermute(line, BOTH, second(2))  3.11 us
  transfers between devices with their start and end apart: 15, of which 11 were waited for; matrix products, arithmetic and copies ran while one was open for 0% of the time, Pallas kernels for 3%

profile of v5, /device:TPU:96, one launch (start us, length us, event | category | flops | bytes accessed | tf_op | source)
XLA Modules:
  0.0 58.1 jit_solution(15910304999593008056)
XLA Ops:
  0.0 3.0 %collective-permute-start.2 = (bf16[2,128,128]{2,1,0:T(8,128)(2,1)}, bf16[2,128,128]{2,1,0:T(8,128)(2,1)S(1)}, u32[]{:S(2)}, u32[]{:S(2)}) collective-permute-start(bf16[2,128,128]{2,1,0:T(8,128)(2,1)} %bitcast.21), channel_id=1, source_target_pairs={{0,3},{1,2},{2,1},{3,0},{4,7},{5,6},{6,5},{7,4},{8,11},{9,10},{10,... | collective-permute-start | bytes 196616 | tf_op jit(solution)/shard_map/ppermute | solution.py:124
  4.1 0.9 %copy-done.1 = bf16[1,2,128,128]{3,2,1,0:T(8,128)(2,1)S(1)} copy-done((bf16[1,2,128,128]{3,2,1,0:T(8,128)(2,1)S(1)}, bf16[1,2,128,128]{3,2,1,0:T(8,128)(2,1)}, u32[]{:S(2)}) %copy-start.1) | copy-done | bytes 65560
  5.0 0.7 %collective-permute-done.2 = bf16[2,128,128]{2,1,0:T(8,128)(2,1)S(1)} collective-permute-done((bf16[2,128,128]{2,1,0:T(8,128)(2,1)}, bf16[2,128,128]{2,1,0:T(8,128)(2,1)S(1)}, u32[]{:S(2)}, u32[]{:S(2)}) %collective-permute-start.2) | collective-permute-done | bytes 65568 | tf_op jit(solution)/shard_map/ppermute | solution.py:124
  5.7 3.3 %collective-permute-done.1 = bf16[2,128,128]{2,1,0:T(8,128)(2,1)S(1)} collective-permute-done((bf16[2,128,128]{2,1,0:T(8,128)(2,1)}, bf16[2,128,128]{2,1,0:T(8,128)(2,1)S(1)}, u32[]{:S(2)}, u32[]{:S(2)}) %collective-permute-start.1) | collective-permute-done | bytes 65568 | tf_op jit(solution)/shard_map/ppermute | solution.py:124
  9.0 1.9 %collective-permute-start.4 = (bf16[8,128,128]{2,1,0:T(8,128)(2,1)S(1)}, bf16[8,128,128]{2,1,0:T(8,128)(2,1)S(1)}, u32[]{:S(2)}, u32[]{:S(2)}) collective-permute-start(bf16[8,128,128]{2,1,0:T(8,128)(2,1)S(1)} %pad_maximum_fusion), channel_id=1, source_target_pairs={{16,32},{32,16},{48,64},{64,48},{80,96},{96,80},{112,128},{128,112... | collective-permute-start | bytes 786440 | tf_op jit(solution)/shard_map/ppermute | solution.py:135
  11.0 3.1 %collective-permute-start.3 = (bf16[8,128,128]{2,1,0:T(8,128)(2,1)S(1)}, bf16[8,128,128]{2,1,0:T(8,128)(2,1)S(1)}, u32[]{:S(2)}, u32[]{:S(2)}) collective-permute-start(bf16[8,128,128]{2,1,0:T(8,128)(2,1)S(1)} %pad_maximum_fusion), channel_id=1, source_target_pairs={{0,8},{1,9},{2,10},{3,11},{4,12},{5,13},{6,14},{7,15},{8,0},{9,1},... | collective-permute-start | bytes 786440 | tf_op jit(solution)/shard_map/ppermute | solution.py:134
  14.2 2.5 %collective-permute-done.4.near = bf16[8,128,128]{2,1,0:T(8,128)(2,1)S(1)} collective-permute-done((bf16[8,128,128]{2,1,0:T(8,128)(2,1)S(1)}, bf16[8,128,128]{2,1,0:T(8,128)(2,1)S(1)}, u32[]{:S(2)}, u32[]{:S(2)}) %collective-permute-start.4) | collective-permute-done | bytes 262176 | tf_op jit(solution)/shard_map/ppermute | solution.py:135
  16.7 2.2 %collective-permute-done.3 = bf16[8,128,128]{2,1,0:T(8,128)(2,1)S(1)} collective-permute-done((bf16[8,128,128]{2,1,0:T(8,128)(2,1)S(1)}, bf16[8,128,128]{2,1,0:T(8,128)(2,1)S(1)}, u32[]{:S(2)}, u32[]{:S(2)}) %collective-permute-start.3) | collective-permute-done | bytes 262176 | tf_op jit(solution)/shard_map/ppermute | solution.py:134
  19.0 2.8 %collective-permute-start.6 = (bf16[16,128,128]{2,1,0:T(8,128)(2,1)S(1)}, bf16[16,128,128]{2,1,0:T(8,128)(2,1)S(1)}, u32[]{:S(2)}, u32[]{:S(2)}) collective-permute-start(bf16[16,128,128]{2,1,0:T(8,128)(2,1)S(1)} %constant_dynamic-update-slice_fusion), channel_id=1, source_target_pairs={{0,12},{1,13},{2,14},{3,15},{4,8},{5,9},{6,10},{7,11},{8,4},{9,5},... | collective-permute-start | bytes 1572872 | tf_op jit(solution)/shard_map/ppermute | solution.py:139
  22.0 2.0 %collective-permute-start.7 = (bf16[8,128,128]{2,1,0:T(8,128)(2,1)S(1)}, bf16[8,128,128]{2,1,0:T(8,128)(2,1)S(1)}, u32[]{:S(2)}, u32[]{:S(2)}) collective-permute-start(bf16[8,128,128]{2,1,0:T(8,128)(2,1)S(1)} %collective-permute-done.3), channel_id=1, source_target_pairs={{16,32},{32,16},{48,64},{64,48},{80,96},{96,80},{112,128},{128,112... | collective-permute-start | bytes 786440 | tf_op jit(solution)/shard_map/ppermute | solution.py:140
  24.0 5.7 %collective-permute-done.7.far = bf16[8,128,128]{2,1,0:T(8,128)(2,1)S(1)} collective-permute-done((bf16[8,128,128]{2,1,0:T(8,128)(2,1)S(1)}, bf16[8,128,128]{2,1,0:T(8,128)(2,1)S(1)}, u32[]{:S(2)}, u32[]{:S(2)}) %collective-permute-start.7) | collective-permute-done | bytes 262176 | tf_op jit(solution)/shard_map/ppermute | solution.py:140
  29.7 1.3 %collective-permute-done.5.f = bf16[16,128,128]{2,1,0:T(8,128)(2,1)S(1)} collective-permute-done((bf16[16,128,128]{2,1,0:T(8,128)(2,1)S(1)}, bf16[16,128,128]{2,1,0:T(8,128)(2,1)S(1)}, u32[]{:S(2)}, u32[]{:S(2)}) %collective-permute-start.5) | collective-permute-done | bytes 524320 | tf_op jit(solution)/shard_map/ppermute | solution.py:138
  31.1 1.6 %collective-permute-start.8 = (bf16[32,128,128]{2,1,0:T(8,128)(2,1)S(1)}, bf16[32,128,128]{2,1,0:T(8,128)(2,1)S(1)}, u32[]{:S(2)}, u32[]{:S(2)}) collective-permute-start(bf16[32,128,128]{2,1,0:T(8,128)(2,1)S(1)} %slice_dynamic-update-slice_fusion.plane), channel_id=1, source_target_pairs={{0,16},{16,0},{32,48},{48,32},{64,80},{80,64},{96,112},{112,96},{1... | collective-permute-start | bytes 3145736 | tf_op jit(solution)/shard_map/ppermute | solution.py:143
  34.1 1.5 %lift.1.split = bf16[32,256,256]{2,1,0:T(8,128)(2,1)S(1)} custom-call(s32[2,256]{1,0:T(2,128)S(1)} %bitcast.25, s32[32]{0:T(128)S(1)} %copy-done.4, bf16[16,2,128,128]{3,2,1,0:T(8,128)(2,1)S(1)} %copy-done, bf16[32,128,128]{2,1,0:T(8,128)(2,1)S(1)} %slice_dynamic-update-slice_fusion.plane), custom_call_target="tpu_custom_call" | custom-call | tf_op jit(solution)/shard_map/lift/pallas_call | solution.py:146
  35.6 2.4 %bands.1 = (f32[4,2,8,768]{3,2,1,0:T(8,128)S(1)}, f32[4,2,8,768]{3,2,1,0:T(8,128)S(1)}, f32[4,2,8,768]{3,2,1,0:T(8,128)S(1)}, f32[4,2,8,768]{3,2,1,0:T(8,128)S(1)}) custom-call(s32[2,16]{1,0:T(2,128)S(1)} %bitcast.27, s32[2,256]{1,0:T(2,128)S(1)} %bitcast.26, s32[32]{0:T(128)S(1)} %copy-done.4, bf16[32,256,256]{2,1,0:T(8,128)(2,1)S(1)} %lift.1.split, ...), custom_call_target="tpu_custom_call" | custom-call | tf_op jit(solution)/shard_map/bands/pallas_call | solution.py:155
  38.1 1.8 %collective-permute-start.9 = (f32[4,2,8,768]{3,2,1,0:T(8,128)S(1)}, f32[4,2,8,768]{3,2,1,0:T(8,128)S(1)}, u32[]{:S(2)}, u32[]{:S(2)}) collective-permute-start(f32[4,2,8,768]{3,2,1,0:T(8,128)S(1)} %get-tuple-element.20), channel_id=1, source_target_pairs={{0,1},{1,0},{2,3},{3,2},{4,5},{5,4},{6,7},{7,6},{8,9},{9,8},{10,11... | collective-permute-start | bytes 589832 | tf_op jit(solution)/shard_map/ppermute | solution.py:168
  40.5 2.3 %collective-permute-start.11 = (f32[4,2,8,768]{3,2,1,0:T(8,128)S(1)}, f32[4,2,8,768]{3,2,1,0:T(8,128)S(1)}, u32[]{:S(2)}, u32[]{:S(2)}) collective-permute-start(f32[4,2,8,768]{3,2,1,0:T(8,128)S(1)} %get-tuple-element.22), channel_id=1, source_target_pairs={{0,3},{1,2},{2,1},{3,0},{4,7},{5,6},{6,5},{7,4},{8,11},{9,10},{10,... | collective-permute-start | bytes 589832 | tf_op jit(solution)/shard_map/ppermute | solution.py:168
  42.9 1.0 %collective-permute-done.9 = f32[4,2,8,768]{3,2,1,0:T(8,128)S(1)} collective-permute-done((f32[4,2,8,768]{3,2,1,0:T(8,128)S(1)}, f32[4,2,8,768]{3,2,1,0:T(8,128)S(1)}, u32[]{:S(2)}, u32[]{:S(2)}) %collective-permute-start.9) | collective-permute-done | bytes 196640 | tf_op jit(solution)/shard_map/ppermute | solution.py:168
  43.8 3.4 %collective-permute-done.10 = f32[4,2,8,768]{3,2,1,0:T(8,128)S(1)} collective-permute-done((f32[4,2,8,768]{3,2,1,0:T(8,128)S(1)}, f32[4,2,8,768]{3,2,1,0:T(8,128)S(1)}, u32[]{:S(2)}, u32[]{:S(2)}) %collective-permute-start.10) | collective-permute-done | bytes 196640 | tf_op jit(solution)/shard_map/ppermute | solution.py:168
  47.2 2.0 %collective-permute-done.11 = f32[4,2,8,768]{3,2,1,0:T(8,128)S(1)} collective-permute-done((f32[4,2,8,768]{3,2,1,0:T(8,128)S(1)}, f32[4,2,8,768]{3,2,1,0:T(8,128)S(1)}, u32[]{:S(2)}, u32[]{:S(2)}) %collective-permute-start.11) | collective-permute-done | bytes 196640 | tf_op jit(solution)/shard_map/ppermute | solution.py:168
  49.5 2.4 %collective-permute-start.14 = (f32[2,8,768]{2,1,0:T(8,128)S(1)}, f32[2,8,768]{2,1,0:T(8,128)S(1)}, u32[]{:S(2)}, u32[]{:S(2)}) collective-permute-start(f32[2,8,768]{2,1,0:T(8,128)S(1)} %get-tuple-element.24), channel_id=1, source_target_pairs={{0,12},{1,13},{2,14},{3,15},{4,8},{5,9},{6,10},{7,11},{8,4},{9,5},... | collective-permute-start | bytes 147464 | tf_op jit(solution)/shard_map/ppermute | solution.py:170
  51.9 1.5 %collective-permute-start.13 = (f32[2,8,768]{2,1,0:T(8,128)S(1)}, f32[2,8,768]{2,1,0:T(8,128)S(1)}, u32[]{:S(2)}, u32[]{:S(2)}) collective-permute-start(f32[2,8,768]{2,1,0:T(8,128)S(1)} %get-tuple-element.25), channel_id=1, source_target_pairs={{0,8},{1,9},{2,10},{3,11},{4,12},{5,13},{6,14},{7,15},{8,0},{9,1},... | collective-permute-start | bytes 147464 | tf_op jit(solution)/shard_map/ppermute | solution.py:170
  53.4 1.4 %collective-permute-done.14 = f32[2,8,768]{2,1,0:T(8,128)S(1)} collective-permute-done((f32[2,8,768]{2,1,0:T(8,128)S(1)}, f32[2,8,768]{2,1,0:T(8,128)S(1)}, u32[]{:S(2)}, u32[]{:S(2)}) %collective-permute-start.14) | collective-permute-done | bytes 49184 | tf_op jit(solution)/shard_map/ppermute | solution.py:170
  54.8 2.7 %collective-permute-done.13 = f32[2,8,768]{2,1,0:T(8,128)S(1)} collective-permute-done((f32[2,8,768]{2,1,0:T(8,128)S(1)}, f32[2,8,768]{2,1,0:T(8,128)S(1)}, u32[]{:S(2)}, u32[]{:S(2)}) %collective-permute-start.13) | collective-permute-done | bytes 49184 | tf_op jit(solution)/shard_map/ppermute | solution.py:170
  (32 shorter events, 4.6 us)
Async XLA Ops:
  0.0 32.7 %copy-start = (bf16[16,2,128,128]{3,2,1,0:T(8,128)(2,1)S(1)}, bf16[16,2,128,128]{3,2,1,0:T(8,128)(2,1)}, u32[]{:S(2)}) copy-start(bf16[16,2,128,128]{3,2,1,0:T(8,128)(2,1)} %a.1) | copy-start | bytes 3145732
  0.0 5.7 %collective-permute-start.2 = (bf16[2,128,128]{2,1,0:T(8,128)(2,1)}, bf16[2,128,128]{2,1,0:T(8,128)(2,1)S(1)}, u32[]{:S(2)}, u32[]{:S(2)}) collective-permute-start(bf16[2,128,128]{2,1,0:T(8,128)(2,1)} %bitcast.21), channel_id=1, source_target_pairs={{0,3},{1,2},{2,1},{3,0},{4,7},{5,6},{6,5},{7,4},{8,11},{9,10},{10,... | collective-permute-start | bytes 196616 | tf_op jit(solution)/shard_map/ppermute | solution.py:124
  3.0 6.0 %collective-permute-start.1 = (bf16[2,128,128]{2,1,0:T(8,128)(2,1)}, bf16[2,128,128]{2,1,0:T(8,128)(2,1)S(1)}, u32[]{:S(2)}, u32[]{:S(2)}) collective-permute-start(bf16[2,128,128]{2,1,0:T(8,128)(2,1)} %bitcast.22), channel_id=1, source_target_pairs={{0,2},{1,3},{2,0},{3,1},{4,6},{5,7},{6,4},{7,5},{8,10},{9,11},{10,... | collective-permute-start | bytes 196616 | tf_op jit(solution)/shard_map/ppermute | solution.py:124
  3.6 5.4 %collective-permute-start = (bf16[2,128,128]{2,1,0:T(8,128)(2,1)}, bf16[2,128,128]{2,1,0:T(8,128)(2,1)S(1)}, u32[]{:S(2)}, u32[]{:S(2)}) collective-permute-start(bf16[2,128,128]{2,1,0:T(8,128)(2,1)} %bitcast.23), channel_id=1, source_target_pairs={{0,1},{1,0},{2,3},{3,2},{4,5},{5,4},{6,7},{7,6},{8,9},{9,8},{10,11... | collective-permute-start | bytes 196616 | tf_op jit(solution)/shard_map/ppermute | solution.py:124
  4.1 0.9 %copy-start.1 = (bf16[1,2,128,128]{3,2,1,0:T(8,128)(2,1)S(1)}, bf16[1,2,128,128]{3,2,1,0:T(8,128)(2,1)}, u32[]{:S(2)}) copy-start(bf16[1,2,128,128]{3,2,1,0:T(8,128)(2,1)} %param.7) | copy-start | bytes 196612
  9.0 7.7 %collective-permute-start.4 = (bf16[8,128,128]{2,1,0:T(8,128)(2,1)S(1)}, bf16[8,128,128]{2,1,0:T(8,128)(2,1)S(1)}, u32[]{:S(2)}, u32[]{:S(2)}) collective-permute-start(bf16[8,128,128]{2,1,0:T(8,128)(2,1)S(1)} %pad_maximum_fusion), channel_id=1, source_target_pairs={{16,32},{32,16},{48,64},{64,48},{80,96},{96,80},{112,128},{128,112... | collective-permute-start | bytes 786440 | tf_op jit(solution)/shard_map/ppermute | solution.py:135
  11.0 8.0 %collective-permute-start.3 = (bf16[8,128,128]{2,1,0:T(8,128)(2,1)S(1)}, bf16[8,128,128]{2,1,0:T(8,128)(2,1)S(1)}, u32[]{:S(2)}, u32[]{:S(2)}) collective-permute-start(bf16[8,128,128]{2,1,0:T(8,128)(2,1)S(1)} %pad_maximum_fusion), channel_id=1, source_target_pairs={{0,8},{1,9},{2,10},{3,11},{4,12},{5,13},{6,14},{7,15},{8,0},{9,1},... | collective-permute-start | bytes 786440 | tf_op jit(solution)/shard_map/ppermute | solution.py:134
  18.9 16.7 %copy-start.3 = (s32[256,2]{0,1:T(2,128)S(1)}, s32[256,2]{0,1:T(2,128)}, u32[]{:S(2)}) copy-start(s32[256,2]{0,1:T(2,128)} %param.8) | copy-start | bytes 6148
  18.9 16.7 %copy-start.5 = (s32[16,2]{0,1:T(2,128)S(1)}, s32[16,2]{0,1:T(2,128)}, u32[]{:S(2)}) copy-start(s32[16,2]{0,1:T(2,128)} %param.6) | copy-start | bytes 388
  19.0 10.8 %collective-permute-start.6 = (bf16[16,128,128]{2,1,0:T(8,128)(2,1)S(1)}, bf16[16,128,128]{2,1,0:T(8,128)(2,1)S(1)}, u32[]{:S(2)}, u32[]{:S(2)}) collective-permute-start(bf16[16,128,128]{2,1,0:T(8,128)(2,1)S(1)} %constant_dynamic-update-slice_fusion), channel_id=1, source_target_pairs={{0,12},{1,13},{2,14},{3,15},{4,8},{5,9},{6,10},{7,11},{8,4},{9,5},... | collective-permute-start | bytes 1572872 | tf_op jit(solution)/shard_map/ppermute | solution.py:139
  21.8 9.2 %collective-permute-start.5 = (bf16[16,128,128]{2,1,0:T(8,128)(2,1)S(1)}, bf16[16,128,128]{2,1,0:T(8,128)(2,1)S(1)}, u32[]{:S(2)}, u32[]{:S(2)}) collective-permute-start(bf16[16,128,128]{2,1,0:T(8,128)(2,1)S(1)} %constant_dynamic-update-slice_fusion), channel_id=1, source_target_pairs={{0,4},{1,5},{2,6},{3,7},{4,0},{5,1},{6,2},{7,3},{8,12},{9,13},{10,... | collective-permute-start | bytes 1572872 | tf_op jit(solution)/shard_map/ppermute | solution.py:138
  22.0 7.7 %collective-permute-start.7 = (bf16[8,128,128]{2,1,0:T(8,128)(2,1)S(1)}, bf16[8,128,128]{2,1,0:T(8,128)(2,1)S(1)}, u32[]{:S(2)}, u32[]{:S(2)}) collective-permute-start(bf16[8,128,128]{2,1,0:T(8,128)(2,1)S(1)} %collective-permute-done.3), channel_id=1, source_target_pairs={{16,32},{32,16},{48,64},{64,48},{80,96},{96,80},{112,128},{128,112... | collective-permute-start | bytes 786440 | tf_op jit(solution)/shard_map/ppermute | solution.py:140
  31.1 4.5 %collective-permute-start.8 = (bf16[32,128,128]{2,1,0:T(8,128)(2,1)S(1)}, bf16[32,128,128]{2,1,0:T(8,128)(2,1)S(1)}, u32[]{:S(2)}, u32[]{:S(2)}) collective-permute-start(bf16[32,128,128]{2,1,0:T(8,128)(2,1)S(1)} %slice_dynamic-update-slice_fusion.plane), channel_id=1, source_target_pairs={{0,16},{16,0},{32,48},{48,32},{64,80},{80,64},{96,112},{112,96},{1... | collective-permute-start | bytes 3145736 | tf_op jit(solution)/shard_map/ppermute | solution.py:143
  32.7 0.7 %copy-start.2 = (s32[256,2]{0,1:T(2,128)S(1)}, s32[256,2]{0,1:T(2,128)}, u32[]{:S(2)}) copy-start(s32[256,2]{0,1:T(2,128)} %param.8) | copy-start | bytes 6148
  33.4 0.7 %copy-start.4 = (s32[32]{0:T(128)S(1)}, s32[32]{0:T(128)}, u32[]{:S(2)}) copy-start(s32[32]{0:T(128)} %agglo.3) | copy-start | bytes 388
  38.1 5.8 %collective-permute-start.9 = (f32[4,2,8,768]{3,2,1,0:T(8,128)S(1)}, f32[4,2,8,768]{3,2,1,0:T(8,128)S(1)}, u32[]{:S(2)}, u32[]{:S(2)}) collective-permute-start(f32[4,2,8,768]{3,2,1,0:T(8,128)S(1)} %get-tuple-element.20), channel_id=1, source_target_pairs={{0,1},{1,0},{2,3},{3,2},{4,5},{5,4},{6,7},{7,6},{8,9},{9,8},{10,11... | collective-permute-start | bytes 589832 | tf_op jit(solution)/shard_map/ppermute | solution.py:168
  39.9 7.3 %collective-permute-start.10 = (f32[4,2,8,768]{3,2,1,0:T(8,128)S(1)}, f32[4,2,8,768]{3,2,1,0:T(8,128)S(1)}, u32[]{:S(2)}, u32[]{:S(2)}) collective-permute-start(f32[4,2,8,768]{3,2,1,0:T(8,128)S(1)} %get-tuple-element.21), channel_id=1, source_target_pairs={{0,2},{1,3},{2,0},{3,1},{4,6},{5,7},{6,4},{7,5},{8,10},{9,11},{10,... | collective-permute-start | bytes 589832 | tf_op jit(solution)/shard_map/ppermute | solution.py:168
  40.5 8.7 %collective-permute-start.11 = (f32[4,2,8,768]{3,2,1,0:T(8,128)S(1)}, f32[4,2,8,768]{3,2,1,0:T(8,128)S(1)}, u32[]{:S(2)}, u32[]{:S(2)}) collective-permute-start(f32[4,2,8,768]{3,2,1,0:T(8,128)S(1)} %get-tuple-element.22), channel_id=1, source_target_pairs={{0,3},{1,2},{2,1},{3,0},{4,7},{5,6},{6,5},{7,4},{8,11},{9,10},{10,... | collective-permute-start | bytes 589832 | tf_op jit(solution)/shard_map/ppermute | solution.py:168
  49.2 4.2 %collective-permute-start.12 = (f32[2,8,768]{2,1,0:T(8,128)S(1)}, f32[2,8,768]{2,1,0:T(8,128)S(1)}, u32[]{:S(2)}, u32[]{:S(2)}) collective-permute-start(f32[2,8,768]{2,1,0:T(8,128)S(1)} %get-tuple-element.23), channel_id=1, source_target_pairs={{0,4},{1,5},{2,6},{3,7},{4,0},{5,1},{6,2},{7,3},{8,12},{9,13},{10,... | collective-permute-start | bytes 147464 | tf_op jit(solution)/shard_map/ppermute | solution.py:170
  49.5 5.3 %collective-permute-start.14 = (f32[2,8,768]{2,1,0:T(8,128)S(1)}, f32[2,8,768]{2,1,0:T(8,128)S(1)}, u32[]{:S(2)}, u32[]{:S(2)}) collective-permute-start(f32[2,8,768]{2,1,0:T(8,128)S(1)} %get-tuple-element.24), channel_id=1, source_target_pairs={{0,12},{1,13},{2,14},{3,15},{4,8},{5,9},{6,10},{7,11},{8,4},{9,5},... | collective-permute-start | bytes 147464 | tf_op jit(solution)/shard_map/ppermute | solution.py:170
  51.9 5.6 %collective-permute-start.13 = (f32[2,8,768]{2,1,0:T(8,128)S(1)}, f32[2,8,768]{2,1,0:T(8,128)S(1)}, u32[]{:S(2)}, u32[]{:S(2)}) collective-permute-start(f32[2,8,768]{2,1,0:T(8,128)S(1)} %get-tuple-element.25), channel_id=1, source_target_pairs={{0,8},{1,9},{2,10},{3,11},{4,12},{5,13},{6,14},{7,15},{8,0},{9,1},... | collective-permute-start | bytes 147464 | tf_op jit(solution)/shard_map/ppermute | solution.py:170

commit v6 on v5

--- a/solution.py
+++ b/solution.py
@@ -48,7 +48,8 @@
 
 def slot_of(y, x, j, cross):
     dy, dx = y ^ ((j % ROWS) // SIDE), x ^ (j % SIDE)
-    return jnp.where(cross == 0, dy * SIDE + dx, dx * SIDE + dy)
+    back, along = jnp.where(cross == 0, dy, dx), jnp.where(cross == 0, dx, dy)
+    return ((back >> 1) | ((back & 1) << 1)) * SIDE + along
 
 
 def fetch_kernel(shard, near):
@@ -73,14 +74,12 @@
 
 
 def band_kernel(
-    cols, aggs, agglo, split, plane, near, f, b, far, pair, o0, o1, o2, o3, blocks, acc
+    cols, aggs, agglo, split, own, near, near_13, pair, o0, o1, o2, o3, blocks, acc
 ):
     row, cross, y, x = place()
-    blocks[0:32] = plane[...]
-    blocks[32:40] = near[...]
-    blocks[40:48] = f[8:16]
-    blocks[48:56] = far[...]
-    blocks[56:64] = b[8:16]
+    blocks[0:32] = own[...]
+    blocks[32:48] = near[...]
+    blocks[48:64] = near_13[...]
     blocks[64:96] = pair[...]
     acc[...] = jnp.zeros_like(acc)
     pair_band = 2 - 2 * (row % 2)
@@ -121,7 +120,7 @@
 
 def local(a_blocks, a_cols, p_blocks, p_aggs, agglo):
     shard = p_blocks[0]
-    line_1, line_3, line_2 = (lax.ppermute(shard, BOTH, first(k)) for k in (1, 3, 2))
+    across = lax.ppermute(shard, BOTH, second(2))
     shard_near = pl.pallas_call(
         fetch_kernel,
         out_shape=jax.ShapeDtypeStruct(shard.shape, shard.dtype),
@@ -130,18 +129,19 @@
         compiler_params=params(8),
         name="fetch",
     )(shard)
-    line = jnp.concatenate([shard_near, line_1, line_2, line_3])
-    plane_2 = lax.ppermute(line, BOTH, second(2))
-    near = lax.ppermute(line, "row", row_pairs(1))
-    plane_2, near = lax.optimization_barrier((plane_2, near))
-    lines = jnp.concatenate([line, near])
-    plane_1 = lax.ppermute(lines, BOTH, second(1))
-    plane_3 = lax.ppermute(lines, BOTH, second(3))
-    far = lax.ppermute(plane_2, "row", row_pairs(1))
-    plane_1, plane_3, far = lax.optimization_barrier((plane_1, plane_3, far))
-    plane = jnp.concatenate([line, plane_1[:8], plane_2, plane_3[:8]])
-    pair = lax.ppermute(plane, "row", row_pairs(0))
+    duo = jnp.concatenate([shard_near, across])
+    duo_1, duo_3, duo_2 = (lax.ppermute(duo, BOTH, first(k)) for k in (1, 3, 2))
+    duos = (duo, duo_1, duo_2, duo_3)
+    line = jnp.concatenate([d[:2] for d in duos])
+    lines = jnp.concatenate([line] + [d[2:] for d in duos])
+    near = lax.ppermute(lines, "row", row_pairs(1))
+    own_1 = lax.ppermute(line, BOTH, second(1))
+    own_3 = lax.ppermute(line, BOTH, second(3))
+    near_13 = lax.ppermute(jnp.concatenate([own_1, own_3]), "row", row_pairs(1))
+    own = jnp.concatenate([lines, own_1, own_3])
+    pair = lax.ppermute(own, "row", row_pairs(0))
 
+    cost = pl.CostEstimate(flops=10**6, bytes_accessed=2**12, transcendentals=0)
     cols, aggs = a_cols.T, p_aggs.T
     split = pl.pallas_call(
         lift_kernel,
@@ -149,21 +149,23 @@
         in_specs=[smem(), smem(), vmem(), vmem()],
         out_specs=vmem(),
         compiler_params=params(16),
+        cost_estimate=cost,
         name="lift",
-    )(aggs, agglo, a_blocks, plane)
+    )(aggs, agglo, a_blocks, own)
     piece = jax.ShapeDtypeStruct((SIDE, 2, 8, 768), jnp.float32)
     o0, o1, o2, o3 = pl.pallas_call(
         band_kernel,
         out_shape=[piece] * 4,
-        in_specs=[smem()] * 3 + [vmem()] * 7,
+        in_specs=[smem()] * 3 + [vmem()] * 5,
         out_specs=[vmem()] * 4,
         scratch_shapes=[
             pltpu.VMEM((96, B, B), jnp.bfloat16),
             pltpu.VMEM((3, 256, 256), jnp.float32),
         ],
         compiler_params=params(24),
+        cost_estimate=cost,
         name="bands",
-    )(cols, aggs, agglo, split, plane, near, plane_1, plane_3, far, pair)
+    )(cols, aggs, agglo, split, own, near, near_13, pair)
 
     p1, p3, p2 = (lax.ppermute(o, BOTH, first(k)) for o, k in ((o1, 1), (o3, 3), (o2, 2)))
     sums = [o0[m] + p1[m] + p2[m] + p3[m] for m in range(SIDE)]

time: 58.3 us -> 64.2 us (1.10)
  the two profiles are of different devices: /device:TPU:96 before, /device:TPU:128 now
where the time goes in v6:
time: 64.2 us; the launch traced here: 64.1 us
  waiting for transfers between devices  31.2 us (49%)
  starting transfers between devices  26.9 us (42%)
  Pallas kernels  3.92 us (6%)
  local copies, waits for them, and re-layouts  1.2 us (2%)
  other arithmetic  0.78 us (1%)
    ppermute x1, waiting for transfers between devices, local(): own_1 = lax.ppermute(line, BOTH, second(1))  6.09 us
    ppermute x3, waiting for transfers between devices, local(): lax.ppermute(o, BOTH, first(k))  5.74 us
    ppermute x3, waiting for transfers between devices, local(): duo_1, duo_3, duo_2 = (lax.ppermute(duo, BOTH, first(k)) for k in (1, 3, 2))  5.73 us
    ppermute x1, waiting for transfers between devices, local(): near_13 = lax.ppermute(jnp.concatenate([own_1, own_3]), 'row', row_pairs(1))  5.62 us
    ppermute x3, starting transfers between devices, local(): lax.ppermute(o, BOTH, first(k))  4.79 us
    ppermute x1, starting transfers between devices, local(): near_13 = lax.ppermute(jnp.concatenate([own_1, own_3]), 'row', row_pairs(1))  4.77 us
    ppermute x3, starting transfers between devices, local(): duo_1, duo_3, duo_2 = (lax.ppermute(duo, BOTH, first(k)) for k in (1, 3, 2))  4.5 us
    ppermute x3, starting transfers between devices, local(): q1, q3, q2 = (lax.ppermute(sums[k], BOTH, second(k)) for k in (1, 3, 2))  4.18 us
  transfers between devices with their start and end apart: 15, of which 11 were waited for; matrix products, arithmetic and copies ran while one was open for 0% of the time, Pallas kernels for 2%

profile of v6, /device:TPU:128, one launch (start us, length us, event | category | flops | bytes accessed | tf_op | source)
XLA Modules:
  0.0 64.1 jit_solution(5387509442686154555)
XLA Ops:
  0.0 3.2 %collective-permute-start = (bf16[2,128,128]{2,1,0:T(8,128)(2,1)}, bf16[2,128,128]{2,1,0:T(8,128)(2,1)S(1)}, u32[]{:S(2)}, u32[]{:S(2)}) collective-permute-start(bf16[2,128,128]{2,1,0:T(8,128)(2,1)} %bitcast.21), channel_id=1, source_target_pairs={{0,8},{1,9},{2,10},{3,11},{4,12},{5,13},{6,14},{7,15},{8,0},{9,1},... | collective-permute-start | bytes 196616 | tf_op jit(solution)/shard_map/ppermute | solution.py:123
  3.2 0.9 %copy-done.1 = bf16[1,2,128,128]{3,2,1,0:T(8,128)(2,1)S(1)} copy-done((bf16[1,2,128,128]{3,2,1,0:T(8,128)(2,1)S(1)}, bf16[1,2,128,128]{3,2,1,0:T(8,128)(2,1)}, u32[]{:S(2)}) %copy-start.1) | copy-done | bytes 65560
  4.1 1.9 %collective-permute-done = bf16[2,128,128]{2,1,0:T(8,128)(2,1)S(1)} collective-permute-done((bf16[2,128,128]{2,1,0:T(8,128)(2,1)}, bf16[2,128,128]{2,1,0:T(8,128)(2,1)S(1)}, u32[]{:S(2)}, u32[]{:S(2)}) %collective-permute-start) | collective-permute-done | bytes 65568 | tf_op jit(solution)/shard_map/ppermute | solution.py:123
  6.0 1.6 %collective-permute-start.1 = (bf16[4,128,128]{2,1,0:T(8,128)(2,1)S(1)}, bf16[4,128,128]{2,1,0:T(8,128)(2,1)S(1)}, u32[]{:S(2)}, u32[]{:S(2)}) collective-permute-start(bf16[4,128,128]{2,1,0:T(8,128)(2,1)S(1)} %pad_maximum_fusion.2), channel_id=1, source_target_pairs={{0,1},{1,0},{2,3},{3,2},{4,5},{5,4},{6,7},{7,6},{8,9},{9,8},{10,11... | collective-permute-start | bytes 393224 | tf_op jit(solution)/shard_map/ppermute | solution.py:133
  7.6 2.2 %collective-permute-start.3 = (bf16[4,128,128]{2,1,0:T(8,128)(2,1)S(1)}, bf16[4,128,128]{2,1,0:T(8,128)(2,1)S(1)}, u32[]{:S(2)}, u32[]{:S(2)}) collective-permute-start(bf16[4,128,128]{2,1,0:T(8,128)(2,1)S(1)} %pad_maximum_fusion.2), channel_id=1, source_target_pairs={{0,3},{1,2},{2,1},{3,0},{4,7},{5,6},{6,5},{7,4},{8,11},{9,10},{10,... | collective-permute-start | bytes 393224 | tf_op jit(solution)/shard_map/ppermute | solution.py:133
  9.8 0.7 %collective-permute-start.2 = (bf16[4,128,128]{2,1,0:T(8,128)(2,1)S(1)}, bf16[4,128,128]{2,1,0:T(8,128)(2,1)S(1)}, u32[]{:S(2)}, u32[]{:S(2)}) collective-permute-start(bf16[4,128,128]{2,1,0:T(8,128)(2,1)S(1)} %pad_maximum_fusion.2), channel_id=1, source_target_pairs={{0,2},{1,3},{2,0},{3,1},{4,6},{5,7},{6,4},{7,5},{8,10},{9,11},{10,... | collective-permute-start | bytes 393224 | tf_op jit(solution)/shard_map/ppermute | solution.py:133
  11.1 5.2 %collective-permute-done.2 = bf16[4,128,128]{2,1,0:T(8,128)(2,1)S(1)} collective-permute-done((bf16[4,128,128]{2,1,0:T(8,128)(2,1)S(1)}, bf16[4,128,128]{2,1,0:T(8,128)(2,1)S(1)}, u32[]{:S(2)}, u32[]{:S(2)}) %collective-permute-start.2) | collective-permute-done | bytes 131104 | tf_op jit(solution)/shard_map/ppermute | solution.py:133
  16.5 3.1 %collective-permute-start.5 = (bf16[8,128,128]{2,1,0:T(8,128)(2,1)S(1)}, bf16[8,128,128]{2,1,0:T(8,128)(2,1)S(1)}, u32[]{:S(2)}, u32[]{:S(2)}) collective-permute-start(bf16[8,128,128]{2,1,0:T(8,128)(2,1)S(1)} %pad_maximum_fusion.1), channel_id=1, source_target_pairs={{0,12},{1,13},{2,14},{3,15},{4,8},{5,9},{6,10},{7,11},{8,4},{9,5},... | collective-permute-start | bytes 786440 | tf_op jit(solution)/shard_map/ppermute | solution.py:139
  19.9 6.1 %collective-permute-done.4 = bf16[8,128,128]{2,1,0:T(8,128)(2,1)S(1)} collective-permute-done((bf16[8,128,128]{2,1,0:T(8,128)(2,1)S(1)}, bf16[8,128,128]{2,1,0:T(8,128)(2,1)S(1)}, u32[]{:S(2)}, u32[]{:S(2)}) %collective-permute-start.4) | collective-permute-done | bytes 262176 | tf_op jit(solution)/shard_map/ppermute | solution.py:138
  26.2 2.0 %collective-permute-start.6 = (bf16[16,128,128]{2,1,0:T(8,128)(2,1)S(1)}, bf16[16,128,128]{2,1,0:T(8,128)(2,1)S(1)}, u32[]{:S(2)}, u32[]{:S(2)}) collective-permute-start(bf16[16,128,128]{2,1,0:T(8,128)(2,1)S(1)} %get-tuple-element.16), channel_id=1, source_target_pairs={{16,32},{32,16},{48,64},{64,48},{80,96},{96,80},{112,128},{128,112... | collective-permute-start | bytes 1572872 | tf_op jit(solution)/shard_map/ppermute | solution.py:137
  28.3 4.8 %collective-permute-start.7 = (bf16[16,128,128]{2,1,0:T(8,128)(2,1)S(1)}, bf16[16,128,128]{2,1,0:T(8,128)(2,1)S(1)}, u32[]{:S(2)}, u32[]{:S(2)}) collective-permute-start(bf16[16,128,128]{2,1,0:T(8,128)(2,1)S(1)} %pad_maximum_fusion), channel_id=1, source_target_pairs={{16,32},{32,16},{48,64},{64,48},{80,96},{96,80},{112,128},{128,112... | collective-permute-start | bytes 1572872 | tf_op jit(solution)/shard_map/ppermute | solution.py:140
  33.1 1.5 %lift.1.split = bf16[32,256,256]{2,1,0:T(8,128)(2,1)S(1)} custom-call(s32[2,256]{1,0:T(2,128)S(1)} %bitcast.23, s32[32]{0:T(128)S(1)} %copy-done.3, bf16[16,2,128,128]{3,2,1,0:T(8,128)(2,1)S(1)} %copy-done, bf16[32,128,128]{2,1,0:T(8,128)(2,1)S(1)} %constant_dynamic-update-slice_fusion.plane.own), custom_call_target="tpu_custom_call" | custom-call | flops 1000000 | bytes 4096 | tf_op jit(solution)/shard_map/lift/pallas_call | solution.py:146
  34.6 3.3 %collective-permute-done.6.near = bf16[16,128,128]{2,1,0:T(8,128)(2,1)S(1)} collective-permute-done((bf16[16,128,128]{2,1,0:T(8,128)(2,1)S(1)}, bf16[16,128,128]{2,1,0:T(8,128)(2,1)S(1)}, u32[]{:S(2)}, u32[]{:S(2)}) %collective-permute-start.6) | collective-permute-done | bytes 524320 | tf_op jit(solution)/shard_map/ppermute | solution.py:137
  37.9 5.6 %collective-permute-done.7.near_13 = bf16[16,128,128]{2,1,0:T(8,128)(2,1)S(1)} collective-permute-done((bf16[16,128,128]{2,1,0:T(8,128)(2,1)S(1)}, bf16[16,128,128]{2,1,0:T(8,128)(2,1)S(1)}, u32[]{:S(2)}, u32[]{:S(2)}) %collective-permute-start.7) | collective-permute-done | bytes 524320 | tf_op jit(solution)/shard_map/ppermute | solution.py:140
  43.5 2.4 %bands.1 = (f32[4,2,8,768]{3,2,1,0:T(8,128)S(1)}, f32[4,2,8,768]{3,2,1,0:T(8,128)S(1)}, f32[4,2,8,768]{3,2,1,0:T(8,128)S(1)}, f32[4,2,8,768]{3,2,1,0:T(8,128)S(1)}) custom-call(s32[2,16]{1,0:T(2,128)S(1)} %bitcast.25, s32[2,256]{1,0:T(2,128)S(1)} %bitcast.24, s32[32]{0:T(128)S(1)} %copy-done.3, bf16[32,256,256]{2,1,0:T(8,128)(2,1)S(1)} %lift.1.split, ...), custom_call_target="tpu_custom_call" | custom-call | flops 1000000 | bytes 4096 | tf_op jit(solution)/shard_map/bands/pallas_call | solution.py:156
  46.7 1.9 %collective-permute-start.10 = (f32[4,2,8,768]{3,2,1,0:T(8,128)S(1)}, f32[4,2,8,768]{3,2,1,0:T(8,128)S(1)}, u32[]{:S(2)}, u32[]{:S(2)}) collective-permute-start(f32[4,2,8,768]{3,2,1,0:T(8,128)S(1)} %get-tuple-element.11), channel_id=1, source_target_pairs={{0,2},{1,3},{2,0},{3,1},{4,6},{5,7},{6,4},{7,5},{8,10},{9,11},{10,... | collective-permute-start | bytes 589832 | tf_op jit(solution)/shard_map/ppermute | solution.py:170
  48.6 2.1 %collective-permute-start.11 = (f32[4,2,8,768]{3,2,1,0:T(8,128)S(1)}, f32[4,2,8,768]{3,2,1,0:T(8,128)S(1)}, u32[]{:S(2)}, u32[]{:S(2)}) collective-permute-start(f32[4,2,8,768]{3,2,1,0:T(8,128)S(1)} %get-tuple-element.12), channel_id=1, source_target_pairs={{0,3},{1,2},{2,1},{3,0},{4,7},{5,6},{6,5},{7,4},{8,11},{9,10},{10,... | collective-permute-start | bytes 589832 | tf_op jit(solution)/shard_map/ppermute | solution.py:170
  50.7 1.0 %collective-permute-done.9 = f32[4,2,8,768]{3,2,1,0:T(8,128)S(1)} collective-permute-done((f32[4,2,8,768]{3,2,1,0:T(8,128)S(1)}, f32[4,2,8,768]{3,2,1,0:T(8,128)S(1)}, u32[]{:S(2)}, u32[]{:S(2)}) %collective-permute-start.9) | collective-permute-done | bytes 196640 | tf_op jit(solution)/shard_map/ppermute | solution.py:170
  51.7 2.8 %collective-permute-done.10 = f32[4,2,8,768]{3,2,1,0:T(8,128)S(1)} collective-permute-done((f32[4,2,8,768]{3,2,1,0:T(8,128)S(1)}, f32[4,2,8,768]{3,2,1,0:T(8,128)S(1)}, u32[]{:S(2)}, u32[]{:S(2)}) %collective-permute-start.10) | collective-permute-done | bytes 196640 | tf_op jit(solution)/shard_map/ppermute | solution.py:170
  54.5 2.0 %collective-permute-done.11 = f32[4,2,8,768]{3,2,1,0:T(8,128)S(1)} collective-permute-done((f32[4,2,8,768]{3,2,1,0:T(8,128)S(1)}, f32[4,2,8,768]{3,2,1,0:T(8,128)S(1)}, u32[]{:S(2)}, u32[]{:S(2)}) %collective-permute-start.11) | collective-permute-done | bytes 196640 | tf_op jit(solution)/shard_map/ppermute | solution.py:170
  56.7 1.1 %collective-permute-start.14 = (f32[2,8,768]{2,1,0:T(8,128)S(1)}, f32[2,8,768]{2,1,0:T(8,128)S(1)}, u32[]{:S(2)}, u32[]{:S(2)}) collective-permute-start(f32[2,8,768]{2,1,0:T(8,128)S(1)} %get-tuple-element.14), channel_id=1, source_target_pairs={{0,12},{1,13},{2,14},{3,15},{4,8},{5,9},{6,10},{7,11},{8,4},{9,5},... | collective-permute-start | bytes 147464 | tf_op jit(solution)/shard_map/ppermute | solution.py:172
  57.8 2.8 %collective-permute-start.13 = (f32[2,8,768]{2,1,0:T(8,128)S(1)}, f32[2,8,768]{2,1,0:T(8,128)S(1)}, u32[]{:S(2)}, u32[]{:S(2)}) collective-permute-start(f32[2,8,768]{2,1,0:T(8,128)S(1)} %get-tuple-element.15), channel_id=1, source_target_pairs={{0,8},{1,9},{2,10},{3,11},{4,12},{5,13},{6,14},{7,15},{8,0},{9,1},... | collective-permute-start | bytes 147464 | tf_op jit(solution)/shard_map/ppermute | solution.py:172
  60.7 1.3 %collective-permute-done.14 = f32[2,8,768]{2,1,0:T(8,128)S(1)} collective-permute-done((f32[2,8,768]{2,1,0:T(8,128)S(1)}, f32[2,8,768]{2,1,0:T(8,128)S(1)}, u32[]{:S(2)}, u32[]{:S(2)}) %collective-permute-start.14) | collective-permute-done | bytes 49184 | tf_op jit(solution)/shard_map/ppermute | solution.py:172
  62.0 1.4 %collective-permute-done.13 = f32[2,8,768]{2,1,0:T(8,128)S(1)} collective-permute-done((f32[2,8,768]{2,1,0:T(8,128)S(1)}, f32[2,8,768]{2,1,0:T(8,128)S(1)}, u32[]{:S(2)}, u32[]{:S(2)}) %collective-permute-start.13) | collective-permute-done | bytes 49184 | tf_op jit(solution)/shard_map/ppermute | solution.py:172
  (38 shorter events, 2.9 us)
Async XLA Ops:
  0.0 33.0 %copy-start = (bf16[16,2,128,128]{3,2,1,0:T(8,128)(2,1)S(1)}, bf16[16,2,128,128]{3,2,1,0:T(8,128)(2,1)}, u32[]{:S(2)}) copy-start(bf16[16,2,128,128]{3,2,1,0:T(8,128)(2,1)} %a.1) | copy-start | bytes 3145732
  0.0 6.0 %collective-permute-start = (bf16[2,128,128]{2,1,0:T(8,128)(2,1)}, bf16[2,128,128]{2,1,0:T(8,128)(2,1)S(1)}, u32[]{:S(2)}, u32[]{:S(2)}) collective-permute-start(bf16[2,128,128]{2,1,0:T(8,128)(2,1)} %bitcast.21), channel_id=1, source_target_pairs={{0,8},{1,9},{2,10},{3,11},{4,12},{5,13},{6,14},{7,15},{8,0},{9,1},... | collective-permute-start | bytes 196616 | tf_op jit(solution)/shard_map/ppermute | solution.py:123
  3.2 0.9 %copy-start.1 = (bf16[1,2,128,128]{3,2,1,0:T(8,128)(2,1)S(1)}, bf16[1,2,128,128]{3,2,1,0:T(8,128)(2,1)}, u32[]{:S(2)}) copy-start(bf16[1,2,128,128]{3,2,1,0:T(8,128)(2,1)} %param.7) | copy-start | bytes 196612
  4.1 29.0 %copy-start.2 = (s32[256,2]{0,1:T(2,128)S(1)}, s32[256,2]{0,1:T(2,128)}, u32[]{:S(2)}) copy-start(s32[256,2]{0,1:T(2,128)} %param.8) | copy-start | bytes 6148
  4.1 29.0 %copy-start.3 = (s32[32]{0:T(128)S(1)}, s32[32]{0:T(128)}, u32[]{:S(2)}) copy-start(s32[32]{0:T(128)} %agglo.3) | copy-start | bytes 388
  6.0 5.1 %collective-permute-start.1 = (bf16[4,128,128]{2,1,0:T(8,128)(2,1)S(1)}, bf16[4,128,128]{2,1,0:T(8,128)(2,1)S(1)}, u32[]{:S(2)}, u32[]{:S(2)}) collective-permute-start(bf16[4,128,128]{2,1,0:T(8,128)(2,1)S(1)} %pad_maximum_fusion.2), channel_id=1, source_target_pairs={{0,1},{1,0},{2,3},{3,2},{4,5},{5,4},{6,7},{7,6},{8,9},{9,8},{10,11... | collective-permute-start | bytes 393224 | tf_op jit(solution)/shard_map/ppermute | solution.py:133
  7.6 8.7 %collective-permute-start.3 = (bf16[4,128,128]{2,1,0:T(8,128)(2,1)S(1)}, bf16[4,128,128]{2,1,0:T(8,128)(2,1)S(1)}, u32[]{:S(2)}, u32[]{:S(2)}) collective-permute-start(bf16[4,128,128]{2,1,0:T(8,128)(2,1)S(1)} %pad_maximum_fusion.2), channel_id=1, source_target_pairs={{0,3},{1,2},{2,1},{3,0},{4,7},{5,6},{6,5},{7,4},{8,11},{9,10},{10,... | collective-permute-start | bytes 393224 | tf_op jit(solution)/shard_map/ppermute | solution.py:133
  9.8 6.5 %collective-permute-start.2 = (bf16[4,128,128]{2,1,0:T(8,128)(2,1)S(1)}, bf16[4,128,128]{2,1,0:T(8,128)(2,1)S(1)}, u32[]{:S(2)}, u32[]{:S(2)}) collective-permute-start(bf16[4,128,128]{2,1,0:T(8,128)(2,1)S(1)} %pad_maximum_fusion.2), channel_id=1, source_target_pairs={{0,2},{1,3},{2,0},{3,1},{4,6},{5,7},{6,4},{7,5},{8,10},{9,11},{10,... | collective-permute-start | bytes 393224 | tf_op jit(solution)/shard_map/ppermute | solution.py:133
  16.5 9.5 %collective-permute-start.5 = (bf16[8,128,128]{2,1,0:T(8,128)(2,1)S(1)}, bf16[8,128,128]{2,1,0:T(8,128)(2,1)S(1)}, u32[]{:S(2)}, u32[]{:S(2)}) collective-permute-start(bf16[8,128,128]{2,1,0:T(8,128)(2,1)S(1)} %pad_maximum_fusion.1), channel_id=1, source_target_pairs={{0,12},{1,13},{2,14},{3,15},{4,8},{5,9},{6,10},{7,11},{8,4},{9,5},... | collective-permute-start | bytes 786440 | tf_op jit(solution)/shard_map/ppermute | solution.py:139
  19.6 6.4 %collective-permute-start.4 = (bf16[8,128,128]{2,1,0:T(8,128)(2,1)S(1)}, bf16[8,128,128]{2,1,0:T(8,128)(2,1)S(1)}, u32[]{:S(2)}, u32[]{:S(2)}) collective-permute-start(bf16[8,128,128]{2,1,0:T(8,128)(2,1)S(1)} %pad_maximum_fusion.1), channel_id=1, source_target_pairs={{0,4},{1,5},{2,6},{3,7},{4,0},{5,1},{6,2},{7,3},{8,12},{9,13},{10,... | collective-permute-start | bytes 786440 | tf_op jit(solution)/shard_map/ppermute | solution.py:138
  19.9 23.6 %copy-start.4 = (s32[16,2]{0,1:T(2,128)S(1)}, s32[16,2]{0,1:T(2,128)}, u32[]{:S(2)}) copy-start(s32[16,2]{0,1:T(2,128)} %param.6) | copy-start | bytes 388
  26.1 17.4 %collective-permute-start.8 = (bf16[32,128,128]{2,1,0:T(8,128)(2,1)S(1)}, bf16[32,128,128]{2,1,0:T(8,128)(2,1)S(1)}, u32[]{:S(2)}, u32[]{:S(2)}) collective-permute-start(bf16[32,128,128]{2,1,0:T(8,128)(2,1)S(1)} %constant_dynamic-update-slice_fusion.plane.own), channel_id=1, source_target_pairs={{0,16},{16,0},{32,48},{48,32},{64,80},{80,64},{96,112},{112,96},{1... | collective-permute-start | bytes 3145736 | tf_op jit(solution)/shard_map/ppermute | solution.py:142
  26.2 11.7 %collective-permute-start.6 = (bf16[16,128,128]{2,1,0:T(8,128)(2,1)S(1)}, bf16[16,128,128]{2,1,0:T(8,128)(2,1)S(1)}, u32[]{:S(2)}, u32[]{:S(2)}) collective-permute-start(bf16[16,128,128]{2,1,0:T(8,128)(2,1)S(1)} %get-tuple-element.16), channel_id=1, source_target_pairs={{16,32},{32,16},{48,64},{64,48},{80,96},{96,80},{112,128},{128,112... | collective-permute-start | bytes 1572872 | tf_op jit(solution)/shard_map/ppermute | solution.py:137
  28.3 15.3 %collective-permute-start.7 = (bf16[16,128,128]{2,1,0:T(8,128)(2,1)S(1)}, bf16[16,128,128]{2,1,0:T(8,128)(2,1)S(1)}, u32[]{:S(2)}, u32[]{:S(2)}) collective-permute-start(bf16[16,128,128]{2,1,0:T(8,128)(2,1)S(1)} %pad_maximum_fusion), channel_id=1, source_target_pairs={{16,32},{32,16},{48,64},{64,48},{80,96},{96,80},{112,128},{128,112... | collective-permute-start | bytes 1572872 | tf_op jit(solution)/shard_map/ppermute | solution.py:140
  45.9 5.8 %collective-permute-start.9 = (f32[4,2,8,768]{3,2,1,0:T(8,128)S(1)}, f32[4,2,8,768]{3,2,1,0:T(8,128)S(1)}, u32[]{:S(2)}, u32[]{:S(2)}) collective-permute-start(f32[4,2,8,768]{3,2,1,0:T(8,128)S(1)} %get-tuple-element.10), channel_id=1, source_target_pairs={{0,1},{1,0},{2,3},{3,2},{4,5},{5,4},{6,7},{7,6},{8,9},{9,8},{10,11... | collective-permute-start | bytes 589832 | tf_op jit(solution)/shard_map/ppermute | solution.py:170
  46.7 7.8 %collective-permute-start.10 = (f32[4,2,8,768]{3,2,1,0:T(8,128)S(1)}, f32[4,2,8,768]{3,2,1,0:T(8,128)S(1)}, u32[]{:S(2)}, u32[]{:S(2)}) collective-permute-start(f32[4,2,8,768]{3,2,1,0:T(8,128)S(1)} %get-tuple-element.11), channel_id=1, source_target_pairs={{0,2},{1,3},{2,0},{3,1},{4,6},{5,7},{6,4},{7,5},{8,10},{9,11},{10,... | collective-permute-start | bytes 589832 | tf_op jit(solution)/shard_map/ppermute | solution.py:170
  48.6 7.9 %collective-permute-start.11 = (f32[4,2,8,768]{3,2,1,0:T(8,128)S(1)}, f32[4,2,8,768]{3,2,1,0:T(8,128)S(1)}, u32[]{:S(2)}, u32[]{:S(2)}) collective-permute-start(f32[4,2,8,768]{3,2,1,0:T(8,128)S(1)} %get-tuple-element.12), channel_id=1, source_target_pairs={{0,3},{1,2},{2,1},{3,0},{4,7},{5,6},{6,5},{7,4},{8,11},{9,10},{10,... | collective-permute-start | bytes 589832 | tf_op jit(solution)/shard_map/ppermute | solution.py:170
  56.5 4.2 %collective-permute-start.12 = (f32[2,8,768]{2,1,0:T(8,128)S(1)}, f32[2,8,768]{2,1,0:T(8,128)S(1)}, u32[]{:S(2)}, u32[]{:S(2)}) collective-permute-start(f32[2,8,768]{2,1,0:T(8,128)S(1)} %get-tuple-element.13), channel_id=1, source_target_pairs={{0,4},{1,5},{2,6},{3,7},{4,0},{5,1},{6,2},{7,3},{8,12},{9,13},{10,... | collective-permute-start | bytes 147464 | tf_op jit(solution)/shard_map/ppermute | solution.py:172
  56.7 5.3 %collective-permute-start.14 = (f32[2,8,768]{2,1,0:T(8,128)S(1)}, f32[2,8,768]{2,1,0:T(8,128)S(1)}, u32[]{:S(2)}, u32[]{:S(2)}) collective-permute-start(f32[2,8,768]{2,1,0:T(8,128)S(1)} %get-tuple-element.14), channel_id=1, source_target_pairs={{0,12},{1,13},{2,14},{3,15},{4,8},{5,9},{6,10},{7,11},{8,4},{9,5},... | collective-permute-start | bytes 147464 | tf_op jit(solution)/shard_map/ppermute | solution.py:172
  57.8 5.6 %collective-permute-start.13 = (f32[2,8,768]{2,1,0:T(8,128)S(1)}, f32[2,8,768]{2,1,0:T(8,128)S(1)}, u32[]{:S(2)}, u32[]{:S(2)}) collective-permute-start(f32[2,8,768]{2,1,0:T(8,128)S(1)} %get-tuple-element.15), channel_id=1, source_target_pairs={{0,8},{1,9},{2,10},{3,11},{4,12},{5,13},{6,14},{7,15},{8,0},{9,1},... | collective-permute-start | bytes 147464 | tf_op jit(solution)/shard_map/ppermute | solution.py:172

commit v7 on v5

--- a/solution.py
+++ b/solution.py
@@ -72,29 +72,8 @@
             split[i * 2 + s, :, B:] = low[:, s * B : (s + 1) * B]
 
 
-def band_kernel(
-    cols, aggs, agglo, split, plane, near, f, b, far, pair, o0, o1, o2, o3, blocks, acc
-):
-    row, cross, y, x = place()
-    blocks[0:32] = plane[...]
-    blocks[32:40] = near[...]
-    blocks[40:48] = f[8:16]
-    blocks[48:56] = far[...]
-    blocks[56:64] = b[8:16]
-    blocks[64:96] = pair[...]
-    acc[...] = jnp.zeros_like(acc)
-    pair_band = 2 - 2 * (row % 2)
-    for i in range(ROWS):
-        for s in range(2):
-            j = cols[s, i]
-            swap = agglo[aggs[0, j]] & 1
-            band = j // ROWS - row + 1
-            base = jnp.where(band == 1, 0, jnp.where(band == pair_band, 64, 32))
-            spot = base + slot_of(y, x, j, jnp.where(band == pair_band, 1 - cross, cross)) * 2
-            right = jnp.concatenate([blocks[spot + swap], blocks[spot + 1 - swap]], axis=1)
-            right = jnp.concatenate([right, right], axis=0)
-            acc[band] += jnp.dot(split[i * 2 + s], right, preferred_element_type=jnp.float32)
-    for rel, out in enumerate((o0, o1, o2, o3)):
+def scatter_rows(cross, y, x, acc, outs, bands):
+    for rel, out in enumerate(outs):
         for m in range(SIDE):
             d = jnp.where(
                 cross == 0,
@@ -103,8 +82,51 @@
             )
             for k in range(2):
                 start = pl.multiple_of(k * B + d * 8, 8)
-                for t in range(3):
+                for t in range(bands):
                     out[m, k, :, t * 256 : (t + 1) * 256] = acc[t, pl.ds(start, 8), :]
+
+
+def add_products(cols, aggs, agglo, split, blocks, acc, target):
+    acc[...] = jnp.zeros_like(acc)
+    for i in range(ROWS):
+        for s in range(2):
+            j = cols[s, i]
+            swap = agglo[aggs[0, j]] & 1
+            t, spot = target(j)
+            right = jnp.concatenate([blocks[spot + swap], blocks[spot + 1 - swap]], axis=1)
+            right = jnp.concatenate([right, right], axis=0)
+            acc[t] += jnp.dot(split[i * 2 + s], right, preferred_element_type=jnp.float32)
+
+
+def home_kernel(cols, aggs, agglo, split, own, pair, o0, o1, o2, o3, blocks, acc):
+    row, cross, y, x = place()
+    blocks[0:32] = own[...]
+    blocks[32:64] = pair[...]
+    pair_band = 2 - 2 * (row % 2)
+
+    def target(j):
+        band = j // ROWS - row + 1
+        of_pair = band == pair_band
+        spot = slot_of(y, x, j, jnp.where(of_pair, 1 - cross, cross)) * 2
+        t = jnp.where(band == 1, 0, jnp.where(of_pair, 1, 2))
+        return t, jnp.where(of_pair, 32, 0) + spot
+
+    add_products(cols, aggs, agglo, split, blocks, acc, target)
+    scatter_rows(cross, y, x, acc, (o0, o1, o2, o3), 2)
+
+
+def beside_kernel(cols, aggs, agglo, split, near, near_rest, o0, o1, o2, o3, blocks, acc):
+    row, cross, y, x = place()
+    blocks[0:8] = near[...]
+    blocks[8:32] = near_rest[...]
+    band_beside = 2 * (row % 2)
+
+    def target(j):
+        t = jnp.where(j // ROWS - row + 1 == band_beside, 0, 1)
+        return t, slot_of(y, x, j, cross) * 2
+
+    add_products(cols, aggs, agglo, split, blocks, acc, target)
+    scatter_rows(cross, y, x, acc, (o0, o1, o2, o3), 1)
 
 
 def vmem():
@@ -131,42 +153,56 @@
         name="fetch",
     )(shard)
     line = jnp.concatenate([shard_near, line_1, line_2, line_3])
-    plane_2 = lax.ppermute(line, BOTH, second(2))
     near = lax.ppermute(line, "row", row_pairs(1))
-    plane_2, near = lax.optimization_barrier((plane_2, near))
-    lines = jnp.concatenate([line, near])
-    plane_1 = lax.ppermute(lines, BOTH, second(1))
-    plane_3 = lax.ppermute(lines, BOTH, second(3))
-    far = lax.ppermute(plane_2, "row", row_pairs(1))
-    plane_1, plane_3, far = lax.optimization_barrier((plane_1, plane_3, far))
-    plane = jnp.concatenate([line, plane_1[:8], plane_2, plane_3[:8]])
-    pair = lax.ppermute(plane, "row", row_pairs(0))
+    own_1, own_3, own_2 = (lax.ppermute(line, BOTH, second(k)) for k in (1, 3, 2))
+    near, own_1, own_2, own_3 = lax.optimization_barrier((near, own_1, own_2, own_3))
+    near_rest = lax.ppermute(jnp.concatenate([own_1, own_2, own_3]), "row", row_pairs(1))
+    own = jnp.concatenate([line, own_1, own_2, own_3])
+    pair = lax.ppermute(own, "row", row_pairs(0))
 
     cols, aggs = a_cols.T, p_aggs.T
+    cost = pl.CostEstimate(flops=10**6, bytes_accessed=2**12, transcendentals=0)
     split = pl.pallas_call(
         lift_kernel,
         out_shape=jax.ShapeDtypeStruct((2 * ROWS, 256, 256), jnp.bfloat16),
         in_specs=[smem(), smem(), vmem(), vmem()],
         out_specs=vmem(),
         compiler_params=params(16),
+        cost_estimate=cost,
         name="lift",
-    )(aggs, agglo, a_blocks, plane)
-    piece = jax.ShapeDtypeStruct((SIDE, 2, 8, 768), jnp.float32)
-    o0, o1, o2, o3 = pl.pallas_call(
-        band_kernel,
-        out_shape=[piece] * 4,
-        in_specs=[smem()] * 3 + [vmem()] * 7,
-        out_specs=[vmem()] * 4,
-        scratch_shapes=[
-            pltpu.VMEM((96, B, B), jnp.bfloat16),
-            pltpu.VMEM((3, 256, 256), jnp.float32),
-        ],
-        compiler_params=params(24),
-        name="bands",
-    )(cols, aggs, agglo, split, plane, near, plane_1, plane_3, far, pair)
-
-    p1, p3, p2 = (lax.ppermute(o, BOTH, first(k)) for o, k in ((o1, 1), (o3, 3), (o2, 2)))
-    sums = [o0[m] + p1[m] + p2[m] + p3[m] for m in range(SIDE)]
+    )(aggs, agglo, a_blocks, own)
+
+    def partial_sums(kernel, name, width, slots, bands, *planes):
+        return pl.pallas_call(
+            kernel,
+            out_shape=[jax.ShapeDtypeStruct((SIDE, 2, 8, width), jnp.float32)] * SIDE,
+            in_specs=[smem()] * 3 + [vmem()] * 3,
+            out_specs=[vmem()] * SIDE,
+            scratch_shapes=[
+                pltpu.VMEM((slots, B, B), jnp.bfloat16),
+                pltpu.VMEM((bands, 256, 256), jnp.float32),
+            ],
+            compiler_params=params(16),
+            cost_estimate=cost,
+            name=name,
+        )(cols, aggs, agglo, split, *planes)
+
+    def reduced(o0, o1, o2, o3):
+        p1, p3, p2 = (lax.ppermute(o, BOTH, first(k)) for o, k in ((o1, 1), (o3, 3), (o2, 2)))
+        return o0, p1, p2, p3
+
+    home = reduced(*partial_sums(home_kernel, "home", 512, 64, 3, own, pair))
+    *home, near_rest = lax.optimization_barrier((*home, near_rest))
+    beside = reduced(*partial_sums(beside_kernel, "beside", 256, 32, 2, near, near_rest))
+    even = (lax.axis_index("row") & 1) == 0
+
+    def ordered(m):
+        mine, side = (sum(p[m] for p in parts) for parts in (home, beside))
+        centre, partner = mine[..., :256], mine[..., 256:]
+        low, high = jnp.where(even, side, partner), jnp.where(even, partner, side)
+        return jnp.concatenate([low, centre, high], axis=-1)
+
+    sums = [ordered(m) for m in range(SIDE)]
     q1, q3, q2 = (lax.ppermute(sums[k], BOTH, second(k)) for k in (1, 3, 2))
     return (sums[0] + q1 + q2 + q3).reshape(2, 8, 6, B)
 

time: 58.3 us -> 68.8 us (1.18)
  starting transfers between devices: 24.7 us -> 29.8 us
  Pallas kernels: 3.95 us -> 8.69 us
  local copies, waits for them, and re-layouts: 2.46 us -> 5.19 us
  waiting for transfers between devices: 26.1 us -> 23.8 us
    pallas_call x1 -> x2, Pallas kernels: 2.43 us -> 7.17 us  [partial_sums(): pl.pallas_call(kernel, out_shape=[jax.ShapeDtypeStruct((SIDE, 2, 8, width...]
    ppermute x8 -> x11, starting transfers between devices: 14.6 us -> 18.2 us  [the longest x6 9.48 us: reduced(): lax.ppermute(o, BOTH, first(k))]
    unnamed x18 -> x20, local copies, waits for them, and re-layouts: 2.39 us -> 5.16 us
    ppermute x1, waiting for transfers between devices: 2.55 us -> 0.92 us  [local(): near = lax.ppermute(line, 'row', row_pairs(1))]
    ppermute x3, waiting for transfers between devices: 4.09 us -> 2.54 us  [local(): q1, q3, q2 = (lax.ppermute(sums[k], BOTH, second(k)) for k in (1, 3, 2))]
    ppermute x3, starting transfers between devices: 4.18 us -> 4.93 us  [local(): q1, q3, q2 = (lax.ppermute(sums[k], BOTH, second(k)) for k in (1, 3, 2))]
    ppermute x8 -> x11, waiting for transfers between devices: 15.5 us -> 15.8 us  [the longest x3 8.51 us: local(): lax.ppermute(line, BOTH, second(k))]
  transfers between devices with their start and end apart: 15 -> 18, of which waited for: 11 -> 12; matrix products, arithmetic and copies ran while one was open for 0% -> 0% of each run, Pallas kernels for 3% -> 8%
where the time goes in v7:
time: 68.8 us; the launch traced here: 68.6 us
  starting transfers between devices  29.8 us (43%)
  waiting for transfers between devices  23.8 us (35%)
  Pallas kernels  8.69 us (13%)
  local copies, waits for them, and re-layouts  5.19 us (8%)
  other arithmetic  0.86 us (1%)
    ppermute x6, starting transfers between devices, reduced(): lax.ppermute(o, BOTH, first(k))  9.48 us
    ppermute x3, waiting for transfers between devices, local(): lax.ppermute(line, BOTH, second(k))  8.51 us
    ppermute x6, waiting for transfers between devices, reduced(): lax.ppermute(o, BOTH, first(k))  7.3 us
    pallas_call x2, Pallas kernels, partial_sums(): pl.pallas_call(kernel, out_shape=[jax.ShapeDtypeStruct((SIDE, 2, 8, width...  7.17 us
    unnamed x20, local copies, waits for them, and re-layouts  5.16 us
    ppermute x3, starting transfers between devices, local(): q1, q3, q2 = (lax.ppermute(sums[k], BOTH, second(k)) for k in (1, 3, 2))  4.93 us
    ppermute x3, starting transfers between devices, local(): lax.ppermute(line, BOTH, second(k))  4.78 us
    ppermute x3, starting transfers between devices, local(): lax.ppermute(shard, BOTH, first(k))  4.7 us
  transfers between devices with their start and end apart: 18, of which 12 were waited for; matrix products, arithmetic and copies ran while one was open for 0% of the time, Pallas kernels for 8%

profile of v7, /device:TPU:96, one launch (start us, length us, event | category | flops | bytes accessed | tf_op | source)
XLA Modules:
  0.0 68.6 jit_solution(5503584999774852177)
XLA Ops:
  0.0 1.6 %collective-permute-start = (bf16[2,128,128]{2,1,0:T(8,128)(2,1)}, bf16[2,128,128]{2,1,0:T(8,128)(2,1)S(1)}, u32[]{:S(2)}, u32[]{:S(2)}) collective-permute-start(bf16[2,128,128]{2,1,0:T(8,128)(2,1)} %bitcast.25), channel_id=1, source_target_pairs={{0,1},{1,0},{2,3},{3,2},{4,5},{5,4},{6,7},{7,6},{8,9},{9,8},{10,11... | collective-permute-start | bytes 196616 | tf_op jit(solution)/shard_map/ppermute | solution.py:146
  1.6 2.9 %collective-permute-start.1 = (bf16[2,128,128]{2,1,0:T(8,128)(2,1)}, bf16[2,128,128]{2,1,0:T(8,128)(2,1)S(1)}, u32[]{:S(2)}, u32[]{:S(2)}) collective-permute-start(bf16[2,128,128]{2,1,0:T(8,128)(2,1)} %bitcast.26), channel_id=1, source_target_pairs={{0,2},{1,3},{2,0},{3,1},{4,6},{5,7},{6,4},{7,5},{8,10},{9,11},{10,... | collective-permute-start | bytes 196616 | tf_op jit(solution)/shard_map/ppermute | solution.py:146
  5.6 2.0 %collective-permute-done.1 = bf16[2,128,128]{2,1,0:T(8,128)(2,1)S(1)} collective-permute-done((bf16[2,128,128]{2,1,0:T(8,128)(2,1)}, bf16[2,128,128]{2,1,0:T(8,128)(2,1)S(1)}, u32[]{:S(2)}, u32[]{:S(2)}) %collective-permute-start.1) | collective-permute-done | bytes 65568 | tf_op jit(solution)/shard_map/ppermute | solution.py:146
  7.6 2.5 %collective-permute-done.2 = bf16[2,128,128]{2,1,0:T(8,128)(2,1)S(1)} collective-permute-done((bf16[2,128,128]{2,1,0:T(8,128)(2,1)}, bf16[2,128,128]{2,1,0:T(8,128)(2,1)S(1)}, u32[]{:S(2)}, u32[]{:S(2)}) %collective-permute-start.2) | collective-permute-done | bytes 65568 | tf_op jit(solution)/shard_map/ppermute | solution.py:146
  10.2 1.9 %collective-permute-start.3 = (bf16[8,128,128]{2,1,0:T(8,128)(2,1)S(1)}, bf16[8,128,128]{2,1,0:T(8,128)(2,1)S(1)}, u32[]{:S(2)}, u32[]{:S(2)}) collective-permute-start(bf16[8,128,128]{2,1,0:T(8,128)(2,1)S(1)} %pad_maximum_fusion.1), channel_id=1, source_target_pairs={{16,32},{32,16},{48,64},{64,48},{80,96},{96,80},{112,128},{128,112... | collective-permute-start | bytes 786440 | tf_op jit(solution)/shard_map/ppermute | solution.py:156
  12.1 1.6 %collective-permute-start.4 = (bf16[8,128,128]{2,1,0:T(8,128)(2,1)S(1)}, bf16[8,128,128]{2,1,0:T(8,128)(2,1)S(1)}, u32[]{:S(2)}, u32[]{:S(2)}) collective-permute-start(bf16[8,128,128]{2,1,0:T(8,128)(2,1)S(1)} %pad_maximum_fusion.1), channel_id=1, source_target_pairs={{0,4},{1,5},{2,6},{3,7},{4,0},{5,1},{6,2},{7,3},{8,12},{9,13},{10,... | collective-permute-start | bytes 786440 | tf_op jit(solution)/shard_map/ppermute | solution.py:157
  13.7 2.7 %collective-permute-start.5 = (bf16[8,128,128]{2,1,0:T(8,128)(2,1)S(1)}, bf16[8,128,128]{2,1,0:T(8,128)(2,1)S(1)}, u32[]{:S(2)}, u32[]{:S(2)}) collective-permute-start(bf16[8,128,128]{2,1,0:T(8,128)(2,1)S(1)} %pad_maximum_fusion.1), channel_id=1, source_target_pairs={{0,8},{1,9},{2,10},{3,11},{4,12},{5,13},{6,14},{7,15},{8,0},{9,1},... | collective-permute-start | bytes 786440 | tf_op jit(solution)/shard_map/ppermute | solution.py:157
  18.6 5.1 %collective-permute-done.5 = bf16[8,128,128]{2,1,0:T(8,128)(2,1)S(1)} collective-permute-done((bf16[8,128,128]{2,1,0:T(8,128)(2,1)S(1)}, bf16[8,128,128]{2,1,0:T(8,128)(2,1)S(1)}, u32[]{:S(2)}, u32[]{:S(2)}) %collective-permute-start.5) | collective-permute-done | bytes 262176 | tf_op jit(solution)/shard_map/ppermute | solution.py:157
  23.7 2.7 %collective-permute-done.6 = bf16[8,128,128]{2,1,0:T(8,128)(2,1)S(1)} collective-permute-done((bf16[8,128,128]{2,1,0:T(8,128)(2,1)S(1)}, bf16[8,128,128]{2,1,0:T(8,128)(2,1)S(1)}, u32[]{:S(2)}, u32[]{:S(2)}) %collective-permute-start.6) | collective-permute-done | bytes 262176 | tf_op jit(solution)/shard_map/ppermute | solution.py:157
  26.5 2.0 %collective-permute-start.7 = (bf16[32,128,128]{2,1,0:T(8,128)(2,1)S(1)}, bf16[32,128,128]{2,1,0:T(8,128)(2,1)S(1)}, u32[]{:S(2)}, u32[]{:S(2)}) collective-permute-start(bf16[32,128,128]{2,1,0:T(8,128)(2,1)S(1)} %constant_dynamic-update-slice_fusion.plane.own), channel_id=1, source_target_pairs={{0,16},{16,0},{32,48},{48,32},{64,80},{80,64},{96,112},{112,96},{1... | collective-permute-start | bytes 3145736 | tf_op jit(solution)/shard_map/ppermute | solution.py:161
  28.7 1.9 %collective-permute-start.11 = (bf16[24,128,128]{2,1,0:T(8,128)(2,1)S(1)}, bf16[24,128,128]{2,1,0:T(8,128)(2,1)S(1)}, u32[]{:S(2)}, u32[]{:S(2)}) collective-permute-start(bf16[24,128,128]{2,1,0:T(8,128)(2,1)S(1)} %pad_maximum_fusion), channel_id=1, source_target_pairs={{16,32},{32,16},{48,64},{64,48},{80,96},{96,80},{112,128},{128,112... | collective-permute-start | bytes 2359304 | tf_op jit(solution)/shard_map/ppermute | solution.py:159
  30.6 1.5 %lift.1.split = bf16[32,256,256]{2,1,0:T(8,128)(2,1)S(1)} custom-call(s32[2,256]{1,0:T(2,128)S(1)} %bitcast.29, s32[32]{0:T(128)S(1)} %copy-done.5, bf16[16,2,128,128]{3,2,1,0:T(8,128)(2,1)S(1)} %copy-done.2, bf16[32,128,128]{2,1,0:T(8,128)(2,1)S(1)} %constant_dynamic-update-slice_fusion.plane.own), custom_call_target="tpu_custom_call" | custom-call | flops 1000000 | bytes 4096 | tf_op jit(solution)/shard_map/lift/pallas_call | solution.py:165
  32.2 3.9 %home.1 = (f32[4,2,8,512]{3,2,1,0:T(8,128)S(1)}, f32[4,2,8,512]{3,2,1,0:T(8,128)S(1)}, f32[4,2,8,512]{3,2,1,0:T(8,128)S(1)}, f32[4,2,8,512]{3,2,1,0:T(8,128)S(1)}) custom-call(s32[2,16]{1,0:T(2,128)S(1)} %bitcast.32, s32[2,256]{1,0:T(2,128)S(1)} %bitcast.30, s32[32]{0:T(128)S(1)} %copy-done.5, bf16[32,256,256]{2,1,0:T(8,128)(2,1)S(1)} %lift.1.split, ...), custom_call_target="tpu_custom_call" | custom-call | flops 1000000 | bytes 4096 | tf_op jit(solution)/shard_map/home/pallas_call | solution.py:176
  36.1 2.0 %copy-done = bf16[32,256,256]{2,1,0:T(8,128)(2,1)} copy-done((bf16[32,256,256]{2,1,0:T(8,128)(2,1)}, bf16[32,256,256]{2,1,0:T(8,128)(2,1)S(1)}, u32[]{:S(2)}) %copy-start) | copy-done | bytes 4194328
  38.3 4.4 %collective-permute-start.9 = (f32[4,2,8,512]{3,2,1,0:T(8,128)S(1)}, f32[4,2,8,512]{3,2,1,0:T(8,128)S(1)}, u32[]{:S(2)}, u32[]{:S(2)}) collective-permute-start(f32[4,2,8,512]{3,2,1,0:T(8,128)S(1)} %get-tuple-element.28), channel_id=1, source_target_pairs={{0,2},{1,3},{2,0},{3,1},{4,6},{5,7},{6,4},{7,5},{8,10},{9,11},{10,... | collective-permute-start | bytes 393224 | tf_op jit(solution)/shard_map/ppermute | solution.py:191
  44.2 2.9 %collective-permute-done.9 = f32[4,2,8,512]{3,2,1,0:T(8,128)S(1)} collective-permute-done((f32[4,2,8,512]{3,2,1,0:T(8,128)S(1)}, f32[4,2,8,512]{3,2,1,0:T(8,128)S(1)}, u32[]{:S(2)}, u32[]{:S(2)}) %collective-permute-start.9) | collective-permute-done | bytes 131104 | tf_op jit(solution)/shard_map/ppermute | solution.py:191
  47.1 2.2 %copy-done.1 = bf16[32,256,256]{2,1,0:T(8,128)(2,1)S(1)} copy-done((bf16[32,256,256]{2,1,0:T(8,128)(2,1)S(1)}, bf16[32,256,256]{2,1,0:T(8,128)(2,1)}, u32[]{:S(2)}) %copy-start.1) | copy-done | bytes 4194328
  49.3 3.3 %beside.1 = (f32[4,2,8,256]{3,2,1,0:T(8,128)S(1)}, f32[4,2,8,256]{3,2,1,0:T(8,128)S(1)}, f32[4,2,8,256]{3,2,1,0:T(8,128)S(1)}, f32[4,2,8,256]{3,2,1,0:T(8,128)S(1)}) custom-call(s32[2,16]{1,0:T(2,128)S(1)} %bitcast.33, s32[2,256]{1,0:T(2,128)S(1)} %bitcast.31, s32[32]{0:T(128)S(1)} %copy-done.5, bf16[32,256,256]{2,1,0:T(8,128)(2,1)S(1)} %copy-done.1, ...), custom_call_target="tpu_custom_call" | custom-call | flops 1000000 | bytes 4096 | tf_op jit(solution)/shard_map/beside/pallas_call | solution.py:176
  52.7 2.2 %collective-permute-start.13 = (f32[4,2,8,256]{3,2,1,0:T(8,128)S(1)}, f32[4,2,8,256]{3,2,1,0:T(8,128)S(1)}, u32[]{:S(2)}, u32[]{:S(2)}) collective-permute-start(f32[4,2,8,256]{3,2,1,0:T(8,128)S(1)} %get-tuple-element.33), channel_id=1, source_target_pairs={{0,2},{1,3},{2,0},{3,1},{4,6},{5,7},{6,4},{7,5},{8,10},{9,11},{10,... | collective-permute-start | bytes 196616 | tf_op jit(solution)/shard_map/ppermute | solution.py:191
  54.9 2.5 %collective-permute-start.14 = (f32[4,2,8,256]{3,2,1,0:T(8,128)S(1)}, f32[4,2,8,256]{3,2,1,0:T(8,128)S(1)}, u32[]{:S(2)}, u32[]{:S(2)}) collective-permute-start(f32[4,2,8,256]{3,2,1,0:T(8,128)S(1)} %get-tuple-element.34), channel_id=1, source_target_pairs={{0,3},{1,2},{2,1},{3,0},{4,7},{5,6},{6,5},{7,4},{8,11},{9,10},{10,... | collective-permute-start | bytes 196616 | tf_op jit(solution)/shard_map/ppermute | solution.py:191
  58.5 1.8 %collective-permute-done.14 = f32[4,2,8,256]{3,2,1,0:T(8,128)S(1)} collective-permute-done((f32[4,2,8,256]{3,2,1,0:T(8,128)S(1)}, f32[4,2,8,256]{3,2,1,0:T(8,128)S(1)}, u32[]{:S(2)}, u32[]{:S(2)}) %collective-permute-start.14) | collective-permute-done | bytes 65568 | tf_op jit(solution)/shard_map/ppermute | solution.py:191
  60.5 2.0 %collective-permute-start.16 = (f32[2,8,768]{2,1,0:T(8,128)S(1)}, f32[2,8,768]{2,1,0:T(8,128)S(1)}, u32[]{:S(2)}, u32[]{:S(2)}) collective-permute-start(f32[2,8,768]{2,1,0:T(8,128)S(1)} %pad_maximum_fusion.3), channel_id=1, source_target_pairs={{0,8},{1,9},{2,10},{3,11},{4,12},{5,13},{6,14},{7,15},{8,0},{9,1},... | collective-permute-start | bytes 147464 | tf_op jit(solution)/shard_map/ppermute | solution.py:206
  62.6 2.8 %collective-permute-start.17 = (f32[2,8,768]{2,1,0:T(8,128)S(1)}, f32[2,8,768]{2,1,0:T(8,128)S(1)}, u32[]{:S(2)}, u32[]{:S(2)}) collective-permute-start(f32[2,8,768]{2,1,0:T(8,128)S(1)} %pad_maximum_fusion.4), channel_id=1, source_target_pairs={{0,12},{1,13},{2,14},{3,15},{4,8},{5,9},{6,10},{7,11},{8,4},{9,5},... | collective-permute-start | bytes 147464 | tf_op jit(solution)/shard_map/ppermute | solution.py:206
  66.2 1.7 %collective-permute-done.17 = f32[2,8,768]{2,1,0:T(8,128)S(1)} collective-permute-done((f32[2,8,768]{2,1,0:T(8,128)S(1)}, f32[2,8,768]{2,1,0:T(8,128)S(1)}, u32[]{:S(2)}, u32[]{:S(2)}) %collective-permute-start.17) | collective-permute-done | bytes 49184 | tf_op jit(solution)/shard_map/ppermute | solution.py:206
  (50 shorter events, 8.1 us)
Async XLA Ops:
  0.0 30.6 %copy-start.2 = (bf16[16,2,128,128]{3,2,1,0:T(8,128)(2,1)S(1)}, bf16[16,2,128,128]{3,2,1,0:T(8,128)(2,1)}, u32[]{:S(2)}) copy-start(bf16[16,2,128,128]{3,2,1,0:T(8,128)(2,1)} %a.1) | copy-start | bytes 3145732
  0.0 5.6 %collective-permute-start = (bf16[2,128,128]{2,1,0:T(8,128)(2,1)}, bf16[2,128,128]{2,1,0:T(8,128)(2,1)S(1)}, u32[]{:S(2)}, u32[]{:S(2)}) collective-permute-start(bf16[2,128,128]{2,1,0:T(8,128)(2,1)} %bitcast.25), channel_id=1, source_target_pairs={{0,1},{1,0},{2,3},{3,2},{4,5},{5,4},{6,7},{7,6},{8,9},{9,8},{10,11... | collective-permute-start | bytes 196616 | tf_op jit(solution)/shard_map/ppermute | solution.py:146
  1.6 6.1 %collective-permute-start.1 = (bf16[2,128,128]{2,1,0:T(8,128)(2,1)}, bf16[2,128,128]{2,1,0:T(8,128)(2,1)S(1)}, u32[]{:S(2)}, u32[]{:S(2)}) collective-permute-start(bf16[2,128,128]{2,1,0:T(8,128)(2,1)} %bitcast.26), channel_id=1, source_target_pairs={{0,2},{1,3},{2,0},{3,1},{4,6},{5,7},{6,4},{7,5},{8,10},{9,11},{10,... | collective-permute-start | bytes 196616 | tf_op jit(solution)/shard_map/ppermute | solution.py:146
  4.5 5.7 %collective-permute-start.2 = (bf16[2,128,128]{2,1,0:T(8,128)(2,1)}, bf16[2,128,128]{2,1,0:T(8,128)(2,1)S(1)}, u32[]{:S(2)}, u32[]{:S(2)}) collective-permute-start(bf16[2,128,128]{2,1,0:T(8,128)(2,1)} %bitcast.27), channel_id=1, source_target_pairs={{0,3},{1,2},{2,1},{3,0},{4,7},{5,6},{6,5},{7,4},{8,11},{9,10},{10,... | collective-permute-start | bytes 196616 | tf_op jit(solution)/shard_map/ppermute | solution.py:146
  5.6 25.0 %copy-start.4 = (s32[256,2]{0,1:T(2,128)S(1)}, s32[256,2]{0,1:T(2,128)}, u32[]{:S(2)}) copy-start(s32[256,2]{0,1:T(2,128)} %param.8) | copy-start | bytes 6148
  5.6 25.0 %copy-start.5 = (s32[32]{0:T(128)S(1)}, s32[32]{0:T(128)}, u32[]{:S(2)}) copy-start(s32[32]{0:T(128)} %agglo.5) | copy-start | bytes 388
  10.2 7.7 %collective-permute-start.3 = (bf16[8,128,128]{2,1,0:T(8,128)(2,1)S(1)}, bf16[8,128,128]{2,1,0:T(8,128)(2,1)S(1)}, u32[]{:S(2)}, u32[]{:S(2)}) collective-permute-start(bf16[8,128,128]{2,1,0:T(8,128)(2,1)S(1)} %pad_maximum_fusion.1), channel_id=1, source_target_pairs={{16,32},{32,16},{48,64},{64,48},{80,96},{96,80},{112,128},{128,112... | collective-permute-start | bytes 786440 | tf_op jit(solution)/shard_map/ppermute | solution.py:156
  12.1 6.5 %collective-permute-start.4 = (bf16[8,128,128]{2,1,0:T(8,128)(2,1)S(1)}, bf16[8,128,128]{2,1,0:T(8,128)(2,1)S(1)}, u32[]{:S(2)}, u32[]{:S(2)}) collective-permute-start(bf16[8,128,128]{2,1,0:T(8,128)(2,1)S(1)} %pad_maximum_fusion.1), channel_id=1, source_target_pairs={{0,4},{1,5},{2,6},{3,7},{4,0},{5,1},{6,2},{7,3},{8,12},{9,13},{10,... | collective-permute-start | bytes 786440 | tf_op jit(solution)/shard_map/ppermute | solution.py:157
  13.7 10.0 %collective-permute-start.5 = (bf16[8,128,128]{2,1,0:T(8,128)(2,1)S(1)}, bf16[8,128,128]{2,1,0:T(8,128)(2,1)S(1)}, u32[]{:S(2)}, u32[]{:S(2)}) collective-permute-start(bf16[8,128,128]{2,1,0:T(8,128)(2,1)S(1)} %pad_maximum_fusion.1), channel_id=1, source_target_pairs={{0,8},{1,9},{2,10},{3,11},{4,12},{5,13},{6,14},{7,15},{8,0},{9,1},... | collective-permute-start | bytes 786440 | tf_op jit(solution)/shard_map/ppermute | solution.py:157
  16.4 10.0 %collective-permute-start.6 = (bf16[8,128,128]{2,1,0:T(8,128)(2,1)S(1)}, bf16[8,128,128]{2,1,0:T(8,128)(2,1)S(1)}, u32[]{:S(2)}, u32[]{:S(2)}) collective-permute-start(bf16[8,128,128]{2,1,0:T(8,128)(2,1)S(1)} %pad_maximum_fusion.1), channel_id=1, source_target_pairs={{0,12},{1,13},{2,14},{3,15},{4,8},{5,9},{6,10},{7,11},{8,4},{9,5},... | collective-permute-start | bytes 786440 | tf_op jit(solution)/shard_map/ppermute | solution.py:157
  26.5 5.7 %copy-start.6 = (s32[16,2]{0,1:T(2,128)S(1)}, s32[16,2]{0,1:T(2,128)}, u32[]{:S(2)}) copy-start(s32[16,2]{0,1:T(2,128)} %param.6) | copy-start | bytes 388
  26.5 5.6 %collective-permute-start.7 = (bf16[32,128,128]{2,1,0:T(8,128)(2,1)S(1)}, bf16[32,128,128]{2,1,0:T(8,128)(2,1)S(1)}, u32[]{:S(2)}, u32[]{:S(2)}) collective-permute-start(bf16[32,128,128]{2,1,0:T(8,128)(2,1)S(1)} %constant_dynamic-update-slice_fusion.plane.own), channel_id=1, source_target_pairs={{0,16},{16,0},{32,48},{48,32},{64,80},{80,64},{96,112},{112,96},{1... | collective-permute-start | bytes 3145736 | tf_op jit(solution)/shard_map/ppermute | solution.py:161
  28.7 14.0 %collective-permute-start.11 = (bf16[24,128,128]{2,1,0:T(8,128)(2,1)S(1)}, bf16[24,128,128]{2,1,0:T(8,128)(2,1)S(1)}, u32[]{:S(2)}, u32[]{:S(2)}) collective-permute-start(bf16[24,128,128]{2,1,0:T(8,128)(2,1)S(1)} %pad_maximum_fusion), channel_id=1, source_target_pairs={{16,32},{32,16},{48,64},{64,48},{80,96},{96,80},{112,128},{128,112... | collective-permute-start | bytes 2359304 | tf_op jit(solution)/shard_map/ppermute | solution.py:159
  36.1 2.0 %copy-start = (bf16[32,256,256]{2,1,0:T(8,128)(2,1)}, bf16[32,256,256]{2,1,0:T(8,128)(2,1)S(1)}, u32[]{:S(2)}) copy-start(bf16[32,256,256]{2,1,0:T(8,128)(2,1)S(1)} %lift.1.split) | copy-start | bytes 12582916
  38.0 6.2 %collective-permute-start.10 = (f32[4,2,8,512]{3,2,1,0:T(8,128)S(1)}, f32[4,2,8,512]{3,2,1,0:T(8,128)S(1)}, u32[]{:S(2)}, u32[]{:S(2)}) collective-permute-start(f32[4,2,8,512]{3,2,1,0:T(8,128)S(1)} %get-tuple-element.29), channel_id=1, source_target_pairs={{0,3},{1,2},{2,1},{3,0},{4,7},{5,6},{6,5},{7,4},{8,11},{9,10},{10,... | collective-permute-start | bytes 393224 | tf_op jit(solution)/shard_map/ppermute | solution.py:191
  38.3 5.9 %collective-permute-start.8 = (f32[4,2,8,512]{3,2,1,0:T(8,128)S(1)}, f32[4,2,8,512]{3,2,1,0:T(8,128)S(1)}, u32[]{:S(2)}, u32[]{:S(2)}) collective-permute-start(f32[4,2,8,512]{3,2,1,0:T(8,128)S(1)} %get-tuple-element.27), channel_id=1, source_target_pairs={{0,1},{1,0},{2,3},{3,2},{4,5},{5,4},{6,7},{7,6},{8,9},{9,8},{10,11... | collective-permute-start | bytes 393224 | tf_op jit(solution)/shard_map/ppermute | solution.py:191
  38.3 8.8 %collective-permute-start.9 = (f32[4,2,8,512]{3,2,1,0:T(8,128)S(1)}, f32[4,2,8,512]{3,2,1,0:T(8,128)S(1)}, u32[]{:S(2)}, u32[]{:S(2)}) collective-permute-start(f32[4,2,8,512]{3,2,1,0:T(8,128)S(1)} %get-tuple-element.28), channel_id=1, source_target_pairs={{0,2},{1,3},{2,0},{3,1},{4,6},{5,7},{6,4},{7,5},{8,10},{9,11},{10,... | collective-permute-start | bytes 393224 | tf_op jit(solution)/shard_map/ppermute | solution.py:191
  47.1 2.2 %copy-start.1 = (bf16[32,256,256]{2,1,0:T(8,128)(2,1)S(1)}, bf16[32,256,256]{2,1,0:T(8,128)(2,1)}, u32[]{:S(2)}) copy-start(bf16[32,256,256]{2,1,0:T(8,128)(2,1)} %copy-done) | copy-start | bytes 12582916
  52.6 4.8 %collective-permute-start.12 = (f32[4,2,8,256]{3,2,1,0:T(8,128)S(1)}, f32[4,2,8,256]{3,2,1,0:T(8,128)S(1)}, u32[]{:S(2)}, u32[]{:S(2)}) collective-permute-start(f32[4,2,8,256]{3,2,1,0:T(8,128)S(1)} %get-tuple-element.32), channel_id=1, source_target_pairs={{0,1},{1,0},{2,3},{3,2},{4,5},{5,4},{6,7},{7,6},{8,9},{9,8},{10,11... | collective-permute-start | bytes 196616 | tf_op jit(solution)/shard_map/ppermute | solution.py:191
  52.7 5.9 %collective-permute-start.13 = (f32[4,2,8,256]{3,2,1,0:T(8,128)S(1)}, f32[4,2,8,256]{3,2,1,0:T(8,128)S(1)}, u32[]{:S(2)}, u32[]{:S(2)}) collective-permute-start(f32[4,2,8,256]{3,2,1,0:T(8,128)S(1)} %get-tuple-element.33), channel_id=1, source_target_pairs={{0,2},{1,3},{2,0},{3,1},{4,6},{5,7},{6,4},{7,5},{8,10},{9,11},{10,... | collective-permute-start | bytes 196616 | tf_op jit(solution)/shard_map/ppermute | solution.py:191
  54.9 5.5 %collective-permute-start.14 = (f32[4,2,8,256]{3,2,1,0:T(8,128)S(1)}, f32[4,2,8,256]{3,2,1,0:T(8,128)S(1)}, u32[]{:S(2)}, u32[]{:S(2)}) collective-permute-start(f32[4,2,8,256]{3,2,1,0:T(8,128)S(1)} %get-tuple-element.34), channel_id=1, source_target_pairs={{0,3},{1,2},{2,1},{3,0},{4,7},{5,6},{6,5},{7,4},{8,11},{9,10},{10,... | collective-permute-start | bytes 196616 | tf_op jit(solution)/shard_map/ppermute | solution.py:191
  60.4 5.0 %collective-permute-start.15 = (f32[2,8,768]{2,1,0:T(8,128)S(1)}, f32[2,8,768]{2,1,0:T(8,128)S(1)}, u32[]{:S(2)}, u32[]{:S(2)}) collective-permute-start(f32[2,8,768]{2,1,0:T(8,128)S(1)} %pad_maximum_fusion.2), channel_id=1, source_target_pairs={{0,4},{1,5},{2,6},{3,7},{4,0},{5,1},{6,2},{7,3},{8,12},{9,13},{10,... | collective-permute-start | bytes 147464 | tf_op jit(solution)/shard_map/ppermute | solution.py:206
  60.5 5.7 %collective-permute-start.16 = (f32[2,8,768]{2,1,0:T(8,128)S(1)}, f32[2,8,768]{2,1,0:T(8,128)S(1)}, u32[]{:S(2)}, u32[]{:S(2)}) collective-permute-start(f32[2,8,768]{2,1,0:T(8,128)S(1)} %pad_maximum_fusion.3), channel_id=1, source_target_pairs={{0,8},{1,9},{2,10},{3,11},{4,12},{5,13},{6,14},{7,15},{8,0},{9,1},... | collective-permute-start | bytes 147464 | tf_op jit(solution)/shard_map/ppermute | solution.py:206
  62.6 5.4 %collective-permute-start.17 = (f32[2,8,768]{2,1,0:T(8,128)S(1)}, f32[2,8,768]{2,1,0:T(8,128)S(1)}, u32[]{:S(2)}, u32[]{:S(2)}) collective-permute-start(f32[2,8,768]{2,1,0:T(8,128)S(1)} %pad_maximum_fusion.4), channel_id=1, source_target_pairs={{0,12},{1,13},{2,14},{3,15},{4,8},{5,9},{6,10},{7,11},{8,4},{9,5},... | collective-permute-start | bytes 147464 | tf_op jit(solution)/shard_map/ppermute | solution.py:206
  (1 other events, 0.9 us)

commit v8 on v6

--- a/solution.py
+++ b/solution.py
@@ -74,13 +74,16 @@
 
 
 def band_kernel(
-    cols, aggs, agglo, split, own, near, near_13, pair, o0, o1, o2, o3, blocks, acc
+    cols, aggs, agglo, split, own, near, near_2, f, b, pair, pair_rest, o0, o1, o2, o3, blocks, acc
 ):
     row, cross, y, x = place()
     blocks[0:32] = own[...]
-    blocks[32:48] = near[...]
-    blocks[48:64] = near_13[...]
-    blocks[64:96] = pair[...]
+    blocks[32:40] = near[...]
+    blocks[40:48] = near_2[...]
+    blocks[48:56] = f[8:16]
+    blocks[56:64] = b[8:16]
+    blocks[64:80] = pair[...]
+    blocks[80:96] = pair_rest[...]
     acc[...] = jnp.zeros_like(acc)
     pair_band = 2 - 2 * (row % 2)
     for i in range(ROWS):
@@ -121,6 +124,7 @@
 def local(a_blocks, a_cols, p_blocks, p_aggs, agglo):
     shard = p_blocks[0]
     across = lax.ppermute(shard, BOTH, second(2))
+    beside = lax.ppermute(shard, "row", row_pairs(1))
     shard_near = pl.pallas_call(
         fetch_kernel,
         out_shape=jax.ShapeDtypeStruct(shard.shape, shard.dtype),
@@ -129,19 +133,23 @@
         compiler_params=params(8),
         name="fetch",
     )(shard)
-    duo = jnp.concatenate([shard_near, across])
-    duo_1, duo_3, duo_2 = (lax.ppermute(duo, BOTH, first(k)) for k in (1, 3, 2))
-    duos = (duo, duo_1, duo_2, duo_3)
-    line = jnp.concatenate([d[:2] for d in duos])
-    lines = jnp.concatenate([line] + [d[2:] for d in duos])
-    near = lax.ppermute(lines, "row", row_pairs(1))
-    own_1 = lax.ppermute(line, BOTH, second(1))
-    own_3 = lax.ppermute(line, BOTH, second(3))
-    near_13 = lax.ppermute(jnp.concatenate([own_1, own_3]), "row", row_pairs(1))
-    own = jnp.concatenate([lines, own_1, own_3])
-    pair = lax.ppermute(own, "row", row_pairs(0))
+    trio = jnp.concatenate([shard_near, across, beside])
+    trio_1, trio_3, trio_2 = (lax.ppermute(trio, BOTH, first(k)) for k in (1, 3, 2))
+    line, line_2, near = (
+        jnp.concatenate([t[2 * n : 2 * n + 2] for t in (trio, trio_1, trio_2, trio_3)])
+        for n in range(3)
+    )
+    lines = jnp.concatenate([line, near])
+    lines_1 = lax.ppermute(lines, BOTH, second(1))
+    lines_3 = lax.ppermute(lines, BOTH, second(3))
+    near_2 = lax.ppermute(line_2, "row", row_pairs(1))
+    home = jnp.concatenate([line, line_2])
+    pair = lax.ppermute(home, "row", row_pairs(0))
+    lines_1, lines_3, near_2, pair = lax.optimization_barrier((lines_1, lines_3, near_2, pair))
+    rest = jnp.concatenate([lines_1[:8], lines_3[:8]])
+    pair_rest = lax.ppermute(rest, "row", row_pairs(0))
+    own = jnp.concatenate([home, rest])
 
-    cost = pl.CostEstimate(flops=10**6, bytes_accessed=2**12, transcendentals=0)
     cols, aggs = a_cols.T, p_aggs.T
     split = pl.pallas_call(
         lift_kernel,
@@ -149,23 +157,21 @@
         in_specs=[smem(), smem(), vmem(), vmem()],
         out_specs=vmem(),
         compiler_params=params(16),
-        cost_estimate=cost,
         name="lift",
     )(aggs, agglo, a_blocks, own)
     piece = jax.ShapeDtypeStruct((SIDE, 2, 8, 768), jnp.float32)
     o0, o1, o2, o3 = pl.pallas_call(
         band_kernel,
         out_shape=[piece] * 4,
-        in_specs=[smem()] * 3 + [vmem()] * 5,
+        in_specs=[smem()] * 3 + [vmem()] * 8,
         out_specs=[vmem()] * 4,
         scratch_shapes=[
             pltpu.VMEM((96, B, B), jnp.bfloat16),
             pltpu.VMEM((3, 256, 256), jnp.float32),
         ],
         compiler_params=params(24),
-        cost_estimate=cost,
         name="bands",
-    )(cols, aggs, agglo, split, own, near, near_13, pair)
+    )(cols, aggs, agglo, split, own, near, near_2, lines_1, lines_3, pair, pair_rest)
 
     p1, p3, p2 = (lax.ppermute(o, BOTH, first(k)) for o, k in ((o1, 1), (o3, 3), (o2, 2)))
     sums = [o0[m] + p1[m] + p2[m] + p3[m] for m in range(SIDE)]

time: 64.2 us -> 56.6 us (0.88)
  the two profiles are of different devices: /device:TPU:128 before, /device:TPU:96 now
where the time goes in v8:
time: 56.6 us; the launch traced here: 56.4 us
  waiting for transfers between devices  25.7 us (45%)
  starting transfers between devices  24.3 us (43%)
  Pallas kernels  3.92 us (7%)
  local copies, waits for them, and re-layouts  1.43 us (3%)
  other arithmetic  0.83 us (1%)
    ppermute x3, waiting for transfers between devices, local(): lax.ppermute(o, BOTH, first(k))  7.02 us
    ppermute x3, waiting for transfers between devices, local(): lax.ppermute(trio, BOTH, first(k))  6.33 us
    ppermute x1, waiting for transfers between devices, local(): near_2 = lax.ppermute(line_2, 'row', row_pairs(1))  5.76 us
    ppermute x3, starting transfers between devices, local(): lax.ppermute(o, BOTH, first(k))  4.78 us
    ppermute x3, starting transfers between devices, local(): lax.ppermute(trio, BOTH, first(k))  4.75 us
    ppermute x3, starting transfers between devices, local(): q1, q3, q2 = (lax.ppermute(sums[k], BOTH, second(k)) for k in (1, 3, 2))  4.18 us
    ppermute x3, waiting for transfers between devices, local(): q1, q3, q2 = (lax.ppermute(sums[k], BOTH, second(k)) for k in (1, 3, 2))  3.28 us
    ppermute x1, starting transfers between devices, local(): across = lax.ppermute(shard, BOTH, second(2))  3.11 us
  transfers between devices with their start and end apart: 16, of which 10 were waited for; matrix products, arithmetic and copies ran while one was open for 0% of the time, Pallas kernels for 3%

profile of v8, /device:TPU:96, one launch (start us, length us, event | category | flops | bytes accessed | tf_op | source)
XLA Modules:
  0.0 56.4 jit_solution(1492637526315867685)
XLA Ops:
  0.0 2.0 %collective-permute-start.1 = (bf16[2,128,128]{2,1,0:T(8,128)(2,1)}, bf16[2,128,128]{2,1,0:T(8,128)(2,1)S(1)}, u32[]{:S(2)}, u32[]{:S(2)}) collective-permute-start(bf16[2,128,128]{2,1,0:T(8,128)(2,1)} %bitcast.21), channel_id=1, source_target_pairs={{16,32},{32,16},{48,64},{64,48},{80,96},{96,80},{112,128},{128,112... | collective-permute-start | bytes 196616 | tf_op jit(solution)/shard_map/ppermute | solution.py:127
  2.0 3.1 %collective-permute-start = (bf16[2,128,128]{2,1,0:T(8,128)(2,1)}, bf16[2,128,128]{2,1,0:T(8,128)(2,1)S(1)}, u32[]{:S(2)}, u32[]{:S(2)}) collective-permute-start(bf16[2,128,128]{2,1,0:T(8,128)(2,1)} %bitcast.22), channel_id=1, source_target_pairs={{0,8},{1,9},{2,10},{3,11},{4,12},{5,13},{6,14},{7,15},{8,0},{9,1},... | collective-permute-start | bytes 196616 | tf_op jit(solution)/shard_map/ppermute | solution.py:126
  5.2 0.9 %copy-done.1 = bf16[1,2,128,128]{3,2,1,0:T(8,128)(2,1)S(1)} copy-done((bf16[1,2,128,128]{3,2,1,0:T(8,128)(2,1)S(1)}, bf16[1,2,128,128]{3,2,1,0:T(8,128)(2,1)}, u32[]{:S(2)}) %copy-start.1) | copy-done | bytes 65560
  6.1 2.1 %collective-permute-done = bf16[2,128,128]{2,1,0:T(8,128)(2,1)S(1)} collective-permute-done((bf16[2,128,128]{2,1,0:T(8,128)(2,1)}, bf16[2,128,128]{2,1,0:T(8,128)(2,1)S(1)}, u32[]{:S(2)}, u32[]{:S(2)}) %collective-permute-start) | collective-permute-done | bytes 65568 | tf_op jit(solution)/shard_map/ppermute | solution.py:126
  8.1 1.7 %collective-permute-start.2 = (bf16[6,128,128]{2,1,0:T(8,128)(2,1)S(1)}, bf16[6,128,128]{2,1,0:T(8,128)(2,1)S(1)}, u32[]{:S(2)}, u32[]{:S(2)}) collective-permute-start(bf16[6,128,128]{2,1,0:T(8,128)(2,1)S(1)} %pad_maximum_fusion.3), channel_id=1, source_target_pairs={{0,1},{1,0},{2,3},{3,2},{4,5},{5,4},{6,7},{7,6},{8,9},{9,8},{10,11... | collective-permute-start | bytes 589832 | tf_op jit(solution)/shard_map/ppermute | solution.py:137
  9.8 2.3 %collective-permute-start.4 = (bf16[6,128,128]{2,1,0:T(8,128)(2,1)S(1)}, bf16[6,128,128]{2,1,0:T(8,128)(2,1)S(1)}, u32[]{:S(2)}, u32[]{:S(2)}) collective-permute-start(bf16[6,128,128]{2,1,0:T(8,128)(2,1)S(1)} %pad_maximum_fusion.3), channel_id=1, source_target_pairs={{0,3},{1,2},{2,1},{3,0},{4,7},{5,6},{6,5},{7,4},{8,11},{9,10},{10,... | collective-permute-start | bytes 589832 | tf_op jit(solution)/shard_map/ppermute | solution.py:137
  12.9 1.0 %collective-permute-done.2 = bf16[6,128,128]{2,1,0:T(8,128)(2,1)S(1)} collective-permute-done((bf16[6,128,128]{2,1,0:T(8,128)(2,1)S(1)}, bf16[6,128,128]{2,1,0:T(8,128)(2,1)S(1)}, u32[]{:S(2)}, u32[]{:S(2)}) %collective-permute-start.2) | collective-permute-done | bytes 196640 | tf_op jit(solution)/shard_map/ppermute | solution.py:137
  13.9 5.3 %collective-permute-done.3 = bf16[6,128,128]{2,1,0:T(8,128)(2,1)S(1)} collective-permute-done((bf16[6,128,128]{2,1,0:T(8,128)(2,1)S(1)}, bf16[6,128,128]{2,1,0:T(8,128)(2,1)S(1)}, u32[]{:S(2)}, u32[]{:S(2)}) %collective-permute-start.3) | collective-permute-done | bytes 196640 | tf_op jit(solution)/shard_map/ppermute | solution.py:137
  20.0 2.7 %collective-permute-start.6 = (bf16[16,128,128]{2,1,0:T(8,128)(2,1)S(1)}, bf16[16,128,128]{2,1,0:T(8,128)(2,1)S(1)}, u32[]{:S(2)}, u32[]{:S(2)}) collective-permute-start(bf16[16,128,128]{2,1,0:T(8,128)(2,1)S(1)} %get-tuple-element.40), channel_id=1, source_target_pairs={{0,12},{1,13},{2,14},{3,15},{4,8},{5,9},{6,10},{7,11},{8,4},{9,5},... | collective-permute-start | bytes 1572872 | tf_op jit(solution)/shard_map/ppermute | solution.py:144
  22.9 1.9 %collective-permute-start.7 = (bf16[8,128,128]{2,1,0:T(8,128)(2,1)S(1)}, bf16[8,128,128]{2,1,0:T(8,128)(2,1)S(1)}, u32[]{:S(2)}, u32[]{:S(2)}) collective-permute-start(bf16[8,128,128]{2,1,0:T(8,128)(2,1)S(1)} %pad_maximum_fusion.1), channel_id=1, source_target_pairs={{16,32},{32,16},{48,64},{64,48},{80,96},{96,80},{112,128},{128,112... | collective-permute-start | bytes 786440 | tf_op jit(solution)/shard_map/ppermute | solution.py:145
  24.8 5.8 %collective-permute-done.7.near_2 = bf16[8,128,128]{2,1,0:T(8,128)(2,1)S(1)} collective-permute-done((bf16[8,128,128]{2,1,0:T(8,128)(2,1)S(1)}, bf16[8,128,128]{2,1,0:T(8,128)(2,1)S(1)}, u32[]{:S(2)}, u32[]{:S(2)}) %collective-permute-start.7) | collective-permute-done | bytes 262176 | tf_op jit(solution)/shard_map/ppermute | solution.py:145
  30.6 1.2 %collective-permute-done.5.f = bf16[16,128,128]{2,1,0:T(8,128)(2,1)S(1)} collective-permute-done((bf16[16,128,128]{2,1,0:T(8,128)(2,1)S(1)}, bf16[16,128,128]{2,1,0:T(8,128)(2,1)S(1)}, u32[]{:S(2)}, u32[]{:S(2)}) %collective-permute-start.5) | collective-permute-done | bytes 524320 | tf_op jit(solution)/shard_map/ppermute | solution.py:143
  32.5 1.5 %lift.1.split = bf16[32,256,256]{2,1,0:T(8,128)(2,1)S(1)} custom-call(s32[2,256]{1,0:T(2,128)S(1)} %bitcast.24, s32[32]{0:T(128)S(1)} %copy-done.3, bf16[16,2,128,128]{3,2,1,0:T(8,128)(2,1)S(1)} %copy-done, bf16[32,128,128]{2,1,0:T(8,128)(2,1)S(1)} %get-tuple-element.27.plane.own), custom_call_target="tpu_custom_call" | custom-call | tf_op jit(solution)/shard_map/lift/pallas_call | solution.py:154
  34.0 2.4 %bands.1 = (f32[4,2,8,768]{3,2,1,0:T(8,128)S(1)}, f32[4,2,8,768]{3,2,1,0:T(8,128)S(1)}, f32[4,2,8,768]{3,2,1,0:T(8,128)S(1)}, f32[4,2,8,768]{3,2,1,0:T(8,128)S(1)}) custom-call(s32[2,16]{1,0:T(2,128)S(1)} %bitcast.26, s32[2,256]{1,0:T(2,128)S(1)} %bitcast.25, s32[32]{0:T(128)S(1)} %copy-done.3, bf16[32,256,256]{2,1,0:T(8,128)(2,1)S(1)} %lift.1.split, ...), custom_call_target="tpu_custom_call" | custom-call | tf_op jit(solution)/shard_map/bands/pallas_call | solution.py:163
  36.5 2.0 %collective-permute-start.10 = (f32[4,2,8,768]{3,2,1,0:T(8,128)S(1)}, f32[4,2,8,768]{3,2,1,0:T(8,128)S(1)}, u32[]{:S(2)}, u32[]{:S(2)}) collective-permute-start(f32[4,2,8,768]{3,2,1,0:T(8,128)S(1)} %get-tuple-element.18), channel_id=1, source_target_pairs={{0,1},{1,0},{2,3},{3,2},{4,5},{5,4},{6,7},{7,6},{8,9},{9,8},{10,11... | collective-permute-start | bytes 589832 | tf_op jit(solution)/shard_map/ppermute | solution.py:176
  38.4 2.0 %collective-permute-start.11 = (f32[4,2,8,768]{3,2,1,0:T(8,128)S(1)}, f32[4,2,8,768]{3,2,1,0:T(8,128)S(1)}, u32[]{:S(2)}, u32[]{:S(2)}) collective-permute-start(f32[4,2,8,768]{3,2,1,0:T(8,128)S(1)} %get-tuple-element.19), channel_id=1, source_target_pairs={{0,2},{1,3},{2,0},{3,1},{4,6},{5,7},{6,4},{7,5},{8,10},{9,11},{10,... | collective-permute-start | bytes 589832 | tf_op jit(solution)/shard_map/ppermute | solution.py:176
  40.4 0.8 %collective-permute-start.12 = (f32[4,2,8,768]{3,2,1,0:T(8,128)S(1)}, f32[4,2,8,768]{3,2,1,0:T(8,128)S(1)}, u32[]{:S(2)}, u32[]{:S(2)}) collective-permute-start(f32[4,2,8,768]{3,2,1,0:T(8,128)S(1)} %get-tuple-element.20), channel_id=1, source_target_pairs={{0,3},{1,2},{2,1},{3,0},{4,7},{5,6},{6,5},{7,4},{8,11},{9,10},{10,... | collective-permute-start | bytes 589832 | tf_op jit(solution)/shard_map/ppermute | solution.py:176
  41.2 1.0 %collective-permute-done.10 = f32[4,2,8,768]{3,2,1,0:T(8,128)S(1)} collective-permute-done((f32[4,2,8,768]{3,2,1,0:T(8,128)S(1)}, f32[4,2,8,768]{3,2,1,0:T(8,128)S(1)}, u32[]{:S(2)}, u32[]{:S(2)}) %collective-permute-start.10) | collective-permute-done | bytes 196640 | tf_op jit(solution)/shard_map/ppermute | solution.py:176
  42.2 4.1 %collective-permute-done.11 = f32[4,2,8,768]{3,2,1,0:T(8,128)S(1)} collective-permute-done((f32[4,2,8,768]{3,2,1,0:T(8,128)S(1)}, f32[4,2,8,768]{3,2,1,0:T(8,128)S(1)}, u32[]{:S(2)}, u32[]{:S(2)}) %collective-permute-start.11) | collective-permute-done | bytes 196640 | tf_op jit(solution)/shard_map/ppermute | solution.py:176
  46.3 2.0 %collective-permute-done.12 = f32[4,2,8,768]{3,2,1,0:T(8,128)S(1)} collective-permute-done((f32[4,2,8,768]{3,2,1,0:T(8,128)S(1)}, f32[4,2,8,768]{3,2,1,0:T(8,128)S(1)}, u32[]{:S(2)}, u32[]{:S(2)}) %collective-permute-start.12) | collective-permute-done | bytes 196640 | tf_op jit(solution)/shard_map/ppermute | solution.py:176
  49.0 1.2 %collective-permute-start.15 = (f32[2,8,768]{2,1,0:T(8,128)S(1)}, f32[2,8,768]{2,1,0:T(8,128)S(1)}, u32[]{:S(2)}, u32[]{:S(2)}) collective-permute-start(f32[2,8,768]{2,1,0:T(8,128)S(1)} %get-tuple-element.22), channel_id=1, source_target_pairs={{0,12},{1,13},{2,14},{3,15},{4,8},{5,9},{6,10},{7,11},{8,4},{9,5},... | collective-permute-start | bytes 147464 | tf_op jit(solution)/shard_map/ppermute | solution.py:178
  50.2 2.3 %collective-permute-start.14 = (f32[2,8,768]{2,1,0:T(8,128)S(1)}, f32[2,8,768]{2,1,0:T(8,128)S(1)}, u32[]{:S(2)}, u32[]{:S(2)}) collective-permute-start(f32[2,8,768]{2,1,0:T(8,128)S(1)} %get-tuple-element.23), channel_id=1, source_target_pairs={{0,8},{1,9},{2,10},{3,11},{4,12},{5,13},{6,14},{7,15},{8,0},{9,1},... | collective-permute-start | bytes 147464 | tf_op jit(solution)/shard_map/ppermute | solution.py:178
  52.5 1.8 %collective-permute-done.15 = f32[2,8,768]{2,1,0:T(8,128)S(1)} collective-permute-done((f32[2,8,768]{2,1,0:T(8,128)S(1)}, f32[2,8,768]{2,1,0:T(8,128)S(1)}, u32[]{:S(2)}, u32[]{:S(2)}) %collective-permute-start.15) | collective-permute-done | bytes 49184 | tf_op jit(solution)/shard_map/ppermute | solution.py:178
  54.3 1.5 %collective-permute-done.14 = f32[2,8,768]{2,1,0:T(8,128)S(1)} collective-permute-done((f32[2,8,768]{2,1,0:T(8,128)S(1)}, f32[2,8,768]{2,1,0:T(8,128)S(1)}, u32[]{:S(2)}, u32[]{:S(2)}) %collective-permute-start.14) | collective-permute-done | bytes 49184 | tf_op jit(solution)/shard_map/ppermute | solution.py:178
  (39 shorter events, 3.8 us)
Async XLA Ops:
  0.0 32.5 %copy-start = (bf16[16,2,128,128]{3,2,1,0:T(8,128)(2,1)S(1)}, bf16[16,2,128,128]{3,2,1,0:T(8,128)(2,1)}, u32[]{:S(2)}) copy-start(bf16[16,2,128,128]{3,2,1,0:T(8,128)(2,1)} %a.1) | copy-start | bytes 3145732
  0.0 6.0 %collective-permute-start.1 = (bf16[2,128,128]{2,1,0:T(8,128)(2,1)}, bf16[2,128,128]{2,1,0:T(8,128)(2,1)S(1)}, u32[]{:S(2)}, u32[]{:S(2)}) collective-permute-start(bf16[2,128,128]{2,1,0:T(8,128)(2,1)} %bitcast.21), channel_id=1, source_target_pairs={{16,32},{32,16},{48,64},{64,48},{80,96},{96,80},{112,128},{128,112... | collective-permute-start | bytes 196616 | tf_op jit(solution)/shard_map/ppermute | solution.py:127
  2.0 6.1 %collective-permute-start = (bf16[2,128,128]{2,1,0:T(8,128)(2,1)}, bf16[2,128,128]{2,1,0:T(8,128)(2,1)S(1)}, u32[]{:S(2)}, u32[]{:S(2)}) collective-permute-start(bf16[2,128,128]{2,1,0:T(8,128)(2,1)} %bitcast.22), channel_id=1, source_target_pairs={{0,8},{1,9},{2,10},{3,11},{4,12},{5,13},{6,14},{7,15},{8,0},{9,1},... | collective-permute-start | bytes 196616 | tf_op jit(solution)/shard_map/ppermute | solution.py:126
  5.2 0.9 %copy-start.1 = (bf16[1,2,128,128]{3,2,1,0:T(8,128)(2,1)S(1)}, bf16[1,2,128,128]{3,2,1,0:T(8,128)(2,1)}, u32[]{:S(2)}) copy-start(bf16[1,2,128,128]{3,2,1,0:T(8,128)(2,1)} %param.7) | copy-start | bytes 196612
  6.0 26.5 %copy-start.2 = (s32[256,2]{0,1:T(2,128)S(1)}, s32[256,2]{0,1:T(2,128)}, u32[]{:S(2)}) copy-start(s32[256,2]{0,1:T(2,128)} %param.8) | copy-start | bytes 6148
  6.0 26.5 %copy-start.3 = (s32[32]{0:T(128)S(1)}, s32[32]{0:T(128)}, u32[]{:S(2)}) copy-start(s32[32]{0:T(128)} %agglo.3) | copy-start | bytes 388
  8.1 5.8 %collective-permute-start.2 = (bf16[6,128,128]{2,1,0:T(8,128)(2,1)S(1)}, bf16[6,128,128]{2,1,0:T(8,128)(2,1)S(1)}, u32[]{:S(2)}, u32[]{:S(2)}) collective-permute-start(bf16[6,128,128]{2,1,0:T(8,128)(2,1)S(1)} %pad_maximum_fusion.3), channel_id=1, source_target_pairs={{0,1},{1,0},{2,3},{3,2},{4,5},{5,4},{6,7},{7,6},{8,9},{9,8},{10,11... | collective-permute-start | bytes 589832 | tf_op jit(solution)/shard_map/ppermute | solution.py:137
  9.8 9.5 %collective-permute-start.4 = (bf16[6,128,128]{2,1,0:T(8,128)(2,1)S(1)}, bf16[6,128,128]{2,1,0:T(8,128)(2,1)S(1)}, u32[]{:S(2)}, u32[]{:S(2)}) collective-permute-start(bf16[6,128,128]{2,1,0:T(8,128)(2,1)S(1)} %pad_maximum_fusion.3), channel_id=1, source_target_pairs={{0,3},{1,2},{2,1},{3,0},{4,7},{5,6},{6,5},{7,4},{8,11},{9,10},{10,... | collective-permute-start | bytes 589832 | tf_op jit(solution)/shard_map/ppermute | solution.py:137
  12.1 7.2 %collective-permute-start.3 = (bf16[6,128,128]{2,1,0:T(8,128)(2,1)S(1)}, bf16[6,128,128]{2,1,0:T(8,128)(2,1)S(1)}, u32[]{:S(2)}, u32[]{:S(2)}) collective-permute-start(bf16[6,128,128]{2,1,0:T(8,128)(2,1)S(1)} %pad_maximum_fusion.3), channel_id=1, source_target_pairs={{0,2},{1,3},{2,0},{3,1},{4,6},{5,7},{6,4},{7,5},{8,10},{9,11},{10,... | collective-permute-start | bytes 589832 | tf_op jit(solution)/shard_map/ppermute | solution.py:137
  19.7 10.9 %collective-permute-start.8 = (bf16[16,128,128]{2,1,0:T(8,128)(2,1)S(1)}, bf16[16,128,128]{2,1,0:T(8,128)(2,1)S(1)}, u32[]{:S(2)}, u32[]{:S(2)}) collective-permute-start(bf16[16,128,128]{2,1,0:T(8,128)(2,1)S(1)} %get-tuple-element.41), channel_id=1, source_target_pairs={{0,16},{16,0},{32,48},{48,32},{64,80},{80,64},{96,112},{112,96},{1... | collective-permute-start | bytes 1572872 | tf_op jit(solution)/shard_map/ppermute | solution.py:147
  20.0 10.6 %collective-permute-start.6 = (bf16[16,128,128]{2,1,0:T(8,128)(2,1)S(1)}, bf16[16,128,128]{2,1,0:T(8,128)(2,1)S(1)}, u32[]{:S(2)}, u32[]{:S(2)}) collective-permute-start(bf16[16,128,128]{2,1,0:T(8,128)(2,1)S(1)} %get-tuple-element.40), channel_id=1, source_target_pairs={{0,12},{1,13},{2,14},{3,15},{4,8},{5,9},{6,10},{7,11},{8,4},{9,5},... | collective-permute-start | bytes 1572872 | tf_op jit(solution)/shard_map/ppermute | solution.py:144
  22.6 9.2 %collective-permute-start.5 = (bf16[16,128,128]{2,1,0:T(8,128)(2,1)S(1)}, bf16[16,128,128]{2,1,0:T(8,128)(2,1)S(1)}, u32[]{:S(2)}, u32[]{:S(2)}) collective-permute-start(bf16[16,128,128]{2,1,0:T(8,128)(2,1)S(1)} %get-tuple-element.40), channel_id=1, source_target_pairs={{0,4},{1,5},{2,6},{3,7},{4,0},{5,1},{6,2},{7,3},{8,12},{9,13},{10,... | collective-permute-start | bytes 1572872 | tf_op jit(solution)/shard_map/ppermute | solution.py:143
  22.9 7.7 %collective-permute-start.7 = (bf16[8,128,128]{2,1,0:T(8,128)(2,1)S(1)}, bf16[8,128,128]{2,1,0:T(8,128)(2,1)S(1)}, u32[]{:S(2)}, u32[]{:S(2)}) collective-permute-start(bf16[8,128,128]{2,1,0:T(8,128)(2,1)S(1)} %pad_maximum_fusion.1), channel_id=1, source_target_pairs={{16,32},{32,16},{48,64},{64,48},{80,96},{96,80},{112,128},{128,112... | collective-permute-start | bytes 786440 | tf_op jit(solution)/shard_map/ppermute | solution.py:145
  31.9 2.2 %copy-start.4 = (s32[16,2]{0,1:T(2,128)S(1)}, s32[16,2]{0,1:T(2,128)}, u32[]{:S(2)}) copy-start(s32[16,2]{0,1:T(2,128)} %param.6) | copy-start | bytes 388
  32.0 2.0 %collective-permute-start.9 = (bf16[16,128,128]{2,1,0:T(8,128)(2,1)S(1)}, bf16[16,128,128]{2,1,0:T(8,128)(2,1)S(1)}, u32[]{:S(2)}, u32[]{:S(2)}) collective-permute-start(bf16[16,128,128]{2,1,0:T(8,128)(2,1)S(1)} %pad_maximum_fusion), channel_id=1, source_target_pairs={{0,16},{16,0},{32,48},{48,32},{64,80},{80,64},{96,112},{112,96},{1... | collective-permute-start | bytes 1572872 | tf_op jit(solution)/shard_map/ppermute | solution.py:150
  36.5 5.8 %collective-permute-start.10 = (f32[4,2,8,768]{3,2,1,0:T(8,128)S(1)}, f32[4,2,8,768]{3,2,1,0:T(8,128)S(1)}, u32[]{:S(2)}, u32[]{:S(2)}) collective-permute-start(f32[4,2,8,768]{3,2,1,0:T(8,128)S(1)} %get-tuple-element.18), channel_id=1, source_target_pairs={{0,1},{1,0},{2,3},{3,2},{4,5},{5,4},{6,7},{7,6},{8,9},{9,8},{10,11... | collective-permute-start | bytes 589832 | tf_op jit(solution)/shard_map/ppermute | solution.py:176
  38.4 7.8 %collective-permute-start.11 = (f32[4,2,8,768]{3,2,1,0:T(8,128)S(1)}, f32[4,2,8,768]{3,2,1,0:T(8,128)S(1)}, u32[]{:S(2)}, u32[]{:S(2)}) collective-permute-start(f32[4,2,8,768]{3,2,1,0:T(8,128)S(1)} %get-tuple-element.19), channel_id=1, source_target_pairs={{0,2},{1,3},{2,0},{3,1},{4,6},{5,7},{6,4},{7,5},{8,10},{9,11},{10,... | collective-permute-start | bytes 589832 | tf_op jit(solution)/shard_map/ppermute | solution.py:176
  40.4 7.9 %collective-permute-start.12 = (f32[4,2,8,768]{3,2,1,0:T(8,128)S(1)}, f32[4,2,8,768]{3,2,1,0:T(8,128)S(1)}, u32[]{:S(2)}, u32[]{:S(2)}) collective-permute-start(f32[4,2,8,768]{3,2,1,0:T(8,128)S(1)} %get-tuple-element.20), channel_id=1, source_target_pairs={{0,3},{1,2},{2,1},{3,0},{4,7},{5,6},{6,5},{7,4},{8,11},{9,10},{10,... | collective-permute-start | bytes 589832 | tf_op jit(solution)/shard_map/ppermute | solution.py:176
  48.3 4.2 %collective-permute-start.13 = (f32[2,8,768]{2,1,0:T(8,128)S(1)}, f32[2,8,768]{2,1,0:T(8,128)S(1)}, u32[]{:S(2)}, u32[]{:S(2)}) collective-permute-start(f32[2,8,768]{2,1,0:T(8,128)S(1)} %get-tuple-element.21), channel_id=1, source_target_pairs={{0,4},{1,5},{2,6},{3,7},{4,0},{5,1},{6,2},{7,3},{8,12},{9,13},{10,... | collective-permute-start | bytes 147464 | tf_op jit(solution)/shard_map/ppermute | solution.py:178
  49.0 5.3 %collective-permute-start.15 = (f32[2,8,768]{2,1,0:T(8,128)S(1)}, f32[2,8,768]{2,1,0:T(8,128)S(1)}, u32[]{:S(2)}, u32[]{:S(2)}) collective-permute-start(f32[2,8,768]{2,1,0:T(8,128)S(1)} %get-tuple-element.22), channel_id=1, source_target_pairs={{0,12},{1,13},{2,14},{3,15},{4,8},{5,9},{6,10},{7,11},{8,4},{9,5},... | collective-permute-start | bytes 147464 | tf_op jit(solution)/shard_map/ppermute | solution.py:178
  50.2 5.6 %collective-permute-start.14 = (f32[2,8,768]{2,1,0:T(8,128)S(1)}, f32[2,8,768]{2,1,0:T(8,128)S(1)}, u32[]{:S(2)}, u32[]{:S(2)}) collective-permute-start(f32[2,8,768]{2,1,0:T(8,128)S(1)} %get-tuple-element.23), channel_id=1, source_target_pairs={{0,8},{1,9},{2,10},{3,11},{4,12},{5,13},{6,14},{7,15},{8,0},{9,1},... | collective-permute-start | bytes 147464 | tf_op jit(solution)/shard_map/ppermute | solution.py:178

commit v9 on v8

--- a/solution.py
+++ b/solution.py
@@ -46,14 +46,31 @@
     return row, crossed(row), col // SIDE, col % SIDE
 
 
+def groups_of_eight():
+    groups = []
+    for r in range(1, ROWS, 2):
+        for q in range(SIDE):
+            group = []
+            for row in (r, (r + 1) % ROWS):
+                for c in range(SIDE):
+                    y, x = (c, q) if crossed(row) else (q, c)
+                    group.append(row * ROWS + y * SIDE + x)
+            groups.append(group)
+    return groups
+
+
 def slot_of(y, x, j, cross):
-    dy, dx = y ^ ((j % ROWS) // SIDE), x ^ (j % SIDE)
-    back, along = jnp.where(cross == 0, dy, dx), jnp.where(cross == 0, dx, dy)
+    y2, x2 = (j % ROWS) // SIDE, j % SIDE
+    back, along = jnp.where(cross == 0, y ^ y2, x ^ x2), jnp.where(cross == 0, x2, y2)
     return ((back >> 1) | ((back & 1) << 1)) * SIDE + along
 
 
-def fetch_kernel(shard, near):
-    near[...] = shard[...]
+def spread_kernel(shard, copies, sems):
+    sent = [pltpu.make_async_copy(shard, copies.at[pl.ds(n, 1)], sems.at[n]) for n in range(8)]
+    for copy in sent:
+        copy.start()
+    for copy in sent:
+        copy.wait()
 
 
 def lift_kernel(aggs, agglo, a, plane, split):
@@ -74,14 +91,15 @@
 
 
 def band_kernel(
-    cols, aggs, agglo, split, own, near, near_2, f, b, pair, pair_rest, o0, o1, o2, o3, blocks, acc
+    cols, aggs, agglo, split, own, lines, near_2, f, b, pair, pair_rest, o0, o1, o2, o3, blocks, acc
 ):
     row, cross, y, x = place()
+    other = pl.ds((row % 2) * 8, 8)
     blocks[0:32] = own[...]
-    blocks[32:40] = near[...]
+    blocks[32:40] = lines[other]
     blocks[40:48] = near_2[...]
-    blocks[48:56] = f[8:16]
-    blocks[56:64] = b[8:16]
+    blocks[48:56] = f[other]
+    blocks[56:64] = b[other]
     blocks[64:80] = pair[...]
     blocks[80:96] = pair_rest[...]
     acc[...] = jnp.zeros_like(acc)
@@ -122,31 +140,32 @@
 
 
 def local(a_blocks, a_cols, p_blocks, p_aggs, agglo):
-    shard = p_blocks[0]
-    across = lax.ppermute(shard, BOTH, second(2))
-    beside = lax.ppermute(shard, "row", row_pairs(1))
-    shard_near = pl.pallas_call(
-        fetch_kernel,
-        out_shape=jax.ShapeDtypeStruct(shard.shape, shard.dtype),
-        in_specs=[vmem()],
-        out_specs=vmem(),
+    half = (1 - (lax.axis_index("row") & 1)) * 8
+
+    def own_half(lines):
+        return lax.dynamic_slice_in_dim(lines, half, 8, 0)
+
+    copies = pl.pallas_call(
+        spread_kernel,
+        out_shape=jax.ShapeDtypeStruct((8, 2, B, B), jnp.bfloat16),
+        in_specs=[pl.BlockSpec(memory_space=pltpu.HBM)],
+        out_specs=pl.BlockSpec(memory_space=pltpu.HBM),
+        scratch_shapes=[pltpu.SemaphoreType.DMA((8,))],
         compiler_params=params(8),
-        name="fetch",
-    )(shard)
-    trio = jnp.concatenate([shard_near, across, beside])
-    trio_1, trio_3, trio_2 = (lax.ppermute(trio, BOTH, first(k)) for k in (1, 3, 2))
-    line, line_2, near = (
-        jnp.concatenate([t[2 * n : 2 * n + 2] for t in (trio, trio_1, trio_2, trio_3)])
-        for n in range(3)
-    )
-    lines = jnp.concatenate([line, near])
+        name="spread",
+    )(p_blocks)
+    lines = lax.all_to_all(
+        copies, BOTH, 0, 0, axis_index_groups=groups_of_eight(), tiled=True
+    ).reshape(16, B, B)
+    line = own_half(lines)
+    line_2 = lax.ppermute(line, BOTH, second(2))
     lines_1 = lax.ppermute(lines, BOTH, second(1))
     lines_3 = lax.ppermute(lines, BOTH, second(3))
     near_2 = lax.ppermute(line_2, "row", row_pairs(1))
     home = jnp.concatenate([line, line_2])
     pair = lax.ppermute(home, "row", row_pairs(0))
     lines_1, lines_3, near_2, pair = lax.optimization_barrier((lines_1, lines_3, near_2, pair))
-    rest = jnp.concatenate([lines_1[:8], lines_3[:8]])
+    rest = jnp.concatenate([own_half(lines_1), own_half(lines_3)])
     pair_rest = lax.ppermute(rest, "row", row_pairs(0))
     own = jnp.concatenate([home, rest])
 
@@ -171,7 +190,7 @@
         ],
         compiler_params=params(24),
         name="bands",
-    )(cols, aggs, agglo, split, own, near, near_2, lines_1, lines_3, pair, pair_rest)
+    )(cols, aggs, agglo, split, own, lines, near_2, lines_1, lines_3, pair, pair_rest)
 
     p1, p3, p2 = (lax.ppermute(o, BOTH, first(k)) for o, k in ((o1, 1), (o3, 3), (o2, 2)))
     sums = [o0[m] + p1[m] + p2[m] + p3[m] for m in range(SIDE)]

time: 56.6 us -> 59.6 us (1.053); the launches traced: 56.4 us -> 58.7 us
  waiting for transfers between devices: 25.7 us -> 27.8 us
  Pallas kernels: 3.92 us -> 4.8 us
    all_to_all x0 -> x1, waiting for transfers between devices: none -> 7.23 us  [local(): lax.all_to_all(copies, BOTH, 0, 0, axis_index_groups=groups_of_eight(), t...]
    ppermute x5 -> x1, starting transfers between devices: 9.9 us -> 3.11 us  [local(): line_2 = lax.ppermute(line, BOTH, second(2))]
    all_to_all x0 -> x1, starting transfers between devices: none -> 5.66 us  [local(): lax.all_to_all(copies, BOTH, 0, 0, axis_index_groups=groups_of_eight(), t...]
    ppermute x5 -> x1, waiting for transfers between devices: 8.39 us -> 3.71 us  [local(): line_2 = lax.ppermute(line, BOTH, second(2))]
    ppermute x1, starting transfers between devices: 0.29 us -> 1.96 us  [local(): pair = lax.ppermute(home, 'row', row_pairs(0))]
    ppermute x1, starting transfers between devices: 2.66 us -> 1.14 us  [local(): lines_3 = lax.ppermute(lines, BOTH, second(3))]
    ppermute x1, waiting for transfers between devices: 1.22 us -> 0.01 us  [local(): lines_1 = lax.ppermute(lines, BOTH, second(1))]
    ppermute x1, starting transfers between devices: 0.39 us -> 1.32 us  [local(): pair_rest = lax.ppermute(rest, 'row', row_pairs(0))]
  transfers between devices with their start and end apart: 16 -> 13, of which waited for: 10 -> 8; matrix products, arithmetic and copies ran while one was open for 0% -> 0% of each run, Pallas kernels for 3% -> 3%
where the time goes in v9:
time: 59.6 us; the launch traced here: 58.7 us
  waiting for transfers between devices  27.8 us (47%)
  starting transfers between devices  24.1 us (40%)
  Pallas kernels  4.8 us (8%)
  local copies, waits for them, and re-layouts  1.01 us (2%)
  other arithmetic  0.9 us (2%)
    ppermute x3, waiting for transfers between devices, local(): lax.ppermute(o, BOTH, first(k))  7.72 us
    all_to_all x1, waiting for transfers between devices, local(): lax.all_to_all(copies, BOTH, 0, 0, axis_index_groups=groups_of_eight(), t...  7.23 us
    ppermute x1, waiting for transfers between devices, local(): near_2 = lax.ppermute(line_2, 'row', row_pairs(1))  5.76 us
    all_to_all x1, starting transfers between devices, local(): lax.all_to_all(copies, BOTH, 0, 0, axis_index_groups=groups_of_eight(), t...  5.66 us
    ppermute x3, starting transfers between devices, local(): lax.ppermute(o, BOTH, first(k))  4.78 us
    ppermute x3, starting transfers between devices, local(): q1, q3, q2 = (lax.ppermute(sums[k], BOTH, second(k)) for k in (1, 3, 2))  4.17 us
    ppermute x1, waiting for transfers between devices, local(): line_2 = lax.ppermute(line, BOTH, second(2))  3.71 us
    ppermute x3, waiting for transfers between devices, local(): q1, q3, q2 = (lax.ppermute(sums[k], BOTH, second(k)) for k in (1, 3, 2))  3.33 us
  transfers between devices with their start and end apart: 13, of which 8 were waited for; matrix products, arithmetic and copies ran while one was open for 0% of the time, Pallas kernels for 3%

profile of v9, /device:TPU:96, one launch (start us, length us, event | category | flops | bytes accessed | tf_op | source)
XLA Modules:
  0.0 58.7 jit_solution(393188688563129629)
XLA Ops:
  0.0 0.9 %copy-done.1 = bf16[1,2,128,128]{3,2,1,0:T(8,128)(2,1)S(1)} copy-done((bf16[1,2,128,128]{3,2,1,0:T(8,128)(2,1)S(1)}, bf16[1,2,128,128]{3,2,1,0:T(8,128)(2,1)}, u32[]{:S(2)}) %copy-start.1) | copy-done | bytes 65560
  0.9 0.9 %spread.1 = bf16[8,2,128,128]{3,2,1,0:T(8,128)(2,1)} custom-call(bf16[1,2,128,128]{3,2,1,0:T(8,128)(2,1)S(1)} %copy-done.1), custom_call_target="tpu_custom_call" | custom-call | tf_op jit(solution)/shard_map/spread/pallas_call | solution.py:148
  1.8 5.7 %all-to-all-start = ((bf16[8,2,128,128]{3,2,1,0:T(8,128)(2,1)}), bf16[8,2,128,128]{3,2,1,0:T(8,128)(2,1)S(1)}, u32[]{:S(2)}, u32[]{:S(2)}) async-start(bf16[8,2,128,128]{3,2,1,0:T(8,128)(2,1)} %spread.1), calls=%async_computation | async-start | bytes 1048576 | tf_op jit(solution)/shard_map/all_to_all | solution.py:157
  7.5 7.2 %all-to-all-done = bf16[8,2,128,128]{3,2,1,0:T(8,128)(2,1)S(1)} async-done(((bf16[8,2,128,128]{3,2,1,0:T(8,128)(2,1)}), bf16[8,2,128,128]{3,2,1,0:T(8,128)(2,1)S(1)}, u32[]{:S(2)}, u32[]{:S(2)}) %all-to-all-start) | async-done | bytes 524320 | tf_op jit(solution)/shard_map/all_to_all | solution.py:157
  14.7 3.1 %collective-permute-start = (bf16[8,128,128]{2,1,0:T(8,128)(2,1)S(1)}, bf16[8,128,128]{2,1,0:T(8,128)(2,1)S(1)}, u32[]{:S(2)}, u32[]{:S(2)}) collective-permute-start(bf16[8,128,128]{2,1,0:T(8,128)(2,1)S(1)} %constant_dynamic-slice_fusion.2), channel_id=1, source_target_pairs={{0,8},{1,9},{2,10},{3,11},{4,12},{5,13},{6,14},{7,15},{8,0},{9,1},... | collective-permute-start | bytes 786440 | tf_op jit(solution)/shard_map/ppermute | solution.py:161
  17.8 1.1 %collective-permute-start.2 = (bf16[16,128,128]{2,1,0:T(8,128)(2,1)S(1)}, bf16[16,128,128]{2,1,0:T(8,128)(2,1)S(1)}, u32[]{:S(2)}, u32[]{:S(2)}) collective-permute-start(bf16[16,128,128]{2,1,0:T(8,128)(2,1)S(1)} %bitcast.22), channel_id=1, source_target_pairs={{0,12},{1,13},{2,14},{3,15},{4,8},{5,9},{6,10},{7,11},{8,4},{9,5},... | collective-permute-start | bytes 1572872 | tf_op jit(solution)/shard_map/ppermute | solution.py:163
  19.0 3.7 %collective-permute-done = bf16[8,128,128]{2,1,0:T(8,128)(2,1)S(1)} collective-permute-done((bf16[8,128,128]{2,1,0:T(8,128)(2,1)S(1)}, bf16[8,128,128]{2,1,0:T(8,128)(2,1)S(1)}, u32[]{:S(2)}, u32[]{:S(2)}) %collective-permute-start) | collective-permute-done | bytes 262176 | tf_op jit(solution)/shard_map/ppermute | solution.py:161
  22.8 2.0 %collective-permute-start.4 = (bf16[16,128,128]{2,1,0:T(8,128)(2,1)S(1)}, bf16[16,128,128]{2,1,0:T(8,128)(2,1)S(1)}, u32[]{:S(2)}, u32[]{:S(2)}) collective-permute-start(bf16[16,128,128]{2,1,0:T(8,128)(2,1)S(1)} %pad_maximum_fusion.1), channel_id=1, source_target_pairs={{0,16},{16,0},{32,48},{48,32},{64,80},{80,64},{96,112},{112,96},{1... | collective-permute-start | bytes 1572872 | tf_op jit(solution)/shard_map/ppermute | solution.py:166
  24.7 1.9 %collective-permute-start.3 = (bf16[8,128,128]{2,1,0:T(8,128)(2,1)S(1)}, bf16[8,128,128]{2,1,0:T(8,128)(2,1)S(1)}, u32[]{:S(2)}, u32[]{:S(2)}) collective-permute-start(bf16[8,128,128]{2,1,0:T(8,128)(2,1)S(1)} %collective-permute-done), channel_id=1, source_target_pairs={{16,32},{32,16},{48,64},{64,48},{80,96},{96,80},{112,128},{128,112... | collective-permute-start | bytes 786440 | tf_op jit(solution)/shard_map/ppermute | solution.py:164
  26.6 5.8 %collective-permute-done.3.near_2 = bf16[8,128,128]{2,1,0:T(8,128)(2,1)S(1)} collective-permute-done((bf16[8,128,128]{2,1,0:T(8,128)(2,1)S(1)}, bf16[8,128,128]{2,1,0:T(8,128)(2,1)S(1)}, u32[]{:S(2)}, u32[]{:S(2)}) %collective-permute-start.3) | collective-permute-done | bytes 262176 | tf_op jit(solution)/shard_map/ppermute | solution.py:164
  32.5 1.3 %collective-permute-start.5 = (bf16[16,128,128]{2,1,0:T(8,128)(2,1)S(1)}, bf16[16,128,128]{2,1,0:T(8,128)(2,1)S(1)}, u32[]{:S(2)}, u32[]{:S(2)}) collective-permute-start(bf16[16,128,128]{2,1,0:T(8,128)(2,1)S(1)} %pad_maximum_fusion.2), channel_id=1, source_target_pairs={{0,16},{16,0},{32,48},{48,32},{64,80},{80,64},{96,112},{112,96},{1... | collective-permute-start | bytes 1572872 | tf_op jit(solution)/shard_map/ppermute | solution.py:169
  34.0 1.5 %lift.1.split = bf16[32,256,256]{2,1,0:T(8,128)(2,1)S(1)} custom-call(s32[2,256]{1,0:T(2,128)S(1)} %bitcast.25, s32[32]{0:T(128)S(1)} %copy-done.3, bf16[16,2,128,128]{3,2,1,0:T(8,128)(2,1)S(1)} %copy-done, bf16[32,128,128]{2,1,0:T(8,128)(2,1)S(1)} %pad_maximum_fusion.plane.own), custom_call_target="tpu_custom_call" | custom-call | tf_op jit(solution)/shard_map/lift/pallas_call | solution.py:173
  35.6 2.4 %bands.1 = (f32[4,2,8,768]{3,2,1,0:T(8,128)S(1)}, f32[4,2,8,768]{3,2,1,0:T(8,128)S(1)}, f32[4,2,8,768]{3,2,1,0:T(8,128)S(1)}, f32[4,2,8,768]{3,2,1,0:T(8,128)S(1)}) custom-call(s32[2,16]{1,0:T(2,128)S(1)} %bitcast.27, s32[2,256]{1,0:T(2,128)S(1)} %bitcast.26, s32[32]{0:T(128)S(1)} %copy-done.3, bf16[32,256,256]{2,1,0:T(8,128)(2,1)S(1)} %lift.1.split, ...), custom_call_target="tpu_custom_call" | custom-call | tf_op jit(solution)/shard_map/bands/pallas_call | solution.py:182
  38.0 2.0 %collective-permute-start.6 = (f32[4,2,8,768]{3,2,1,0:T(8,128)S(1)}, f32[4,2,8,768]{3,2,1,0:T(8,128)S(1)}, u32[]{:S(2)}, u32[]{:S(2)}) collective-permute-start(f32[4,2,8,768]{3,2,1,0:T(8,128)S(1)} %get-tuple-element.18), channel_id=1, source_target_pairs={{0,1},{1,0},{2,3},{3,2},{4,5},{5,4},{6,7},{7,6},{8,9},{9,8},{10,11... | collective-permute-start | bytes 589832 | tf_op jit(solution)/shard_map/ppermute | solution.py:195
  40.0 2.7 %collective-permute-start.7 = (f32[4,2,8,768]{3,2,1,0:T(8,128)S(1)}, f32[4,2,8,768]{3,2,1,0:T(8,128)S(1)}, u32[]{:S(2)}, u32[]{:S(2)}) collective-permute-start(f32[4,2,8,768]{3,2,1,0:T(8,128)S(1)} %get-tuple-element.19), channel_id=1, source_target_pairs={{0,2},{1,3},{2,0},{3,1},{4,6},{5,7},{6,4},{7,5},{8,10},{9,11},{10,... | collective-permute-start | bytes 589832 | tf_op jit(solution)/shard_map/ppermute | solution.py:195
  42.6 0.1 collective-permute-start.8
  42.8 1.0 %collective-permute-done.6 = f32[4,2,8,768]{3,2,1,0:T(8,128)S(1)} collective-permute-done((f32[4,2,8,768]{3,2,1,0:T(8,128)S(1)}, f32[4,2,8,768]{3,2,1,0:T(8,128)S(1)}, u32[]{:S(2)}, u32[]{:S(2)}) %collective-permute-start.6) | collective-permute-done | bytes 196640 | tf_op jit(solution)/shard_map/ppermute | solution.py:195
  43.7 4.7 %collective-permute-done.7 = f32[4,2,8,768]{3,2,1,0:T(8,128)S(1)} collective-permute-done((f32[4,2,8,768]{3,2,1,0:T(8,128)S(1)}, f32[4,2,8,768]{3,2,1,0:T(8,128)S(1)}, u32[]{:S(2)}, u32[]{:S(2)}) %collective-permute-start.7) | collective-permute-done | bytes 196640 | tf_op jit(solution)/shard_map/ppermute | solution.py:195
  48.5 2.0 %collective-permute-done.8 = f32[4,2,8,768]{3,2,1,0:T(8,128)S(1)} collective-permute-done((f32[4,2,8,768]{3,2,1,0:T(8,128)S(1)}, f32[4,2,8,768]{3,2,1,0:T(8,128)S(1)}, u32[]{:S(2)}, u32[]{:S(2)}) %collective-permute-start.8) | collective-permute-done | bytes 196640 | tf_op jit(solution)/shard_map/ppermute | solution.py:195
  50.6 1.8 %collective-permute-start.11 = (f32[2,8,768]{2,1,0:T(8,128)S(1)}, f32[2,8,768]{2,1,0:T(8,128)S(1)}, u32[]{:S(2)}, u32[]{:S(2)}) collective-permute-start(f32[2,8,768]{2,1,0:T(8,128)S(1)} %get-tuple-element.22), channel_id=1, source_target_pairs={{0,12},{1,13},{2,14},{3,15},{4,8},{5,9},{6,10},{7,11},{8,4},{9,5},... | collective-permute-start | bytes 147464 | tf_op jit(solution)/shard_map/ppermute | solution.py:197
  52.4 2.3 %collective-permute-start.10 = (f32[2,8,768]{2,1,0:T(8,128)S(1)}, f32[2,8,768]{2,1,0:T(8,128)S(1)}, u32[]{:S(2)}, u32[]{:S(2)}) collective-permute-start(f32[2,8,768]{2,1,0:T(8,128)S(1)} %get-tuple-element.23), channel_id=1, source_target_pairs={{0,8},{1,9},{2,10},{3,11},{4,12},{5,13},{6,14},{7,15},{8,0},{9,1},... | collective-permute-start | bytes 147464 | tf_op jit(solution)/shard_map/ppermute | solution.py:197
  54.7 1.3 %collective-permute-done.11 = f32[2,8,768]{2,1,0:T(8,128)S(1)} collective-permute-done((f32[2,8,768]{2,1,0:T(8,128)S(1)}, f32[2,8,768]{2,1,0:T(8,128)S(1)}, u32[]{:S(2)}, u32[]{:S(2)}) %collective-permute-start.11) | collective-permute-done | bytes 49184 | tf_op jit(solution)/shard_map/ppermute | solution.py:197
  56.0 2.0 %collective-permute-done.10 = f32[2,8,768]{2,1,0:T(8,128)S(1)} collective-permute-done((f32[2,8,768]{2,1,0:T(8,128)S(1)}, f32[2,8,768]{2,1,0:T(8,128)S(1)}, u32[]{:S(2)}, u32[]{:S(2)}) %collective-permute-start.10) | collective-permute-done | bytes 49184 | tf_op jit(solution)/shard_map/ppermute | solution.py:197
  58.0 0.6 %fusion.7 = f32[2,8,6,128]{3,1,2,0:T(8,128)} fusion(f32[2,8,768]{2,1,0:T(8,128)S(1)} %collective-permute-done.11, f32[2,8,768]{2,1,0:T(8,128)S(1)} %collective-permute-done.10, f32[2,8,768]{2,1,0:T(8,128)S(1)} %collective-permute-done.9, f32[4,2,8,768]{3,2,1,0:T(8,128)S(1)} %collective-permute-done.8, f32[4,2,8,768]{3,2,1,0:T(8,128)S(1)} %collective-permute-done.7, ...), kind=kLoop, calls=%fused_computation.20 | loop fusion | flops 73728 | bytes 393216 | tf_op jit(solution)/shard_map/reshape | solution.py:198
  (22 shorter events, 0.5 us)
Async XLA Ops:
  0.0 34.0 %copy-start = (bf16[16,2,128,128]{3,2,1,0:T(8,128)(2,1)S(1)}, bf16[16,2,128,128]{3,2,1,0:T(8,128)(2,1)}, u32[]{:S(2)}) copy-start(bf16[16,2,128,128]{3,2,1,0:T(8,128)(2,1)} %a.1) | copy-start | bytes 3145732
  0.0 0.9 %copy-start.1 = (bf16[1,2,128,128]{3,2,1,0:T(8,128)(2,1)S(1)}, bf16[1,2,128,128]{3,2,1,0:T(8,128)(2,1)}, u32[]{:S(2)}) copy-start(bf16[1,2,128,128]{3,2,1,0:T(8,128)(2,1)} %shard.1) | copy-start | bytes 196612
  0.9 33.1 %copy-start.2 = (s32[256,2]{0,1:T(2,128)S(1)}, s32[256,2]{0,1:T(2,128)}, u32[]{:S(2)}) copy-start(s32[256,2]{0,1:T(2,128)} %param.8) | copy-start | bytes 6148
  0.9 33.1 %copy-start.3 = (s32[32]{0:T(128)S(1)}, s32[32]{0:T(128)}, u32[]{:S(2)}) copy-start(s32[32]{0:T(128)} %agglo.3) | copy-start | bytes 388
  1.8 12.9 %all-to-all-start = ((bf16[8,2,128,128]{3,2,1,0:T(8,128)(2,1)}), bf16[8,2,128,128]{3,2,1,0:T(8,128)(2,1)S(1)}, u32[]{:S(2)}, u32[]{:S(2)}) async-start(bf16[8,2,128,128]{3,2,1,0:T(8,128)(2,1)} %spread.1), calls=%async_computation | async-start | bytes 1048576 | tf_op jit(solution)/shard_map/all_to_all | solution.py:157
  14.7 8.0 %collective-permute-start = (bf16[8,128,128]{2,1,0:T(8,128)(2,1)S(1)}, bf16[8,128,128]{2,1,0:T(8,128)(2,1)S(1)}, u32[]{:S(2)}, u32[]{:S(2)}) collective-permute-start(bf16[8,128,128]{2,1,0:T(8,128)(2,1)S(1)} %constant_dynamic-slice_fusion.2), channel_id=1, source_target_pairs={{0,8},{1,9},{2,10},{3,11},{4,12},{5,13},{6,14},{7,15},{8,0},{9,1},... | collective-permute-start | bytes 786440 | tf_op jit(solution)/shard_map/ppermute | solution.py:161
  17.8 14.6 %collective-permute-start.2 = (bf16[16,128,128]{2,1,0:T(8,128)(2,1)S(1)}, bf16[16,128,128]{2,1,0:T(8,128)(2,1)S(1)}, u32[]{:S(2)}, u32[]{:S(2)}) collective-permute-start(bf16[16,128,128]{2,1,0:T(8,128)(2,1)S(1)} %bitcast.22), channel_id=1, source_target_pairs={{0,12},{1,13},{2,14},{3,15},{4,8},{5,9},{6,10},{7,11},{8,4},{9,5},... | collective-permute-start | bytes 1572872 | tf_op jit(solution)/shard_map/ppermute | solution.py:163
  19.0 13.4 %collective-permute-start.1 = (bf16[16,128,128]{2,1,0:T(8,128)(2,1)S(1)}, bf16[16,128,128]{2,1,0:T(8,128)(2,1)S(1)}, u32[]{:S(2)}, u32[]{:S(2)}) collective-permute-start(bf16[16,128,128]{2,1,0:T(8,128)(2,1)S(1)} %bitcast.23), channel_id=1, source_target_pairs={{0,4},{1,5},{2,6},{3,7},{4,0},{5,1},{6,2},{7,3},{8,12},{9,13},{10,... | collective-permute-start | bytes 1572872 | tf_op jit(solution)/shard_map/ppermute | solution.py:162
  22.8 9.7 %collective-permute-start.4 = (bf16[16,128,128]{2,1,0:T(8,128)(2,1)S(1)}, bf16[16,128,128]{2,1,0:T(8,128)(2,1)S(1)}, u32[]{:S(2)}, u32[]{:S(2)}) collective-permute-start(bf16[16,128,128]{2,1,0:T(8,128)(2,1)S(1)} %pad_maximum_fusion.1), channel_id=1, source_target_pairs={{0,16},{16,0},{32,48},{48,32},{64,80},{80,64},{96,112},{112,96},{1... | collective-permute-start | bytes 1572872 | tf_op jit(solution)/shard_map/ppermute | solution.py:166
  24.7 7.7 %collective-permute-start.3 = (bf16[8,128,128]{2,1,0:T(8,128)(2,1)S(1)}, bf16[8,128,128]{2,1,0:T(8,128)(2,1)S(1)}, u32[]{:S(2)}, u32[]{:S(2)}) collective-permute-start(bf16[8,128,128]{2,1,0:T(8,128)(2,1)S(1)} %collective-permute-done), channel_id=1, source_target_pairs={{16,32},{32,16},{48,64},{64,48},{80,96},{96,80},{112,128},{128,112... | collective-permute-start | bytes 786440 | tf_op jit(solution)/shard_map/ppermute | solution.py:164
  32.5 3.0 %copy-start.4 = (s32[16,2]{0,1:T(2,128)S(1)}, s32[16,2]{0,1:T(2,128)}, u32[]{:S(2)}) copy-start(s32[16,2]{0,1:T(2,128)} %param.6) | copy-start | bytes 388
  32.5 3.0 %collective-permute-start.5 = (bf16[16,128,128]{2,1,0:T(8,128)(2,1)S(1)}, bf16[16,128,128]{2,1,0:T(8,128)(2,1)S(1)}, u32[]{:S(2)}, u32[]{:S(2)}) collective-permute-start(bf16[16,128,128]{2,1,0:T(8,128)(2,1)S(1)} %pad_maximum_fusion.2), channel_id=1, source_target_pairs={{0,16},{16,0},{32,48},{48,32},{64,80},{80,64},{96,112},{112,96},{1... | collective-permute-start | bytes 1572872 | tf_op jit(solution)/shard_map/ppermute | solution.py:169
  38.0 5.8 %collective-permute-start.6 = (f32[4,2,8,768]{3,2,1,0:T(8,128)S(1)}, f32[4,2,8,768]{3,2,1,0:T(8,128)S(1)}, u32[]{:S(2)}, u32[]{:S(2)}) collective-permute-start(f32[4,2,8,768]{3,2,1,0:T(8,128)S(1)} %get-tuple-element.18), channel_id=1, source_target_pairs={{0,1},{1,0},{2,3},{3,2},{4,5},{5,4},{6,7},{7,6},{8,9},{9,8},{10,11... | collective-permute-start | bytes 589832 | tf_op jit(solution)/shard_map/ppermute | solution.py:195
  40.0 8.5 %collective-permute-start.7 = (f32[4,2,8,768]{3,2,1,0:T(8,128)S(1)}, f32[4,2,8,768]{3,2,1,0:T(8,128)S(1)}, u32[]{:S(2)}, u32[]{:S(2)}) collective-permute-start(f32[4,2,8,768]{3,2,1,0:T(8,128)S(1)} %get-tuple-element.19), channel_id=1, source_target_pairs={{0,2},{1,3},{2,0},{3,1},{4,6},{5,7},{6,4},{7,5},{8,10},{9,11},{10,... | collective-permute-start | bytes 589832 | tf_op jit(solution)/shard_map/ppermute | solution.py:195
  42.6 7.9 %collective-permute-start.8 = (f32[4,2,8,768]{3,2,1,0:T(8,128)S(1)}, f32[4,2,8,768]{3,2,1,0:T(8,128)S(1)}, u32[]{:S(2)}, u32[]{:S(2)}) collective-permute-start(f32[4,2,8,768]{3,2,1,0:T(8,128)S(1)} %get-tuple-element.20), channel_id=1, source_target_pairs={{0,3},{1,2},{2,1},{3,0},{4,7},{5,6},{6,5},{7,4},{8,11},{9,10},{10,... | collective-permute-start | bytes 589832 | tf_op jit(solution)/shard_map/ppermute | solution.py:195
  50.5 4.2 %collective-permute-start.9 = (f32[2,8,768]{2,1,0:T(8,128)S(1)}, f32[2,8,768]{2,1,0:T(8,128)S(1)}, u32[]{:S(2)}, u32[]{:S(2)}) collective-permute-start(f32[2,8,768]{2,1,0:T(8,128)S(1)} %get-tuple-element.21), channel_id=1, source_target_pairs={{0,4},{1,5},{2,6},{3,7},{4,0},{5,1},{6,2},{7,3},{8,12},{9,13},{10,... | collective-permute-start | bytes 147464 | tf_op jit(solution)/shard_map/ppermute | solution.py:197
  50.6 5.4 %collective-permute-start.11 = (f32[2,8,768]{2,1,0:T(8,128)S(1)}, f32[2,8,768]{2,1,0:T(8,128)S(1)}, u32[]{:S(2)}, u32[]{:S(2)}) collective-permute-start(f32[2,8,768]{2,1,0:T(8,128)S(1)} %get-tuple-element.22), channel_id=1, source_target_pairs={{0,12},{1,13},{2,14},{3,15},{4,8},{5,9},{6,10},{7,11},{8,4},{9,5},... | collective-permute-start | bytes 147464 | tf_op jit(solution)/shard_map/ppermute | solution.py:197
  52.4 5.6 %collective-permute-start.10 = (f32[2,8,768]{2,1,0:T(8,128)S(1)}, f32[2,8,768]{2,1,0:T(8,128)S(1)}, u32[]{:S(2)}, u32[]{:S(2)}) collective-permute-start(f32[2,8,768]{2,1,0:T(8,128)S(1)} %get-tuple-element.23), channel_id=1, source_target_pairs={{0,8},{1,9},{2,10},{3,11},{4,12},{5,13},{6,14},{7,15},{8,0},{9,1},... | collective-permute-start | bytes 147464 | tf_op jit(solution)/shard_map/ppermute | solution.py:197

commit v10 on v8

--- a/solution.py
+++ b/solution.py
@@ -15,22 +15,23 @@
     return (row + 1) // 2 % 2
 
 
-def swapped(along, k):
+def moved(along, move):
     pairs = []
     for r in range(ROWS):
-        dy, dx = ((0, k), (k, 0))[crossed(r) ^ along]
+        on_y = crossed(r) ^ along
         for y in range(SIDE):
             for x in range(SIDE):
-                pairs.append((r * ROWS + y * SIDE + x, r * ROWS + (y ^ dy) * SIDE + (x ^ dx)))
+                to = (move(y), x) if on_y else (y, move(x))
+                pairs.append((r * ROWS + y * SIDE + x, r * ROWS + to[0] * SIDE + to[1]))
     return pairs
 
 
-def first(k):
-    return swapped(0, k)
+def shift(step):
+    return moved(0, lambda c: (c + step) % SIDE)
 
 
-def second(k):
-    return swapped(1, k)
+def swap(k):
+    return moved(1, lambda c: c ^ k)
 
 
 def row_pairs(start):
@@ -47,8 +48,9 @@
 
 
 def slot_of(y, x, j, cross):
-    dy, dx = y ^ ((j % ROWS) // SIDE), x ^ (j % SIDE)
-    back, along = jnp.where(cross == 0, dy, dx), jnp.where(cross == 0, dx, dy)
+    y2, x2 = (j % ROWS) // SIDE, j % SIDE
+    back = jnp.where(cross == 0, y ^ y2, x ^ x2)
+    along = jnp.where(cross == 0, x - x2, y - y2) & 3
     return ((back >> 1) | ((back & 1) << 1)) * SIDE + along
 
 
@@ -97,11 +99,11 @@
             right = jnp.concatenate([right, right], axis=0)
             acc[band] += jnp.dot(split[i * 2 + s], right, preferred_element_type=jnp.float32)
     for rel, out in enumerate((o0, o1, o2, o3)):
-        for m in range(SIDE):
+        for m, back in enumerate((0, 1, 3, 2)):
             d = jnp.where(
                 cross == 0,
-                (y ^ m) * SIDE + (x ^ rel),
-                (y ^ rel) * SIDE + (x ^ m),
+                (y ^ back) * SIDE + ((x + rel) & 3),
+                ((y + rel) & 3) * SIDE + (x ^ back),
             )
             for k in range(2):
                 start = pl.multiple_of(k * B + d * 8, 8)
@@ -123,7 +125,7 @@
 
 def local(a_blocks, a_cols, p_blocks, p_aggs, agglo):
     shard = p_blocks[0]
-    across = lax.ppermute(shard, BOTH, second(2))
+    across = lax.ppermute(shard, BOTH, swap(2))
     beside = lax.ppermute(shard, "row", row_pairs(1))
     shard_near = pl.pallas_call(
         fetch_kernel,
@@ -134,14 +136,14 @@
         name="fetch",
     )(shard)
     trio = jnp.concatenate([shard_near, across, beside])
-    trio_1, trio_3, trio_2 = (lax.ppermute(trio, BOTH, first(k)) for k in (1, 3, 2))
+    trio_1, trio_3, trio_2 = (lax.ppermute(trio, BOTH, shift(k)) for k in (1, 3, 2))
     line, line_2, near = (
         jnp.concatenate([t[2 * n : 2 * n + 2] for t in (trio, trio_1, trio_2, trio_3)])
         for n in range(3)
     )
     lines = jnp.concatenate([line, near])
-    lines_1 = lax.ppermute(lines, BOTH, second(1))
-    lines_3 = lax.ppermute(lines, BOTH, second(3))
+    lines_1 = lax.ppermute(lines, BOTH, swap(1))
+    lines_3 = lax.ppermute(lines, BOTH, swap(3))
     near_2 = lax.ppermute(line_2, "row", row_pairs(1))
     home = jnp.concatenate([line, line_2])
     pair = lax.ppermute(home, "row", row_pairs(0))
@@ -173,10 +175,12 @@
         name="bands",
     )(cols, aggs, agglo, split, own, near, near_2, lines_1, lines_3, pair, pair_rest)
 
-    p1, p3, p2 = (lax.ppermute(o, BOTH, first(k)) for o, k in ((o1, 1), (o3, 3), (o2, 2)))
-    sums = [o0[m] + p1[m] + p2[m] + p3[m] for m in range(SIDE)]
-    q1, q3, q2 = (lax.ppermute(sums[k], BOTH, second(k)) for k in (1, 3, 2))
-    return (sums[0] + q1 + q2 + q3).reshape(2, 8, 6, B)
+    p2 = lax.ppermute(o2, BOTH, shift(2))
+    p1 = lax.ppermute(o1, BOTH, shift(1))
+    p3 = lax.ppermute(o3, BOTH, shift(3))
+    kept, sent = (o0[h] + p1[h] + p3[h] + p2[h] for h in (slice(0, 2), slice(2, 4)))
+    kept = kept + lax.ppermute(sent, BOTH, swap(3))
+    return (kept[0] + lax.ppermute(kept[1], BOTH, swap(1))).reshape(2, 8, 6, B)
 
 
 def solution(mesh):

time: 56.6 us -> 58.1 us (1.027)
  waiting for transfers between devices: 25.7 us -> 28.2 us
  starting transfers between devices: 24.3 us -> 22.8 us
    ppermute x12 -> x11, waiting for transfers between devices: 19.9 us -> 22.4 us  [the longest x3 5.16 us: local(): lax.ppermute(trio, BOTH, shift(k))]
    ppermute x12 -> x11, starting transfers between devices: 19.7 us -> 17.8 us  [the longest x3 5.37 us: local(): lax.ppermute(trio, BOTH, shift(k))]
  transfers between devices with their start and end apart: 16 -> 15, of which waited for: 10 -> 10; matrix products, arithmetic and copies ran while one was open for 0% -> 0% of each run, Pallas kernels for 3% -> 3%
where the time goes in v10:
time: 58.1 us; the launch traced here: 57.4 us
  waiting for transfers between devices  28.2 us (49%)
  starting transfers between devices  22.8 us (39%)
  Pallas kernels  3.97 us (7%)
  local copies, waits for them, and re-layouts  1.44 us (2%)
  other arithmetic  0.84 us (1%)
    ppermute x1, waiting for transfers between devices, local(): near_2 = lax.ppermute(line_2, 'row', row_pairs(1))  5.76 us
    ppermute x3, starting transfers between devices, local(): lax.ppermute(trio, BOTH, shift(k))  5.37 us
    ppermute x3, waiting for transfers between devices, local(): lax.ppermute(trio, BOTH, shift(k))  5.16 us
    ppermute x1, waiting for transfers between devices, local(): return (kept[0] + lax.ppermute(kept[1], BOTH, swap(1))).reshape(2, 8, 6, B)  4.08 us
    ppermute x1, waiting for transfers between devices, local(): kept = kept + lax.ppermute(sent, BOTH, swap(3))  4.06 us
    ppermute x1, starting transfers between devices, local(): across = lax.ppermute(shard, BOTH, swap(2))  3.11 us
    ppermute x1, waiting for transfers between devices, local(): p2 = lax.ppermute(o2, BOTH, shift(2))  2.85 us
    ppermute x1, starting transfers between devices, local(): lines_3 = lax.ppermute(lines, BOTH, swap(3))  2.46 us
  transfers between devices with their start and end apart: 15, of which 10 were waited for; matrix products, arithmetic and copies ran while one was open for 0% of the time, Pallas kernels for 3%

profile of v10, /device:TPU:96, one launch (start us, length us, event | category | flops | bytes accessed | tf_op | source)
XLA Modules:
  0.0 57.4 jit_solution(8346926921584801247)
XLA Ops:
  0.0 2.0 %collective-permute-start.1 = (bf16[2,128,128]{2,1,0:T(8,128)(2,1)}, bf16[2,128,128]{2,1,0:T(8,128)(2,1)S(1)}, u32[]{:S(2)}, u32[]{:S(2)}) collective-permute-start(bf16[2,128,128]{2,1,0:T(8,128)(2,1)} %bitcast.13), channel_id=1, source_target_pairs={{16,32},{32,16},{48,64},{64,48},{80,96},{96,80},{112,128},{128,112... | collective-permute-start | bytes 196616 | tf_op jit(solution)/shard_map/ppermute | solution.py:129
  2.0 3.1 %collective-permute-start = (bf16[2,128,128]{2,1,0:T(8,128)(2,1)}, bf16[2,128,128]{2,1,0:T(8,128)(2,1)S(1)}, u32[]{:S(2)}, u32[]{:S(2)}) collective-permute-start(bf16[2,128,128]{2,1,0:T(8,128)(2,1)} %bitcast.14), channel_id=1, source_target_pairs={{0,8},{1,9},{2,10},{3,11},{4,12},{5,13},{6,14},{7,15},{8,0},{9,1},... | collective-permute-start | bytes 196616 | tf_op jit(solution)/shard_map/ppermute | solution.py:128
  5.2 0.9 %copy-done.1 = bf16[1,2,128,128]{3,2,1,0:T(8,128)(2,1)S(1)} copy-done((bf16[1,2,128,128]{3,2,1,0:T(8,128)(2,1)S(1)}, bf16[1,2,128,128]{3,2,1,0:T(8,128)(2,1)}, u32[]{:S(2)}) %copy-start.1) | copy-done | bytes 65560
  6.1 2.1 %collective-permute-done = bf16[2,128,128]{2,1,0:T(8,128)(2,1)S(1)} collective-permute-done((bf16[2,128,128]{2,1,0:T(8,128)(2,1)}, bf16[2,128,128]{2,1,0:T(8,128)(2,1)S(1)}, u32[]{:S(2)}, u32[]{:S(2)}) %collective-permute-start) | collective-permute-done | bytes 65568 | tf_op jit(solution)/shard_map/ppermute | solution.py:128
  8.1 1.7 %collective-permute-start.2 = (bf16[6,128,128]{2,1,0:T(8,128)(2,1)S(1)}, bf16[6,128,128]{2,1,0:T(8,128)(2,1)S(1)}, u32[]{:S(2)}, u32[]{:S(2)}) collective-permute-start(bf16[6,128,128]{2,1,0:T(8,128)(2,1)S(1)} %pad_maximum_fusion.3), channel_id=1, source_target_pairs={{0,1},{1,2},{2,3},{3,0},{4,5},{5,6},{6,7},{7,4},{8,9},{9,10},{10,1... | collective-permute-start | bytes 589832 | tf_op jit(solution)/shard_map/ppermute | solution.py:139
  9.8 1.7 %collective-permute-start.4 = (bf16[6,128,128]{2,1,0:T(8,128)(2,1)S(1)}, bf16[6,128,128]{2,1,0:T(8,128)(2,1)S(1)}, u32[]{:S(2)}, u32[]{:S(2)}) collective-permute-start(bf16[6,128,128]{2,1,0:T(8,128)(2,1)S(1)} %pad_maximum_fusion.3), channel_id=1, source_target_pairs={{0,3},{1,0},{2,1},{3,2},{4,7},{5,4},{6,5},{7,6},{8,11},{9,8},{10,9... | collective-permute-start | bytes 589832 | tf_op jit(solution)/shard_map/ppermute | solution.py:139
  11.6 2.0 %collective-permute-start.3 = (bf16[6,128,128]{2,1,0:T(8,128)(2,1)S(1)}, bf16[6,128,128]{2,1,0:T(8,128)(2,1)S(1)}, u32[]{:S(2)}, u32[]{:S(2)}) collective-permute-start(bf16[6,128,128]{2,1,0:T(8,128)(2,1)S(1)} %pad_maximum_fusion.3), channel_id=1, source_target_pairs={{0,2},{1,3},{2,0},{3,1},{4,6},{5,7},{6,4},{7,5},{8,10},{9,11},{10,... | collective-permute-start | bytes 589832 | tf_op jit(solution)/shard_map/ppermute | solution.py:139
  13.5 1.6 %collective-permute-done.2 = bf16[6,128,128]{2,1,0:T(8,128)(2,1)S(1)} collective-permute-done((bf16[6,128,128]{2,1,0:T(8,128)(2,1)S(1)}, bf16[6,128,128]{2,1,0:T(8,128)(2,1)S(1)}, u32[]{:S(2)}, u32[]{:S(2)}) %collective-permute-start.2) | collective-permute-done | bytes 196640 | tf_op jit(solution)/shard_map/ppermute | solution.py:139
  15.1 3.6 %collective-permute-done.3 = bf16[6,128,128]{2,1,0:T(8,128)(2,1)S(1)} collective-permute-done((bf16[6,128,128]{2,1,0:T(8,128)(2,1)S(1)}, bf16[6,128,128]{2,1,0:T(8,128)(2,1)S(1)}, u32[]{:S(2)}, u32[]{:S(2)}) %collective-permute-start.3) | collective-permute-done | bytes 196640 | tf_op jit(solution)/shard_map/ppermute | solution.py:139
  19.6 2.5 %collective-permute-start.6 = (bf16[16,128,128]{2,1,0:T(8,128)(2,1)S(1)}, bf16[16,128,128]{2,1,0:T(8,128)(2,1)S(1)}, u32[]{:S(2)}, u32[]{:S(2)}) collective-permute-start(bf16[16,128,128]{2,1,0:T(8,128)(2,1)S(1)} %get-tuple-element.37), channel_id=1, source_target_pairs={{0,12},{1,13},{2,14},{3,15},{4,8},{5,9},{6,10},{7,11},{8,4},{9,5},... | collective-permute-start | bytes 1572872 | tf_op jit(solution)/shard_map/ppermute | solution.py:146
  22.3 1.9 %collective-permute-start.7 = (bf16[8,128,128]{2,1,0:T(8,128)(2,1)S(1)}, bf16[8,128,128]{2,1,0:T(8,128)(2,1)S(1)}, u32[]{:S(2)}, u32[]{:S(2)}) collective-permute-start(bf16[8,128,128]{2,1,0:T(8,128)(2,1)S(1)} %pad_maximum_fusion.1), channel_id=1, source_target_pairs={{16,32},{32,16},{48,64},{64,48},{80,96},{96,80},{112,128},{128,112... | collective-permute-start | bytes 786440 | tf_op jit(solution)/shard_map/ppermute | solution.py:147
  24.3 5.8 %collective-permute-done.7.near_2 = bf16[8,128,128]{2,1,0:T(8,128)(2,1)S(1)} collective-permute-done((bf16[8,128,128]{2,1,0:T(8,128)(2,1)S(1)}, bf16[8,128,128]{2,1,0:T(8,128)(2,1)S(1)}, u32[]{:S(2)}, u32[]{:S(2)}) %collective-permute-start.7) | collective-permute-done | bytes 262176 | tf_op jit(solution)/shard_map/ppermute | solution.py:147
  30.0 1.2 %collective-permute-done.5.f = bf16[16,128,128]{2,1,0:T(8,128)(2,1)S(1)} collective-permute-done((bf16[16,128,128]{2,1,0:T(8,128)(2,1)S(1)}, bf16[16,128,128]{2,1,0:T(8,128)(2,1)S(1)}, u32[]{:S(2)}, u32[]{:S(2)}) %collective-permute-start.5) | collective-permute-done | bytes 524320 | tf_op jit(solution)/shard_map/ppermute | solution.py:145
  32.1 1.5 %lift.1.split = bf16[32,256,256]{2,1,0:T(8,128)(2,1)S(1)} custom-call(s32[2,256]{1,0:T(2,128)S(1)} %bitcast.16, s32[32]{0:T(128)S(1)} %copy-done.3, bf16[16,2,128,128]{3,2,1,0:T(8,128)(2,1)S(1)} %copy-done, bf16[32,128,128]{2,1,0:T(8,128)(2,1)S(1)} %get-tuple-element.24.plane.own), custom_call_target="tpu_custom_call" | custom-call | tf_op jit(solution)/shard_map/lift/pallas_call | solution.py:156
  33.7 2.5 %bands.1 = (f32[4,2,8,768]{3,2,1,0:T(8,128)S(1)}, f32[4,2,8,768]{3,2,1,0:T(8,128)S(1)}, f32[4,2,8,768]{3,2,1,0:T(8,128)S(1)}, f32[4,2,8,768]{3,2,1,0:T(8,128)S(1)}) custom-call(s32[2,16]{1,0:T(2,128)S(1)} %bitcast.18, s32[2,256]{1,0:T(2,128)S(1)} %bitcast.17, s32[32]{0:T(128)S(1)} %copy-done.3, bf16[32,256,256]{2,1,0:T(8,128)(2,1)S(1)} %lift.1.split, ...), custom_call_target="tpu_custom_call" | custom-call | tf_op jit(solution)/shard_map/bands/pallas_call | solution.py:165
  36.1 2.0 %collective-permute-start.10 = (f32[4,2,8,768]{3,2,1,0:T(8,128)S(1)}, f32[4,2,8,768]{3,2,1,0:T(8,128)S(1)}, u32[]{:S(2)}, u32[]{:S(2)}) collective-permute-start(f32[4,2,8,768]{3,2,1,0:T(8,128)S(1)} %get-tuple-element.18), channel_id=1, source_target_pairs={{0,1},{1,2},{2,3},{3,0},{4,5},{5,6},{6,7},{7,4},{8,9},{9,10},{10,1... | collective-permute-start | bytes 589832 | tf_op jit(solution)/shard_map/ppermute | solution.py:179
  38.1 1.3 %collective-permute-start.11 = (f32[4,2,8,768]{3,2,1,0:T(8,128)S(1)}, f32[4,2,8,768]{3,2,1,0:T(8,128)S(1)}, u32[]{:S(2)}, u32[]{:S(2)}) collective-permute-start(f32[4,2,8,768]{3,2,1,0:T(8,128)S(1)} %get-tuple-element.19), channel_id=1, source_target_pairs={{0,3},{1,0},{2,1},{3,2},{4,7},{5,4},{6,5},{7,6},{8,11},{9,8},{10,9... | collective-permute-start | bytes 589832 | tf_op jit(solution)/shard_map/ppermute | solution.py:180
  39.5 1.4 %collective-permute-start.12 = (f32[4,2,8,768]{3,2,1,0:T(8,128)S(1)}, f32[4,2,8,768]{3,2,1,0:T(8,128)S(1)}, u32[]{:S(2)}, u32[]{:S(2)}) collective-permute-start(f32[4,2,8,768]{3,2,1,0:T(8,128)S(1)} %get-tuple-element.20), channel_id=1, source_target_pairs={{0,2},{1,3},{2,0},{3,1},{4,6},{5,7},{6,4},{7,5},{8,10},{9,11},{10,... | collective-permute-start | bytes 589832 | tf_op jit(solution)/shard_map/ppermute | solution.py:178
  40.8 2.3 %collective-permute-done.10 = f32[4,2,8,768]{3,2,1,0:T(8,128)S(1)} collective-permute-done((f32[4,2,8,768]{3,2,1,0:T(8,128)S(1)}, f32[4,2,8,768]{3,2,1,0:T(8,128)S(1)}, u32[]{:S(2)}, u32[]{:S(2)}) %collective-permute-start.10) | collective-permute-done | bytes 196640 | tf_op jit(solution)/shard_map/ppermute | solution.py:179
  43.1 0.7 %collective-permute-done.11 = f32[4,2,8,768]{3,2,1,0:T(8,128)S(1)} collective-permute-done((f32[4,2,8,768]{3,2,1,0:T(8,128)S(1)}, f32[4,2,8,768]{3,2,1,0:T(8,128)S(1)}, u32[]{:S(2)}, u32[]{:S(2)}) %collective-permute-start.11) | collective-permute-done | bytes 196640 | tf_op jit(solution)/shard_map/ppermute | solution.py:180
  43.8 2.9 %collective-permute-done.12 = f32[4,2,8,768]{3,2,1,0:T(8,128)S(1)} collective-permute-done((f32[4,2,8,768]{3,2,1,0:T(8,128)S(1)}, f32[4,2,8,768]{3,2,1,0:T(8,128)S(1)}, u32[]{:S(2)}, u32[]{:S(2)}) %collective-permute-start.12) | collective-permute-done | bytes 196640 | tf_op jit(solution)/shard_map/ppermute | solution.py:178
  46.7 1.9 %collective-permute-start.13 = (f32[2,2,8,768]{3,2,1,0:T(8,128)S(1)}, f32[2,2,8,768]{3,2,1,0:T(8,128)S(1)}, u32[]{:S(2)}, u32[]{:S(2)}) collective-permute-start(f32[2,2,8,768]{3,2,1,0:T(8,128)S(1)} %slice_add_fusion), channel_id=1, source_target_pairs={{0,12},{1,13},{2,14},{3,15},{4,8},{5,9},{6,10},{7,11},{8,4},{9,5},... | collective-permute-start | bytes 294920 | tf_op jit(solution)/shard_map/ppermute | solution.py:182
  48.5 4.1 %collective-permute-done.13 = f32[2,2,8,768]{3,2,1,0:T(8,128)S(1)} collective-permute-done((f32[2,2,8,768]{3,2,1,0:T(8,128)S(1)}, f32[2,2,8,768]{3,2,1,0:T(8,128)S(1)}, u32[]{:S(2)}, u32[]{:S(2)}) %collective-permute-start.13) | collective-permute-done | bytes 98336 | tf_op jit(solution)/shard_map/ppermute | solution.py:182
  52.7 4.1 %collective-permute-done.14 = f32[2,8,768]{2,1,0:T(8,128)S(1)} collective-permute-done((f32[2,8,768]{2,1,0:T(8,128)S(1)}, f32[2,8,768]{2,1,0:T(8,128)S(1)}, u32[]{:S(2)}, u32[]{:S(2)}) %collective-permute-start.14) | collective-permute-done | bytes 49184 | tf_op jit(solution)/shard_map/ppermute | solution.py:183
  (39 shorter events, 2.8 us)
Async XLA Ops:
  0.0 32.1 %copy-start = (bf16[16,2,128,128]{3,2,1,0:T(8,128)(2,1)S(1)}, bf16[16,2,128,128]{3,2,1,0:T(8,128)(2,1)}, u32[]{:S(2)}) copy-start(bf16[16,2,128,128]{3,2,1,0:T(8,128)(2,1)} %a.1) | copy-start | bytes 3145732
  0.0 6.0 %collective-permute-start.1 = (bf16[2,128,128]{2,1,0:T(8,128)(2,1)}, bf16[2,128,128]{2,1,0:T(8,128)(2,1)S(1)}, u32[]{:S(2)}, u32[]{:S(2)}) collective-permute-start(bf16[2,128,128]{2,1,0:T(8,128)(2,1)} %bitcast.13), channel_id=1, source_target_pairs={{16,32},{32,16},{48,64},{64,48},{80,96},{96,80},{112,128},{128,112... | collective-permute-start | bytes 196616 | tf_op jit(solution)/shard_map/ppermute | solution.py:129
  2.0 6.1 %collective-permute-start = (bf16[2,128,128]{2,1,0:T(8,128)(2,1)}, bf16[2,128,128]{2,1,0:T(8,128)(2,1)S(1)}, u32[]{:S(2)}, u32[]{:S(2)}) collective-permute-start(bf16[2,128,128]{2,1,0:T(8,128)(2,1)} %bitcast.14), channel_id=1, source_target_pairs={{0,8},{1,9},{2,10},{3,11},{4,12},{5,13},{6,14},{7,15},{8,0},{9,1},... | collective-permute-start | bytes 196616 | tf_op jit(solution)/shard_map/ppermute | solution.py:128
  5.2 0.9 %copy-start.1 = (bf16[1,2,128,128]{3,2,1,0:T(8,128)(2,1)S(1)}, bf16[1,2,128,128]{3,2,1,0:T(8,128)(2,1)}, u32[]{:S(2)}) copy-start(bf16[1,2,128,128]{3,2,1,0:T(8,128)(2,1)} %param.7) | copy-start | bytes 196612
  6.0 26.1 %copy-start.2 = (s32[256,2]{0,1:T(2,128)S(1)}, s32[256,2]{0,1:T(2,128)}, u32[]{:S(2)}) copy-start(s32[256,2]{0,1:T(2,128)} %param.8) | copy-start | bytes 6148
  6.0 26.1 %copy-start.3 = (s32[32]{0:T(128)S(1)}, s32[32]{0:T(128)}, u32[]{:S(2)}) copy-start(s32[32]{0:T(128)} %agglo.3) | copy-start | bytes 388
  8.1 7.0 %collective-permute-start.2 = (bf16[6,128,128]{2,1,0:T(8,128)(2,1)S(1)}, bf16[6,128,128]{2,1,0:T(8,128)(2,1)S(1)}, u32[]{:S(2)}, u32[]{:S(2)}) collective-permute-start(bf16[6,128,128]{2,1,0:T(8,128)(2,1)S(1)} %pad_maximum_fusion.3), channel_id=1, source_target_pairs={{0,1},{1,2},{2,3},{3,0},{4,5},{5,6},{6,7},{7,4},{8,9},{9,10},{10,1... | collective-permute-start | bytes 589832 | tf_op jit(solution)/shard_map/ppermute | solution.py:139
  9.8 8.9 %collective-permute-start.4 = (bf16[6,128,128]{2,1,0:T(8,128)(2,1)S(1)}, bf16[6,128,128]{2,1,0:T(8,128)(2,1)S(1)}, u32[]{:S(2)}, u32[]{:S(2)}) collective-permute-start(bf16[6,128,128]{2,1,0:T(8,128)(2,1)S(1)} %pad_maximum_fusion.3), channel_id=1, source_target_pairs={{0,3},{1,0},{2,1},{3,2},{4,7},{5,4},{6,5},{7,6},{8,11},{9,8},{10,9... | collective-permute-start | bytes 589832 | tf_op jit(solution)/shard_map/ppermute | solution.py:139
  11.6 7.2 %collective-permute-start.3 = (bf16[6,128,128]{2,1,0:T(8,128)(2,1)S(1)}, bf16[6,128,128]{2,1,0:T(8,128)(2,1)S(1)}, u32[]{:S(2)}, u32[]{:S(2)}) collective-permute-start(bf16[6,128,128]{2,1,0:T(8,128)(2,1)S(1)} %pad_maximum_fusion.3), channel_id=1, source_target_pairs={{0,2},{1,3},{2,0},{3,1},{4,6},{5,7},{6,4},{7,5},{8,10},{9,11},{10,... | collective-permute-start | bytes 589832 | tf_op jit(solution)/shard_map/ppermute | solution.py:139
  19.1 10.9 %collective-permute-start.8 = (bf16[16,128,128]{2,1,0:T(8,128)(2,1)S(1)}, bf16[16,128,128]{2,1,0:T(8,128)(2,1)S(1)}, u32[]{:S(2)}, u32[]{:S(2)}) collective-permute-start(bf16[16,128,128]{2,1,0:T(8,128)(2,1)S(1)} %get-tuple-element.38), channel_id=1, source_target_pairs={{0,16},{16,0},{32,48},{48,32},{64,80},{80,64},{96,112},{112,96},{1... | collective-permute-start | bytes 1572872 | tf_op jit(solution)/shard_map/ppermute | solution.py:149
  19.6 10.4 %collective-permute-start.6 = (bf16[16,128,128]{2,1,0:T(8,128)(2,1)S(1)}, bf16[16,128,128]{2,1,0:T(8,128)(2,1)S(1)}, u32[]{:S(2)}, u32[]{:S(2)}) collective-permute-start(bf16[16,128,128]{2,1,0:T(8,128)(2,1)S(1)} %get-tuple-element.37), channel_id=1, source_target_pairs={{0,12},{1,13},{2,14},{3,15},{4,8},{5,9},{6,10},{7,11},{8,4},{9,5},... | collective-permute-start | bytes 1572872 | tf_op jit(solution)/shard_map/ppermute | solution.py:146
  22.1 9.2 %collective-permute-start.5 = (bf16[16,128,128]{2,1,0:T(8,128)(2,1)S(1)}, bf16[16,128,128]{2,1,0:T(8,128)(2,1)S(1)}, u32[]{:S(2)}, u32[]{:S(2)}) collective-permute-start(bf16[16,128,128]{2,1,0:T(8,128)(2,1)S(1)} %get-tuple-element.37), channel_id=1, source_target_pairs={{0,4},{1,5},{2,6},{3,7},{4,0},{5,1},{6,2},{7,3},{8,12},{9,13},{10,... | collective-permute-start | bytes 1572872 | tf_op jit(solution)/shard_map/ppermute | solution.py:145
  22.3 7.7 %collective-permute-start.7 = (bf16[8,128,128]{2,1,0:T(8,128)(2,1)S(1)}, bf16[8,128,128]{2,1,0:T(8,128)(2,1)S(1)}, u32[]{:S(2)}, u32[]{:S(2)}) collective-permute-start(bf16[8,128,128]{2,1,0:T(8,128)(2,1)S(1)} %pad_maximum_fusion.1), channel_id=1, source_target_pairs={{16,32},{32,16},{48,64},{64,48},{80,96},{96,80},{112,128},{128,112... | collective-permute-start | bytes 786440 | tf_op jit(solution)/shard_map/ppermute | solution.py:147
  31.3 2.3 %copy-start.4 = (s32[16,2]{0,1:T(2,128)S(1)}, s32[16,2]{0,1:T(2,128)}, u32[]{:S(2)}) copy-start(s32[16,2]{0,1:T(2,128)} %param.6) | copy-start | bytes 388
  31.5 2.2 %collective-permute-start.9 = (bf16[16,128,128]{2,1,0:T(8,128)(2,1)S(1)}, bf16[16,128,128]{2,1,0:T(8,128)(2,1)S(1)}, u32[]{:S(2)}, u32[]{:S(2)}) collective-permute-start(bf16[16,128,128]{2,1,0:T(8,128)(2,1)S(1)} %pad_maximum_fusion), channel_id=1, source_target_pairs={{0,16},{16,0},{32,48},{48,32},{64,80},{80,64},{96,112},{112,96},{1... | collective-permute-start | bytes 1572872 | tf_op jit(solution)/shard_map/ppermute | solution.py:152
  36.1 7.0 %collective-permute-start.10 = (f32[4,2,8,768]{3,2,1,0:T(8,128)S(1)}, f32[4,2,8,768]{3,2,1,0:T(8,128)S(1)}, u32[]{:S(2)}, u32[]{:S(2)}) collective-permute-start(f32[4,2,8,768]{3,2,1,0:T(8,128)S(1)} %get-tuple-element.18), channel_id=1, source_target_pairs={{0,1},{1,2},{2,3},{3,0},{4,5},{5,6},{6,7},{7,4},{8,9},{9,10},{10,1... | collective-permute-start | bytes 589832 | tf_op jit(solution)/shard_map/ppermute | solution.py:179
  38.1 5.7 %collective-permute-start.11 = (f32[4,2,8,768]{3,2,1,0:T(8,128)S(1)}, f32[4,2,8,768]{3,2,1,0:T(8,128)S(1)}, u32[]{:S(2)}, u32[]{:S(2)}) collective-permute-start(f32[4,2,8,768]{3,2,1,0:T(8,128)S(1)} %get-tuple-element.19), channel_id=1, source_target_pairs={{0,3},{1,0},{2,1},{3,2},{4,7},{5,4},{6,5},{7,6},{8,11},{9,8},{10,9... | collective-permute-start | bytes 589832 | tf_op jit(solution)/shard_map/ppermute | solution.py:180
  39.5 7.2 %collective-permute-start.12 = (f32[4,2,8,768]{3,2,1,0:T(8,128)S(1)}, f32[4,2,8,768]{3,2,1,0:T(8,128)S(1)}, u32[]{:S(2)}, u32[]{:S(2)}) collective-permute-start(f32[4,2,8,768]{3,2,1,0:T(8,128)S(1)} %get-tuple-element.20), channel_id=1, source_target_pairs={{0,2},{1,3},{2,0},{3,1},{4,6},{5,7},{6,4},{7,5},{8,10},{9,11},{10,... | collective-permute-start | bytes 589832 | tf_op jit(solution)/shard_map/ppermute | solution.py:178
  46.7 5.9 %collective-permute-start.13 = (f32[2,2,8,768]{3,2,1,0:T(8,128)S(1)}, f32[2,2,8,768]{3,2,1,0:T(8,128)S(1)}, u32[]{:S(2)}, u32[]{:S(2)}) collective-permute-start(f32[2,2,8,768]{3,2,1,0:T(8,128)S(1)} %slice_add_fusion), channel_id=1, source_target_pairs={{0,12},{1,13},{2,14},{3,15},{4,8},{5,9},{6,10},{7,11},{8,4},{9,5},... | collective-permute-start | bytes 294920 | tf_op jit(solution)/shard_map/ppermute | solution.py:182
  52.6 4.2 %collective-permute-start.14 = (f32[2,8,768]{2,1,0:T(8,128)S(1)}, f32[2,8,768]{2,1,0:T(8,128)S(1)}, u32[]{:S(2)}, u32[]{:S(2)}) collective-permute-start(f32[2,8,768]{2,1,0:T(8,128)S(1)} %slice_bitcast_fusion), channel_id=1, source_target_pairs={{0,4},{1,5},{2,6},{3,7},{4,0},{5,1},{6,2},{7,3},{8,12},{9,13},{10,... | collective-permute-start | bytes 147464 | tf_op jit(solution)/shard_map/ppermute | solution.py:183

commit v11 on v10

--- a/solution.py
+++ b/solution.py
@@ -1,3 +1,5 @@
+import functools
+
 import jax
 import jax.numpy as jnp
 from jax import lax
@@ -26,8 +28,8 @@
     return pairs
 
 
-def shift(step):
-    return moved(0, lambda c: (c + step) % SIDE)
+def shift(step, along=0):
+    return moved(along, lambda c: (c + step) % SIDE)
 
 
 def swap(k):
@@ -58,12 +60,19 @@
     near[...] = shard[...]
 
 
-def lift_kernel(aggs, agglo, a, plane, split):
+def row_at(y, x, slot, cross):
+    back, along = (0, 2, 1, 3)[slot // SIDE], slot % SIDE
+    y2 = jnp.where(cross == 0, y ^ back, (y - along) & 3)
+    x2 = jnp.where(cross == 0, (x - along) & 3, x ^ back)
+    return y2 * SIDE + x2
+
+
+def lift_kernel(first_slot, aggs, agglo, a, blocks, split):
     row, cross, y, x = place()
-    for i in range(ROWS):
+    for p in range(ROWS // 2):
+        i = row_at(y, x, first_slot + p, cross)
         swap = agglo[aggs[0, row * ROWS + i]] & 1
-        spot = slot_of(y, x, i, cross) * 2
-        left = jnp.concatenate([plane[spot + swap], plane[spot + 1 - swap]], axis=1)
+        left = jnp.concatenate([blocks[p * 2 + swap], blocks[p * 2 + 1 - swap]], axis=1)
         right = jnp.concatenate([a[i, 0], a[i, 1]], axis=1)
         lifted = lax.dot_general(
             left, right, (((0,), (0,)), ((), ())), preferred_element_type=jnp.float32
@@ -71,15 +80,17 @@
         high = lifted.astype(jnp.bfloat16)
         low = (lifted - high.astype(jnp.float32)).astype(jnp.bfloat16)
         for s in range(2):
-            split[i * 2 + s, :, :B] = high[:, s * B : (s + 1) * B]
-            split[i * 2 + s, :, B:] = low[:, s * B : (s + 1) * B]
+            split[p * 2 + s, :, :B] = high[:, s * B : (s + 1) * B]
+            split[p * 2 + s, :, B:] = low[:, s * B : (s + 1) * B]
 
 
 def band_kernel(
-    cols, aggs, agglo, split, own, near, near_2, f, b, pair, pair_rest, o0, o1, o2, o3, blocks, acc
+    cols, aggs, agglo, split, split_rest, home, rest, near, near_2, f, b, pair, pair_rest,
+    o0, o1, o2, o3, blocks, acc
 ):
     row, cross, y, x = place()
-    blocks[0:32] = own[...]
+    blocks[0:16] = home[...]
+    blocks[16:32] = rest[...]
     blocks[32:40] = near[...]
     blocks[40:48] = near_2[...]
     blocks[48:56] = f[8:16]
@@ -88,7 +99,9 @@
     blocks[80:96] = pair_rest[...]
     acc[...] = jnp.zeros_like(acc)
     pair_band = 2 - 2 * (row % 2)
-    for i in range(ROWS):
+    for p in range(ROWS):
+        i = row_at(y, x, p, cross)
+        part = split if p < ROWS // 2 else split_rest
         for s in range(2):
             j = cols[s, i]
             swap = agglo[aggs[0, j]] & 1
@@ -97,13 +110,13 @@
             spot = base + slot_of(y, x, j, jnp.where(band == pair_band, 1 - cross, cross)) * 2
             right = jnp.concatenate([blocks[spot + swap], blocks[spot + 1 - swap]], axis=1)
             right = jnp.concatenate([right, right], axis=0)
-            acc[band] += jnp.dot(split[i * 2 + s], right, preferred_element_type=jnp.float32)
+            acc[band] += jnp.dot(part[p % 8 * 2 + s], right, preferred_element_type=jnp.float32)
     for rel, out in enumerate((o0, o1, o2, o3)):
-        for m, back in enumerate((0, 1, 3, 2)):
+        for m in range(SIDE):
             d = jnp.where(
                 cross == 0,
-                (y ^ back) * SIDE + ((x + rel) & 3),
-                ((y + rel) & 3) * SIDE + (x ^ back),
+                ((y + m) & 3) * SIDE + ((x + rel) & 3),
+                ((y + rel) & 3) * SIDE + ((x + m) & 3),
             )
             for k in range(2):
                 start = pl.multiple_of(k * B + d * 8, 8)
@@ -147,25 +160,30 @@
     near_2 = lax.ppermute(line_2, "row", row_pairs(1))
     home = jnp.concatenate([line, line_2])
     pair = lax.ppermute(home, "row", row_pairs(0))
-    lines_1, lines_3, near_2, pair = lax.optimization_barrier((lines_1, lines_3, near_2, pair))
+    cols, aggs = a_cols.T, p_aggs.T
+
+    def lift(first_slot, blocks, name):
+        return pl.pallas_call(
+            functools.partial(lift_kernel, first_slot),
+            out_shape=jax.ShapeDtypeStruct((ROWS, 256, 256), jnp.bfloat16),
+            in_specs=[smem(), smem(), vmem(), vmem()],
+            out_specs=vmem(),
+            compiler_params=params(16),
+            name=name,
+        )(aggs, agglo, a_blocks, blocks)
+
+    split = lift(0, home, "lift_home")
+    lines_1, lines_3, near_2, pair, split = lax.optimization_barrier(
+        (lines_1, lines_3, near_2, pair, split)
+    )
     rest = jnp.concatenate([lines_1[:8], lines_3[:8]])
     pair_rest = lax.ppermute(rest, "row", row_pairs(0))
-    own = jnp.concatenate([home, rest])
-
-    cols, aggs = a_cols.T, p_aggs.T
-    split = pl.pallas_call(
-        lift_kernel,
-        out_shape=jax.ShapeDtypeStruct((2 * ROWS, 256, 256), jnp.bfloat16),
-        in_specs=[smem(), smem(), vmem(), vmem()],
-        out_specs=vmem(),
-        compiler_params=params(16),
-        name="lift",
-    )(aggs, agglo, a_blocks, own)
+    split_rest = lift(ROWS // 2, rest, "lift_rest")
     piece = jax.ShapeDtypeStruct((SIDE, 2, 8, 768), jnp.float32)
     o0, o1, o2, o3 = pl.pallas_call(
         band_kernel,
         out_shape=[piece] * 4,
-        in_specs=[smem()] * 3 + [vmem()] * 8,
+        in_specs=[smem()] * 3 + [vmem()] * 10,
         out_specs=[vmem()] * 4,
         scratch_shapes=[
             pltpu.VMEM((96, B, B), jnp.bfloat16),
@@ -173,14 +191,16 @@
         ],
         compiler_params=params(24),
         name="bands",
-    )(cols, aggs, agglo, split, own, near, near_2, lines_1, lines_3, pair, pair_rest)
+    )(cols, aggs, agglo, split, split_rest, home, rest, near, near_2, lines_1, lines_3, pair, pair_rest)
 
     p2 = lax.ppermute(o2, BOTH, shift(2))
     p1 = lax.ppermute(o1, BOTH, shift(1))
     p3 = lax.ppermute(o3, BOTH, shift(3))
-    kept, sent = (o0[h] + p1[h] + p3[h] + p2[h] for h in (slice(0, 2), slice(2, 4)))
-    kept = kept + lax.ppermute(sent, BOTH, swap(3))
-    return (kept[0] + lax.ppermute(kept[1], BOTH, swap(1))).reshape(2, 8, 6, B)
+    kept, to_1, to_2, to_3 = (o0[m] + p1[m] + p3[m] + p2[m] for m in range(SIDE))
+    q1 = lax.ppermute(to_1, BOTH, shift(1, 1))
+    q3 = lax.ppermute(to_3, BOTH, shift(3, 1))
+    q2 = lax.ppermute(to_2, BOTH, shift(2, 1))
+    return (kept + q1 + q3 + q2).reshape(2, 8, 6, B)
 
 
 def solution(mesh):

time: 58.1 us -> 54.6 us (0.940)
  waiting for transfers between devices: 28.2 us -> 22.3 us
  starting transfers between devices: 22.8 us -> 25.2 us
  Pallas kernels: 3.97 us -> 4.65 us
    ppermute x2 -> x3, waiting for transfers between devices: 8.14 us -> 2.82 us  [the longest x1 2.1 us: local(): q2 = lax.ppermute(to_2, BOTH, shift(2, 1))]
    ppermute x2 -> x3, starting transfers between devices: 1.94 us -> 4.65 us  [the longest x1 1.88 us: local(): q1 = lax.ppermute(to_1, BOTH, shift(1, 1))]
    ppermute x1, waiting for transfers between devices: 5.76 us -> 4.45 us  [local(): near_2 = lax.ppermute(line_2, 'row', row_pairs(1))]
    pallas_call x1 -> x2, Pallas kernels: 1.52 us -> 2.26 us  [lift(): pl.pallas_call(functools.partial(lift_kernel, first_slot), out_shape=jax....]
    ppermute x1, starting transfers between devices: 1.36 us -> 0.78 us  [local(): p2 = lax.ppermute(o2, BOTH, shift(2))]
    ppermute x1, waiting for transfers between devices: 2.28 us -> 2.86 us  [local(): p1 = lax.ppermute(o1, BOTH, shift(1))]
  transfers between devices with their start and end apart: 15 -> 16, of which waited for: 10 -> 11; matrix products, arithmetic and copies ran while one was open for 0% -> 0% of each run, Pallas kernels for 3% -> 4%
where the time goes in v11:
time: 54.6 us; the launch traced here: 54.3 us
  starting transfers between devices  25.2 us (46%)
  waiting for transfers between devices  22.3 us (41%)
  Pallas kernels  4.65 us (9%)
  local copies, waits for them, and re-layouts  1.18 us (2%)
  other arithmetic  0.83 us (2%)
    ppermute x3, starting transfers between devices, local(): lax.ppermute(trio, BOTH, shift(k))  5.3 us
    ppermute x3, waiting for transfers between devices, local(): lax.ppermute(trio, BOTH, shift(k))  5.18 us
    ppermute x1, waiting for transfers between devices, local(): near_2 = lax.ppermute(line_2, 'row', row_pairs(1))  4.45 us
    ppermute x1, starting transfers between devices, local(): across = lax.ppermute(shard, BOTH, swap(2))  3.11 us
    ppermute x1, waiting for transfers between devices, local(): p2 = lax.ppermute(o2, BOTH, shift(2))  2.88 us
    ppermute x1, waiting for transfers between devices, local(): p1 = lax.ppermute(o1, BOTH, shift(1))  2.86 us
    ppermute x1, starting transfers between devices, local(): lines_3 = lax.ppermute(lines, BOTH, swap(3))  2.84 us
    pallas_call x1, Pallas kernels, local(): pl.pallas_call(band_kernel, out_shape=[piece] * 4, in_specs=[smem()] * 3...  2.38 us
  transfers between devices with their start and end apart: 16, of which 11 were waited for; matrix products, arithmetic and copies ran while one was open for 0% of the time, Pallas kernels for 4%

profile of v11, /device:TPU:96, one launch (start us, length us, event | category | flops | bytes accessed | tf_op | source)
XLA Modules:
  0.0 54.3 jit_solution(6930836591614963942)
XLA Ops:
  0.0 2.0 %collective-permute-start.1 = (bf16[2,128,128]{2,1,0:T(8,128)(2,1)}, bf16[2,128,128]{2,1,0:T(8,128)(2,1)S(1)}, u32[]{:S(2)}, u32[]{:S(2)}) collective-permute-start(bf16[2,128,128]{2,1,0:T(8,128)(2,1)} %bitcast.21), channel_id=1, source_target_pairs={{16,32},{32,16},{48,64},{64,48},{80,96},{96,80},{112,128},{128,112... | collective-permute-start | bytes 196616 | tf_op jit(solution)/shard_map/ppermute | solution.py:142
  2.0 3.1 %collective-permute-start = (bf16[2,128,128]{2,1,0:T(8,128)(2,1)}, bf16[2,128,128]{2,1,0:T(8,128)(2,1)S(1)}, u32[]{:S(2)}, u32[]{:S(2)}) collective-permute-start(bf16[2,128,128]{2,1,0:T(8,128)(2,1)} %bitcast.22), channel_id=1, source_target_pairs={{0,8},{1,9},{2,10},{3,11},{4,12},{5,13},{6,14},{7,15},{8,0},{9,1},... | collective-permute-start | bytes 196616 | tf_op jit(solution)/shard_map/ppermute | solution.py:141
  5.2 0.9 %copy-done.1 = bf16[1,2,128,128]{3,2,1,0:T(8,128)(2,1)S(1)} copy-done((bf16[1,2,128,128]{3,2,1,0:T(8,128)(2,1)S(1)}, bf16[1,2,128,128]{3,2,1,0:T(8,128)(2,1)}, u32[]{:S(2)}) %copy-start.1) | copy-done | bytes 65560
  6.1 2.1 %collective-permute-done = bf16[2,128,128]{2,1,0:T(8,128)(2,1)S(1)} collective-permute-done((bf16[2,128,128]{2,1,0:T(8,128)(2,1)}, bf16[2,128,128]{2,1,0:T(8,128)(2,1)S(1)}, u32[]{:S(2)}, u32[]{:S(2)}) %collective-permute-start) | collective-permute-done | bytes 65568 | tf_op jit(solution)/shard_map/ppermute | solution.py:141
  8.1 1.7 %collective-permute-start.2 = (bf16[6,128,128]{2,1,0:T(8,128)(2,1)S(1)}, bf16[6,128,128]{2,1,0:T(8,128)(2,1)S(1)}, u32[]{:S(2)}, u32[]{:S(2)}) collective-permute-start(bf16[6,128,128]{2,1,0:T(8,128)(2,1)S(1)} %pad_maximum_fusion.3), channel_id=1, source_target_pairs={{0,1},{1,2},{2,3},{3,0},{4,5},{5,6},{6,7},{7,4},{8,9},{9,10},{10,1... | collective-permute-start | bytes 589832 | tf_op jit(solution)/shard_map/ppermute | solution.py:152
  9.8 1.7 %collective-permute-start.4 = (bf16[6,128,128]{2,1,0:T(8,128)(2,1)S(1)}, bf16[6,128,128]{2,1,0:T(8,128)(2,1)S(1)}, u32[]{:S(2)}, u32[]{:S(2)}) collective-permute-start(bf16[6,128,128]{2,1,0:T(8,128)(2,1)S(1)} %pad_maximum_fusion.3), channel_id=1, source_target_pairs={{0,3},{1,0},{2,1},{3,2},{4,7},{5,4},{6,5},{7,6},{8,11},{9,8},{10,9... | collective-permute-start | bytes 589832 | tf_op jit(solution)/shard_map/ppermute | solution.py:152
  11.5 2.0 %collective-permute-start.3 = (bf16[6,128,128]{2,1,0:T(8,128)(2,1)S(1)}, bf16[6,128,128]{2,1,0:T(8,128)(2,1)S(1)}, u32[]{:S(2)}, u32[]{:S(2)}) collective-permute-start(bf16[6,128,128]{2,1,0:T(8,128)(2,1)S(1)} %pad_maximum_fusion.3), channel_id=1, source_target_pairs={{0,2},{1,3},{2,0},{3,1},{4,6},{5,7},{6,4},{7,5},{8,10},{9,11},{10,... | collective-permute-start | bytes 589832 | tf_op jit(solution)/shard_map/ppermute | solution.py:152
  13.4 1.7 %collective-permute-done.2 = bf16[6,128,128]{2,1,0:T(8,128)(2,1)S(1)} collective-permute-done((bf16[6,128,128]{2,1,0:T(8,128)(2,1)S(1)}, bf16[6,128,128]{2,1,0:T(8,128)(2,1)S(1)}, u32[]{:S(2)}, u32[]{:S(2)}) %collective-permute-start.2) | collective-permute-done | bytes 196640 | tf_op jit(solution)/shard_map/ppermute | solution.py:152
  15.1 3.5 %collective-permute-done.3 = bf16[6,128,128]{2,1,0:T(8,128)(2,1)S(1)} collective-permute-done((bf16[6,128,128]{2,1,0:T(8,128)(2,1)S(1)}, bf16[6,128,128]{2,1,0:T(8,128)(2,1)S(1)}, u32[]{:S(2)}, u32[]{:S(2)}) %collective-permute-start.3) | collective-permute-done | bytes 196640 | tf_op jit(solution)/shard_map/ppermute | solution.py:152
  18.9 2.8 %collective-permute-start.6 = (bf16[16,128,128]{2,1,0:T(8,128)(2,1)S(1)}, bf16[16,128,128]{2,1,0:T(8,128)(2,1)S(1)}, u32[]{:S(2)}, u32[]{:S(2)}) collective-permute-start(bf16[16,128,128]{2,1,0:T(8,128)(2,1)S(1)} %get-tuple-element.36), channel_id=1, source_target_pairs={{0,12},{1,13},{2,14},{3,15},{4,8},{5,9},{6,10},{7,11},{8,4},{9,5},... | collective-permute-start | bytes 1572872 | tf_op jit(solution)/shard_map/ppermute | solution.py:159
  22.3 2.1 %collective-permute-start.7 = (bf16[8,128,128]{2,1,0:T(8,128)(2,1)S(1)}, bf16[8,128,128]{2,1,0:T(8,128)(2,1)S(1)}, u32[]{:S(2)}, u32[]{:S(2)}) collective-permute-start(bf16[8,128,128]{2,1,0:T(8,128)(2,1)S(1)} %pad_maximum_fusion.1), channel_id=1, source_target_pairs={{16,32},{32,16},{48,64},{64,48},{80,96},{96,80},{112,128},{128,112... | collective-permute-start | bytes 786440 | tf_op jit(solution)/shard_map/ppermute | solution.py:160
  24.4 1.1 %lift_home.1.split = bf16[16,256,256]{2,1,0:T(8,128)(2,1)S(1)} custom-call(s32[2,256]{1,0:T(2,128)S(1)} %bitcast.24, s32[32]{0:T(128)S(1)} %copy-done.3, bf16[16,2,128,128]{3,2,1,0:T(8,128)(2,1)S(1)} %copy-done, bf16[16,128,128]{2,1,0:T(8,128)(2,1)S(1)} %get-tuple-element.35.blocks.home), custom_call_target="tpu_custom_call" | custom-call | tf_op jit(solution)/shard_map/lift_home/pallas_call | solution.py:166
  25.5 4.5 %collective-permute-done.7.near_2 = bf16[8,128,128]{2,1,0:T(8,128)(2,1)S(1)} collective-permute-done((bf16[8,128,128]{2,1,0:T(8,128)(2,1)S(1)}, bf16[8,128,128]{2,1,0:T(8,128)(2,1)S(1)}, u32[]{:S(2)}, u32[]{:S(2)}) %collective-permute-start.7) | collective-permute-done | bytes 262176 | tf_op jit(solution)/shard_map/ppermute | solution.py:160
  30.0 1.0 %collective-permute-done.5.f = bf16[16,128,128]{2,1,0:T(8,128)(2,1)S(1)} collective-permute-done((bf16[16,128,128]{2,1,0:T(8,128)(2,1)S(1)}, bf16[16,128,128]{2,1,0:T(8,128)(2,1)S(1)}, u32[]{:S(2)}, u32[]{:S(2)}) %collective-permute-start.5) | collective-permute-done | bytes 524320 | tf_op jit(solution)/shard_map/ppermute | solution.py:158
  31.7 1.1 %lift_rest.1.split_rest = bf16[16,256,256]{2,1,0:T(8,128)(2,1)S(1)} custom-call(s32[2,256]{1,0:T(2,128)S(1)} %bitcast.25, s32[32]{0:T(128)S(1)} %copy-done.3, bf16[16,2,128,128]{3,2,1,0:T(8,128)(2,1)S(1)} %copy-done, bf16[16,128,128]{2,1,0:T(8,128)(2,1)S(1)} %pad_maximum_fusion.blocks.rest), custom_call_target="tpu_custom_call" | custom-call | tf_op jit(solution)/shard_map/lift_rest/pallas_call | solution.py:166
  33.2 2.4 %bands.1 = (f32[4,2,8,768]{3,2,1,0:T(8,128)S(1)}, f32[4,2,8,768]{3,2,1,0:T(8,128)S(1)}, f32[4,2,8,768]{3,2,1,0:T(8,128)S(1)}, f32[4,2,8,768]{3,2,1,0:T(8,128)S(1)}) custom-call(s32[2,16]{1,0:T(2,128)S(1)} %bitcast.27, s32[2,256]{1,0:T(2,128)S(1)} %bitcast.26, s32[32]{0:T(128)S(1)} %copy-done.3, bf16[16,256,256]{2,1,0:T(8,128)(2,1)S(1)} %lift_home.1.split, ...), custom_call_target="tpu_custom_call" | custom-call | tf_op jit(solution)/shard_map/bands/pallas_call | solution.py:183
  35.6 1.9 %collective-permute-start.10 = (f32[4,2,8,768]{3,2,1,0:T(8,128)S(1)}, f32[4,2,8,768]{3,2,1,0:T(8,128)S(1)}, u32[]{:S(2)}, u32[]{:S(2)}) collective-permute-start(f32[4,2,8,768]{3,2,1,0:T(8,128)S(1)} %get-tuple-element.20), channel_id=1, source_target_pairs={{0,1},{1,2},{2,3},{3,0},{4,5},{5,6},{6,7},{7,4},{8,9},{9,10},{10,1... | collective-permute-start | bytes 589832 | tf_op jit(solution)/shard_map/ppermute | solution.py:197
  37.5 1.4 %collective-permute-start.11 = (f32[4,2,8,768]{3,2,1,0:T(8,128)S(1)}, f32[4,2,8,768]{3,2,1,0:T(8,128)S(1)}, u32[]{:S(2)}, u32[]{:S(2)}) collective-permute-start(f32[4,2,8,768]{3,2,1,0:T(8,128)S(1)} %get-tuple-element.21), channel_id=1, source_target_pairs={{0,3},{1,0},{2,1},{3,2},{4,7},{5,4},{6,5},{7,6},{8,11},{9,8},{10,9... | collective-permute-start | bytes 589832 | tf_op jit(solution)/shard_map/ppermute | solution.py:198
  39.7 2.9 %collective-permute-done.10 = f32[4,2,8,768]{3,2,1,0:T(8,128)S(1)} collective-permute-done((f32[4,2,8,768]{3,2,1,0:T(8,128)S(1)}, f32[4,2,8,768]{3,2,1,0:T(8,128)S(1)}, u32[]{:S(2)}, u32[]{:S(2)}) %collective-permute-start.10) | collective-permute-done | bytes 196640 | tf_op jit(solution)/shard_map/ppermute | solution.py:197
  43.2 2.9 %collective-permute-done.12 = f32[4,2,8,768]{3,2,1,0:T(8,128)S(1)} collective-permute-done((f32[4,2,8,768]{3,2,1,0:T(8,128)S(1)}, f32[4,2,8,768]{3,2,1,0:T(8,128)S(1)}, u32[]{:S(2)}, u32[]{:S(2)}) %collective-permute-start.12) | collective-permute-done | bytes 196640 | tf_op jit(solution)/shard_map/ppermute | solution.py:196
  46.1 1.9 %collective-permute-start.13 = (f32[2,8,768]{2,1,0:T(8,128)S(1)}, f32[2,8,768]{2,1,0:T(8,128)S(1)}, u32[]{:S(2)}, u32[]{:S(2)}) collective-permute-start(f32[2,8,768]{2,1,0:T(8,128)S(1)} %get-tuple-element.23), channel_id=1, source_target_pairs={{0,4},{1,5},{2,6},{3,7},{4,8},{5,9},{6,10},{7,11},{8,12},{9,13},{1... | collective-permute-start | bytes 147464 | tf_op jit(solution)/shard_map/ppermute | solution.py:200
  48.0 1.4 %collective-permute-start.15 = (f32[2,8,768]{2,1,0:T(8,128)S(1)}, f32[2,8,768]{2,1,0:T(8,128)S(1)}, u32[]{:S(2)}, u32[]{:S(2)}) collective-permute-start(f32[2,8,768]{2,1,0:T(8,128)S(1)} %get-tuple-element.24), channel_id=1, source_target_pairs={{0,8},{1,9},{2,10},{3,11},{4,12},{5,13},{6,14},{7,15},{8,0},{9,1},... | collective-permute-start | bytes 147464 | tf_op jit(solution)/shard_map/ppermute | solution.py:202
  49.4 1.4 %collective-permute-start.14 = (f32[2,8,768]{2,1,0:T(8,128)S(1)}, f32[2,8,768]{2,1,0:T(8,128)S(1)}, u32[]{:S(2)}, u32[]{:S(2)}) collective-permute-start(f32[2,8,768]{2,1,0:T(8,128)S(1)} %get-tuple-element.25), channel_id=1, source_target_pairs={{0,12},{1,13},{2,14},{3,15},{4,0},{5,1},{6,2},{7,3},{8,4},{9,5},{1... | collective-permute-start | bytes 147464 | tf_op jit(solution)/shard_map/ppermute | solution.py:201
  51.5 2.1 %collective-permute-done.15 = f32[2,8,768]{2,1,0:T(8,128)S(1)} collective-permute-done((f32[2,8,768]{2,1,0:T(8,128)S(1)}, f32[2,8,768]{2,1,0:T(8,128)S(1)}, u32[]{:S(2)}, u32[]{:S(2)}) %collective-permute-start.15) | collective-permute-done | bytes 49184 | tf_op jit(solution)/shard_map/ppermute | solution.py:202
  (40 shorter events, 4.7 us)
Async XLA Ops:
  0.0 24.4 %copy-start = (bf16[16,2,128,128]{3,2,1,0:T(8,128)(2,1)S(1)}, bf16[16,2,128,128]{3,2,1,0:T(8,128)(2,1)}, u32[]{:S(2)}) copy-start(bf16[16,2,128,128]{3,2,1,0:T(8,128)(2,1)} %a.3) | copy-start | bytes 3145732
  0.0 6.0 %collective-permute-start.1 = (bf16[2,128,128]{2,1,0:T(8,128)(2,1)}, bf16[2,128,128]{2,1,0:T(8,128)(2,1)S(1)}, u32[]{:S(2)}, u32[]{:S(2)}) collective-permute-start(bf16[2,128,128]{2,1,0:T(8,128)(2,1)} %bitcast.21), channel_id=1, source_target_pairs={{16,32},{32,16},{48,64},{64,48},{80,96},{96,80},{112,128},{128,112... | collective-permute-start | bytes 196616 | tf_op jit(solution)/shard_map/ppermute | solution.py:142
  2.0 6.1 %collective-permute-start = (bf16[2,128,128]{2,1,0:T(8,128)(2,1)}, bf16[2,128,128]{2,1,0:T(8,128)(2,1)S(1)}, u32[]{:S(2)}, u32[]{:S(2)}) collective-permute-start(bf16[2,128,128]{2,1,0:T(8,128)(2,1)} %bitcast.22), channel_id=1, source_target_pairs={{0,8},{1,9},{2,10},{3,11},{4,12},{5,13},{6,14},{7,15},{8,0},{9,1},... | collective-permute-start | bytes 196616 | tf_op jit(solution)/shard_map/ppermute | solution.py:141
  5.2 0.9 %copy-start.1 = (bf16[1,2,128,128]{3,2,1,0:T(8,128)(2,1)S(1)}, bf16[1,2,128,128]{3,2,1,0:T(8,128)(2,1)}, u32[]{:S(2)}) copy-start(bf16[1,2,128,128]{3,2,1,0:T(8,128)(2,1)} %param.7) | copy-start | bytes 196612
  6.0 18.3 %copy-start.2 = (s32[256,2]{0,1:T(2,128)S(1)}, s32[256,2]{0,1:T(2,128)}, u32[]{:S(2)}) copy-start(s32[256,2]{0,1:T(2,128)} %param.8) | copy-start | bytes 6148
  6.0 18.3 %copy-start.3 = (s32[32]{0:T(128)S(1)}, s32[32]{0:T(128)}, u32[]{:S(2)}) copy-start(s32[32]{0:T(128)} %agglo.5) | copy-start | bytes 388
  8.1 7.0 %collective-permute-start.2 = (bf16[6,128,128]{2,1,0:T(8,128)(2,1)S(1)}, bf16[6,128,128]{2,1,0:T(8,128)(2,1)S(1)}, u32[]{:S(2)}, u32[]{:S(2)}) collective-permute-start(bf16[6,128,128]{2,1,0:T(8,128)(2,1)S(1)} %pad_maximum_fusion.3), channel_id=1, source_target_pairs={{0,1},{1,2},{2,3},{3,0},{4,5},{5,6},{6,7},{7,4},{8,9},{9,10},{10,1... | collective-permute-start | bytes 589832 | tf_op jit(solution)/shard_map/ppermute | solution.py:152
  9.8 8.9 %collective-permute-start.4 = (bf16[6,128,128]{2,1,0:T(8,128)(2,1)S(1)}, bf16[6,128,128]{2,1,0:T(8,128)(2,1)S(1)}, u32[]{:S(2)}, u32[]{:S(2)}) collective-permute-start(bf16[6,128,128]{2,1,0:T(8,128)(2,1)S(1)} %pad_maximum_fusion.3), channel_id=1, source_target_pairs={{0,3},{1,0},{2,1},{3,2},{4,7},{5,4},{6,5},{7,6},{8,11},{9,8},{10,9... | collective-permute-start | bytes 589832 | tf_op jit(solution)/shard_map/ppermute | solution.py:152
  11.5 7.2 %collective-permute-start.3 = (bf16[6,128,128]{2,1,0:T(8,128)(2,1)S(1)}, bf16[6,128,128]{2,1,0:T(8,128)(2,1)S(1)}, u32[]{:S(2)}, u32[]{:S(2)}) collective-permute-start(bf16[6,128,128]{2,1,0:T(8,128)(2,1)S(1)} %pad_maximum_fusion.3), channel_id=1, source_target_pairs={{0,2},{1,3},{2,0},{3,1},{4,6},{5,7},{6,4},{7,5},{8,10},{9,11},{10,... | collective-permute-start | bytes 589832 | tf_op jit(solution)/shard_map/ppermute | solution.py:152
  18.9 11.0 %collective-permute-start.6 = (bf16[16,128,128]{2,1,0:T(8,128)(2,1)S(1)}, bf16[16,128,128]{2,1,0:T(8,128)(2,1)S(1)}, u32[]{:S(2)}, u32[]{:S(2)}) collective-permute-start(bf16[16,128,128]{2,1,0:T(8,128)(2,1)S(1)} %get-tuple-element.36), channel_id=1, source_target_pairs={{0,12},{1,13},{2,14},{3,15},{4,8},{5,9},{6,10},{7,11},{8,4},{9,5},... | collective-permute-start | bytes 1572872 | tf_op jit(solution)/shard_map/ppermute | solution.py:159
  21.8 9.2 %collective-permute-start.5 = (bf16[16,128,128]{2,1,0:T(8,128)(2,1)S(1)}, bf16[16,128,128]{2,1,0:T(8,128)(2,1)S(1)}, u32[]{:S(2)}, u32[]{:S(2)}) collective-permute-start(bf16[16,128,128]{2,1,0:T(8,128)(2,1)S(1)} %get-tuple-element.36), channel_id=1, source_target_pairs={{0,4},{1,5},{2,6},{3,7},{4,0},{5,1},{6,2},{7,3},{8,12},{9,13},{10,... | collective-permute-start | bytes 1572872 | tf_op jit(solution)/shard_map/ppermute | solution.py:158
  22.0 9.0 %collective-permute-start.8 = (bf16[16,128,128]{2,1,0:T(8,128)(2,1)S(1)}, bf16[16,128,128]{2,1,0:T(8,128)(2,1)S(1)}, u32[]{:S(2)}, u32[]{:S(2)}) collective-permute-start(bf16[16,128,128]{2,1,0:T(8,128)(2,1)S(1)} %get-tuple-element.35.blocks.home), channel_id=1, source_target_pairs={{0,16},{16,0},{32,48},{48,32},{64,80},{80,64},{96,112},{112,96},{1... | collective-permute-start | bytes 1572872 | tf_op jit(solution)/shard_map/ppermute | solution.py:162
  22.3 7.7 %collective-permute-start.7 = (bf16[8,128,128]{2,1,0:T(8,128)(2,1)S(1)}, bf16[8,128,128]{2,1,0:T(8,128)(2,1)S(1)}, u32[]{:S(2)}, u32[]{:S(2)}) collective-permute-start(bf16[8,128,128]{2,1,0:T(8,128)(2,1)S(1)} %pad_maximum_fusion.1), channel_id=1, source_target_pairs={{16,32},{32,16},{48,64},{64,48},{80,96},{96,80},{112,128},{128,112... | collective-permute-start | bytes 786440 | tf_op jit(solution)/shard_map/ppermute | solution.py:160
  31.1 2.1 %collective-permute-start.9 = (bf16[16,128,128]{2,1,0:T(8,128)(2,1)S(1)}, bf16[16,128,128]{2,1,0:T(8,128)(2,1)S(1)}, u32[]{:S(2)}, u32[]{:S(2)}) collective-permute-start(bf16[16,128,128]{2,1,0:T(8,128)(2,1)S(1)} %pad_maximum_fusion.blocks.rest), channel_id=1, source_target_pairs={{0,16},{16,0},{32,48},{48,32},{64,80},{80,64},{96,112},{112,96},{1... | collective-permute-start | bytes 1572872 | tf_op jit(solution)/shard_map/ppermute | solution.py:180
  31.7 1.5 %copy-start.4 = (s32[16,2]{0,1:T(2,128)S(1)}, s32[16,2]{0,1:T(2,128)}, u32[]{:S(2)}) copy-start(s32[16,2]{0,1:T(2,128)} %param.6) | copy-start | bytes 388
  35.6 7.0 %collective-permute-start.10 = (f32[4,2,8,768]{3,2,1,0:T(8,128)S(1)}, f32[4,2,8,768]{3,2,1,0:T(8,128)S(1)}, u32[]{:S(2)}, u32[]{:S(2)}) collective-permute-start(f32[4,2,8,768]{3,2,1,0:T(8,128)S(1)} %get-tuple-element.20), channel_id=1, source_target_pairs={{0,1},{1,2},{2,3},{3,0},{4,5},{5,6},{6,7},{7,4},{8,9},{9,10},{10,1... | collective-permute-start | bytes 589832 | tf_op jit(solution)/shard_map/ppermute | solution.py:197
  37.5 5.7 %collective-permute-start.11 = (f32[4,2,8,768]{3,2,1,0:T(8,128)S(1)}, f32[4,2,8,768]{3,2,1,0:T(8,128)S(1)}, u32[]{:S(2)}, u32[]{:S(2)}) collective-permute-start(f32[4,2,8,768]{3,2,1,0:T(8,128)S(1)} %get-tuple-element.21), channel_id=1, source_target_pairs={{0,3},{1,0},{2,1},{3,2},{4,7},{5,4},{6,5},{7,6},{8,11},{9,8},{10,9... | collective-permute-start | bytes 589832 | tf_op jit(solution)/shard_map/ppermute | solution.py:198
  38.9 7.2 %collective-permute-start.12 = (f32[4,2,8,768]{3,2,1,0:T(8,128)S(1)}, f32[4,2,8,768]{3,2,1,0:T(8,128)S(1)}, u32[]{:S(2)}, u32[]{:S(2)}) collective-permute-start(f32[4,2,8,768]{3,2,1,0:T(8,128)S(1)} %get-tuple-element.22), channel_id=1, source_target_pairs={{0,2},{1,3},{2,0},{3,1},{4,6},{5,7},{6,4},{7,5},{8,10},{9,11},{10,... | collective-permute-start | bytes 589832 | tf_op jit(solution)/shard_map/ppermute | solution.py:196
  46.1 5.4 %collective-permute-start.13 = (f32[2,8,768]{2,1,0:T(8,128)S(1)}, f32[2,8,768]{2,1,0:T(8,128)S(1)}, u32[]{:S(2)}, u32[]{:S(2)}) collective-permute-start(f32[2,8,768]{2,1,0:T(8,128)S(1)} %get-tuple-element.23), channel_id=1, source_target_pairs={{0,4},{1,5},{2,6},{3,7},{4,8},{5,9},{6,10},{7,11},{8,12},{9,13},{1... | collective-permute-start | bytes 147464 | tf_op jit(solution)/shard_map/ppermute | solution.py:200
  48.0 5.6 %collective-permute-start.15 = (f32[2,8,768]{2,1,0:T(8,128)S(1)}, f32[2,8,768]{2,1,0:T(8,128)S(1)}, u32[]{:S(2)}, u32[]{:S(2)}) collective-permute-start(f32[2,8,768]{2,1,0:T(8,128)S(1)} %get-tuple-element.24), channel_id=1, source_target_pairs={{0,8},{1,9},{2,10},{3,11},{4,12},{5,13},{6,14},{7,15},{8,0},{9,1},... | collective-permute-start | bytes 147464 | tf_op jit(solution)/shard_map/ppermute | solution.py:202
  49.4 4.2 %collective-permute-start.14 = (f32[2,8,768]{2,1,0:T(8,128)S(1)}, f32[2,8,768]{2,1,0:T(8,128)S(1)}, u32[]{:S(2)}, u32[]{:S(2)}) collective-permute-start(f32[2,8,768]{2,1,0:T(8,128)S(1)} %get-tuple-element.25), channel_id=1, source_target_pairs={{0,12},{1,13},{2,14},{3,15},{4,0},{5,1},{6,2},{7,3},{8,4},{9,5},{1... | collective-permute-start | bytes 147464 | tf_op jit(solution)/shard_map/ppermute | solution.py:201

commit v12 on v11

--- a/solution.py
+++ b/solution.py
@@ -148,9 +148,9 @@
         compiler_params=params(8),
         name="fetch",
     )(shard)
-    trio = jnp.concatenate([shard_near, across, beside])
+    trio = jnp.concatenate([shard_near, beside, across])
     trio_1, trio_3, trio_2 = (lax.ppermute(trio, BOTH, shift(k)) for k in (1, 3, 2))
-    line, line_2, near = (
+    line, near, line_2 = (
         jnp.concatenate([t[2 * n : 2 * n + 2] for t in (trio, trio_1, trio_2, trio_3)])
         for n in range(3)
     )
@@ -197,9 +197,9 @@
     p1 = lax.ppermute(o1, BOTH, shift(1))
     p3 = lax.ppermute(o3, BOTH, shift(3))
     kept, to_1, to_2, to_3 = (o0[m] + p1[m] + p3[m] + p2[m] for m in range(SIDE))
+    q2 = lax.ppermute(to_2, BOTH, shift(2, 1))
     q1 = lax.ppermute(to_1, BOTH, shift(1, 1))
     q3 = lax.ppermute(to_3, BOTH, shift(3, 1))
-    q2 = lax.ppermute(to_2, BOTH, shift(2, 1))
     return (kept + q1 + q3 + q2).reshape(2, 8, 6, B)
 
 

time: 54.6 us -> 55.6 us (1.018)
  the two profiles are of different devices: /device:TPU:96 before, /device:TPU:152 now
where the time goes in v12:
time: 55.6 us; the launch traced here: 55.4 us
  waiting for transfers between devices  28 us (50%)
  starting transfers between devices  20.6 us (37%)
  Pallas kernels  4.66 us (8%)
  local copies, waits for them, and re-layouts  1.15 us (2%)
  other arithmetic  0.83 us (1%)
    ppermute x1, waiting for transfers between devices, local(): near_2 = lax.ppermute(line_2, 'row', row_pairs(1))  5.8 us
    ppermute x3, waiting for transfers between devices, local(): lax.ppermute(trio, BOTH, shift(k))  5.35 us
    ppermute x3, starting transfers between devices, local(): lax.ppermute(trio, BOTH, shift(k))  5.13 us
    ppermute x1, waiting for transfers between devices, local(): p1 = lax.ppermute(o1, BOTH, shift(1))  2.96 us
    ppermute x1, waiting for transfers between devices, local(): q2 = lax.ppermute(to_2, BOTH, shift(2, 1))  2.72 us
    ppermute x1, starting transfers between devices, local(): q2 = lax.ppermute(to_2, BOTH, shift(2, 1))  2.66 us
    pallas_call x1, Pallas kernels, local(): pl.pallas_call(band_kernel, out_shape=[piece] * 4, in_specs=[smem()] * 3...  2.39 us
    ppermute x1, waiting for transfers between devices, local(): q3 = lax.ppermute(to_3, BOTH, shift(3, 1))  2.36 us
  transfers between devices with their start and end apart: 16, of which 13 were waited for; matrix products, arithmetic and copies ran while one was open for 0% of the time, Pallas kernels for 4%

profile of v12, /device:TPU:152, one launch (start us, length us, event | category | flops | bytes accessed | tf_op | source)
XLA Modules:
  0.0 55.4 jit_solution(8386094378677754211)
XLA Ops:
  0.0 1.2 %collective-permute-start.1 = (bf16[2,128,128]{2,1,0:T(8,128)(2,1)}, bf16[2,128,128]{2,1,0:T(8,128)(2,1)S(1)}, u32[]{:S(2)}, u32[]{:S(2)}) collective-permute-start(bf16[2,128,128]{2,1,0:T(8,128)(2,1)} %bitcast.21), channel_id=1, source_target_pairs={{0,8},{1,9},{2,10},{3,11},{4,12},{5,13},{6,14},{7,15},{8,0},{9,1},... | collective-permute-start | bytes 196616 | tf_op jit(solution)/shard_map/ppermute | solution.py:141
  1.2 1.9 %collective-permute-start = (bf16[2,128,128]{2,1,0:T(8,128)(2,1)}, bf16[2,128,128]{2,1,0:T(8,128)(2,1)S(1)}, u32[]{:S(2)}, u32[]{:S(2)}) collective-permute-start(bf16[2,128,128]{2,1,0:T(8,128)(2,1)} %bitcast.22), channel_id=1, source_target_pairs={{16,32},{32,16},{48,64},{64,48},{80,96},{96,80},{112,128},{128,112... | collective-permute-start | bytes 196616 | tf_op jit(solution)/shard_map/ppermute | solution.py:142
  4.0 2.0 %collective-permute-done.1 = bf16[2,128,128]{2,1,0:T(8,128)(2,1)S(1)} collective-permute-done((bf16[2,128,128]{2,1,0:T(8,128)(2,1)}, bf16[2,128,128]{2,1,0:T(8,128)(2,1)S(1)}, u32[]{:S(2)}, u32[]{:S(2)}) %collective-permute-start.1) | collective-permute-done | bytes 65568 | tf_op jit(solution)/shard_map/ppermute | solution.py:141
  6.0 2.2 %collective-permute-done = bf16[2,128,128]{2,1,0:T(8,128)(2,1)S(1)} collective-permute-done((bf16[2,128,128]{2,1,0:T(8,128)(2,1)}, bf16[2,128,128]{2,1,0:T(8,128)(2,1)S(1)}, u32[]{:S(2)}, u32[]{:S(2)}) %collective-permute-start) | collective-permute-done | bytes 65568 | tf_op jit(solution)/shard_map/ppermute | solution.py:142
  8.3 1.6 %collective-permute-start.2 = (bf16[6,128,128]{2,1,0:T(8,128)(2,1)S(1)}, bf16[6,128,128]{2,1,0:T(8,128)(2,1)S(1)}, u32[]{:S(2)}, u32[]{:S(2)}) collective-permute-start(bf16[6,128,128]{2,1,0:T(8,128)(2,1)S(1)} %pad_maximum_fusion.3), channel_id=1, source_target_pairs={{0,1},{1,2},{2,3},{3,0},{4,5},{5,6},{6,7},{7,4},{8,9},{9,10},{10,1... | collective-permute-start | bytes 589832 | tf_op jit(solution)/shard_map/ppermute | solution.py:152
  9.8 1.7 %collective-permute-start.4 = (bf16[6,128,128]{2,1,0:T(8,128)(2,1)S(1)}, bf16[6,128,128]{2,1,0:T(8,128)(2,1)S(1)}, u32[]{:S(2)}, u32[]{:S(2)}) collective-permute-start(bf16[6,128,128]{2,1,0:T(8,128)(2,1)S(1)} %pad_maximum_fusion.3), channel_id=1, source_target_pairs={{0,3},{1,0},{2,1},{3,2},{4,7},{5,4},{6,5},{7,6},{8,11},{9,8},{10,9... | collective-permute-start | bytes 589832 | tf_op jit(solution)/shard_map/ppermute | solution.py:152
  11.6 1.8 %collective-permute-start.3 = (bf16[6,128,128]{2,1,0:T(8,128)(2,1)S(1)}, bf16[6,128,128]{2,1,0:T(8,128)(2,1)S(1)}, u32[]{:S(2)}, u32[]{:S(2)}) collective-permute-start(bf16[6,128,128]{2,1,0:T(8,128)(2,1)S(1)} %pad_maximum_fusion.3), channel_id=1, source_target_pairs={{0,2},{1,3},{2,0},{3,1},{4,6},{5,7},{6,4},{7,5},{8,10},{9,11},{10,... | collective-permute-start | bytes 589832 | tf_op jit(solution)/shard_map/ppermute | solution.py:152
  13.4 1.8 %collective-permute-done.2 = bf16[6,128,128]{2,1,0:T(8,128)(2,1)S(1)} collective-permute-done((bf16[6,128,128]{2,1,0:T(8,128)(2,1)S(1)}, bf16[6,128,128]{2,1,0:T(8,128)(2,1)S(1)}, u32[]{:S(2)}, u32[]{:S(2)}) %collective-permute-start.2) | collective-permute-done | bytes 196640 | tf_op jit(solution)/shard_map/ppermute | solution.py:152
  15.2 3.5 %collective-permute-done.3 = bf16[6,128,128]{2,1,0:T(8,128)(2,1)S(1)} collective-permute-done((bf16[6,128,128]{2,1,0:T(8,128)(2,1)S(1)}, bf16[6,128,128]{2,1,0:T(8,128)(2,1)S(1)}, u32[]{:S(2)}, u32[]{:S(2)}) %collective-permute-start.3) | collective-permute-done | bytes 196640 | tf_op jit(solution)/shard_map/ppermute | solution.py:152
  19.0 2.3 %collective-permute-start.6 = (bf16[16,128,128]{2,1,0:T(8,128)(2,1)S(1)}, bf16[16,128,128]{2,1,0:T(8,128)(2,1)S(1)}, u32[]{:S(2)}, u32[]{:S(2)}) collective-permute-start(bf16[16,128,128]{2,1,0:T(8,128)(2,1)S(1)} %get-tuple-element.36), channel_id=1, source_target_pairs={{0,12},{1,13},{2,14},{3,15},{4,8},{5,9},{6,10},{7,11},{8,4},{9,5},... | collective-permute-start | bytes 1572872 | tf_op jit(solution)/shard_map/ppermute | solution.py:159
  21.4 1.9 %collective-permute-start.7 = (bf16[8,128,128]{2,1,0:T(8,128)(2,1)S(1)}, bf16[8,128,128]{2,1,0:T(8,128)(2,1)S(1)}, u32[]{:S(2)}, u32[]{:S(2)}) collective-permute-start(bf16[8,128,128]{2,1,0:T(8,128)(2,1)S(1)} %pad_maximum_fusion.1), channel_id=1, source_target_pairs={{16,32},{32,16},{48,64},{64,48},{80,96},{96,80},{112,128},{128,112... | collective-permute-start | bytes 786440 | tf_op jit(solution)/shard_map/ppermute | solution.py:160
  23.4 1.1 %lift_home.1.split = bf16[16,256,256]{2,1,0:T(8,128)(2,1)S(1)} custom-call(s32[2,256]{1,0:T(2,128)S(1)} %bitcast.24, s32[32]{0:T(128)S(1)} %copy-done.3, bf16[16,2,128,128]{3,2,1,0:T(8,128)(2,1)S(1)} %copy-done, bf16[16,128,128]{2,1,0:T(8,128)(2,1)S(1)} %get-tuple-element.35.blocks.home), custom_call_target="tpu_custom_call" | custom-call | tf_op jit(solution)/shard_map/lift_home/pallas_call | solution.py:166
  24.5 5.8 %collective-permute-done.7.near_2 = bf16[8,128,128]{2,1,0:T(8,128)(2,1)S(1)} collective-permute-done((bf16[8,128,128]{2,1,0:T(8,128)(2,1)S(1)}, bf16[8,128,128]{2,1,0:T(8,128)(2,1)S(1)}, u32[]{:S(2)}, u32[]{:S(2)}) %collective-permute-start.7) | collective-permute-done | bytes 262176 | tf_op jit(solution)/shard_map/ppermute | solution.py:160
  30.8 1.1 %lift_rest.1.split_rest = bf16[16,256,256]{2,1,0:T(8,128)(2,1)S(1)} custom-call(s32[2,256]{1,0:T(2,128)S(1)} %bitcast.25, s32[32]{0:T(128)S(1)} %copy-done.3, bf16[16,2,128,128]{3,2,1,0:T(8,128)(2,1)S(1)} %copy-done, bf16[16,128,128]{2,1,0:T(8,128)(2,1)S(1)} %pad_maximum_fusion.blocks.rest), custom_call_target="tpu_custom_call" | custom-call | tf_op jit(solution)/shard_map/lift_rest/pallas_call | solution.py:166
  32.6 2.4 %bands.1 = (f32[4,2,8,768]{3,2,1,0:T(8,128)S(1)}, f32[4,2,8,768]{3,2,1,0:T(8,128)S(1)}, f32[4,2,8,768]{3,2,1,0:T(8,128)S(1)}, f32[4,2,8,768]{3,2,1,0:T(8,128)S(1)}) custom-call(s32[2,16]{1,0:T(2,128)S(1)} %bitcast.27, s32[2,256]{1,0:T(2,128)S(1)} %bitcast.26, s32[32]{0:T(128)S(1)} %copy-done.3, bf16[16,256,256]{2,1,0:T(8,128)(2,1)S(1)} %lift_home.1.split, ...), custom_call_target="tpu_custom_call" | custom-call | tf_op jit(solution)/shard_map/bands/pallas_call | solution.py:183
  35.0 1.1 %collective-permute-start.10 = (f32[4,2,8,768]{3,2,1,0:T(8,128)S(1)}, f32[4,2,8,768]{3,2,1,0:T(8,128)S(1)}, u32[]{:S(2)}, u32[]{:S(2)}) collective-permute-start(f32[4,2,8,768]{3,2,1,0:T(8,128)S(1)} %get-tuple-element.20), channel_id=1, source_target_pairs={{0,1},{1,2},{2,3},{3,0},{4,5},{5,6},{6,7},{7,4},{8,9},{9,10},{10,1... | collective-permute-start | bytes 589832 | tf_op jit(solution)/shard_map/ppermute | solution.py:197
  36.1 2.2 %collective-permute-start.11 = (f32[4,2,8,768]{3,2,1,0:T(8,128)S(1)}, f32[4,2,8,768]{3,2,1,0:T(8,128)S(1)}, u32[]{:S(2)}, u32[]{:S(2)}) collective-permute-start(f32[4,2,8,768]{3,2,1,0:T(8,128)S(1)} %get-tuple-element.21), channel_id=1, source_target_pairs={{0,3},{1,0},{2,1},{3,2},{4,7},{5,4},{6,5},{7,6},{8,11},{9,8},{10,9... | collective-permute-start | bytes 589832 | tf_op jit(solution)/shard_map/ppermute | solution.py:198
  39.0 3.0 %collective-permute-done.10 = f32[4,2,8,768]{3,2,1,0:T(8,128)S(1)} collective-permute-done((f32[4,2,8,768]{3,2,1,0:T(8,128)S(1)}, f32[4,2,8,768]{3,2,1,0:T(8,128)S(1)}, u32[]{:S(2)}, u32[]{:S(2)}) %collective-permute-start.10) | collective-permute-done | bytes 196640 | tf_op jit(solution)/shard_map/ppermute | solution.py:197
  42.0 1.7 %collective-permute-done.11 = f32[4,2,8,768]{3,2,1,0:T(8,128)S(1)} collective-permute-done((f32[4,2,8,768]{3,2,1,0:T(8,128)S(1)}, f32[4,2,8,768]{3,2,1,0:T(8,128)S(1)}, u32[]{:S(2)}, u32[]{:S(2)}) %collective-permute-start.11) | collective-permute-done | bytes 196640 | tf_op jit(solution)/shard_map/ppermute | solution.py:198
  43.7 1.8 %collective-permute-done.12 = f32[4,2,8,768]{3,2,1,0:T(8,128)S(1)} collective-permute-done((f32[4,2,8,768]{3,2,1,0:T(8,128)S(1)}, f32[4,2,8,768]{3,2,1,0:T(8,128)S(1)}, u32[]{:S(2)}, u32[]{:S(2)}) %collective-permute-start.12) | collective-permute-done | bytes 196640 | tf_op jit(solution)/shard_map/ppermute | solution.py:196
  45.5 1.3 %collective-permute-start.13 = (f32[2,8,768]{2,1,0:T(8,128)S(1)}, f32[2,8,768]{2,1,0:T(8,128)S(1)}, u32[]{:S(2)}, u32[]{:S(2)}) collective-permute-start(f32[2,8,768]{2,1,0:T(8,128)S(1)} %get-tuple-element.23), channel_id=1, source_target_pairs={{0,4},{1,5},{2,6},{3,7},{4,8},{5,9},{6,10},{7,11},{8,12},{9,13},{1... | collective-permute-start | bytes 147464 | tf_op jit(solution)/shard_map/ppermute | solution.py:201
  46.8 2.7 %collective-permute-start.15 = (f32[2,8,768]{2,1,0:T(8,128)S(1)}, f32[2,8,768]{2,1,0:T(8,128)S(1)}, u32[]{:S(2)}, u32[]{:S(2)}) collective-permute-start(f32[2,8,768]{2,1,0:T(8,128)S(1)} %get-tuple-element.24), channel_id=1, source_target_pairs={{0,8},{1,9},{2,10},{3,11},{4,12},{5,13},{6,14},{7,15},{8,0},{9,1},... | collective-permute-start | bytes 147464 | tf_op jit(solution)/shard_map/ppermute | solution.py:200
  49.7 2.7 %collective-permute-done.15 = f32[2,8,768]{2,1,0:T(8,128)S(1)} collective-permute-done((f32[2,8,768]{2,1,0:T(8,128)S(1)}, f32[2,8,768]{2,1,0:T(8,128)S(1)}, u32[]{:S(2)}, u32[]{:S(2)}) %collective-permute-start.15) | collective-permute-done | bytes 49184 | tf_op jit(solution)/shard_map/ppermute | solution.py:200
  52.4 2.4 %collective-permute-done.14 = f32[2,8,768]{2,1,0:T(8,128)S(1)} collective-permute-done((f32[2,8,768]{2,1,0:T(8,128)S(1)}, f32[2,8,768]{2,1,0:T(8,128)S(1)}, u32[]{:S(2)}, u32[]{:S(2)}) %collective-permute-start.14) | collective-permute-done | bytes 49184 | tf_op jit(solution)/shard_map/ppermute | solution.py:202
  (40 shorter events, 3.9 us)
Async XLA Ops:
  0.0 23.4 %copy-start = (bf16[16,2,128,128]{3,2,1,0:T(8,128)(2,1)S(1)}, bf16[16,2,128,128]{3,2,1,0:T(8,128)(2,1)}, u32[]{:S(2)}) copy-start(bf16[16,2,128,128]{3,2,1,0:T(8,128)(2,1)} %a.3) | copy-start | bytes 3145732
  0.0 6.0 %collective-permute-start.1 = (bf16[2,128,128]{2,1,0:T(8,128)(2,1)}, bf16[2,128,128]{2,1,0:T(8,128)(2,1)S(1)}, u32[]{:S(2)}, u32[]{:S(2)}) collective-permute-start(bf16[2,128,128]{2,1,0:T(8,128)(2,1)} %bitcast.21), channel_id=1, source_target_pairs={{0,8},{1,9},{2,10},{3,11},{4,12},{5,13},{6,14},{7,15},{8,0},{9,1},... | collective-permute-start | bytes 196616 | tf_op jit(solution)/shard_map/ppermute | solution.py:141
  1.2 7.0 %collective-permute-start = (bf16[2,128,128]{2,1,0:T(8,128)(2,1)}, bf16[2,128,128]{2,1,0:T(8,128)(2,1)S(1)}, u32[]{:S(2)}, u32[]{:S(2)}) collective-permute-start(bf16[2,128,128]{2,1,0:T(8,128)(2,1)} %bitcast.22), channel_id=1, source_target_pairs={{16,32},{32,16},{48,64},{64,48},{80,96},{96,80},{112,128},{128,112... | collective-permute-start | bytes 196616 | tf_op jit(solution)/shard_map/ppermute | solution.py:142
  3.2 0.9 %copy-start.1 = (bf16[1,2,128,128]{3,2,1,0:T(8,128)(2,1)S(1)}, bf16[1,2,128,128]{3,2,1,0:T(8,128)(2,1)}, u32[]{:S(2)}) copy-start(bf16[1,2,128,128]{3,2,1,0:T(8,128)(2,1)} %param.7) | copy-start | bytes 196612
  4.0 19.4 %copy-start.2 = (s32[256,2]{0,1:T(2,128)S(1)}, s32[256,2]{0,1:T(2,128)}, u32[]{:S(2)}) copy-start(s32[256,2]{0,1:T(2,128)} %param.8) | copy-start | bytes 6148
  4.0 19.4 %copy-start.3 = (s32[32]{0:T(128)S(1)}, s32[32]{0:T(128)}, u32[]{:S(2)}) copy-start(s32[32]{0:T(128)} %agglo.5) | copy-start | bytes 388
  8.3 7.0 %collective-permute-start.2 = (bf16[6,128,128]{2,1,0:T(8,128)(2,1)S(1)}, bf16[6,128,128]{2,1,0:T(8,128)(2,1)S(1)}, u32[]{:S(2)}, u32[]{:S(2)}) collective-permute-start(bf16[6,128,128]{2,1,0:T(8,128)(2,1)S(1)} %pad_maximum_fusion.3), channel_id=1, source_target_pairs={{0,1},{1,2},{2,3},{3,0},{4,5},{5,6},{6,7},{7,4},{8,9},{9,10},{10,1... | collective-permute-start | bytes 589832 | tf_op jit(solution)/shard_map/ppermute | solution.py:152
  9.8 8.9 %collective-permute-start.4 = (bf16[6,128,128]{2,1,0:T(8,128)(2,1)S(1)}, bf16[6,128,128]{2,1,0:T(8,128)(2,1)S(1)}, u32[]{:S(2)}, u32[]{:S(2)}) collective-permute-start(bf16[6,128,128]{2,1,0:T(8,128)(2,1)S(1)} %pad_maximum_fusion.3), channel_id=1, source_target_pairs={{0,3},{1,0},{2,1},{3,2},{4,7},{5,4},{6,5},{7,6},{8,11},{9,8},{10,9... | collective-permute-start | bytes 589832 | tf_op jit(solution)/shard_map/ppermute | solution.py:152
  11.6 7.2 %collective-permute-start.3 = (bf16[6,128,128]{2,1,0:T(8,128)(2,1)S(1)}, bf16[6,128,128]{2,1,0:T(8,128)(2,1)S(1)}, u32[]{:S(2)}, u32[]{:S(2)}) collective-permute-start(bf16[6,128,128]{2,1,0:T(8,128)(2,1)S(1)} %pad_maximum_fusion.3), channel_id=1, source_target_pairs={{0,2},{1,3},{2,0},{3,1},{4,6},{5,7},{6,4},{7,5},{8,10},{9,11},{10,... | collective-permute-start | bytes 589832 | tf_op jit(solution)/shard_map/ppermute | solution.py:152
  19.0 11.3 %collective-permute-start.6 = (bf16[16,128,128]{2,1,0:T(8,128)(2,1)S(1)}, bf16[16,128,128]{2,1,0:T(8,128)(2,1)S(1)}, u32[]{:S(2)}, u32[]{:S(2)}) collective-permute-start(bf16[16,128,128]{2,1,0:T(8,128)(2,1)S(1)} %get-tuple-element.36), channel_id=1, source_target_pairs={{0,12},{1,13},{2,14},{3,15},{4,8},{5,9},{6,10},{7,11},{8,4},{9,5},... | collective-permute-start | bytes 1572872 | tf_op jit(solution)/shard_map/ppermute | solution.py:159
  21.3 9.2 %collective-permute-start.5 = (bf16[16,128,128]{2,1,0:T(8,128)(2,1)S(1)}, bf16[16,128,128]{2,1,0:T(8,128)(2,1)S(1)}, u32[]{:S(2)}, u32[]{:S(2)}) collective-permute-start(bf16[16,128,128]{2,1,0:T(8,128)(2,1)S(1)} %get-tuple-element.36), channel_id=1, source_target_pairs={{0,4},{1,5},{2,6},{3,7},{4,0},{5,1},{6,2},{7,3},{8,12},{9,13},{10,... | collective-permute-start | bytes 1572872 | tf_op jit(solution)/shard_map/ppermute | solution.py:158
  21.4 9.1 %collective-permute-start.8 = (bf16[16,128,128]{2,1,0:T(8,128)(2,1)S(1)}, bf16[16,128,128]{2,1,0:T(8,128)(2,1)S(1)}, u32[]{:S(2)}, u32[]{:S(2)}) collective-permute-start(bf16[16,128,128]{2,1,0:T(8,128)(2,1)S(1)} %get-tuple-element.35.blocks.home), channel_id=1, source_target_pairs={{0,16},{16,0},{32,48},{48,32},{64,80},{80,64},{96,112},{112,96},{1... | collective-permute-start | bytes 1572872 | tf_op jit(solution)/shard_map/ppermute | solution.py:162
  21.4 8.9 %collective-permute-start.7 = (bf16[8,128,128]{2,1,0:T(8,128)(2,1)S(1)}, bf16[8,128,128]{2,1,0:T(8,128)(2,1)S(1)}, u32[]{:S(2)}, u32[]{:S(2)}) collective-permute-start(bf16[8,128,128]{2,1,0:T(8,128)(2,1)S(1)} %pad_maximum_fusion.1), channel_id=1, source_target_pairs={{16,32},{32,16},{48,64},{64,48},{80,96},{96,80},{112,128},{128,112... | collective-permute-start | bytes 786440 | tf_op jit(solution)/shard_map/ppermute | solution.py:160
  30.6 2.0 %collective-permute-start.9 = (bf16[16,128,128]{2,1,0:T(8,128)(2,1)S(1)}, bf16[16,128,128]{2,1,0:T(8,128)(2,1)S(1)}, u32[]{:S(2)}, u32[]{:S(2)}) collective-permute-start(bf16[16,128,128]{2,1,0:T(8,128)(2,1)S(1)} %pad_maximum_fusion.blocks.rest), channel_id=1, source_target_pairs={{0,16},{16,0},{32,48},{48,32},{64,80},{80,64},{96,112},{112,96},{1... | collective-permute-start | bytes 1572872 | tf_op jit(solution)/shard_map/ppermute | solution.py:180
  30.7 1.9 %copy-start.4 = (s32[16,2]{0,1:T(2,128)S(1)}, s32[16,2]{0,1:T(2,128)}, u32[]{:S(2)}) copy-start(s32[16,2]{0,1:T(2,128)} %param.6) | copy-start | bytes 388
  35.0 7.0 %collective-permute-start.10 = (f32[4,2,8,768]{3,2,1,0:T(8,128)S(1)}, f32[4,2,8,768]{3,2,1,0:T(8,128)S(1)}, u32[]{:S(2)}, u32[]{:S(2)}) collective-permute-start(f32[4,2,8,768]{3,2,1,0:T(8,128)S(1)} %get-tuple-element.20), channel_id=1, source_target_pairs={{0,1},{1,2},{2,3},{3,0},{4,5},{5,6},{6,7},{7,4},{8,9},{9,10},{10,1... | collective-permute-start | bytes 589832 | tf_op jit(solution)/shard_map/ppermute | solution.py:197
  36.1 7.6 %collective-permute-start.11 = (f32[4,2,8,768]{3,2,1,0:T(8,128)S(1)}, f32[4,2,8,768]{3,2,1,0:T(8,128)S(1)}, u32[]{:S(2)}, u32[]{:S(2)}) collective-permute-start(f32[4,2,8,768]{3,2,1,0:T(8,128)S(1)} %get-tuple-element.21), channel_id=1, source_target_pairs={{0,3},{1,0},{2,1},{3,2},{4,7},{5,4},{6,5},{7,6},{8,11},{9,8},{10,9... | collective-permute-start | bytes 589832 | tf_op jit(solution)/shard_map/ppermute | solution.py:198
  38.3 7.2 %collective-permute-start.12 = (f32[4,2,8,768]{3,2,1,0:T(8,128)S(1)}, f32[4,2,8,768]{3,2,1,0:T(8,128)S(1)}, u32[]{:S(2)}, u32[]{:S(2)}) collective-permute-start(f32[4,2,8,768]{3,2,1,0:T(8,128)S(1)} %get-tuple-element.22), channel_id=1, source_target_pairs={{0,2},{1,3},{2,0},{3,1},{4,6},{5,7},{6,4},{7,5},{8,10},{9,11},{10,... | collective-permute-start | bytes 589832 | tf_op jit(solution)/shard_map/ppermute | solution.py:196
  45.5 4.2 %collective-permute-start.13 = (f32[2,8,768]{2,1,0:T(8,128)S(1)}, f32[2,8,768]{2,1,0:T(8,128)S(1)}, u32[]{:S(2)}, u32[]{:S(2)}) collective-permute-start(f32[2,8,768]{2,1,0:T(8,128)S(1)} %get-tuple-element.23), channel_id=1, source_target_pairs={{0,4},{1,5},{2,6},{3,7},{4,8},{5,9},{6,10},{7,11},{8,12},{9,13},{1... | collective-permute-start | bytes 147464 | tf_op jit(solution)/shard_map/ppermute | solution.py:201
  46.8 5.6 %collective-permute-start.15 = (f32[2,8,768]{2,1,0:T(8,128)S(1)}, f32[2,8,768]{2,1,0:T(8,128)S(1)}, u32[]{:S(2)}, u32[]{:S(2)}) collective-permute-start(f32[2,8,768]{2,1,0:T(8,128)S(1)} %get-tuple-element.24), channel_id=1, source_target_pairs={{0,8},{1,9},{2,10},{3,11},{4,12},{5,13},{6,14},{7,15},{8,0},{9,1},... | collective-permute-start | bytes 147464 | tf_op jit(solution)/shard_map/ppermute | solution.py:200
  49.5 5.3 %collective-permute-start.14 = (f32[2,8,768]{2,1,0:T(8,128)S(1)}, f32[2,8,768]{2,1,0:T(8,128)S(1)}, u32[]{:S(2)}, u32[]{:S(2)}) collective-permute-start(f32[2,8,768]{2,1,0:T(8,128)S(1)} %get-tuple-element.25), channel_id=1, source_target_pairs={{0,12},{1,13},{2,14},{3,15},{4,0},{5,1},{6,2},{7,3},{8,4},{9,5},{1... | collective-permute-start | bytes 147464 | tf_op jit(solution)/shard_map/ppermute | solution.py:202

commit v13 on v11

--- a/solution.py
+++ b/solution.py
@@ -85,7 +85,7 @@
 
 
 def band_kernel(
-    cols, aggs, agglo, split, split_rest, home, rest, near, near_2, f, b, pair, pair_rest,
+    cols, aggs, agglo, split, split_rest, home, rest, near, near_2, f, b, pair, pair_1, pair_3,
     o0, o1, o2, o3, blocks, acc
 ):
     row, cross, y, x = place()
@@ -96,7 +96,8 @@
     blocks[48:56] = f[8:16]
     blocks[56:64] = b[8:16]
     blocks[64:80] = pair[...]
-    blocks[80:96] = pair_rest[...]
+    blocks[80:88] = pair_1[...]
+    blocks[88:96] = pair_3[...]
     acc[...] = jnp.zeros_like(acc)
     pair_band = 2 - 2 * (row % 2)
     for p in range(ROWS):
@@ -173,17 +174,16 @@
         )(aggs, agglo, a_blocks, blocks)
 
     split = lift(0, home, "lift_home")
-    lines_1, lines_3, near_2, pair, split = lax.optimization_barrier(
-        (lines_1, lines_3, near_2, pair, split)
-    )
+    lines_3, near_2, pair, split = lax.optimization_barrier((lines_3, near_2, pair, split))
+    pair_3 = lax.ppermute(lines_3[:8], "row", row_pairs(0))
+    pair_1 = lax.ppermute(lines_1[:8], "row", row_pairs(0))
     rest = jnp.concatenate([lines_1[:8], lines_3[:8]])
-    pair_rest = lax.ppermute(rest, "row", row_pairs(0))
     split_rest = lift(ROWS // 2, rest, "lift_rest")
     piece = jax.ShapeDtypeStruct((SIDE, 2, 8, 768), jnp.float32)
     o0, o1, o2, o3 = pl.pallas_call(
         band_kernel,
         out_shape=[piece] * 4,
-        in_specs=[smem()] * 3 + [vmem()] * 10,
+        in_specs=[smem()] * 3 + [vmem()] * 11,
         out_specs=[vmem()] * 4,
         scratch_shapes=[
             pltpu.VMEM((96, B, B), jnp.bfloat16),
@@ -191,7 +191,7 @@
         ],
         compiler_params=params(24),
         name="bands",
-    )(cols, aggs, agglo, split, split_rest, home, rest, near, near_2, lines_1, lines_3, pair, pair_rest)
+    )(cols, aggs, agglo, split, split_rest, home, rest, near, near_2, lines_1, lines_3, pair, pair_1, pair_3)
 
     p2 = lax.ppermute(o2, BOTH, shift(2))
     p1 = lax.ppermute(o1, BOTH, shift(1))

time: 54.6 us -> 55.8 us (1.022)
  the two profiles are of different devices: /device:TPU:96 before, /device:TPU:224 now
where the time goes in v13:
time: 55.8 us; the launch traced here: 55.6 us
  starting transfers between devices  27.5 us (49%)
  waiting for transfers between devices  21.3 us (38%)
  Pallas kernels  4.66 us (8%)
  local copies, waits for them, and re-layouts  1.17 us (2%)
  other arithmetic  0.84 us (2%)
    ppermute x3, starting transfers between devices, local(): lax.ppermute(trio, BOTH, shift(k))  5.3 us
    ppermute x3, waiting for transfers between devices, local(): lax.ppermute(trio, BOTH, shift(k))  5.18 us
    ppermute x1, starting transfers between devices, local(): q2 = lax.ppermute(to_2, BOTH, shift(2, 1))  4.1 us
    ppermute x1, starting transfers between devices, local(): lines_3 = lax.ppermute(lines, BOTH, swap(3))  3.42 us
    ppermute x1, waiting for transfers between devices, local(): near_2 = lax.ppermute(line_2, 'row', row_pairs(1))  3.35 us
    ppermute x1, starting transfers between devices, local(): across = lax.ppermute(shard, BOTH, swap(2))  3.11 us
    ppermute x1, starting transfers between devices, local(): beside = lax.ppermute(shard, 'row', row_pairs(1))  2.47 us
    ppermute x1, waiting for transfers between devices, local(): p2 = lax.ppermute(o2, BOTH, shift(2))  2.44 us
  transfers between devices with their start and end apart: 17, of which 12 were waited for; matrix products, arithmetic and copies ran while one was open for 0% of the time, Pallas kernels for 4%

profile of v13, /device:TPU:224, one launch (start us, length us, event | category | flops | bytes accessed | tf_op | source)
XLA Modules:
  0.0 55.6 jit_solution(9808385149258957347)
XLA Ops:
  0.0 2.5 %collective-permute-start.1 = (bf16[2,128,128]{2,1,0:T(8,128)(2,1)}, bf16[2,128,128]{2,1,0:T(8,128)(2,1)S(1)}, u32[]{:S(2)}, u32[]{:S(2)}) collective-permute-start(bf16[2,128,128]{2,1,0:T(8,128)(2,1)} %bitcast.21), channel_id=1, source_target_pairs={{16,32},{32,16},{48,64},{64,48},{80,96},{96,80},{112,128},{128,112... | collective-permute-start | bytes 196616 | tf_op jit(solution)/shard_map/ppermute | solution.py:143
  2.5 3.1 %collective-permute-start = (bf16[2,128,128]{2,1,0:T(8,128)(2,1)}, bf16[2,128,128]{2,1,0:T(8,128)(2,1)S(1)}, u32[]{:S(2)}, u32[]{:S(2)}) collective-permute-start(bf16[2,128,128]{2,1,0:T(8,128)(2,1)} %bitcast.22), channel_id=1, source_target_pairs={{0,8},{1,9},{2,10},{3,11},{4,12},{5,13},{6,14},{7,15},{8,0},{9,1},... | collective-permute-start | bytes 196616 | tf_op jit(solution)/shard_map/ppermute | solution.py:142
  6.5 2.1 %collective-permute-done = bf16[2,128,128]{2,1,0:T(8,128)(2,1)S(1)} collective-permute-done((bf16[2,128,128]{2,1,0:T(8,128)(2,1)}, bf16[2,128,128]{2,1,0:T(8,128)(2,1)S(1)}, u32[]{:S(2)}, u32[]{:S(2)}) %collective-permute-start) | collective-permute-done | bytes 65568 | tf_op jit(solution)/shard_map/ppermute | solution.py:142
  8.6 1.7 %collective-permute-start.2 = (bf16[6,128,128]{2,1,0:T(8,128)(2,1)S(1)}, bf16[6,128,128]{2,1,0:T(8,128)(2,1)S(1)}, u32[]{:S(2)}, u32[]{:S(2)}) collective-permute-start(bf16[6,128,128]{2,1,0:T(8,128)(2,1)S(1)} %pad_maximum_fusion.3), channel_id=1, source_target_pairs={{0,1},{1,2},{2,3},{3,0},{4,5},{5,6},{6,7},{7,4},{8,9},{9,10},{10,1... | collective-permute-start | bytes 589832 | tf_op jit(solution)/shard_map/ppermute | solution.py:153
  10.2 1.7 %collective-permute-start.4 = (bf16[6,128,128]{2,1,0:T(8,128)(2,1)S(1)}, bf16[6,128,128]{2,1,0:T(8,128)(2,1)S(1)}, u32[]{:S(2)}, u32[]{:S(2)}) collective-permute-start(bf16[6,128,128]{2,1,0:T(8,128)(2,1)S(1)} %pad_maximum_fusion.3), channel_id=1, source_target_pairs={{0,3},{1,0},{2,1},{3,2},{4,7},{5,4},{6,5},{7,6},{8,11},{9,8},{10,9... | collective-permute-start | bytes 589832 | tf_op jit(solution)/shard_map/ppermute | solution.py:153
  11.9 2.0 %collective-permute-start.3 = (bf16[6,128,128]{2,1,0:T(8,128)(2,1)S(1)}, bf16[6,128,128]{2,1,0:T(8,128)(2,1)S(1)}, u32[]{:S(2)}, u32[]{:S(2)}) collective-permute-start(bf16[6,128,128]{2,1,0:T(8,128)(2,1)S(1)} %pad_maximum_fusion.3), channel_id=1, source_target_pairs={{0,2},{1,3},{2,0},{3,1},{4,6},{5,7},{6,4},{7,5},{8,10},{9,11},{10,... | collective-permute-start | bytes 589832 | tf_op jit(solution)/shard_map/ppermute | solution.py:153
  13.9 1.7 %collective-permute-done.2 = bf16[6,128,128]{2,1,0:T(8,128)(2,1)S(1)} collective-permute-done((bf16[6,128,128]{2,1,0:T(8,128)(2,1)S(1)}, bf16[6,128,128]{2,1,0:T(8,128)(2,1)S(1)}, u32[]{:S(2)}, u32[]{:S(2)}) %collective-permute-start.2) | collective-permute-done | bytes 196640 | tf_op jit(solution)/shard_map/ppermute | solution.py:153
  15.6 3.5 %collective-permute-done.3 = bf16[6,128,128]{2,1,0:T(8,128)(2,1)S(1)} collective-permute-done((bf16[6,128,128]{2,1,0:T(8,128)(2,1)S(1)}, bf16[6,128,128]{2,1,0:T(8,128)(2,1)S(1)}, u32[]{:S(2)}, u32[]{:S(2)}) %collective-permute-start.3) | collective-permute-done | bytes 196640 | tf_op jit(solution)/shard_map/ppermute | solution.py:153
  19.4 1.6 %collective-permute-start.8 = (bf16[16,128,128]{2,1,0:T(8,128)(2,1)S(1)}, bf16[16,128,128]{2,1,0:T(8,128)(2,1)S(1)}, u32[]{:S(2)}, u32[]{:S(2)}) collective-permute-start(bf16[16,128,128]{2,1,0:T(8,128)(2,1)S(1)} %get-tuple-element.34), channel_id=1, source_target_pairs={{0,4},{1,5},{2,6},{3,7},{4,0},{5,1},{6,2},{7,3},{8,12},{9,13},{10,... | collective-permute-start | bytes 1572872 | tf_op jit(solution)/shard_map/ppermute | solution.py:159
  20.9 3.4 %collective-permute-start.5 = (bf16[16,128,128]{2,1,0:T(8,128)(2,1)S(1)}, bf16[16,128,128]{2,1,0:T(8,128)(2,1)S(1)}, u32[]{:S(2)}, u32[]{:S(2)}) collective-permute-start(bf16[16,128,128]{2,1,0:T(8,128)(2,1)S(1)} %get-tuple-element.34), channel_id=1, source_target_pairs={{0,12},{1,13},{2,14},{3,15},{4,8},{5,9},{6,10},{7,11},{8,4},{9,5},... | collective-permute-start | bytes 1572872 | tf_op jit(solution)/shard_map/ppermute | solution.py:160
  24.4 1.9 %collective-permute-start.6 = (bf16[8,128,128]{2,1,0:T(8,128)(2,1)S(1)}, bf16[8,128,128]{2,1,0:T(8,128)(2,1)S(1)}, u32[]{:S(2)}, u32[]{:S(2)}) collective-permute-start(bf16[8,128,128]{2,1,0:T(8,128)(2,1)S(1)} %pad_maximum_fusion.1), channel_id=1, source_target_pairs={{16,32},{32,16},{48,64},{64,48},{80,96},{96,80},{112,128},{128,112... | collective-permute-start | bytes 786440 | tf_op jit(solution)/shard_map/ppermute | solution.py:161
  26.4 1.1 %lift_home.1.split = bf16[16,256,256]{2,1,0:T(8,128)(2,1)S(1)} custom-call(s32[2,256]{1,0:T(2,128)S(1)} %bitcast.24, s32[32]{0:T(128)S(1)} %copy-done.3, bf16[16,2,128,128]{3,2,1,0:T(8,128)(2,1)S(1)} %copy-done, bf16[16,128,128]{2,1,0:T(8,128)(2,1)S(1)} %get-tuple-element.33.blocks.home), custom_call_target="tpu_custom_call" | custom-call | tf_op jit(solution)/shard_map/lift_home/pallas_call | solution.py:167
  27.5 1.1 %collective-permute-done.8.f = bf16[16,128,128]{2,1,0:T(8,128)(2,1)S(1)} collective-permute-done((bf16[16,128,128]{2,1,0:T(8,128)(2,1)S(1)}, bf16[16,128,128]{2,1,0:T(8,128)(2,1)S(1)}, u32[]{:S(2)}, u32[]{:S(2)}) %collective-permute-start.8) | collective-permute-done | bytes 524320 | tf_op jit(solution)/shard_map/ppermute | solution.py:159
  28.8 3.3 %collective-permute-done.6.near_2 = bf16[8,128,128]{2,1,0:T(8,128)(2,1)S(1)} collective-permute-done((bf16[8,128,128]{2,1,0:T(8,128)(2,1)S(1)}, bf16[8,128,128]{2,1,0:T(8,128)(2,1)S(1)}, u32[]{:S(2)}, u32[]{:S(2)}) %collective-permute-start.6) | collective-permute-done | bytes 262176 | tf_op jit(solution)/shard_map/ppermute | solution.py:161
  32.3 1.1 %lift_rest.1.split_rest = bf16[16,256,256]{2,1,0:T(8,128)(2,1)S(1)} custom-call(s32[2,256]{1,0:T(2,128)S(1)} %bitcast.25, s32[32]{0:T(128)S(1)} %copy-done.3, bf16[16,2,128,128]{3,2,1,0:T(8,128)(2,1)S(1)} %copy-done, bf16[16,128,128]{2,1,0:T(8,128)(2,1)S(1)} %pad_maximum_fusion.blocks.rest), custom_call_target="tpu_custom_call" | custom-call | tf_op jit(solution)/shard_map/lift_rest/pallas_call | solution.py:167
  33.8 2.4 %bands.1 = (f32[4,2,8,768]{3,2,1,0:T(8,128)S(1)}, f32[4,2,8,768]{3,2,1,0:T(8,128)S(1)}, f32[4,2,8,768]{3,2,1,0:T(8,128)S(1)}, f32[4,2,8,768]{3,2,1,0:T(8,128)S(1)}) custom-call(s32[2,16]{1,0:T(2,128)S(1)} %bitcast.27, s32[2,256]{1,0:T(2,128)S(1)} %bitcast.26, s32[32]{0:T(128)S(1)} %copy-done.3, bf16[16,256,256]{2,1,0:T(8,128)(2,1)S(1)} %lift_home.1.split, ...), custom_call_target="tpu_custom_call" | custom-call | tf_op jit(solution)/shard_map/bands/pallas_call | solution.py:183
  36.2 2.4 %collective-permute-start.11 = (f32[4,2,8,768]{3,2,1,0:T(8,128)S(1)}, f32[4,2,8,768]{3,2,1,0:T(8,128)S(1)}, u32[]{:S(2)}, u32[]{:S(2)}) collective-permute-start(f32[4,2,8,768]{3,2,1,0:T(8,128)S(1)} %get-tuple-element.18), channel_id=1, source_target_pairs={{0,1},{1,2},{2,3},{3,0},{4,5},{5,6},{6,7},{7,4},{8,9},{9,10},{10,1... | collective-permute-start | bytes 589832 | tf_op jit(solution)/shard_map/ppermute | solution.py:197
  39.5 2.0 %collective-permute-start.13 = (f32[4,2,8,768]{3,2,1,0:T(8,128)S(1)}, f32[4,2,8,768]{3,2,1,0:T(8,128)S(1)}, u32[]{:S(2)}, u32[]{:S(2)}) collective-permute-start(f32[4,2,8,768]{3,2,1,0:T(8,128)S(1)} %get-tuple-element.20), channel_id=1, source_target_pairs={{0,2},{1,3},{2,0},{3,1},{4,6},{5,7},{6,4},{7,5},{8,10},{9,11},{10,... | collective-permute-start | bytes 589832 | tf_op jit(solution)/shard_map/ppermute | solution.py:196
  41.4 1.7 %collective-permute-done.11 = f32[4,2,8,768]{3,2,1,0:T(8,128)S(1)} collective-permute-done((f32[4,2,8,768]{3,2,1,0:T(8,128)S(1)}, f32[4,2,8,768]{3,2,1,0:T(8,128)S(1)}, u32[]{:S(2)}, u32[]{:S(2)}) %collective-permute-start.11) | collective-permute-done | bytes 196640 | tf_op jit(solution)/shard_map/ppermute | solution.py:197
  44.2 2.4 %collective-permute-done.13 = f32[4,2,8,768]{3,2,1,0:T(8,128)S(1)} collective-permute-done((f32[4,2,8,768]{3,2,1,0:T(8,128)S(1)}, f32[4,2,8,768]{3,2,1,0:T(8,128)S(1)}, u32[]{:S(2)}, u32[]{:S(2)}) %collective-permute-start.13) | collective-permute-done | bytes 196640 | tf_op jit(solution)/shard_map/ppermute | solution.py:196
  46.8 4.1 %collective-permute-start.16 = (f32[2,8,768]{2,1,0:T(8,128)S(1)}, f32[2,8,768]{2,1,0:T(8,128)S(1)}, u32[]{:S(2)}, u32[]{:S(2)}) collective-permute-start(f32[2,8,768]{2,1,0:T(8,128)S(1)} %get-tuple-element.22), channel_id=1, source_target_pairs={{0,8},{1,9},{2,10},{3,11},{4,12},{5,13},{6,14},{7,15},{8,0},{9,1},... | collective-permute-start | bytes 147464 | tf_op jit(solution)/shard_map/ppermute | solution.py:202
  50.9 1.2 %collective-permute-done.14 = f32[2,8,768]{2,1,0:T(8,128)S(1)} collective-permute-done((f32[2,8,768]{2,1,0:T(8,128)S(1)}, f32[2,8,768]{2,1,0:T(8,128)S(1)}, u32[]{:S(2)}, u32[]{:S(2)}) %collective-permute-start.14) | collective-permute-done | bytes 49184 | tf_op jit(solution)/shard_map/ppermute | solution.py:200
  52.1 1.4 %collective-permute-done.16 = f32[2,8,768]{2,1,0:T(8,128)S(1)} collective-permute-done((f32[2,8,768]{2,1,0:T(8,128)S(1)}, f32[2,8,768]{2,1,0:T(8,128)S(1)}, u32[]{:S(2)}, u32[]{:S(2)}) %collective-permute-start.16) | collective-permute-done | bytes 49184 | tf_op jit(solution)/shard_map/ppermute | solution.py:202
  53.5 1.5 %collective-permute-done.15 = f32[2,8,768]{2,1,0:T(8,128)S(1)} collective-permute-done((f32[2,8,768]{2,1,0:T(8,128)S(1)}, f32[2,8,768]{2,1,0:T(8,128)S(1)}, u32[]{:S(2)}, u32[]{:S(2)}) %collective-permute-start.15) | collective-permute-done | bytes 49184 | tf_op jit(solution)/shard_map/ppermute | solution.py:201
  (42 shorter events, 4.6 us)
Async XLA Ops:
  0.0 26.3 %copy-start = (bf16[16,2,128,128]{3,2,1,0:T(8,128)(2,1)S(1)}, bf16[16,2,128,128]{3,2,1,0:T(8,128)(2,1)}, u32[]{:S(2)}) copy-start(bf16[16,2,128,128]{3,2,1,0:T(8,128)(2,1)} %a.3) | copy-start | bytes 3145732
  0.0 6.5 %collective-permute-start.1 = (bf16[2,128,128]{2,1,0:T(8,128)(2,1)}, bf16[2,128,128]{2,1,0:T(8,128)(2,1)S(1)}, u32[]{:S(2)}, u32[]{:S(2)}) collective-permute-start(bf16[2,128,128]{2,1,0:T(8,128)(2,1)} %bitcast.21), channel_id=1, source_target_pairs={{16,32},{32,16},{48,64},{64,48},{80,96},{96,80},{112,128},{128,112... | collective-permute-start | bytes 196616 | tf_op jit(solution)/shard_map/ppermute | solution.py:143
  2.5 6.1 %collective-permute-start = (bf16[2,128,128]{2,1,0:T(8,128)(2,1)}, bf16[2,128,128]{2,1,0:T(8,128)(2,1)S(1)}, u32[]{:S(2)}, u32[]{:S(2)}) collective-permute-start(bf16[2,128,128]{2,1,0:T(8,128)(2,1)} %bitcast.22), channel_id=1, source_target_pairs={{0,8},{1,9},{2,10},{3,11},{4,12},{5,13},{6,14},{7,15},{8,0},{9,1},... | collective-permute-start | bytes 196616 | tf_op jit(solution)/shard_map/ppermute | solution.py:142
  5.6 0.9 %copy-start.1 = (bf16[1,2,128,128]{3,2,1,0:T(8,128)(2,1)S(1)}, bf16[1,2,128,128]{3,2,1,0:T(8,128)(2,1)}, u32[]{:S(2)}) copy-start(bf16[1,2,128,128]{3,2,1,0:T(8,128)(2,1)} %param.7) | copy-start | bytes 196612
  6.5 19.9 %copy-start.2 = (s32[256,2]{0,1:T(2,128)S(1)}, s32[256,2]{0,1:T(2,128)}, u32[]{:S(2)}) copy-start(s32[256,2]{0,1:T(2,128)} %param.8) | copy-start | bytes 6148
  6.5 19.9 %copy-start.3 = (s32[32]{0:T(128)S(1)}, s32[32]{0:T(128)}, u32[]{:S(2)}) copy-start(s32[32]{0:T(128)} %agglo.5) | copy-start | bytes 388
  8.6 7.0 %collective-permute-start.2 = (bf16[6,128,128]{2,1,0:T(8,128)(2,1)S(1)}, bf16[6,128,128]{2,1,0:T(8,128)(2,1)S(1)}, u32[]{:S(2)}, u32[]{:S(2)}) collective-permute-start(bf16[6,128,128]{2,1,0:T(8,128)(2,1)S(1)} %pad_maximum_fusion.3), channel_id=1, source_target_pairs={{0,1},{1,2},{2,3},{3,0},{4,5},{5,6},{6,7},{7,4},{8,9},{9,10},{10,1... | collective-permute-start | bytes 589832 | tf_op jit(solution)/shard_map/ppermute | solution.py:153
  10.2 8.9 %collective-permute-start.4 = (bf16[6,128,128]{2,1,0:T(8,128)(2,1)S(1)}, bf16[6,128,128]{2,1,0:T(8,128)(2,1)S(1)}, u32[]{:S(2)}, u32[]{:S(2)}) collective-permute-start(bf16[6,128,128]{2,1,0:T(8,128)(2,1)S(1)} %pad_maximum_fusion.3), channel_id=1, source_target_pairs={{0,3},{1,0},{2,1},{3,2},{4,7},{5,4},{6,5},{7,6},{8,11},{9,8},{10,9... | collective-permute-start | bytes 589832 | tf_op jit(solution)/shard_map/ppermute | solution.py:153
  11.9 7.2 %collective-permute-start.3 = (bf16[6,128,128]{2,1,0:T(8,128)(2,1)S(1)}, bf16[6,128,128]{2,1,0:T(8,128)(2,1)S(1)}, u32[]{:S(2)}, u32[]{:S(2)}) collective-permute-start(bf16[6,128,128]{2,1,0:T(8,128)(2,1)S(1)} %pad_maximum_fusion.3), channel_id=1, source_target_pairs={{0,2},{1,3},{2,0},{3,1},{4,6},{5,7},{6,4},{7,5},{8,10},{9,11},{10,... | collective-permute-start | bytes 589832 | tf_op jit(solution)/shard_map/ppermute | solution.py:153
  19.4 9.3 %collective-permute-start.8 = (bf16[16,128,128]{2,1,0:T(8,128)(2,1)S(1)}, bf16[16,128,128]{2,1,0:T(8,128)(2,1)S(1)}, u32[]{:S(2)}, u32[]{:S(2)}) collective-permute-start(bf16[16,128,128]{2,1,0:T(8,128)(2,1)S(1)} %get-tuple-element.34), channel_id=1, source_target_pairs={{0,4},{1,5},{2,6},{3,7},{4,0},{5,1},{6,2},{7,3},{8,12},{9,13},{10,... | collective-permute-start | bytes 1572872 | tf_op jit(solution)/shard_map/ppermute | solution.py:159
  20.9 11.2 %collective-permute-start.5 = (bf16[16,128,128]{2,1,0:T(8,128)(2,1)S(1)}, bf16[16,128,128]{2,1,0:T(8,128)(2,1)S(1)}, u32[]{:S(2)}, u32[]{:S(2)}) collective-permute-start(bf16[16,128,128]{2,1,0:T(8,128)(2,1)S(1)} %get-tuple-element.34), channel_id=1, source_target_pairs={{0,12},{1,13},{2,14},{3,15},{4,8},{5,9},{6,10},{7,11},{8,4},{9,5},... | collective-permute-start | bytes 1572872 | tf_op jit(solution)/shard_map/ppermute | solution.py:160
  24.4 7.7 %collective-permute-start.7 = (bf16[16,128,128]{2,1,0:T(8,128)(2,1)S(1)}, bf16[16,128,128]{2,1,0:T(8,128)(2,1)S(1)}, u32[]{:S(2)}, u32[]{:S(2)}) collective-permute-start(bf16[16,128,128]{2,1,0:T(8,128)(2,1)S(1)} %get-tuple-element.33.blocks.home), channel_id=1, source_target_pairs={{0,16},{16,0},{32,48},{48,32},{64,80},{80,64},{96,112},{112,96},{1... | collective-permute-start | bytes 1572872 | tf_op jit(solution)/shard_map/ppermute | solution.py:163
  24.4 7.7 %collective-permute-start.6 = (bf16[8,128,128]{2,1,0:T(8,128)(2,1)S(1)}, bf16[8,128,128]{2,1,0:T(8,128)(2,1)S(1)}, u32[]{:S(2)}, u32[]{:S(2)}) collective-permute-start(bf16[8,128,128]{2,1,0:T(8,128)(2,1)S(1)} %pad_maximum_fusion.1), channel_id=1, source_target_pairs={{16,32},{32,16},{48,64},{64,48},{80,96},{96,80},{112,128},{128,112... | collective-permute-start | bytes 786440 | tf_op jit(solution)/shard_map/ppermute | solution.py:161
  28.7 4.8 %collective-permute-start.9 = (bf16[8,128,128]{2,1,0:T(8,128)(2,1)S(1)}, bf16[8,128,128]{2,1,0:T(8,128)(2,1)S(1)}, u32[]{:S(2)}, u32[]{:S(2)}) collective-permute-start(bf16[8,128,128]{2,1,0:T(8,128)(2,1)S(1)} %slice.119), channel_id=1, source_target_pairs={{0,16},{16,0},{32,48},{48,32},{64,80},{80,64},{96,112},{112,96},{1... | collective-permute-start | bytes 786440 | tf_op jit(solution)/shard_map/ppermute | solution.py:179
  32.1 1.6 %collective-permute-start.10 = (bf16[8,128,128]{2,1,0:T(8,128)(2,1)S(1)}, bf16[8,128,128]{2,1,0:T(8,128)(2,1)S(1)}, u32[]{:S(2)}, u32[]{:S(2)}) collective-permute-start(bf16[8,128,128]{2,1,0:T(8,128)(2,1)S(1)} %slice.93), channel_id=1, source_target_pairs={{0,16},{16,0},{32,48},{48,32},{64,80},{80,64},{96,112},{112,96},{1... | collective-permute-start | bytes 786440 | tf_op jit(solution)/shard_map/ppermute | solution.py:178
  32.3 1.4 %copy-start.4 = (s32[16,2]{0,1:T(2,128)S(1)}, s32[16,2]{0,1:T(2,128)}, u32[]{:S(2)}) copy-start(s32[16,2]{0,1:T(2,128)} %param.6) | copy-start | bytes 388
  36.2 7.0 %collective-permute-start.11 = (f32[4,2,8,768]{3,2,1,0:T(8,128)S(1)}, f32[4,2,8,768]{3,2,1,0:T(8,128)S(1)}, u32[]{:S(2)}, u32[]{:S(2)}) collective-permute-start(f32[4,2,8,768]{3,2,1,0:T(8,128)S(1)} %get-tuple-element.18), channel_id=1, source_target_pairs={{0,1},{1,2},{2,3},{3,0},{4,5},{5,6},{6,7},{7,4},{8,9},{9,10},{10,1... | collective-permute-start | bytes 589832 | tf_op jit(solution)/shard_map/ppermute | solution.py:197
  38.5 5.7 %collective-permute-start.12 = (f32[4,2,8,768]{3,2,1,0:T(8,128)S(1)}, f32[4,2,8,768]{3,2,1,0:T(8,128)S(1)}, u32[]{:S(2)}, u32[]{:S(2)}) collective-permute-start(f32[4,2,8,768]{3,2,1,0:T(8,128)S(1)} %get-tuple-element.19), channel_id=1, source_target_pairs={{0,3},{1,0},{2,1},{3,2},{4,7},{5,4},{6,5},{7,6},{8,11},{9,8},{10,9... | collective-permute-start | bytes 589832 | tf_op jit(solution)/shard_map/ppermute | solution.py:198
  39.5 7.2 %collective-permute-start.13 = (f32[4,2,8,768]{3,2,1,0:T(8,128)S(1)}, f32[4,2,8,768]{3,2,1,0:T(8,128)S(1)}, u32[]{:S(2)}, u32[]{:S(2)}) collective-permute-start(f32[4,2,8,768]{3,2,1,0:T(8,128)S(1)} %get-tuple-element.20), channel_id=1, source_target_pairs={{0,2},{1,3},{2,0},{3,1},{4,6},{5,7},{6,4},{7,5},{8,10},{9,11},{10,... | collective-permute-start | bytes 589832 | tf_op jit(solution)/shard_map/ppermute | solution.py:196
  46.7 5.4 %collective-permute-start.14 = (f32[2,8,768]{2,1,0:T(8,128)S(1)}, f32[2,8,768]{2,1,0:T(8,128)S(1)}, u32[]{:S(2)}, u32[]{:S(2)}) collective-permute-start(f32[2,8,768]{2,1,0:T(8,128)S(1)} %get-tuple-element.21), channel_id=1, source_target_pairs={{0,4},{1,5},{2,6},{3,7},{4,8},{5,9},{6,10},{7,11},{8,12},{9,13},{1... | collective-permute-start | bytes 147464 | tf_op jit(solution)/shard_map/ppermute | solution.py:200
  46.8 6.7 %collective-permute-start.16 = (f32[2,8,768]{2,1,0:T(8,128)S(1)}, f32[2,8,768]{2,1,0:T(8,128)S(1)}, u32[]{:S(2)}, u32[]{:S(2)}) collective-permute-start(f32[2,8,768]{2,1,0:T(8,128)S(1)} %get-tuple-element.22), channel_id=1, source_target_pairs={{0,8},{1,9},{2,10},{3,11},{4,12},{5,13},{6,14},{7,15},{8,0},{9,1},... | collective-permute-start | bytes 147464 | tf_op jit(solution)/shard_map/ppermute | solution.py:202
  50.9 4.1 %collective-permute-start.15 = (f32[2,8,768]{2,1,0:T(8,128)S(1)}, f32[2,8,768]{2,1,0:T(8,128)S(1)}, u32[]{:S(2)}, u32[]{:S(2)}) collective-permute-start(f32[2,8,768]{2,1,0:T(8,128)S(1)} %get-tuple-element.23), channel_id=1, source_target_pairs={{0,12},{1,13},{2,14},{3,15},{4,0},{5,1},{6,2},{7,3},{8,4},{9,5},{1... | collective-permute-start | bytes 147464 | tf_op jit(solution)/shard_map/ppermute | solution.py:201

commit v14 on v13

--- a/solution.py
+++ b/solution.py
@@ -174,7 +174,7 @@
         )(aggs, agglo, a_blocks, blocks)
 
     split = lift(0, home, "lift_home")
-    lines_3, near_2, pair, split = lax.optimization_barrier((lines_3, near_2, pair, split))
+    lines_1, near_2, pair, split = lax.optimization_barrier((lines_1, near_2, pair, split))
     pair_3 = lax.ppermute(lines_3[:8], "row", row_pairs(0))
     pair_1 = lax.ppermute(lines_1[:8], "row", row_pairs(0))
     rest = jnp.concatenate([lines_1[:8], lines_3[:8]])

time: 55.8 us -> 54.3 us (0.973)
  the two profiles are of different devices: /device:TPU:224 before, /device:TPU:96 now
where the time goes in v14:
time: 54.3 us; the launch traced here: 53.9 us
  starting transfers between devices  25.2 us (46%)
  waiting for transfers between devices  21.8 us (40%)
  Pallas kernels  4.66 us (9%)
  local copies, waits for them, and re-layouts  1.18 us (2%)
  other arithmetic  0.82 us (2%)
    ppermute x3, starting transfers between devices, local(): lax.ppermute(trio, BOTH, shift(k))  5.3 us
    ppermute x3, waiting for transfers between devices, local(): lax.ppermute(trio, BOTH, shift(k))  5.18 us
    ppermute x1, waiting for transfers between devices, local(): lines_3 = lax.ppermute(lines, BOTH, swap(3))  3.89 us
    ppermute x1, starting transfers between devices, local(): across = lax.ppermute(shard, BOTH, swap(2))  3.11 us
    ppermute x1, waiting for transfers between devices, local(): p2 = lax.ppermute(o2, BOTH, shift(2))  2.88 us
    ppermute x1, waiting for transfers between devices, local(): p1 = lax.ppermute(o1, BOTH, shift(1))  2.87 us
    ppermute x1, starting transfers between devices, local(): lines_3 = lax.ppermute(lines, BOTH, swap(3))  2.84 us
    pallas_call x1, Pallas kernels, local(): pl.pallas_call(band_kernel, out_shape=[piece] * 4, in_specs=[smem()] * 3...  2.39 us
  transfers between devices with their start and end apart: 17, of which 11 were waited for; matrix products, arithmetic and copies ran while one was open for 0% of the time, Pallas kernels for 4%

profile of v14, /device:TPU:96, one launch (start us, length us, event | category | flops | bytes accessed | tf_op | source)
XLA Modules:
  0.0 53.9 jit_solution(1814652952496358467)
XLA Ops:
  0.0 2.0 %collective-permute-start.1 = (bf16[2,128,128]{2,1,0:T(8,128)(2,1)}, bf16[2,128,128]{2,1,0:T(8,128)(2,1)S(1)}, u32[]{:S(2)}, u32[]{:S(2)}) collective-permute-start(bf16[2,128,128]{2,1,0:T(8,128)(2,1)} %bitcast.21), channel_id=1, source_target_pairs={{16,32},{32,16},{48,64},{64,48},{80,96},{96,80},{112,128},{128,112... | collective-permute-start | bytes 196616 | tf_op jit(solution)/shard_map/ppermute | solution.py:143
  2.0 3.1 %collective-permute-start = (bf16[2,128,128]{2,1,0:T(8,128)(2,1)}, bf16[2,128,128]{2,1,0:T(8,128)(2,1)S(1)}, u32[]{:S(2)}, u32[]{:S(2)}) collective-permute-start(bf16[2,128,128]{2,1,0:T(8,128)(2,1)} %bitcast.22), channel_id=1, source_target_pairs={{0,8},{1,9},{2,10},{3,11},{4,12},{5,13},{6,14},{7,15},{8,0},{9,1},... | collective-permute-start | bytes 196616 | tf_op jit(solution)/shard_map/ppermute | solution.py:142
  5.2 0.9 %copy-done.1 = bf16[1,2,128,128]{3,2,1,0:T(8,128)(2,1)S(1)} copy-done((bf16[1,2,128,128]{3,2,1,0:T(8,128)(2,1)S(1)}, bf16[1,2,128,128]{3,2,1,0:T(8,128)(2,1)}, u32[]{:S(2)}) %copy-start.1) | copy-done | bytes 65560
  6.1 2.1 %collective-permute-done = bf16[2,128,128]{2,1,0:T(8,128)(2,1)S(1)} collective-permute-done((bf16[2,128,128]{2,1,0:T(8,128)(2,1)}, bf16[2,128,128]{2,1,0:T(8,128)(2,1)S(1)}, u32[]{:S(2)}, u32[]{:S(2)}) %collective-permute-start) | collective-permute-done | bytes 65568 | tf_op jit(solution)/shard_map/ppermute | solution.py:142
  8.1 1.7 %collective-permute-start.2 = (bf16[6,128,128]{2,1,0:T(8,128)(2,1)S(1)}, bf16[6,128,128]{2,1,0:T(8,128)(2,1)S(1)}, u32[]{:S(2)}, u32[]{:S(2)}) collective-permute-start(bf16[6,128,128]{2,1,0:T(8,128)(2,1)S(1)} %pad_maximum_fusion.3), channel_id=1, source_target_pairs={{0,1},{1,2},{2,3},{3,0},{4,5},{5,6},{6,7},{7,4},{8,9},{9,10},{10,1... | collective-permute-start | bytes 589832 | tf_op jit(solution)/shard_map/ppermute | solution.py:153
  9.8 1.7 %collective-permute-start.4 = (bf16[6,128,128]{2,1,0:T(8,128)(2,1)S(1)}, bf16[6,128,128]{2,1,0:T(8,128)(2,1)S(1)}, u32[]{:S(2)}, u32[]{:S(2)}) collective-permute-start(bf16[6,128,128]{2,1,0:T(8,128)(2,1)S(1)} %pad_maximum_fusion.3), channel_id=1, source_target_pairs={{0,3},{1,0},{2,1},{3,2},{4,7},{5,4},{6,5},{7,6},{8,11},{9,8},{10,9... | collective-permute-start | bytes 589832 | tf_op jit(solution)/shard_map/ppermute | solution.py:153
  11.5 2.0 %collective-permute-start.3 = (bf16[6,128,128]{2,1,0:T(8,128)(2,1)S(1)}, bf16[6,128,128]{2,1,0:T(8,128)(2,1)S(1)}, u32[]{:S(2)}, u32[]{:S(2)}) collective-permute-start(bf16[6,128,128]{2,1,0:T(8,128)(2,1)S(1)} %pad_maximum_fusion.3), channel_id=1, source_target_pairs={{0,2},{1,3},{2,0},{3,1},{4,6},{5,7},{6,4},{7,5},{8,10},{9,11},{10,... | collective-permute-start | bytes 589832 | tf_op jit(solution)/shard_map/ppermute | solution.py:153
  13.4 1.7 %collective-permute-done.2 = bf16[6,128,128]{2,1,0:T(8,128)(2,1)S(1)} collective-permute-done((bf16[6,128,128]{2,1,0:T(8,128)(2,1)S(1)}, bf16[6,128,128]{2,1,0:T(8,128)(2,1)S(1)}, u32[]{:S(2)}, u32[]{:S(2)}) %collective-permute-start.2) | collective-permute-done | bytes 196640 | tf_op jit(solution)/shard_map/ppermute | solution.py:153
  15.1 3.5 %collective-permute-done.3 = bf16[6,128,128]{2,1,0:T(8,128)(2,1)S(1)} collective-permute-done((bf16[6,128,128]{2,1,0:T(8,128)(2,1)S(1)}, bf16[6,128,128]{2,1,0:T(8,128)(2,1)S(1)}, u32[]{:S(2)}, u32[]{:S(2)}) %collective-permute-start.3) | collective-permute-done | bytes 196640 | tf_op jit(solution)/shard_map/ppermute | solution.py:153
  18.9 2.8 %collective-permute-start.8 = (bf16[16,128,128]{2,1,0:T(8,128)(2,1)S(1)}, bf16[16,128,128]{2,1,0:T(8,128)(2,1)S(1)}, u32[]{:S(2)}, u32[]{:S(2)}) collective-permute-start(bf16[16,128,128]{2,1,0:T(8,128)(2,1)S(1)} %get-tuple-element.34), channel_id=1, source_target_pairs={{0,12},{1,13},{2,14},{3,15},{4,8},{5,9},{6,10},{7,11},{8,4},{9,5},... | collective-permute-start | bytes 1572872 | tf_op jit(solution)/shard_map/ppermute | solution.py:160
  22.3 2.1 %collective-permute-start.6 = (bf16[8,128,128]{2,1,0:T(8,128)(2,1)S(1)}, bf16[8,128,128]{2,1,0:T(8,128)(2,1)S(1)}, u32[]{:S(2)}, u32[]{:S(2)}) collective-permute-start(bf16[8,128,128]{2,1,0:T(8,128)(2,1)S(1)} %pad_maximum_fusion.1), channel_id=1, source_target_pairs={{16,32},{32,16},{48,64},{64,48},{80,96},{96,80},{112,128},{128,112... | collective-permute-start | bytes 786440 | tf_op jit(solution)/shard_map/ppermute | solution.py:161
  24.4 1.1 %lift_home.1.split = bf16[16,256,256]{2,1,0:T(8,128)(2,1)S(1)} custom-call(s32[2,256]{1,0:T(2,128)S(1)} %bitcast.24, s32[32]{0:T(128)S(1)} %copy-done.3, bf16[16,2,128,128]{3,2,1,0:T(8,128)(2,1)S(1)} %copy-done, bf16[16,128,128]{2,1,0:T(8,128)(2,1)S(1)} %get-tuple-element.33.blocks.home), custom_call_target="tpu_custom_call" | custom-call | tf_op jit(solution)/shard_map/lift_home/pallas_call | solution.py:167
  25.5 3.9 %collective-permute-done.8.b = bf16[16,128,128]{2,1,0:T(8,128)(2,1)S(1)} collective-permute-done((bf16[16,128,128]{2,1,0:T(8,128)(2,1)S(1)}, bf16[16,128,128]{2,1,0:T(8,128)(2,1)S(1)}, u32[]{:S(2)}, u32[]{:S(2)}) %collective-permute-start.8) | collective-permute-done | bytes 524320 | tf_op jit(solution)/shard_map/ppermute | solution.py:160
  30.0 1.0 %collective-permute-done.5.f = bf16[16,128,128]{2,1,0:T(8,128)(2,1)S(1)} collective-permute-done((bf16[16,128,128]{2,1,0:T(8,128)(2,1)S(1)}, bf16[16,128,128]{2,1,0:T(8,128)(2,1)S(1)}, u32[]{:S(2)}, u32[]{:S(2)}) %collective-permute-start.5) | collective-permute-done | bytes 524320 | tf_op jit(solution)/shard_map/ppermute | solution.py:159
  31.7 1.1 %lift_rest.1.split_rest = bf16[16,256,256]{2,1,0:T(8,128)(2,1)S(1)} custom-call(s32[2,256]{1,0:T(2,128)S(1)} %bitcast.25, s32[32]{0:T(128)S(1)} %copy-done.3, bf16[16,2,128,128]{3,2,1,0:T(8,128)(2,1)S(1)} %copy-done, bf16[16,128,128]{2,1,0:T(8,128)(2,1)S(1)} %pad_maximum_fusion.blocks.rest), custom_call_target="tpu_custom_call" | custom-call | tf_op jit(solution)/shard_map/lift_rest/pallas_call | solution.py:167
  32.8 2.4 %bands.1 = (f32[4,2,8,768]{3,2,1,0:T(8,128)S(1)}, f32[4,2,8,768]{3,2,1,0:T(8,128)S(1)}, f32[4,2,8,768]{3,2,1,0:T(8,128)S(1)}, f32[4,2,8,768]{3,2,1,0:T(8,128)S(1)}) custom-call(s32[2,16]{1,0:T(2,128)S(1)} %bitcast.27, s32[2,256]{1,0:T(2,128)S(1)} %bitcast.26, s32[32]{0:T(128)S(1)} %copy-done.3, bf16[16,256,256]{2,1,0:T(8,128)(2,1)S(1)} %lift_home.1.split, ...), custom_call_target="tpu_custom_call" | custom-call | tf_op jit(solution)/shard_map/bands/pallas_call | solution.py:183
  35.3 1.9 %collective-permute-start.11 = (f32[4,2,8,768]{3,2,1,0:T(8,128)S(1)}, f32[4,2,8,768]{3,2,1,0:T(8,128)S(1)}, u32[]{:S(2)}, u32[]{:S(2)}) collective-permute-start(f32[4,2,8,768]{3,2,1,0:T(8,128)S(1)} %get-tuple-element.18), channel_id=1, source_target_pairs={{0,1},{1,2},{2,3},{3,0},{4,5},{5,6},{6,7},{7,4},{8,9},{9,10},{10,1... | collective-permute-start | bytes 589832 | tf_op jit(solution)/shard_map/ppermute | solution.py:197
  37.2 1.4 %collective-permute-start.12 = (f32[4,2,8,768]{3,2,1,0:T(8,128)S(1)}, f32[4,2,8,768]{3,2,1,0:T(8,128)S(1)}, u32[]{:S(2)}, u32[]{:S(2)}) collective-permute-start(f32[4,2,8,768]{3,2,1,0:T(8,128)S(1)} %get-tuple-element.19), channel_id=1, source_target_pairs={{0,3},{1,0},{2,1},{3,2},{4,7},{5,4},{6,5},{7,6},{8,11},{9,8},{10,9... | collective-permute-start | bytes 589832 | tf_op jit(solution)/shard_map/ppermute | solution.py:198
  39.3 2.9 %collective-permute-done.11 = f32[4,2,8,768]{3,2,1,0:T(8,128)S(1)} collective-permute-done((f32[4,2,8,768]{3,2,1,0:T(8,128)S(1)}, f32[4,2,8,768]{3,2,1,0:T(8,128)S(1)}, u32[]{:S(2)}, u32[]{:S(2)}) %collective-permute-start.11) | collective-permute-done | bytes 196640 | tf_op jit(solution)/shard_map/ppermute | solution.py:197
  42.9 2.9 %collective-permute-done.13 = f32[4,2,8,768]{3,2,1,0:T(8,128)S(1)} collective-permute-done((f32[4,2,8,768]{3,2,1,0:T(8,128)S(1)}, f32[4,2,8,768]{3,2,1,0:T(8,128)S(1)}, u32[]{:S(2)}, u32[]{:S(2)}) %collective-permute-start.13) | collective-permute-done | bytes 196640 | tf_op jit(solution)/shard_map/ppermute | solution.py:196
  45.8 1.9 %collective-permute-start.14 = (f32[2,8,768]{2,1,0:T(8,128)S(1)}, f32[2,8,768]{2,1,0:T(8,128)S(1)}, u32[]{:S(2)}, u32[]{:S(2)}) collective-permute-start(f32[2,8,768]{2,1,0:T(8,128)S(1)} %get-tuple-element.21), channel_id=1, source_target_pairs={{0,4},{1,5},{2,6},{3,7},{4,8},{5,9},{6,10},{7,11},{8,12},{9,13},{1... | collective-permute-start | bytes 147464 | tf_op jit(solution)/shard_map/ppermute | solution.py:200
  47.7 1.4 %collective-permute-start.16 = (f32[2,8,768]{2,1,0:T(8,128)S(1)}, f32[2,8,768]{2,1,0:T(8,128)S(1)}, u32[]{:S(2)}, u32[]{:S(2)}) collective-permute-start(f32[2,8,768]{2,1,0:T(8,128)S(1)} %get-tuple-element.22), channel_id=1, source_target_pairs={{0,8},{1,9},{2,10},{3,11},{4,12},{5,13},{6,14},{7,15},{8,0},{9,1},... | collective-permute-start | bytes 147464 | tf_op jit(solution)/shard_map/ppermute | solution.py:202
  49.1 1.4 %collective-permute-start.15 = (f32[2,8,768]{2,1,0:T(8,128)S(1)}, f32[2,8,768]{2,1,0:T(8,128)S(1)}, u32[]{:S(2)}, u32[]{:S(2)}) collective-permute-start(f32[2,8,768]{2,1,0:T(8,128)S(1)} %get-tuple-element.23), channel_id=1, source_target_pairs={{0,12},{1,13},{2,14},{3,15},{4,0},{5,1},{6,2},{7,3},{8,4},{9,5},{1... | collective-permute-start | bytes 147464 | tf_op jit(solution)/shard_map/ppermute | solution.py:201
  51.2 2.1 %collective-permute-done.16 = f32[2,8,768]{2,1,0:T(8,128)S(1)} collective-permute-done((f32[2,8,768]{2,1,0:T(8,128)S(1)}, f32[2,8,768]{2,1,0:T(8,128)S(1)}, u32[]{:S(2)}, u32[]{:S(2)}) %collective-permute-start.16) | collective-permute-done | bytes 49184 | tf_op jit(solution)/shard_map/ppermute | solution.py:202
  (42 shorter events, 4.9 us)
Async XLA Ops:
  0.0 24.4 %copy-start = (bf16[16,2,128,128]{3,2,1,0:T(8,128)(2,1)S(1)}, bf16[16,2,128,128]{3,2,1,0:T(8,128)(2,1)}, u32[]{:S(2)}) copy-start(bf16[16,2,128,128]{3,2,1,0:T(8,128)(2,1)} %a.3) | copy-start | bytes 3145732
  0.0 6.0 %collective-permute-start.1 = (bf16[2,128,128]{2,1,0:T(8,128)(2,1)}, bf16[2,128,128]{2,1,0:T(8,128)(2,1)S(1)}, u32[]{:S(2)}, u32[]{:S(2)}) collective-permute-start(bf16[2,128,128]{2,1,0:T(8,128)(2,1)} %bitcast.21), channel_id=1, source_target_pairs={{16,32},{32,16},{48,64},{64,48},{80,96},{96,80},{112,128},{128,112... | collective-permute-start | bytes 196616 | tf_op jit(solution)/shard_map/ppermute | solution.py:143
  2.0 6.1 %collective-permute-start = (bf16[2,128,128]{2,1,0:T(8,128)(2,1)}, bf16[2,128,128]{2,1,0:T(8,128)(2,1)S(1)}, u32[]{:S(2)}, u32[]{:S(2)}) collective-permute-start(bf16[2,128,128]{2,1,0:T(8,128)(2,1)} %bitcast.22), channel_id=1, source_target_pairs={{0,8},{1,9},{2,10},{3,11},{4,12},{5,13},{6,14},{7,15},{8,0},{9,1},... | collective-permute-start | bytes 196616 | tf_op jit(solution)/shard_map/ppermute | solution.py:142
  5.2 0.9 %copy-start.1 = (bf16[1,2,128,128]{3,2,1,0:T(8,128)(2,1)S(1)}, bf16[1,2,128,128]{3,2,1,0:T(8,128)(2,1)}, u32[]{:S(2)}) copy-start(bf16[1,2,128,128]{3,2,1,0:T(8,128)(2,1)} %param.7) | copy-start | bytes 196612
  6.0 18.3 %copy-start.2 = (s32[256,2]{0,1:T(2,128)S(1)}, s32[256,2]{0,1:T(2,128)}, u32[]{:S(2)}) copy-start(s32[256,2]{0,1:T(2,128)} %param.8) | copy-start | bytes 6148
  6.0 18.3 %copy-start.3 = (s32[32]{0:T(128)S(1)}, s32[32]{0:T(128)}, u32[]{:S(2)}) copy-start(s32[32]{0:T(128)} %agglo.5) | copy-start | bytes 388
  8.1 7.0 %collective-permute-start.2 = (bf16[6,128,128]{2,1,0:T(8,128)(2,1)S(1)}, bf16[6,128,128]{2,1,0:T(8,128)(2,1)S(1)}, u32[]{:S(2)}, u32[]{:S(2)}) collective-permute-start(bf16[6,128,128]{2,1,0:T(8,128)(2,1)S(1)} %pad_maximum_fusion.3), channel_id=1, source_target_pairs={{0,1},{1,2},{2,3},{3,0},{4,5},{5,6},{6,7},{7,4},{8,9},{9,10},{10,1... | collective-permute-start | bytes 589832 | tf_op jit(solution)/shard_map/ppermute | solution.py:153
  9.8 8.9 %collective-permute-start.4 = (bf16[6,128,128]{2,1,0:T(8,128)(2,1)S(1)}, bf16[6,128,128]{2,1,0:T(8,128)(2,1)S(1)}, u32[]{:S(2)}, u32[]{:S(2)}) collective-permute-start(bf16[6,128,128]{2,1,0:T(8,128)(2,1)S(1)} %pad_maximum_fusion.3), channel_id=1, source_target_pairs={{0,3},{1,0},{2,1},{3,2},{4,7},{5,4},{6,5},{7,6},{8,11},{9,8},{10,9... | collective-permute-start | bytes 589832 | tf_op jit(solution)/shard_map/ppermute | solution.py:153
  11.5 7.2 %collective-permute-start.3 = (bf16[6,128,128]{2,1,0:T(8,128)(2,1)S(1)}, bf16[6,128,128]{2,1,0:T(8,128)(2,1)S(1)}, u32[]{:S(2)}, u32[]{:S(2)}) collective-permute-start(bf16[6,128,128]{2,1,0:T(8,128)(2,1)S(1)} %pad_maximum_fusion.3), channel_id=1, source_target_pairs={{0,2},{1,3},{2,0},{3,1},{4,6},{5,7},{6,4},{7,5},{8,10},{9,11},{10,... | collective-permute-start | bytes 589832 | tf_op jit(solution)/shard_map/ppermute | solution.py:153
  18.9 10.5 %collective-permute-start.8 = (bf16[16,128,128]{2,1,0:T(8,128)(2,1)S(1)}, bf16[16,128,128]{2,1,0:T(8,128)(2,1)S(1)}, u32[]{:S(2)}, u32[]{:S(2)}) collective-permute-start(bf16[16,128,128]{2,1,0:T(8,128)(2,1)S(1)} %get-tuple-element.34), channel_id=1, source_target_pairs={{0,12},{1,13},{2,14},{3,15},{4,8},{5,9},{6,10},{7,11},{8,4},{9,5},... | collective-permute-start | bytes 1572872 | tf_op jit(solution)/shard_map/ppermute | solution.py:160
  21.8 9.2 %collective-permute-start.5 = (bf16[16,128,128]{2,1,0:T(8,128)(2,1)S(1)}, bf16[16,128,128]{2,1,0:T(8,128)(2,1)S(1)}, u32[]{:S(2)}, u32[]{:S(2)}) collective-permute-start(bf16[16,128,128]{2,1,0:T(8,128)(2,1)S(1)} %get-tuple-element.34), channel_id=1, source_target_pairs={{0,4},{1,5},{2,6},{3,7},{4,0},{5,1},{6,2},{7,3},{8,12},{9,13},{10,... | collective-permute-start | bytes 1572872 | tf_op jit(solution)/shard_map/ppermute | solution.py:159
  22.0 9.0 %collective-permute-start.7 = (bf16[16,128,128]{2,1,0:T(8,128)(2,1)S(1)}, bf16[16,128,128]{2,1,0:T(8,128)(2,1)S(1)}, u32[]{:S(2)}, u32[]{:S(2)}) collective-permute-start(bf16[16,128,128]{2,1,0:T(8,128)(2,1)S(1)} %get-tuple-element.33.blocks.home), channel_id=1, source_target_pairs={{0,16},{16,0},{32,48},{48,32},{64,80},{80,64},{96,112},{112,96},{1... | collective-permute-start | bytes 1572872 | tf_op jit(solution)/shard_map/ppermute | solution.py:163
  22.3 7.7 %collective-permute-start.6 = (bf16[8,128,128]{2,1,0:T(8,128)(2,1)S(1)}, bf16[8,128,128]{2,1,0:T(8,128)(2,1)S(1)}, u32[]{:S(2)}, u32[]{:S(2)}) collective-permute-start(bf16[8,128,128]{2,1,0:T(8,128)(2,1)S(1)} %pad_maximum_fusion.1), channel_id=1, source_target_pairs={{16,32},{32,16},{48,64},{64,48},{80,96},{96,80},{112,128},{128,112... | collective-permute-start | bytes 786440 | tf_op jit(solution)/shard_map/ppermute | solution.py:161
  29.4 3.4 %collective-permute-start.10 = (bf16[8,128,128]{2,1,0:T(8,128)(2,1)S(1)}, bf16[8,128,128]{2,1,0:T(8,128)(2,1)S(1)}, u32[]{:S(2)}, u32[]{:S(2)}) collective-permute-start(bf16[8,128,128]{2,1,0:T(8,128)(2,1)S(1)} %slice.119), channel_id=1, source_target_pairs={{0,16},{16,0},{32,48},{48,32},{64,80},{80,64},{96,112},{112,96},{1... | collective-permute-start | bytes 786440 | tf_op jit(solution)/shard_map/ppermute | solution.py:178
  31.0 1.8 %collective-permute-start.9 = (bf16[8,128,128]{2,1,0:T(8,128)(2,1)S(1)}, bf16[8,128,128]{2,1,0:T(8,128)(2,1)S(1)}, u32[]{:S(2)}, u32[]{:S(2)}) collective-permute-start(bf16[8,128,128]{2,1,0:T(8,128)(2,1)S(1)} %slice.92), channel_id=1, source_target_pairs={{0,16},{16,0},{32,48},{48,32},{64,80},{80,64},{96,112},{112,96},{1... | collective-permute-start | bytes 786440 | tf_op jit(solution)/shard_map/ppermute | solution.py:179
  31.7 1.2 %copy-start.4 = (s32[16,2]{0,1:T(2,128)S(1)}, s32[16,2]{0,1:T(2,128)}, u32[]{:S(2)}) copy-start(s32[16,2]{0,1:T(2,128)} %param.6) | copy-start | bytes 388
  35.3 7.0 %collective-permute-start.11 = (f32[4,2,8,768]{3,2,1,0:T(8,128)S(1)}, f32[4,2,8,768]{3,2,1,0:T(8,128)S(1)}, u32[]{:S(2)}, u32[]{:S(2)}) collective-permute-start(f32[4,2,8,768]{3,2,1,0:T(8,128)S(1)} %get-tuple-element.18), channel_id=1, source_target_pairs={{0,1},{1,2},{2,3},{3,0},{4,5},{5,6},{6,7},{7,4},{8,9},{9,10},{10,1... | collective-permute-start | bytes 589832 | tf_op jit(solution)/shard_map/ppermute | solution.py:197
  37.2 5.7 %collective-permute-start.12 = (f32[4,2,8,768]{3,2,1,0:T(8,128)S(1)}, f32[4,2,8,768]{3,2,1,0:T(8,128)S(1)}, u32[]{:S(2)}, u32[]{:S(2)}) collective-permute-start(f32[4,2,8,768]{3,2,1,0:T(8,128)S(1)} %get-tuple-element.19), channel_id=1, source_target_pairs={{0,3},{1,0},{2,1},{3,2},{4,7},{5,4},{6,5},{7,6},{8,11},{9,8},{10,9... | collective-permute-start | bytes 589832 | tf_op jit(solution)/shard_map/ppermute | solution.py:198
  38.6 7.2 %collective-permute-start.13 = (f32[4,2,8,768]{3,2,1,0:T(8,128)S(1)}, f32[4,2,8,768]{3,2,1,0:T(8,128)S(1)}, u32[]{:S(2)}, u32[]{:S(2)}) collective-permute-start(f32[4,2,8,768]{3,2,1,0:T(8,128)S(1)} %get-tuple-element.20), channel_id=1, source_target_pairs={{0,2},{1,3},{2,0},{3,1},{4,6},{5,7},{6,4},{7,5},{8,10},{9,11},{10,... | collective-permute-start | bytes 589832 | tf_op jit(solution)/shard_map/ppermute | solution.py:196
  45.8 5.4 %collective-permute-start.14 = (f32[2,8,768]{2,1,0:T(8,128)S(1)}, f32[2,8,768]{2,1,0:T(8,128)S(1)}, u32[]{:S(2)}, u32[]{:S(2)}) collective-permute-start(f32[2,8,768]{2,1,0:T(8,128)S(1)} %get-tuple-element.21), channel_id=1, source_target_pairs={{0,4},{1,5},{2,6},{3,7},{4,8},{5,9},{6,10},{7,11},{8,12},{9,13},{1... | collective-permute-start | bytes 147464 | tf_op jit(solution)/shard_map/ppermute | solution.py:200
  47.7 5.6 %collective-permute-start.16 = (f32[2,8,768]{2,1,0:T(8,128)S(1)}, f32[2,8,768]{2,1,0:T(8,128)S(1)}, u32[]{:S(2)}, u32[]{:S(2)}) collective-permute-start(f32[2,8,768]{2,1,0:T(8,128)S(1)} %get-tuple-element.22), channel_id=1, source_target_pairs={{0,8},{1,9},{2,10},{3,11},{4,12},{5,13},{6,14},{7,15},{8,0},{9,1},... | collective-permute-start | bytes 147464 | tf_op jit(solution)/shard_map/ppermute | solution.py:202
  49.1 4.2 %collective-permute-start.15 = (f32[2,8,768]{2,1,0:T(8,128)S(1)}, f32[2,8,768]{2,1,0:T(8,128)S(1)}, u32[]{:S(2)}, u32[]{:S(2)}) collective-permute-start(f32[2,8,768]{2,1,0:T(8,128)S(1)} %get-tuple-element.23), channel_id=1, source_target_pairs={{0,12},{1,13},{2,14},{3,15},{4,0},{5,1},{6,2},{7,3},{8,4},{9,5},{1... | collective-permute-start | bytes 147464 | tf_op jit(solution)/shard_map/ppermute | solution.py:201
